TPU v7x, 512 devices: a whole 4x4x16 slice. The times are simulated.
512 devices in a mesh: hist: 16 (over z_hi, x, core), user: 32 (over z_lo, y).
Axes of the slice: x: 4, y: 4, z: 16 (z_hi: 2, z_lo: 8; z = z_hi * 8 + z_lo), core: 2. Of those that a mesh axis runs over, the one named last changes fastest.
Arguments:
- cand_embed: bfloat16 [32, 1024, 1024], P('user', 'hist'), may hold values from -6 to 6
- hist_key: bfloat16 [32, 4096, 1024], P('user', 'hist'), may hold values from -6 to 6
- hist_value: bfloat16 [32, 4096, 1024], P('user', 'hist'), may hold values from -6 to 6
- block_owner: int32 [32, 32], P('user'), may hold values from 0 to 3, as said below
- cand_user: int32 [32, 1024], P('user', 'hist'), may hold values from 0 to 3, as said below
- cand_cutoff: int32 [32, 1024], P('user', 'hist'), may hold values from 1 to 4096, as said below
- w_in: bfloat16 [1024, 4096], P('user'), may hold values from -0.1875 to 0.1875
- w_out: bfloat16 [1024, 1024], P('user'), may hold values from -0.1875 to 0.1875
Outputs:
- cand_out: bfloat16 [32, 1024, 1024], P('user', 'hist')
Inputs may be any that keep to these rules, and one draw needn't show every extreme that they name: `block_owner`: in each group the owners never fall along the blocks, and each of the 4 users owns one or more blocks. `cand_user`: every user of a group has candidates. `cand_cutoff`: A candidate's cutoff lies after the first event of its user and not after the user's last event plus one.
All inputs are finite; a program needn't handle non-finite values.
Results may differ from a plain program's by a relative error of at most 0.0055.
Values may be sent and summed in bfloat16 or wider, within the bound.
No kernel may reach another device: no remote copies, remote signals or barrier semaphores. Data moves between devices by JAX's collectives and lax.ppermute only.
A program may use at most 64 MiB of HBM per device.

v0:
```python
import jax
import jax.numpy as jnp
from jax import lax
from jax.sharding import PartitionSpec as P

D = 1024
HEADS = 8
HEAD = 128
BLOCK = 128


def shifted(value, axis, steps):
    count = lax.axis_size(axis)
    pairs = [(source, (source + steps) % count) for source in range(count)]
    return lax.ppermute(value, axis, pairs)


def layer_norm(values):
    mean = jnp.mean(values, axis=-1, keepdims=True)
    centred = values - mean
    var = jnp.mean(centred * centred, axis=-1, keepdims=True)
    return centred * lax.rsqrt(var + 1e-05)


def visible_count(owner, users, cutoffs):
    starts = jnp.arange(owner.shape[0], dtype=jnp.int32) * BLOCK
    inside = jnp.clip(cutoffs[:, None] - starts[None, :], 0, BLOCK)
    same = owner[None, :] == users[:, None]
    return jnp.sum(jnp.where(same, inside, 0), axis=1).astype(jnp.float32)


def pointwise(query, labels, keys, values, event_owner, positions):
    rows = query.shape[0]
    count = keys.shape[0]
    users = labels[:, 0].astype(jnp.int32)
    cutoffs = labels[:, 1].astype(jnp.int32)
    mask = (event_owner[None, :] == users[:, None]) & (positions[None, :] < cutoffs[:, None])
    q_heads = query.reshape(rows, HEADS, HEAD)
    k_heads = keys.reshape(count, HEADS, HEAD)
    scores = jnp.einsum(
        "chd,ehd->hce", q_heads, k_heads, preferred_element_type=jnp.float32
    ) * HEAD ** (-0.5)
    weight = (jax.nn.silu(scores) * mask[None, :, :]).astype(jnp.bfloat16)
    v_heads = values.reshape(count, HEADS, HEAD)
    summed = jnp.einsum("hce,ehd->chd", weight, v_heads, preferred_element_type=jnp.float32)
    return summed.reshape(rows, HEADS * HEAD)


def travel_single(query, labels, keys, values, event_owner, positions, steps):

    def turn(step, carry):
        tile, tags, sums = carry
        sums = sums + pointwise(tile, tags, keys, values, event_owner, positions)
        tile = shifted(tile, "hist", 1)
        sums, tags = shifted((sums, tags), "hist", 1)
        return (tile, tags, sums)

    empty = jnp.zeros((query.shape[0], D), jnp.float32)
    return lax.fori_loop(0, steps, turn, (query, labels, empty))[2]


def body(cand_embed, hist_key, hist_value, block_owner, cand_user, cand_cutoff, w_in, w_out):
    x = cand_embed[0]
    keys = hist_key[0]
    values = hist_value[0]
    owner = block_owner[0]
    users = cand_user[0]
    cutoffs = cand_cutoff[0]
    rows = x.shape[0]
    events = keys.shape[0]
    steps = lax.axis_size("hist")
    index = lax.axis_index("hist")
    normed = layer_norm(x.astype(jnp.float32)).astype(jnp.bfloat16)
    columns = normed
    proj = jnp.dot(
        columns,
        lax.all_gather(w_in, "user", axis=0, tiled=True),
        preferred_element_type=jnp.float32,
    )
    proj = jax.nn.silu(proj).astype(jnp.bfloat16)
    count = visible_count(owner, users, cutoffs)
    local_blocks = lax.dynamic_slice_in_dim(owner, index * (events // BLOCK), events // BLOCK, 0)
    event_owner = jnp.repeat(local_blocks, BLOCK)
    positions = index * events + jnp.arange(events, dtype=jnp.int32)
    labels = jnp.stack([users.astype(jnp.float32), cutoffs.astype(jnp.float32)], axis=1)
    query = proj[:, 2 * D : 3 * D]
    hist_sum = travel_single(query, labels, keys, values, event_owner, positions, steps)
    gate = proj[:, 0:D].astype(jnp.float32)
    val = proj[:, D : 2 * D].astype(jnp.float32).reshape(rows, HEADS, HEAD)
    q_heads = query.astype(jnp.float32).reshape(rows, HEADS, HEAD)
    key_self = proj[:, 3 * D : 4 * D].astype(jnp.float32).reshape(rows, HEADS, HEAD)
    self_weight = jax.nn.silu(jnp.sum(q_heads * key_self, axis=-1) * HEAD ** (-0.5))
    attended = (hist_sum.reshape(rows, HEADS, HEAD) + self_weight[:, :, None] * val) / (
        count[:, None, None] + 1.0
    )
    mixed = (layer_norm(attended).reshape(rows, D) * gate).astype(jnp.bfloat16)
    columns = mixed
    projected = jnp.dot(
        columns,
        lax.all_gather(w_out, "user", axis=0, tiled=True),
        preferred_element_type=jnp.float32,
    )
    out = (x.astype(jnp.float32) + projected).astype(jnp.bfloat16)
    return out[None]


def solution(mesh):
    return jax.shard_map(
        body,
        mesh=mesh,
        in_specs=(
            P("user", "hist", None),
            P("user", "hist", None),
            P("user", "hist", None),
            P("user", None),
            P("user", "hist"),
            P("user", "hist"),
            P("user", None),
            P("user", None),
        ),
        out_specs=P("user", "hist", None),
        check_vma=False,
    )
```

profile of v0, /device:TPU:8, one launch (start us, length us, event | category | flops | bytes accessed | tf_op | source)
XLA Modules:
  0.0 666.6 jit_solution(7719804735872092616)
XLA Ops:
  12.4 238.7 %all-gather.3.cloned.1.call-done = bf16[1024,4096]{1,0:T(8,128)(2,1)} async-done(((bf16[32,4096]{1,0:T(8,128)(2,1)}), bf16[1024,4096]{1,0:T(8,128)(2,1)}) %all-gather.3.cloned.1.call-update) | async-done | bytes 8388624 | tf_op jit(solution)/shard_map/all_gather | solution.py:77
  251.1 5.1 multiply_convert_fusion.1
  257.1 397.1 %while.15 = (s32[]{:T(128)}, bf16[64,1024]{1,0:T(8,128)(2,1)S(1)}, f32[64,2]{0,1:T(2,128)S(1)}, f32[64,1024]{1,0:T(8,128)S(1)}, bf16[1,256,1024]{2,1,0:T(8,128)(...) while((s32[]{:T(128)}, bf16[64,1024]{1,0:T(8,128)(2,1)S(1)}, ...), condition=%wide.region_3.4_spmd.clone, body=%wide.region_2.3_spmd.clone.sunk | while | flops 68157824 | bytes 6300385 | solution.py:59
  258.0 1.9 collective-permute-start.2
  260.0 3.7 collective-permute-start
  263.7 1.9 collective-permute-start.1
  265.6 17.3 %collective-permute-done.1 = f32[64,2]{0,1:T(2,128)S(1)} collective-permute-done((f32[64,2]{0,1:T(2,128)S(1)}, f32[64,2]{0,1:T(2,128)S(1)}, u32[]{:S(2)}, u32[]{:S(2)}) %collective-permute-start.1) | collective-permute-done | bytes 544 | tf_op jit(solution)/shard_map/while/body/eval_jaxpr/ppermute | solution.py:15
  283.9 1.9 collective-permute-start.2
  285.8 1.9 collective-permute-start
  287.8 1.9 collective-permute-start.1
  289.7 17.1 %collective-permute-done.1 = f32[64,2]{0,1:T(2,128)S(1)} collective-permute-done((f32[64,2]{0,1:T(2,128)S(1)}, f32[64,2]{0,1:T(2,128)S(1)}, u32[]{:S(2)}, u32[]{:S(2)}) %collective-permute-start.1) | collective-permute-done | bytes 544 | tf_op jit(solution)/shard_map/while/body/eval_jaxpr/ppermute | solution.py:15
  307.7 1.9 collective-permute-start.2
  309.7 1.9 collective-permute-start
  311.6 1.9 collective-permute-start.1
  313.5 18.6 %collective-permute-done.1 = f32[64,2]{0,1:T(2,128)S(1)} collective-permute-done((f32[64,2]{0,1:T(2,128)S(1)}, f32[64,2]{0,1:T(2,128)S(1)}, u32[]{:S(2)}, u32[]{:S(2)}) %collective-permute-start.1) | collective-permute-done | bytes 544 | tf_op jit(solution)/shard_map/while/body/eval_jaxpr/ppermute | solution.py:15
  333.1 1.9 collective-permute-start.2
  335.0 1.9 collective-permute-start
  336.9 1.9 collective-permute-start.1
  338.9 18.4 %collective-permute-done.1 = f32[64,2]{0,1:T(2,128)S(1)} collective-permute-done((f32[64,2]{0,1:T(2,128)S(1)}, f32[64,2]{0,1:T(2,128)S(1)}, u32[]{:S(2)}, u32[]{:S(2)}) %collective-permute-start.1) | collective-permute-done | bytes 544 | tf_op jit(solution)/shard_map/while/body/eval_jaxpr/ppermute | solution.py:15
  358.2 1.9 collective-permute-start.2
  360.2 1.9 collective-permute-start
  362.1 1.9 collective-permute-start.1
  364.0 18.4 %collective-permute-done.1 = f32[64,2]{0,1:T(2,128)S(1)} collective-permute-done((f32[64,2]{0,1:T(2,128)S(1)}, f32[64,2]{0,1:T(2,128)S(1)}, u32[]{:S(2)}, u32[]{:S(2)}) %collective-permute-start.1) | collective-permute-done | bytes 544 | tf_op jit(solution)/shard_map/while/body/eval_jaxpr/ppermute | solution.py:15
  383.5 1.9 collective-permute-start.2
  385.4 1.9 collective-permute-start
  387.3 1.9 collective-permute-start.1
  389.3 18.5 %collective-permute-done.1 = f32[64,2]{0,1:T(2,128)S(1)} collective-permute-done((f32[64,2]{0,1:T(2,128)S(1)}, f32[64,2]{0,1:T(2,128)S(1)}, u32[]{:S(2)}, u32[]{:S(2)}) %collective-permute-start.1) | collective-permute-done | bytes 544 | tf_op jit(solution)/shard_map/while/body/eval_jaxpr/ppermute | solution.py:15
  408.7 1.9 collective-permute-start.2
  410.6 1.9 collective-permute-start
  412.5 1.9 collective-permute-start.1
  414.5 18.5 %collective-permute-done.1 = f32[64,2]{0,1:T(2,128)S(1)} collective-permute-done((f32[64,2]{0,1:T(2,128)S(1)}, f32[64,2]{0,1:T(2,128)S(1)}, u32[]{:S(2)}, u32[]{:S(2)}) %collective-permute-start.1) | collective-permute-done | bytes 544 | tf_op jit(solution)/shard_map/while/body/eval_jaxpr/ppermute | solution.py:15
  433.9 1.9 collective-permute-start.2
  435.9 1.9 collective-permute-start
  437.8 1.9 collective-permute-start.1
  439.7 18.5 %collective-permute-done.1 = f32[64,2]{0,1:T(2,128)S(1)} collective-permute-done((f32[64,2]{0,1:T(2,128)S(1)}, f32[64,2]{0,1:T(2,128)S(1)}, u32[]{:S(2)}, u32[]{:S(2)}) %collective-permute-start.1) | collective-permute-done | bytes 544 | tf_op jit(solution)/shard_map/while/body/eval_jaxpr/ppermute | solution.py:15
  459.2 1.9 collective-permute-start.2
  461.1 1.9 collective-permute-start
  463.0 1.9 collective-permute-start.1
  464.9 18.5 %collective-permute-done.1 = f32[64,2]{0,1:T(2,128)S(1)} collective-permute-done((f32[64,2]{0,1:T(2,128)S(1)}, f32[64,2]{0,1:T(2,128)S(1)}, u32[]{:S(2)}, u32[]{:S(2)}) %collective-permute-start.1) | collective-permute-done | bytes 544 | tf_op jit(solution)/shard_map/while/body/eval_jaxpr/ppermute | solution.py:15
  484.4 1.9 collective-permute-start.2
  486.3 1.9 collective-permute-start
  488.2 1.9 collective-permute-start.1
  490.2 18.5 %collective-permute-done.1 = f32[64,2]{0,1:T(2,128)S(1)} collective-permute-done((f32[64,2]{0,1:T(2,128)S(1)}, f32[64,2]{0,1:T(2,128)S(1)}, u32[]{:S(2)}, u32[]{:S(2)}) %collective-permute-start.1) | collective-permute-done | bytes 544 | tf_op jit(solution)/shard_map/while/body/eval_jaxpr/ppermute | solution.py:15
  509.6 1.9 collective-permute-start.2
  511.5 1.9 collective-permute-start
  513.5 1.9 collective-permute-start.1
  515.4 18.5 %collective-permute-done.1 = f32[64,2]{0,1:T(2,128)S(1)} collective-permute-done((f32[64,2]{0,1:T(2,128)S(1)}, f32[64,2]{0,1:T(2,128)S(1)}, u32[]{:S(2)}, u32[]{:S(2)}) %collective-permute-start.1) | collective-permute-done | bytes 544 | tf_op jit(solution)/shard_map/while/body/eval_jaxpr/ppermute | solution.py:15
  534.8 1.9 collective-permute-start.2
  536.8 1.9 collective-permute-start
  538.7 1.9 collective-permute-start.1
  540.6 18.5 %collective-permute-done.1 = f32[64,2]{0,1:T(2,128)S(1)} collective-permute-done((f32[64,2]{0,1:T(2,128)S(1)}, f32[64,2]{0,1:T(2,128)S(1)}, u32[]{:S(2)}, u32[]{:S(2)}) %collective-permute-start.1) | collective-permute-done | bytes 544 | tf_op jit(solution)/shard_map/while/body/eval_jaxpr/ppermute | solution.py:15
  560.1 1.9 collective-permute-start.2
  562.0 1.9 collective-permute-start
  563.9 1.9 collective-permute-start.1
  565.9 18.5 %collective-permute-done.1 = f32[64,2]{0,1:T(2,128)S(1)} collective-permute-done((f32[64,2]{0,1:T(2,128)S(1)}, f32[64,2]{0,1:T(2,128)S(1)}, u32[]{:S(2)}, u32[]{:S(2)}) %collective-permute-start.1) | collective-permute-done | bytes 544 | tf_op jit(solution)/shard_map/while/body/eval_jaxpr/ppermute | solution.py:15
  591.1 18.5 %collective-permute-done.1 = f32[64,2]{0,1:T(2,128)S(1)} collective-permute-done((f32[64,2]{0,1:T(2,128)S(1)}, f32[64,2]{0,1:T(2,128)S(1)}, u32[]{:S(2)}, u32[]{:S(2)}) %collective-permute-start.1) | collective-permute-done | bytes 544 | tf_op jit(solution)/shard_map/while/body/eval_jaxpr/ppermute | solution.py:15
  610.5 1.9 collective-permute-start.2
  612.5 1.9 collective-permute-start
  614.4 1.9 collective-permute-start.1
  616.3 16.9 %collective-permute-done.1 = f32[64,2]{0,1:T(2,128)S(1)} collective-permute-done((f32[64,2]{0,1:T(2,128)S(1)}, f32[64,2]{0,1:T(2,128)S(1)}, u32[]{:S(2)}, u32[]{:S(2)}) %collective-permute-start.1) | collective-permute-done | bytes 544 | tf_op jit(solution)/shard_map/while/body/eval_jaxpr/ppermute | solution.py:15
  636.2 1.9 collective-permute-start
  638.1 1.9 collective-permute-start.1
  640.0 14.2 %collective-permute-done.1 = f32[64,2]{0,1:T(2,128)S(1)} collective-permute-done((f32[64,2]{0,1:T(2,128)S(1)}, f32[64,2]{0,1:T(2,128)S(1)}, u32[]{:S(2)}, u32[]{:S(2)}) %collective-permute-start.1) | collective-permute-done | bytes 544 | tf_op jit(solution)/shard_map/while/body/eval_jaxpr/ppermute | solution.py:15
  656.7 3.0 fusion.20
  (237 shorter events, 31.7 us)
Async XLA Ops:
  6.5 244.6 %all-gather.3.cloned.1.call-start = ((), (), s32[]{:S(2)}) async-start(), calls=%async_computation | async-start | bytes 8650752 | tf_op jit(solution)/shard_map/all_gather | solution.py:77
  7.3 249.8 %copy-start = (bf16[1,256,1024]{2,1,0:T(8,128)(2,1)S(1)}, bf16[1,256,1024]{2,1,0:T(8,128)(2,1)}, u32[]{:S(2)}) copy-start(bf16[1,256,1024]{2,1,0:T(8,128)(2,1)} %param.11) | copy-start | bytes 1572868
  7.3 249.8 %copy-start.1 = (bf16[1,256,1024]{2,1,0:T(8,128)(2,1)S(1)}, bf16[1,256,1024]{2,1,0:T(8,128)(2,1)}, u32[]{:S(2)}) copy-start(bf16[1,256,1024]{2,1,0:T(8,128)(2,1)} %param.12) | copy-start | bytes 1572868
  7.3 649.1 %all-gather.5.cloned.1.call-start = ((), (), s32[]{:S(2)}) async-start(), calls=%async_computation.1 | async-start | bytes 2162688 | tf_op jit(solution)/shard_map/all_gather | solution.py:100
  256.3 0.8 copy-start.3
  257.1 399.7 %copy-start.2 = (bf16[1,64,1024]{2,1,0:T(8,128)(2,1)S(1)}, bf16[1,64,1024]{2,1,0:T(8,128)(2,1)}, u32[]{:S(2)}) copy-start(bf16[1,64,1024]{2,1,0:T(8,128)(2,1)} %param.10) | copy-start | bytes 393220
  258.0 24.9 %collective-permute-start.2 = (f32[64,1024]{1,0:T(8,128)S(1)}, f32[64,1024]{1,0:T(8,128)S(1)}, u32[]{:S(2)}, u32[]{:S(2)}) collective-permute-start(f32[64,1024]{1,0:T(8,128)S(1)} %bitcast_add_fusion.2), channel_id=1, source_target_pairs={{0,32},{32,64},{64,96},{96,128},{128,160},{160,192},{192,224},{224... | collective-permute-start | bytes 786440 | tf_op jit(solution)/shard_map/while/body/eval_jaxpr/ppermute | solution.py:15
  260.0 22.9 %collective-permute-start = (bf16[64,1024]{1,0:T(8,128)(2,1)S(1)}, bf16[64,1024]{1,0:T(8,128)(2,1)S(1)}, u32[]{:S(2)}, u32[]{:S(2)}) collective-permute-start(bf16[64,1024]{1,0:T(8,128)(2,1)S(1)} %copy.84), channel_id=1, source_target_pairs={{0,32},{32,64},{64,96},{96,128},{128,160},{160,192},{192,224},{224... | collective-permute-start | bytes 393224 | tf_op jit(solution)/shard_map/while/body/eval_jaxpr/ppermute | solution.py:15
  263.7 19.3 %collective-permute-start.1 = (f32[64,2]{0,1:T(2,128)S(1)}, f32[64,2]{0,1:T(2,128)S(1)}, u32[]{:S(2)}, u32[]{:S(2)}) collective-permute-start(f32[64,2]{0,1:T(2,128)S(1)} %copy.85), channel_id=1, source_target_pairs={{0,32},{32,64},{64,96},{96,128},{128,160},{160,192},{192,224},{224... | collective-permute-start | bytes 1544 | tf_op jit(solution)/shard_map/while/body/eval_jaxpr/ppermute | solution.py:15
  283.9 22.9 %collective-permute-start.2 = (f32[64,1024]{1,0:T(8,128)S(1)}, f32[64,1024]{1,0:T(8,128)S(1)}, u32[]{:S(2)}, u32[]{:S(2)}) collective-permute-start(f32[64,1024]{1,0:T(8,128)S(1)} %bitcast_add_fusion.2), channel_id=1, source_target_pairs={{0,32},{32,64},{64,96},{96,128},{128,160},{160,192},{192,224},{224... | collective-permute-start | bytes 786440 | tf_op jit(solution)/shard_map/while/body/eval_jaxpr/ppermute | solution.py:15
  285.8 20.9 %collective-permute-start = (bf16[64,1024]{1,0:T(8,128)(2,1)S(1)}, bf16[64,1024]{1,0:T(8,128)(2,1)S(1)}, u32[]{:S(2)}, u32[]{:S(2)}) collective-permute-start(bf16[64,1024]{1,0:T(8,128)(2,1)S(1)} %copy.84), channel_id=1, source_target_pairs={{0,32},{32,64},{64,96},{96,128},{128,160},{160,192},{192,224},{224... | collective-permute-start | bytes 393224 | tf_op jit(solution)/shard_map/while/body/eval_jaxpr/ppermute | solution.py:15
  287.8 19.0 %collective-permute-start.1 = (f32[64,2]{0,1:T(2,128)S(1)}, f32[64,2]{0,1:T(2,128)S(1)}, u32[]{:S(2)}, u32[]{:S(2)}) collective-permute-start(f32[64,2]{0,1:T(2,128)S(1)} %copy.85), channel_id=1, source_target_pairs={{0,32},{32,64},{64,96},{96,128},{128,160},{160,192},{192,224},{224... | collective-permute-start | bytes 1544 | tf_op jit(solution)/shard_map/while/body/eval_jaxpr/ppermute | solution.py:15
  307.7 24.3 %collective-permute-start.2 = (f32[64,1024]{1,0:T(8,128)S(1)}, f32[64,1024]{1,0:T(8,128)S(1)}, u32[]{:S(2)}, u32[]{:S(2)}) collective-permute-start(f32[64,1024]{1,0:T(8,128)S(1)} %bitcast_add_fusion.2), channel_id=1, source_target_pairs={{0,32},{32,64},{64,96},{96,128},{128,160},{160,192},{192,224},{224... | collective-permute-start | bytes 786440 | tf_op jit(solution)/shard_map/while/body/eval_jaxpr/ppermute | solution.py:15
  309.7 22.4 %collective-permute-start = (bf16[64,1024]{1,0:T(8,128)(2,1)S(1)}, bf16[64,1024]{1,0:T(8,128)(2,1)S(1)}, u32[]{:S(2)}, u32[]{:S(2)}) collective-permute-start(bf16[64,1024]{1,0:T(8,128)(2,1)S(1)} %copy.84), channel_id=1, source_target_pairs={{0,32},{32,64},{64,96},{96,128},{128,160},{160,192},{192,224},{224... | collective-permute-start | bytes 393224 | tf_op jit(solution)/shard_map/while/body/eval_jaxpr/ppermute | solution.py:15
  311.6 20.5 %collective-permute-start.1 = (f32[64,2]{0,1:T(2,128)S(1)}, f32[64,2]{0,1:T(2,128)S(1)}, u32[]{:S(2)}, u32[]{:S(2)}) collective-permute-start(f32[64,2]{0,1:T(2,128)S(1)} %copy.85), channel_id=1, source_target_pairs={{0,32},{32,64},{64,96},{96,128},{128,160},{160,192},{192,224},{224... | collective-permute-start | bytes 1544 | tf_op jit(solution)/shard_map/while/body/eval_jaxpr/ppermute | solution.py:15
  333.1 24.2 %collective-permute-start.2 = (f32[64,1024]{1,0:T(8,128)S(1)}, f32[64,1024]{1,0:T(8,128)S(1)}, u32[]{:S(2)}, u32[]{:S(2)}) collective-permute-start(f32[64,1024]{1,0:T(8,128)S(1)} %bitcast_add_fusion.2), channel_id=1, source_target_pairs={{0,32},{32,64},{64,96},{96,128},{128,160},{160,192},{192,224},{224... | collective-permute-start | bytes 786440 | tf_op jit(solution)/shard_map/while/body/eval_jaxpr/ppermute | solution.py:15
  335.0 22.3 %collective-permute-start = (bf16[64,1024]{1,0:T(8,128)(2,1)S(1)}, bf16[64,1024]{1,0:T(8,128)(2,1)S(1)}, u32[]{:S(2)}, u32[]{:S(2)}) collective-permute-start(bf16[64,1024]{1,0:T(8,128)(2,1)S(1)} %copy.84), channel_id=1, source_target_pairs={{0,32},{32,64},{64,96},{96,128},{128,160},{160,192},{192,224},{224... | collective-permute-start | bytes 393224 | tf_op jit(solution)/shard_map/while/body/eval_jaxpr/ppermute | solution.py:15
  336.9 20.3 %collective-permute-start.1 = (f32[64,2]{0,1:T(2,128)S(1)}, f32[64,2]{0,1:T(2,128)S(1)}, u32[]{:S(2)}, u32[]{:S(2)}) collective-permute-start(f32[64,2]{0,1:T(2,128)S(1)} %copy.85), channel_id=1, source_target_pairs={{0,32},{32,64},{64,96},{96,128},{128,160},{160,192},{192,224},{224... | collective-permute-start | bytes 1544 | tf_op jit(solution)/shard_map/while/body/eval_jaxpr/ppermute | solution.py:15
  358.2 24.2 %collective-permute-start.2 = (f32[64,1024]{1,0:T(8,128)S(1)}, f32[64,1024]{1,0:T(8,128)S(1)}, u32[]{:S(2)}, u32[]{:S(2)}) collective-permute-start(f32[64,1024]{1,0:T(8,128)S(1)} %bitcast_add_fusion.2), channel_id=1, source_target_pairs={{0,32},{32,64},{64,96},{96,128},{128,160},{160,192},{192,224},{224... | collective-permute-start | bytes 786440 | tf_op jit(solution)/shard_map/while/body/eval_jaxpr/ppermute | solution.py:15
  360.2 22.3 %collective-permute-start = (bf16[64,1024]{1,0:T(8,128)(2,1)S(1)}, bf16[64,1024]{1,0:T(8,128)(2,1)S(1)}, u32[]{:S(2)}, u32[]{:S(2)}) collective-permute-start(bf16[64,1024]{1,0:T(8,128)(2,1)S(1)} %copy.84), channel_id=1, source_target_pairs={{0,32},{32,64},{64,96},{96,128},{128,160},{160,192},{192,224},{224... | collective-permute-start | bytes 393224 | tf_op jit(solution)/shard_map/while/body/eval_jaxpr/ppermute | solution.py:15
  362.1 20.4 %collective-permute-start.1 = (f32[64,2]{0,1:T(2,128)S(1)}, f32[64,2]{0,1:T(2,128)S(1)}, u32[]{:S(2)}, u32[]{:S(2)}) collective-permute-start(f32[64,2]{0,1:T(2,128)S(1)} %copy.85), channel_id=1, source_target_pairs={{0,32},{32,64},{64,96},{96,128},{128,160},{160,192},{192,224},{224... | collective-permute-start | bytes 1544 | tf_op jit(solution)/shard_map/while/body/eval_jaxpr/ppermute | solution.py:15
  383.5 24.2 %collective-permute-start.2 = (f32[64,1024]{1,0:T(8,128)S(1)}, f32[64,1024]{1,0:T(8,128)S(1)}, u32[]{:S(2)}, u32[]{:S(2)}) collective-permute-start(f32[64,1024]{1,0:T(8,128)S(1)} %bitcast_add_fusion.2), channel_id=1, source_target_pairs={{0,32},{32,64},{64,96},{96,128},{128,160},{160,192},{192,224},{224... | collective-permute-start | bytes 786440 | tf_op jit(solution)/shard_map/while/body/eval_jaxpr/ppermute | solution.py:15
  385.4 22.3 %collective-permute-start = (bf16[64,1024]{1,0:T(8,128)(2,1)S(1)}, bf16[64,1024]{1,0:T(8,128)(2,1)S(1)}, u32[]{:S(2)}, u32[]{:S(2)}) collective-permute-start(bf16[64,1024]{1,0:T(8,128)(2,1)S(1)} %copy.84), channel_id=1, source_target_pairs={{0,32},{32,64},{64,96},{96,128},{128,160},{160,192},{192,224},{224... | collective-permute-start | bytes 393224 | tf_op jit(solution)/shard_map/while/body/eval_jaxpr/ppermute | solution.py:15
  387.3 20.4 %collective-permute-start.1 = (f32[64,2]{0,1:T(2,128)S(1)}, f32[64,2]{0,1:T(2,128)S(1)}, u32[]{:S(2)}, u32[]{:S(2)}) collective-permute-start(f32[64,2]{0,1:T(2,128)S(1)} %copy.85), channel_id=1, source_target_pairs={{0,32},{32,64},{64,96},{96,128},{128,160},{160,192},{192,224},{224... | collective-permute-start | bytes 1544 | tf_op jit(solution)/shard_map/while/body/eval_jaxpr/ppermute | solution.py:15
  408.7 24.2 %collective-permute-start.2 = (f32[64,1024]{1,0:T(8,128)S(1)}, f32[64,1024]{1,0:T(8,128)S(1)}, u32[]{:S(2)}, u32[]{:S(2)}) collective-permute-start(f32[64,1024]{1,0:T(8,128)S(1)} %bitcast_add_fusion.2), channel_id=1, source_target_pairs={{0,32},{32,64},{64,96},{96,128},{128,160},{160,192},{192,224},{224... | collective-permute-start | bytes 786440 | tf_op jit(solution)/shard_map/while/body/eval_jaxpr/ppermute | solution.py:15
  410.6 22.3 %collective-permute-start = (bf16[64,1024]{1,0:T(8,128)(2,1)S(1)}, bf16[64,1024]{1,0:T(8,128)(2,1)S(1)}, u32[]{:S(2)}, u32[]{:S(2)}) collective-permute-start(bf16[64,1024]{1,0:T(8,128)(2,1)S(1)} %copy.84), channel_id=1, source_target_pairs={{0,32},{32,64},{64,96},{96,128},{128,160},{160,192},{192,224},{224... | collective-permute-start | bytes 393224 | tf_op jit(solution)/shard_map/while/body/eval_jaxpr/ppermute | solution.py:15
  412.5 20.4 %collective-permute-start.1 = (f32[64,2]{0,1:T(2,128)S(1)}, f32[64,2]{0,1:T(2,128)S(1)}, u32[]{:S(2)}, u32[]{:S(2)}) collective-permute-start(f32[64,2]{0,1:T(2,128)S(1)} %copy.85), channel_id=1, source_target_pairs={{0,32},{32,64},{64,96},{96,128},{128,160},{160,192},{192,224},{224... | collective-permute-start | bytes 1544 | tf_op jit(solution)/shard_map/while/body/eval_jaxpr/ppermute | solution.py:15
  433.9 24.2 %collective-permute-start.2 = (f32[64,1024]{1,0:T(8,128)S(1)}, f32[64,1024]{1,0:T(8,128)S(1)}, u32[]{:S(2)}, u32[]{:S(2)}) collective-permute-start(f32[64,1024]{1,0:T(8,128)S(1)} %bitcast_add_fusion.2), channel_id=1, source_target_pairs={{0,32},{32,64},{64,96},{96,128},{128,160},{160,192},{192,224},{224... | collective-permute-start | bytes 786440 | tf_op jit(solution)/shard_map/while/body/eval_jaxpr/ppermute | solution.py:15
  435.9 22.3 %collective-permute-start = (bf16[64,1024]{1,0:T(8,128)(2,1)S(1)}, bf16[64,1024]{1,0:T(8,128)(2,1)S(1)}, u32[]{:S(2)}, u32[]{:S(2)}) collective-permute-start(bf16[64,1024]{1,0:T(8,128)(2,1)S(1)} %copy.84), channel_id=1, source_target_pairs={{0,32},{32,64},{64,96},{96,128},{128,160},{160,192},{192,224},{224... | collective-permute-start | bytes 393224 | tf_op jit(solution)/shard_map/while/body/eval_jaxpr/ppermute | solution.py:15
  437.8 20.4 %collective-permute-start.1 = (f32[64,2]{0,1:T(2,128)S(1)}, f32[64,2]{0,1:T(2,128)S(1)}, u32[]{:S(2)}, u32[]{:S(2)}) collective-permute-start(f32[64,2]{0,1:T(2,128)S(1)} %copy.85), channel_id=1, source_target_pairs={{0,32},{32,64},{64,96},{96,128},{128,160},{160,192},{192,224},{224... | collective-permute-start | bytes 1544 | tf_op jit(solution)/shard_map/while/body/eval_jaxpr/ppermute | solution.py:15
  459.2 24.2 %collective-permute-start.2 = (f32[64,1024]{1,0:T(8,128)S(1)}, f32[64,1024]{1,0:T(8,128)S(1)}, u32[]{:S(2)}, u32[]{:S(2)}) collective-permute-start(f32[64,1024]{1,0:T(8,128)S(1)} %bitcast_add_fusion.2), channel_id=1, source_target_pairs={{0,32},{32,64},{64,96},{96,128},{128,160},{160,192},{192,224},{224... | collective-permute-start | bytes 786440 | tf_op jit(solution)/shard_map/while/body/eval_jaxpr/ppermute | solution.py:15
  461.1 22.3 %collective-permute-start = (bf16[64,1024]{1,0:T(8,128)(2,1)S(1)}, bf16[64,1024]{1,0:T(8,128)(2,1)S(1)}, u32[]{:S(2)}, u32[]{:S(2)}) collective-permute-start(bf16[64,1024]{1,0:T(8,128)(2,1)S(1)} %copy.84), channel_id=1, source_target_pairs={{0,32},{32,64},{64,96},{96,128},{128,160},{160,192},{192,224},{224... | collective-permute-start | bytes 393224 | tf_op jit(solution)/shard_map/while/body/eval_jaxpr/ppermute | solution.py:15
  463.0 20.4 %collective-permute-start.1 = (f32[64,2]{0,1:T(2,128)S(1)}, f32[64,2]{0,1:T(2,128)S(1)}, u32[]{:S(2)}, u32[]{:S(2)}) collective-permute-start(f32[64,2]{0,1:T(2,128)S(1)} %copy.85), channel_id=1, source_target_pairs={{0,32},{32,64},{64,96},{96,128},{128,160},{160,192},{192,224},{224... | collective-permute-start | bytes 1544 | tf_op jit(solution)/shard_map/while/body/eval_jaxpr/ppermute | solution.py:15
  484.4 24.2 %collective-permute-start.2 = (f32[64,1024]{1,0:T(8,128)S(1)}, f32[64,1024]{1,0:T(8,128)S(1)}, u32[]{:S(2)}, u32[]{:S(2)}) collective-permute-start(f32[64,1024]{1,0:T(8,128)S(1)} %bitcast_add_fusion.2), channel_id=1, source_target_pairs={{0,32},{32,64},{64,96},{96,128},{128,160},{160,192},{192,224},{224... | collective-permute-start | bytes 786440 | tf_op jit(solution)/shard_map/while/body/eval_jaxpr/ppermute | solution.py:15
  486.3 22.3 %collective-permute-start = (bf16[64,1024]{1,0:T(8,128)(2,1)S(1)}, bf16[64,1024]{1,0:T(8,128)(2,1)S(1)}, u32[]{:S(2)}, u32[]{:S(2)}) collective-permute-start(bf16[64,1024]{1,0:T(8,128)(2,1)S(1)} %copy.84), channel_id=1, source_target_pairs={{0,32},{32,64},{64,96},{96,128},{128,160},{160,192},{192,224},{224... | collective-permute-start | bytes 393224 | tf_op jit(solution)/shard_map/while/body/eval_jaxpr/ppermute | solution.py:15
  488.2 20.4 %collective-permute-start.1 = (f32[64,2]{0,1:T(2,128)S(1)}, f32[64,2]{0,1:T(2,128)S(1)}, u32[]{:S(2)}, u32[]{:S(2)}) collective-permute-start(f32[64,2]{0,1:T(2,128)S(1)} %copy.85), channel_id=1, source_target_pairs={{0,32},{32,64},{64,96},{96,128},{128,160},{160,192},{192,224},{224... | collective-permute-start | bytes 1544 | tf_op jit(solution)/shard_map/while/body/eval_jaxpr/ppermute | solution.py:15
  509.6 24.2 %collective-permute-start.2 = (f32[64,1024]{1,0:T(8,128)S(1)}, f32[64,1024]{1,0:T(8,128)S(1)}, u32[]{:S(2)}, u32[]{:S(2)}) collective-permute-start(f32[64,1024]{1,0:T(8,128)S(1)} %bitcast_add_fusion.2), channel_id=1, source_target_pairs={{0,32},{32,64},{64,96},{96,128},{128,160},{160,192},{192,224},{224... | collective-permute-start | bytes 786440 | tf_op jit(solution)/shard_map/while/body/eval_jaxpr/ppermute | solution.py:15
  511.5 22.3 %collective-permute-start = (bf16[64,1024]{1,0:T(8,128)(2,1)S(1)}, bf16[64,1024]{1,0:T(8,128)(2,1)S(1)}, u32[]{:S(2)}, u32[]{:S(2)}) collective-permute-start(bf16[64,1024]{1,0:T(8,128)(2,1)S(1)} %copy.84), channel_id=1, source_target_pairs={{0,32},{32,64},{64,96},{96,128},{128,160},{160,192},{192,224},{224... | collective-permute-start | bytes 393224 | tf_op jit(solution)/shard_map/while/body/eval_jaxpr/ppermute | solution.py:15
  513.5 20.4 %collective-permute-start.1 = (f32[64,2]{0,1:T(2,128)S(1)}, f32[64,2]{0,1:T(2,128)S(1)}, u32[]{:S(2)}, u32[]{:S(2)}) collective-permute-start(f32[64,2]{0,1:T(2,128)S(1)} %copy.85), channel_id=1, source_target_pairs={{0,32},{32,64},{64,96},{96,128},{128,160},{160,192},{192,224},{224... | collective-permute-start | bytes 1544 | tf_op jit(solution)/shard_map/while/body/eval_jaxpr/ppermute | solution.py:15
  534.8 24.2 %collective-permute-start.2 = (f32[64,1024]{1,0:T(8,128)S(1)}, f32[64,1024]{1,0:T(8,128)S(1)}, u32[]{:S(2)}, u32[]{:S(2)}) collective-permute-start(f32[64,1024]{1,0:T(8,128)S(1)} %bitcast_add_fusion.2), channel_id=1, source_target_pairs={{0,32},{32,64},{64,96},{96,128},{128,160},{160,192},{192,224},{224... | collective-permute-start | bytes 786440 | tf_op jit(solution)/shard_map/while/body/eval_jaxpr/ppermute | solution.py:15
  536.8 22.3 %collective-permute-start = (bf16[64,1024]{1,0:T(8,128)(2,1)S(1)}, bf16[64,1024]{1,0:T(8,128)(2,1)S(1)}, u32[]{:S(2)}, u32[]{:S(2)}) collective-permute-start(bf16[64,1024]{1,0:T(8,128)(2,1)S(1)} %copy.84), channel_id=1, source_target_pairs={{0,32},{32,64},{64,96},{96,128},{128,160},{160,192},{192,224},{224... | collective-permute-start | bytes 393224 | tf_op jit(solution)/shard_map/while/body/eval_jaxpr/ppermute | solution.py:15
  538.7 20.4 %collective-permute-start.1 = (f32[64,2]{0,1:T(2,128)S(1)}, f32[64,2]{0,1:T(2,128)S(1)}, u32[]{:S(2)}, u32[]{:S(2)}) collective-permute-start(f32[64,2]{0,1:T(2,128)S(1)} %copy.85), channel_id=1, source_target_pairs={{0,32},{32,64},{64,96},{96,128},{128,160},{160,192},{192,224},{224... | collective-permute-start | bytes 1544 | tf_op jit(solution)/shard_map/while/body/eval_jaxpr/ppermute | solution.py:15
  560.1 24.2 %collective-permute-start.2 = (f32[64,1024]{1,0:T(8,128)S(1)}, f32[64,1024]{1,0:T(8,128)S(1)}, u32[]{:S(2)}, u32[]{:S(2)}) collective-permute-start(f32[64,1024]{1,0:T(8,128)S(1)} %bitcast_add_fusion.2), channel_id=1, source_target_pairs={{0,32},{32,64},{64,96},{96,128},{128,160},{160,192},{192,224},{224... | collective-permute-start | bytes 786440 | tf_op jit(solution)/shard_map/while/body/eval_jaxpr/ppermute | solution.py:15
  562.0 22.3 %collective-permute-start = (bf16[64,1024]{1,0:T(8,128)(2,1)S(1)}, bf16[64,1024]{1,0:T(8,128)(2,1)S(1)}, u32[]{:S(2)}, u32[]{:S(2)}) collective-permute-start(bf16[64,1024]{1,0:T(8,128)(2,1)S(1)} %copy.84), channel_id=1, source_target_pairs={{0,32},{32,64},{64,96},{96,128},{128,160},{160,192},{192,224},{224... | collective-permute-start | bytes 393224 | tf_op jit(solution)/shard_map/while/body/eval_jaxpr/ppermute | solution.py:15
  563.9 20.4 %collective-permute-start.1 = (f32[64,2]{0,1:T(2,128)S(1)}, f32[64,2]{0,1:T(2,128)S(1)}, u32[]{:S(2)}, u32[]{:S(2)}) collective-permute-start(f32[64,2]{0,1:T(2,128)S(1)} %copy.85), channel_id=1, source_target_pairs={{0,32},{32,64},{64,96},{96,128},{128,160},{160,192},{192,224},{224... | collective-permute-start | bytes 1544 | tf_op jit(solution)/shard_map/while/body/eval_jaxpr/ppermute | solution.py:15
  585.3 24.2 %collective-permute-start.2 = (f32[64,1024]{1,0:T(8,128)S(1)}, f32[64,1024]{1,0:T(8,128)S(1)}, u32[]{:S(2)}, u32[]{:S(2)}) collective-permute-start(f32[64,1024]{1,0:T(8,128)S(1)} %bitcast_add_fusion.2), channel_id=1, source_target_pairs={{0,32},{32,64},{64,96},{96,128},{128,160},{160,192},{192,224},{224... | collective-permute-start | bytes 786440 | tf_op jit(solution)/shard_map/while/body/eval_jaxpr/ppermute | solution.py:15
  587.2 22.3 %collective-permute-start = (bf16[64,1024]{1,0:T(8,128)(2,1)S(1)}, bf16[64,1024]{1,0:T(8,128)(2,1)S(1)}, u32[]{:S(2)}, u32[]{:S(2)}) collective-permute-start(bf16[64,1024]{1,0:T(8,128)(2,1)S(1)} %copy.84), channel_id=1, source_target_pairs={{0,32},{32,64},{64,96},{96,128},{128,160},{160,192},{192,224},{224... | collective-permute-start | bytes 393224 | tf_op jit(solution)/shard_map/while/body/eval_jaxpr/ppermute | solution.py:15
  589.2 20.4 %collective-permute-start.1 = (f32[64,2]{0,1:T(2,128)S(1)}, f32[64,2]{0,1:T(2,128)S(1)}, u32[]{:S(2)}, u32[]{:S(2)}) collective-permute-start(f32[64,2]{0,1:T(2,128)S(1)} %copy.85), channel_id=1, source_target_pairs={{0,32},{32,64},{64,96},{96,128},{128,160},{160,192},{192,224},{224... | collective-permute-start | bytes 1544 | tf_op jit(solution)/shard_map/while/body/eval_jaxpr/ppermute | solution.py:15
  610.5 22.7 %collective-permute-start.2 = (f32[64,1024]{1,0:T(8,128)S(1)}, f32[64,1024]{1,0:T(8,128)S(1)}, u32[]{:S(2)}, u32[]{:S(2)}) collective-permute-start(f32[64,1024]{1,0:T(8,128)S(1)} %bitcast_add_fusion.2), channel_id=1, source_target_pairs={{0,32},{32,64},{64,96},{96,128},{128,160},{160,192},{192,224},{224... | collective-permute-start | bytes 786440 | tf_op jit(solution)/shard_map/while/body/eval_jaxpr/ppermute | solution.py:15
  612.5 20.8 %collective-permute-start = (bf16[64,1024]{1,0:T(8,128)(2,1)S(1)}, bf16[64,1024]{1,0:T(8,128)(2,1)S(1)}, u32[]{:S(2)}, u32[]{:S(2)}) collective-permute-start(bf16[64,1024]{1,0:T(8,128)(2,1)S(1)} %copy.84), channel_id=1, source_target_pairs={{0,32},{32,64},{64,96},{96,128},{128,160},{160,192},{192,224},{224... | collective-permute-start | bytes 393224 | tf_op jit(solution)/shard_map/while/body/eval_jaxpr/ppermute | solution.py:15
  614.4 18.8 %collective-permute-start.1 = (f32[64,2]{0,1:T(2,128)S(1)}, f32[64,2]{0,1:T(2,128)S(1)}, u32[]{:S(2)}, u32[]{:S(2)}) collective-permute-start(f32[64,2]{0,1:T(2,128)S(1)} %copy.85), channel_id=1, source_target_pairs={{0,32},{32,64},{64,96},{96,128},{128,160},{160,192},{192,224},{224... | collective-permute-start | bytes 1544 | tf_op jit(solution)/shard_map/while/body/eval_jaxpr/ppermute | solution.py:15
  634.2 20.0 %collective-permute-start.2 = (f32[64,1024]{1,0:T(8,128)S(1)}, f32[64,1024]{1,0:T(8,128)S(1)}, u32[]{:S(2)}, u32[]{:S(2)}) collective-permute-start(f32[64,1024]{1,0:T(8,128)S(1)} %bitcast_add_fusion.2), channel_id=1, source_target_pairs={{0,32},{32,64},{64,96},{96,128},{128,160},{160,192},{192,224},{224... | collective-permute-start | bytes 786440 | tf_op jit(solution)/shard_map/while/body/eval_jaxpr/ppermute | solution.py:15
  636.2 18.0 %collective-permute-start = (bf16[64,1024]{1,0:T(8,128)(2,1)S(1)}, bf16[64,1024]{1,0:T(8,128)(2,1)S(1)}, u32[]{:S(2)}, u32[]{:S(2)}) collective-permute-start(bf16[64,1024]{1,0:T(8,128)(2,1)S(1)} %copy.84), channel_id=1, source_target_pairs={{0,32},{32,64},{64,96},{96,128},{128,160},{160,192},{192,224},{224... | collective-permute-start | bytes 393224 | tf_op jit(solution)/shard_map/while/body/eval_jaxpr/ppermute | solution.py:15
  638.1 16.1 %collective-permute-start.1 = (f32[64,2]{0,1:T(2,128)S(1)}, f32[64,2]{0,1:T(2,128)S(1)}, u32[]{:S(2)}, u32[]{:S(2)}) collective-permute-start(f32[64,2]{0,1:T(2,128)S(1)} %copy.85), channel_id=1, source_target_pairs={{0,32},{32,64},{64,96},{96,128},{128,160},{160,192},{192,224},{224... | collective-permute-start | bytes 1544 | tf_op jit(solution)/shard_map/while/body/eval_jaxpr/ppermute | solution.py:15
Sparse Core Ops, SparseCore 0:
  9.4 241.6 all-gather.2
  253.2 231.7 all-gather.4
where the time goes:
time: 669 us; the launch traced here: 667 us
  waiting for transfers between devices  527 us (79%)
  starting transfers between devices  94 us (14%)
  matrix products  16.6 us (2%)
  between operations  13.6 us (2%)
  other arithmetic  7.57 us (1%)
    ppermute x48, waiting for transfers between devices, shifted(): return lax.ppermute(value, axis, pairs)  287 us
    all_gather x1, waiting for transfers between devices, body(): lax.all_gather(w_in, 'user', axis=0, tiled=True)  239 us
    ppermute x48, starting transfers between devices, shifted(): return lax.ppermute(value, axis, pairs)  93.9 us
  transfers between devices with their start and end apart: 50, of which 17 were waited for; matrix products, arithmetic and copies ran while one was open for 4% of the time, Pallas kernels for 0%

commit v1 on v0

v1 whole, which is shorter than its diff:
```python
import jax
import jax.numpy as jnp
from jax import lax
from jax.experimental import pallas as pl
from jax.experimental.pallas import tpu as pltpu
from jax.sharding import Mesh, PartitionSpec as P

D = 1024
HEADS = 8
HEAD = 128
BLOCK = 128
ROWS = 64
HALF = 512
EVENTS = 2048
USER = ("zl", "y")
LOCAL = ("x", "c")
HIST = ("zh", "x", "c")
SCALE = HEAD ** (-0.5)


def silu(v):
    h = v * 0.5
    return h + h * jnp.tanh(h)


def layer_norm(values):
    mean = jnp.mean(values, axis=-1, keepdims=True)
    centred = values - mean
    var = jnp.mean(centred * centred, axis=-1, keepdims=True)
    return centred * lax.rsqrt(var + 1e-05)


def spread(value, axis, count):
    copies = jnp.broadcast_to(value[None], (count,) + value.shape)
    return lax.all_to_all(copies, axis, 0, 0, tiled=True)


def attend_kernel(q_ref, k_ref, v_ref, lo_ref, hi_ref, out_ref):
    tile, chunk = 128, 512

    def rows(i, carry):
        at = pl.ds(pl.multiple_of(i * tile, tile), tile)
        q = q_ref[at, :]
        lo = jnp.broadcast_to(lo_ref[at, :], (tile, chunk))
        hi = jnp.broadcast_to(hi_ref[at, :], (tile, chunk))
        total = jnp.zeros((tile, HEAD), jnp.float32)
        for e in range(EVENTS // chunk):
            span = pl.ds(e * chunk, chunk)
            s = lax.dot_general(
                q, k_ref[span, :], (((1,), (1,)), ((), ())), preferred_element_type=jnp.float32
            )
            h = s * (0.5 * SCALE)
            w = h + h * jnp.tanh(h)
            event = lax.broadcasted_iota(jnp.int32, (tile, chunk), 1) + e * chunk
            seen = (event >= lo) & (event < hi)
            w = jnp.where(seen, w, 0.0).astype(jnp.bfloat16)
            total = total + jnp.dot(w, v_ref[span, :], preferred_element_type=jnp.float32)
        out_ref[at, :] = total.astype(out_ref.dtype)
        return carry

    lax.fori_loop(0, q_ref.shape[0] // tile, rows, 0)


def attend(query, keys, values, lo, hi, dtype):
    rows = query.shape[0]
    vmem = pl.BlockSpec(memory_space=pltpu.VMEM)
    return pl.pallas_call(
        attend_kernel,
        out_shape=jax.ShapeDtypeStruct((rows, HEAD), dtype),
        in_specs=[vmem] * 5,
        out_specs=vmem,
        cost_estimate=pl.CostEstimate(
            flops=4 * rows * EVENTS * HEAD, bytes_accessed=1 << 21, transcendentals=rows * EVENTS
        ),
        compiler_params=pltpu.CompilerParams(vmem_limit_bytes=32 << 20),
    )(query, keys, values, lo, hi)


def body(cand_embed, hist_key, hist_value, block_owner, cand_user, cand_cutoff, w_in, w_out):
    x = cand_embed[0]
    head = lax.axis_index("x") * 2 + lax.axis_index("c")
    half = lax.axis_index("zh")

    normed = layer_norm(x.astype(jnp.float32)).astype(jnp.bfloat16)
    normed = normed.reshape(ROWS, 8, 4, 32).transpose(0, 2, 1, 3).reshape(ROWS, D)
    before = jnp.sum((block_owner[0][None, :] < cand_user[0][:, None]).astype(jnp.int32), axis=1)
    cutoff = cand_cutoff[0]
    labels = jnp.stack([before, cutoff // 64, cutoff % 64]).astype(jnp.bfloat16)
    labels = jnp.pad(labels, ((0, 5), (0, D - ROWS)))
    mine = jnp.concatenate([normed, labels])
    other = lax.ppermute(mine, "zh", [(0, 1), (1, 0)])

    cols = lax.dynamic_slice_in_dim(w_in.reshape(32, 4, HEADS, HEAD), head, 1, 2).reshape(32, 512)
    cols = jnp.concatenate([cols, lax.dynamic_slice_in_dim(w_out, head * HEAD, HEAD, 1)], axis=1)
    cols = spread(cols, "zl", 8).reshape(256, 640)
    cols = spread(cols, "y", 4).reshape(D, 640)
    w_out_all = spread(cols[:, 512:], LOCAL, 8)

    both = jnp.stack([mine, other])
    both = spread(both, LOCAL, 8)
    normed_own = both[:, 0, :ROWS].reshape(HALF, D)
    normed_other = both[:, 1, :ROWS].reshape(HALF, D)
    tags = both[:, :, ROWS : ROWS + 3, :ROWS].astype(jnp.int32)
    tags = tags.transpose(2, 1, 0, 3).reshape(3, 2, HALF)
    first = tags[0] * BLOCK
    last = tags[1] * 64 + tags[2]
    lo = (first - half * EVENTS)[:, :, None]
    hi = (last - half * EVENTS)[:, :, None]
    count = (last - first)[0].astype(jnp.float32)

    kv = jnp.stack([hist_key[0], hist_value[0]]).reshape(2, 256, HEADS, HEAD)
    kv = lax.all_to_all(kv.transpose(2, 0, 1, 3), LOCAL, 0, 0, tiled=True)
    keys = kv[:, 0].reshape(EVENTS, HEAD)
    values = kv[:, 1].reshape(EVENTS, HEAD)

    q_other = jnp.dot(normed_other, cols[:, 256:384], preferred_element_type=jnp.float32)
    q_other = silu(q_other).astype(jnp.bfloat16)
    away = attend(q_other, keys, values, lo[1], hi[1], jnp.bfloat16)
    home = lax.ppermute(away, "zh", [(0, 1), (1, 0)])

    proj = jnp.dot(normed_own, cols[:, :512], preferred_element_type=jnp.float32)
    proj = silu(proj).astype(jnp.bfloat16)
    query = proj[:, 256:384]
    own = attend(query, keys, values, lo[0], hi[0], jnp.float32)

    gate = proj[:, :128].astype(jnp.float32)
    val = proj[:, 128:256].astype(jnp.float32)
    key_self = proj[:, 384:512].astype(jnp.float32)
    score = jnp.sum(query.astype(jnp.float32) * key_self, axis=-1, keepdims=True)
    self_term = silu(score * SCALE) * val
    attended = (own + home.astype(jnp.float32) + self_term) / (count[:, None] + 1.0)
    mixed = (layer_norm(attended) * gate).astype(jnp.bfloat16)

    mixed = lax.all_to_all(mixed.reshape(8, ROWS, HEAD), LOCAL, 0, 0, tiled=True)
    mixed = mixed.reshape(8, ROWS, 4, 32).transpose(1, 2, 0, 3).reshape(ROWS, D)
    w_out_all = w_out_all.transpose(1, 0, 2).reshape(D, D)
    projected = jnp.dot(mixed, w_out_all, preferred_element_type=jnp.float32)
    return (x.astype(jnp.float32) + projected).astype(jnp.bfloat16)[None]


def solution(mesh):
    parts = Mesh(mesh.devices.reshape(2, 4, 2, 8, 4), ("zh", "x", "c", "zl", "y"))
    return jax.shard_map(
        body,
        mesh=parts,
        in_specs=(
            P(USER, HIST, None),
            P(USER, HIST, None),
            P(USER, HIST, None),
            P(USER, None),
            P(USER, HIST),
            P(USER, HIST),
            P(USER, None),
            P(USER, None),
        ),
        out_specs=P(USER, HIST, None),
        check_vma=False,
    )
```

time: 669 us -> 200 us (0.30)
  the two profiles are of different devices: /device:TPU:8 before, /device:TPU:40 now
where the time goes in v1:
time: 200 us
  waiting for transfers between devices  119 us (60%)
  starting transfers between devices  49 us (24%)
  local copies, waits for them, and re-layouts  17.4 us (9%)
  Pallas kernels  7.45 us (4%)
  other arithmetic  3.29 us (2%)
  matrix products  2.62 us (1%)
    all_to_all x4, waiting for transfers between devices, spread(): return lax.all_to_all(copies, axis, 0, 0, tiled=True)  70.1 us
    ppermute x1, waiting for transfers between devices, body(): other = lax.ppermute(mine, 'zh', [(0, 1), (1, 0)])  25.7 us
    all_to_all x4, starting transfers between devices, spread(): return lax.all_to_all(copies, axis, 0, 0, tiled=True)  24.9 us
    all_to_all x1, waiting for transfers between devices, body(): kv = lax.all_to_all(kv.transpose(2, 0, 1, 3), LOCAL, 0, 0, tiled=True)  15.5 us
    ppermute x1, starting transfers between devices, body(): other = lax.ppermute(mine, 'zh', [(0, 1), (1, 0)])  8.22 us
    ppermute x1, starting transfers between devices, body(): home = lax.ppermute(away, 'zh', [(0, 1), (1, 0)])  8.17 us
    pallas_call x2, Pallas kernels, attend(): pl.pallas_call(attend_kernel, out_shape=jax.ShapeDtypeStruct((rows, HEAD)...  7.45 us
    broadcast_in_dim x5, local copies, waits for them, and re-layouts, spread(): copies = jnp.broadcast_to(value[None], (count,) + value.shape)  5.63 us
  transfers between devices with their start and end apart: 8, of which 7 were waited for; matrix products, arithmetic and copies ran while one was open for 4% of the time, Pallas kernels for 2%

profile of v1, /device:TPU:40, one launch (start us, length us, event | category | flops | bytes accessed | tf_op | source)
XLA Modules:
  0.0 199.6 jit_solution(14007733769978996190)
XLA Ops:
  0.0 1.1 copy.117
  1.1 0.2 dynamic-slice_reduce_fusion
  1.4 0.8 broadcast_in_dim.13
  2.1 12.6 %all-to-all-start.1 = ((bf16[8,32,640]{2,1,0:T(8,128)(2,1)}), bf16[8,32,640]{2,1,0:T(8,128)(2,1)S(1)}, u32[]{:S(2)}, u32[]{:S(2)}) async-start(bf16[8,32,640]{2,1,0:T(8,128)(2,1)} %broadcast_in_dim.13), calls=%async_computation.1 | async-start | bytes 655360 | tf_op jit(solution)/shard_map/all_to_all | solution.py:35
  14.8 0.2 copy.103
  15.0 0.2 copy.102
  15.2 0.1 pad_maximum_fusion
  15.3 0.0 copy-start.9
  15.3 0.0 copy-start.10
  15.3 0.0 copy-start.4
  15.3 0.0 copy-start.11
  15.4 1.3 copy.104
  16.7 17.0 %all-to-all-done.1 = bf16[8,32,640]{2,1,0:T(8,128)(2,1)S(1)} async-done(((bf16[8,32,640]{2,1,0:T(8,128)(2,1)}), bf16[8,32,640]{2,1,0:T(8,128)(2,1)S(1)}, u32[]{:S(2)}, u32[]{:S(2)}) %all-to-all-start.1) | async-done | bytes 327712 | tf_op jit(solution)/shard_map/all_to_all | solution.py:35
  33.7 4.3 %all-to-all-start.3 = ((bf16[8,2,256,128]{3,2,1,0:T(8,128)(2,1)}), bf16[8,2,256,128]{3,2,1,0:T(8,128)(2,1)S(1)}, u32[]{:S(2)}, u32[]{:S(2)}) async-start(bf16[8,2,256,128]{3,2,1,0:T(8,128)(2,1)} %copy.104), calls=%async_computation.3 | async-start | bytes 2097152 | tf_op jit(solution)/shard_map/all_to_all | solution.py:112
  38.0 0.1 convert_reduce_fusion.1
  38.1 0.1 convert_reduce_fusion
  38.3 0.2 copy.100
  38.4 15.5 %all-to-all-done.3 = bf16[8,2,256,128]{3,2,1,0:T(8,128)(2,1)S(1)} async-done(((bf16[8,2,256,128]{3,2,1,0:T(8,128)(2,1)}), bf16[8,2,256,128]{3,2,1,0:T(8,128)(2,1)S(1)}, u32[]{:S(2)}, u32[]{:S(2)}) %all-to-all-start.3) | async-done | bytes 1048608 | tf_op jit(solution)/shard_map/all_to_all | solution.py:112
  54.0 1.3 broadcast_in_dim.15
  55.2 0.1 copy-done.3
  55.4 4.9 %all-to-all-start.2 = ((bf16[4,256,640]{1,2,0:T(8,128)(2,1)}), bf16[4,256,640]{1,2,0:T(8,128)(2,1)S(1)}, u32[]{:S(2)}, u32[]{:S(2)}) async-start(bf16[4,256,640]{1,2,0:T(8,128)(2,1)} %broadcast_in_dim.15), calls=%async_computation.2 | async-start | bytes 2621440 | tf_op jit(solution)/shard_map/all_to_all | solution.py:35
  60.3 0.1 copy.92
  60.4 0.1 copy.94
  60.5 0.2 fusion.10
  60.7 0.1 fusion.7
  60.8 0.1 fusion.6
  60.9 8.2 %collective-permute-start = (bf16[72,1024]{0,1:T(8,128)(2,1)S(1)}, bf16[72,1024]{0,1:T(8,128)(2,1)S(1)}, u32[]{:S(2)}, u32[]{:S(2)}) collective-permute-start(bf16[72,1024]{0,1:T(8,128)(2,1)S(1)} %fusion.6), channel_id=1, source_target_pairs={{0,256},{256,0},{1,257},{257,1},{2,258},{258,2},{3,259},{259,3},{4... | collective-permute-start | bytes 442376 | tf_op jit(solution)/shard_map/ppermute | solution.py:91
  69.2 0.1 fusion.23
  69.2 25.7 %collective-permute-done = bf16[72,1024]{0,1:T(8,128)(2,1)S(1)} collective-permute-done((bf16[72,1024]{0,1:T(8,128)(2,1)S(1)}, bf16[72,1024]{0,1:T(8,128)(2,1)S(1)}, u32[]{:S(2)}, u32[]{:S(2)}) %collective-permute-start) | collective-permute-done | bytes 147488 | tf_op jit(solution)/shard_map/ppermute | solution.py:91
  94.9 0.1 pad_maximum_fusion.1
  95.0 0.2 copy.97
  95.2 1.8 broadcast_in_dim.12
  97.1 3.6 %all-to-all-start = ((bf16[8,2,72,1024]{3,2,1,0:T(8,128)(2,1)}), bf16[8,2,72,1024]{3,2,1,0:T(8,128)(2,1)S(1)}, u32[]{:S(2)}, u32[]{:S(2)}) async-start(bf16[8,2,72,1024]{3,2,1,0:T(8,128)(2,1)} %broadcast_in_dim.12), calls=%async_computation | async-start | bytes 4718592 | tf_op jit(solution)/shard_map/all_to_all | solution.py:35
  100.7 1.3 fusion.18
  102.0 2.4 %copy.101 = bf16[4,256,640]{2,1,0:T(8,128)(2,1)} copy(bf16[4,256,640]{1,2,0:T(8,128)(2,1)} %copy-done.2) | data formatting | bytes 2621440 | tf_op jit(solution)/shard_map/all_to_all | solution.py:35
  104.4 26.2 %all-to-all-done = bf16[8,2,72,1024]{3,2,1,0:T(8,128)(2,1)S(1)} async-done(((bf16[8,2,72,1024]{3,2,1,0:T(8,128)(2,1)}), bf16[8,2,72,1024]{3,2,1,0:T(8,128)(2,1)S(1)}, u32[]{:S(2)}, u32[]{:S(2)}) %all-to-all-start) | async-done | bytes 2359328 | tf_op jit(solution)/shard_map/all_to_all | solution.py:35
  130.6 0.2 fusion.17
  130.8 1.2 copy-done.1
  132.0 0.8 copy-done.6
  132.8 0.7 fusion
  133.5 0.1 multiply_reduce_fusion.1
  133.7 0.4 fusion.5.q_ref
  134.2 0.8 convert_bitcast_fusion
  135.0 0.2 squeeze.24.lo_ref
  135.2 0.2 squeeze.25.hi_ref
  135.4 3.7 %shard_map.83 = bf16[512,128]{1,0:T(8,128)(2,1)S(1)} custom-call(bf16[512,128]{1,0:T(8,128)(2,1)S(1)} %fusion.5.q_ref, bf16[2048,128]{1,0:T(8,128)(2,1)S(1)} %bitcast.56, bf16[2048,128]{1,0:T(8,128)(2,1)S(1)} %bitcast.54, s32[512,1]{1,0:T(8,128)S(1)} %squeeze.24.lo_ref, s32[512,1]{1,0:T(8,128)S(1)} %squeeze.25.hi_ref), custom_call_target="tpu_custom_call" | custom-call | flops 536870912 | bytes 2097152 | tf_op jit(solution)/shard_map/pallas_call | solution.py:67
  139.2 8.2 %collective-permute-start.1 = (bf16[512,128]{1,0:T(8,128)(2,1)S(1)}, bf16[512,128]{1,0:T(8,128)(2,1)S(1)}, u32[]{:S(2)}, u32[]{:S(2)}) collective-permute-start(bf16[512,128]{1,0:T(8,128)(2,1)S(1)} %shard_map.83), channel_id=1, source_target_pairs={{0,256},{256,0},{1,257},{257,1},{2,258},{258,2},{3,259},{259,3},{4... | collective-permute-start | bytes 393224 | tf_op jit(solution)/shard_map/ppermute | solution.py:119
  147.4 0.1 add.97
  147.5 0.2 squeeze.22.lo_ref
  147.7 0.2 squeeze.23.hi_ref
  147.9 3.7 %shard_map.82 = f32[512,128]{1,0:T(8,128)S(1)} custom-call(bf16[512,128]{1,0:T(8,128)(2,1)S(1)} %slice.94.q_ref, bf16[2048,128]{1,0:T(8,128)(2,1)S(1)} %bitcast.57, bf16[2048,128]{1,0:T(8,128)(2,1)S(1)} %bitcast.55, s32[512,1]{1,0:T(8,128)S(1)} %squeeze.22.lo_ref, s32[512,1]{1,0:T(8,128)S(1)} %squeeze.23.hi_ref), custom_call_target="tpu_custom_call" | custom-call | flops 536870912 | bytes 2097152 | tf_op jit(solution)/shard_map/pallas_call | solution.py:67
  151.6 3.2 %collective-permute-done.1 = bf16[512,128]{1,0:T(8,128)(2,1)S(1)} collective-permute-done((bf16[512,128]{1,0:T(8,128)(2,1)S(1)}, bf16[512,128]{1,0:T(8,128)(2,1)S(1)}, u32[]{:S(2)}, u32[]{:S(2)}) %collective-permute-start.1) | collective-permute-done | bytes 131104 | tf_op jit(solution)/shard_map/ppermute | solution.py:119
  154.8 0.3 fusion.16
  155.1 0.2 multiply_reduce_fusion
  155.4 0.9 multiply_convert_fusion.1
  156.3 3.4 %all-to-all-start.4 = ((bf16[8,64,128]{2,1,0:T(8,128)(2,1)}), bf16[8,64,128]{2,1,0:T(8,128)(2,1)S(1)}, u32[]{:S(2)}, u32[]{:S(2)}) async-start(bf16[8,64,128]{2,1,0:T(8,128)(2,1)} %bitcast.18), calls=%async_computation.4 | async-start | bytes 262144 | tf_op jit(solution)/shard_map/all_to_all | solution.py:134
  159.6 1.0 slice.112
  160.6 0.1 copy.112
  160.8 4.9 %all-to-all-done.4 = bf16[8,64,128]{2,1,0:T(8,128)(2,1)S(1)} async-done(((bf16[8,64,128]{2,1,0:T(8,128)(2,1)}), bf16[8,64,128]{2,1,0:T(8,128)(2,1)S(1)}, u32[]{:S(2)}, u32[]{:S(2)}) %all-to-all-start.4) | async-done | bytes 131104 | tf_op jit(solution)/shard_map/all_to_all | solution.py:134
  165.7 1.6 broadcast_in_dim.16
  167.3 3.7 %all-to-all-start.5 = ((bf16[8,1024,128]{1,2,0:T(8,128)(2,1)}), bf16[8,1024,128]{1,2,0:T(8,128)(2,1)S(1)}, u32[]{:S(2)}, u32[]{:S(2)}) async-start(bf16[8,1024,128]{1,2,0:T(8,128)(2,1)} %broadcast_in_dim.16), calls=%async_computation.5 | async-start | bytes 4194304 | tf_op jit(solution)/shard_map/all_to_all | solution.py:35
  171.0 0.2 copy.110
  171.3 26.9 %all-to-all-done.5 = bf16[8,1024,128]{1,2,0:T(8,128)(2,1)S(1)} async-done(((bf16[8,1024,128]{1,2,0:T(8,128)(2,1)}), bf16[8,1024,128]{1,2,0:T(8,128)(2,1)S(1)}, u32[]{:S(2)}, u32[]{:S(2)}) %all-to-all-start.5) | async-done | bytes 2097184 | tf_op jit(solution)/shard_map/all_to_all | solution.py:35
  198.2 1.4 fusion.2
  (35 shorter events, 0.3 us)
Async XLA Ops:
  0.0 1.3 copy-start
  0.0 14.8 %copy-start.7 = (bf16[1,256,1024]{2,1,0:T(8,128)(2,1)S(1)}, bf16[1,256,1024]{2,1,0:T(8,128)(2,1)}, u32[]{:S(2)}) copy-start(bf16[1,256,1024]{2,1,0:T(8,128)(2,1)} %param.10) | copy-start | bytes 1572868
  0.0 15.0 %copy-start.8 = (bf16[1,256,1024]{2,1,0:T(8,128)(2,1)S(1)}, bf16[1,256,1024]{2,1,0:T(8,128)(2,1)}, u32[]{:S(2)}) copy-start(bf16[1,256,1024]{2,1,0:T(8,128)(2,1)} %param.9) | copy-start | bytes 1572868
  2.1 31.5 %all-to-all-start.1 = ((bf16[8,32,640]{2,1,0:T(8,128)(2,1)}), bf16[8,32,640]{2,1,0:T(8,128)(2,1)S(1)}, u32[]{:S(2)}, u32[]{:S(2)}) async-start(bf16[8,32,640]{2,1,0:T(8,128)(2,1)} %broadcast_in_dim.13), calls=%async_computation.1 | async-start | bytes 655360 | tf_op jit(solution)/shard_map/all_to_all | solution.py:35
  15.3 22.7 %copy-start.9 = (s32[1,64]{1,0:T(1,128)S(1)}, s32[1,64]{1,0:T(1,128)}, u32[]{:S(2)}) copy-start(s32[1,64]{1,0:T(1,128)} %param.12) | copy-start | bytes 772
  15.3 22.7 %copy-start.10 = (s32[1,32]{1,0:T(1,128)S(1)}, s32[1,32]{1,0:T(1,128)}, u32[]{:S(2)}) copy-start(s32[1,32]{1,0:T(1,128)} %param.11) | copy-start | bytes 388
  15.3 22.8 %copy-start.4 = (bf16[1,64,1024]{2,1,0:T(8,128)(2,1)S(1)}, bf16[1,64,1024]{2,1,0:T(8,128)(2,1)}, u32[]{:S(2)}) copy-start(bf16[1,64,1024]{2,1,0:T(8,128)(2,1)} %param.8) | copy-start | bytes 393220
  15.3 22.9 %copy-start.11 = (s32[1,64]{1,0:T(1,128)S(1)}, s32[1,64]{1,0:T(1,128)}, u32[]{:S(2)}) copy-start(s32[1,64]{1,0:T(1,128)} %param.13) | copy-start | bytes 772
  33.7 20.3 %all-to-all-start.3 = ((bf16[8,2,256,128]{3,2,1,0:T(8,128)(2,1)}), bf16[8,2,256,128]{3,2,1,0:T(8,128)(2,1)S(1)}, u32[]{:S(2)}, u32[]{:S(2)}) async-start(bf16[8,2,256,128]{3,2,1,0:T(8,128)(2,1)} %copy.104), calls=%async_computation.3 | async-start | bytes 2097152 | tf_op jit(solution)/shard_map/all_to_all | solution.py:112
  54.0 1.4 copy-start.3
  55.4 39.9 %all-to-all-start.2 = ((bf16[4,256,640]{1,2,0:T(8,128)(2,1)}), bf16[4,256,640]{1,2,0:T(8,128)(2,1)S(1)}, u32[]{:S(2)}, u32[]{:S(2)}) async-start(bf16[4,256,640]{1,2,0:T(8,128)(2,1)} %broadcast_in_dim.15), calls=%async_computation.2 | async-start | bytes 2621440 | tf_op jit(solution)/shard_map/all_to_all | solution.py:35
  60.9 34.0 %collective-permute-start = (bf16[72,1024]{0,1:T(8,128)(2,1)S(1)}, bf16[72,1024]{0,1:T(8,128)(2,1)S(1)}, u32[]{:S(2)}, u32[]{:S(2)}) collective-permute-start(bf16[72,1024]{0,1:T(8,128)(2,1)S(1)} %fusion.6), channel_id=1, source_target_pairs={{0,256},{256,0},{1,257},{257,1},{2,258},{258,2},{3,259},{259,3},{4... | collective-permute-start | bytes 442376 | tf_op jit(solution)/shard_map/ppermute | solution.py:91
  95.2 1.8 copy-start.2
  97.1 33.6 %all-to-all-start = ((bf16[8,2,72,1024]{3,2,1,0:T(8,128)(2,1)}), bf16[8,2,72,1024]{3,2,1,0:T(8,128)(2,1)S(1)}, u32[]{:S(2)}, u32[]{:S(2)}) async-start(bf16[8,2,72,1024]{3,2,1,0:T(8,128)(2,1)} %broadcast_in_dim.12), calls=%async_computation | async-start | bytes 4718592 | tf_op jit(solution)/shard_map/all_to_all | solution.py:35
  130.6 1.4 copy-start.1
  130.6 2.2 %copy-start.6 = (bf16[4,256,640]{2,1,0:T(8,128)(2,1)S(1)}, bf16[4,256,640]{2,1,0:T(8,128)(2,1)}, u32[]{:S(2)}) copy-start(bf16[4,256,640]{2,1,0:T(8,128)(2,1)} %copy.101) | copy-start | bytes 3932164
  139.2 15.6 %collective-permute-start.1 = (bf16[512,128]{1,0:T(8,128)(2,1)S(1)}, bf16[512,128]{1,0:T(8,128)(2,1)S(1)}, u32[]{:S(2)}, u32[]{:S(2)}) collective-permute-start(bf16[512,128]{1,0:T(8,128)(2,1)S(1)} %shard_map.83), channel_id=1, source_target_pairs={{0,256},{256,0},{1,257},{257,1},{2,258},{258,2},{3,259},{259,3},{4... | collective-permute-start | bytes 393224 | tf_op jit(solution)/shard_map/ppermute | solution.py:119
  156.3 9.4 %all-to-all-start.4 = ((bf16[8,64,128]{2,1,0:T(8,128)(2,1)}), bf16[8,64,128]{2,1,0:T(8,128)(2,1)S(1)}, u32[]{:S(2)}, u32[]{:S(2)}) async-start(bf16[8,64,128]{2,1,0:T(8,128)(2,1)} %bitcast.18), calls=%async_computation.4 | async-start | bytes 262144 | tf_op jit(solution)/shard_map/all_to_all | solution.py:134
  167.3 30.9 %copy-start.5 = (bf16[1,64,1024]{2,1,0:T(8,128)(2,1)S(1)}, bf16[1,64,1024]{2,1,0:T(8,128)(2,1)}, u32[]{:S(2)}) copy-start(bf16[1,64,1024]{2,1,0:T(8,128)(2,1)} %param.8) | copy-start | bytes 393220
  167.3 30.9 %all-to-all-start.5 = ((bf16[8,1024,128]{1,2,0:T(8,128)(2,1)}), bf16[8,1024,128]{1,2,0:T(8,128)(2,1)S(1)}, u32[]{:S(2)}, u32[]{:S(2)}) async-start(bf16[8,1024,128]{1,2,0:T(8,128)(2,1)} %broadcast_in_dim.16), calls=%async_computation.5 | async-start | bytes 4194304 | tf_op jit(solution)/shard_map/all_to_all | solution.py:35

commit v2 on v1

v2 whole, which is shorter than its diff:
```python
import jax
import jax.numpy as jnp
from jax import lax
from jax.experimental import pallas as pl
from jax.experimental.pallas import tpu as pltpu
from jax.sharding import Mesh, PartitionSpec as P

D = 1024
HEADS = 8
HEAD = 128
BLOCK = 128
ROWS = 64
WIDE = D + 128
HALF = 512
EVENTS = 2048
USER = ("zl", "y")
LOCAL = ("x", "c")
HIST = ("zh", "x", "c")
SCALE = HEAD ** (-0.5)
VMEM = pl.BlockSpec(memory_space=pltpu.VMEM)
ANY = pl.BlockSpec(memory_space=pl.ANY)
SMEM = pl.BlockSpec(memory_space=pltpu.SMEM)
PARAMS = pltpu.CompilerParams(vmem_limit_bytes=40 << 20)
F32 = jnp.float32
BF16 = jnp.bfloat16


def silu(v):
    h = v * 0.5
    return h + h * jnp.tanh(h)


def layer_norm(values):
    mean = jnp.mean(values, axis=-1, keepdims=True)
    centred = values - mean
    var = jnp.mean(centred * centred, axis=-1, keepdims=True)
    return centred * lax.rsqrt(var + 1e-05)


def swap(value, axis):
    return lax.ppermute(value, axis, [(0, 1), (1, 0)])


def along_x(value, steps):
    return lax.ppermute(value, "x", [(i, (i + steps) % 4) for i in range(4)])


def prepare_kernel(owner_ref, x_ref, user_ref, cutoff_ref, out_ref):
    out_ref[:, :D] = layer_norm(x_ref[...].astype(F32)).astype(BF16)
    square = (ROWS, ROWS)
    diagonal = lax.broadcasted_iota(jnp.int32, square, 0) == lax.broadcasted_iota(jnp.int32, square, 1)
    user = user_ref[...]
    before = jnp.zeros(user.shape, jnp.int32)
    for b in range(32):
        before = before + (owner_ref[0, b] < user).astype(jnp.int32)

    def column(row):
        spread_out = jnp.where(diagonal, jnp.broadcast_to(row.astype(F32), square), 0.0)
        return jnp.sum(spread_out, axis=1, keepdims=True)

    cutoff = cutoff_ref[...]
    lane = lax.broadcasted_iota(jnp.int32, (ROWS, 128), 1)
    tags = jnp.where(lane == 0, column(before), 0.0)
    tags = jnp.where(lane == 1, column(cutoff >> 6), tags)
    tags = jnp.where(lane == 2, column(cutoff & 63), tags)
    out_ref[:, D:] = tags.astype(BF16)


def prepare(owner, x, user, cutoff):
    return pl.pallas_call(
        prepare_kernel,
        out_shape=jax.ShapeDtypeStruct((ROWS, WIDE), BF16),
        in_specs=[SMEM, VMEM, VMEM, VMEM],
        out_specs=VMEM,
        compiler_params=PARAMS,
    )(owner, x, user, cutoff)


def columns_kernel(place_ref, in_ref, out_w_ref, out_ref):
    head = place_ref[0] * 2 + place_ref[1]
    for part in range(5):
        if part < 4:
            at = pl.ds(pl.multiple_of(head * HEAD + part * D, HEAD), HEAD)
            block = in_ref[:, at]
        else:
            block = out_w_ref[:, pl.ds(pl.multiple_of(head * HEAD, HEAD), HEAD)]
        for copy in range(8):
            out_ref[copy, :, part * HEAD : part * HEAD + HEAD] = block


def columns(*args):
    return pl.pallas_call(
        columns_kernel,
        out_shape=jax.ShapeDtypeStruct((8, 32, 640), BF16),
        in_specs=[SMEM, VMEM, VMEM],
        out_specs=VMEM,
        compiler_params=PARAMS,
    )(*args)


def pairs_kernel(place_ref, k_ref, v_ref, *out_refs):
    for s in range(4):
        at = pl.ds(pl.multiple_of(((place_ref[0] + s) & 3) * 256, 256), 256)
        out_refs[s][0] = k_ref[:, at]
        out_refs[s][1] = v_ref[:, at]


def pairs(*args):
    return pl.pallas_call(
        pairs_kernel,
        out_shape=[jax.ShapeDtypeStruct((2, 256, 256), BF16)] * 4,
        in_specs=[SMEM, VMEM, VMEM],
        out_specs=[VMEM] * 4,
        compiler_params=PARAMS,
    )(*args)


def give_kernel(place_ref, kv0, kv1, kv2, kv3, out_ref):
    at = pl.ds(pl.multiple_of((1 - place_ref[1]) * HEAD, HEAD), HEAD)
    for s, ref in enumerate((kv0, kv1, kv2, kv3)):
        for i in range(2):
            out_ref[s, i] = ref[i, :, at]


def give(*args):
    return pl.pallas_call(
        give_kernel,
        out_shape=jax.ShapeDtypeStruct((4, 2, 256, HEAD), BF16),
        in_specs=[SMEM] + [VMEM] * 4,
        out_specs=VMEM,
        compiler_params=PARAMS,
    )(*args)


def repeat_kernel(cols_ref, *refs):
    out_ref = refs[-1]
    for y in range(4):
        out_ref[y] = cols_ref[...].reshape(256, 640)


def repeat(cols, *after):
    return pl.pallas_call(
        repeat_kernel,
        out_shape=jax.ShapeDtypeStruct((4, 256, 640), BF16),
        in_specs=[VMEM] + [ANY] * len(after),
        out_specs=VMEM,
        compiler_params=PARAMS,
    )(cols, *after)


def out_part_kernel(cols_ref, after_ref, out_ref):
    out_ref[...] = cols_ref[:, :, 512:]


def out_part(*args):
    return pl.pallas_call(
        out_part_kernel,
        out_shape=jax.ShapeDtypeStruct((4, 256, HEAD), BF16),
        in_specs=[VMEM, ANY],
        out_specs=VMEM,
        compiler_params=PARAMS,
    )(*args)


def join_kernel(mine_ref, other_ref, after_ref, out_ref):
    out_ref[0] = mine_ref[...]
    out_ref[1] = other_ref[...]


def join(*args):
    return pl.pallas_call(
        join_kernel,
        out_shape=jax.ShapeDtypeStruct((2, ROWS, WIDE), BF16),
        in_specs=[VMEM, VMEM, ANY],
        out_specs=VMEM,
        compiler_params=PARAMS,
    )(*args)


def load_events(place_ref, kv_refs, peer_ref, k_all, v_all):
    lanes = pl.ds(pl.multiple_of(place_ref[1] * HEAD, HEAD), HEAD)
    for s in range(4):
        k_all[pl.ds(s * 512, 256), :] = kv_refs[s][0, :, lanes]
        v_all[pl.ds(s * 512, 256), :] = kv_refs[s][1, :, lanes]
        k_all[pl.ds(s * 512 + 256, 256), :] = peer_ref[s, 0]
        v_all[pl.ds(s * 512 + 256, 256), :] = peer_ref[s, 1]


def load_weight(w_ref, w_all, first, count):
    for y in range(4):
        for z in range(8):
            w_all[pl.ds(z * 128 + y * 32, 32), :] = w_ref[y, pl.ds(z * 32, 32), pl.ds(first, count)]


def load_rows(which, own_ref, peer_ref, rows):
    for core, ref in enumerate((own_ref, peer_ref)):
        for s in range(4):
            rows[pl.ds(core * 256 + s * ROWS, ROWS), :] = ref[s, which]


def visible(rows, half):
    tags = rows[:, D:].astype(F32)
    first = tags[:, 0:1] * BLOCK
    last = tags[:, 1:2] * 64.0 + tags[:, 2:3]
    return first, last


def attend_rows(place_ref, q_ref, lo_ref, hi_ref, k_all, v_all, store):
    tile, chunk = 128, 512
    x, core, half = place_ref[0], place_ref[1], place_ref[2]

    def rows(i, carry):
        at = pl.ds(pl.multiple_of(i * tile, tile), tile)
        q = q_ref[at, :]
        lo = jnp.broadcast_to(lo_ref[at, :], (tile, 256))
        hi = jnp.broadcast_to(hi_ref[at, :], (tile, 256))
        total = jnp.zeros((tile, HEAD), F32)
        for s in range(4):
            base = half * EVENTS + ((x - s + 4) & 3) * 512
            span = pl.ds(s * chunk, chunk)
            score = lax.dot_general(
                q, k_all[span, :], (((1,), (1,)), ((), ())), preferred_element_type=F32
            )
            parts = []
            for rel in range(2):
                h = score[:, rel * 256 : rel * 256 + 256] * (0.5 * SCALE)
                w = h + h * jnp.tanh(h)
                event = lax.broadcasted_iota(jnp.int32, (tile, 256), 1) + (base + (core ^ rel) * 256)
                seen = (event >= lo) & (event < hi)
                parts.append(jnp.where(seen, w, 0.0).astype(BF16))
            w = jnp.concatenate(parts, axis=1)
            total = total + jnp.dot(w, v_all[span, :], preferred_element_type=F32)
        store(at, total)
        return carry

    lax.fori_loop(0, HALF // tile, rows, 0)


def other_kernel(
    place_ref, own_ref, peer_ref, w_ref, kv0, kv1, kv2, kv3, kv_peer, out_ref,
    rows, w_all, k_all, v_all, q_all, lo_all, hi_all,
):
    load_rows(1, own_ref, peer_ref, rows)
    load_weight(w_ref, w_all, 256, HEAD)
    load_events(place_ref, (kv0, kv1, kv2, kv3), kv_peer, k_all, v_all)
    first, last = visible(rows, 0)
    lo_all[...] = first.astype(jnp.int32)
    hi_all[...] = last.astype(jnp.int32)
    query = jnp.dot(rows[:, :D], w_all[...], preferred_element_type=F32)
    q_all[...] = silu(query).astype(BF16)

    def store(at, total):
        out_ref[at, :] = total.astype(BF16)

    attend_rows(place_ref, q_all, lo_all, hi_all, k_all, v_all, store)


def own_kernel(
    place_ref, own_ref, peer_ref, w_ref, kv0, kv1, kv2, kv3, kv_peer, sum_ref, gate_ref, den_ref,
    rows, w_all, k_all, v_all, q_all, lo_all, hi_all, self_all,
):
    load_rows(0, own_ref, peer_ref, rows)
    load_weight(w_ref, w_all, 0, 512)
    load_events(place_ref, (kv0, kv1, kv2, kv3), kv_peer, k_all, v_all)
    first, last = visible(rows, 0)
    lo_all[...] = first.astype(jnp.int32)
    hi_all[...] = last.astype(jnp.int32)
    den_ref[...] = jnp.broadcast_to(last - first + 1.0, (HALF, HEAD))
    for i in range(2):
        at = pl.ds(i * 256, 256)
        proj = jnp.dot(rows[at, :D], w_all[...], preferred_element_type=F32)
        proj = silu(proj).astype(BF16)
        gate_ref[at, :] = proj[:, 0:128]
        q_all[at, :] = proj[:, 256:384]
        query = proj[:, 256:384].astype(F32)
        score = jnp.sum(query * proj[:, 384:512].astype(F32), axis=-1, keepdims=True)
        self_all[at, :] = silu(score * SCALE) * proj[:, 128:256].astype(F32)

    def store(at, total):
        sum_ref[at, :] = total + self_all[at, :]

    attend_rows(place_ref, q_all, lo_all, hi_all, k_all, v_all, store)


def scratch(columns):
    return [
        pltpu.VMEM((HALF, WIDE), BF16),
        pltpu.VMEM((D, columns), BF16),
        pltpu.VMEM((EVENTS, HEAD), BF16),
        pltpu.VMEM((EVENTS, HEAD), BF16),
        pltpu.VMEM((HALF, HEAD), BF16),
        pltpu.VMEM((HALF, 1), jnp.int32),
        pltpu.VMEM((HALF, 1), jnp.int32),
    ]


def attend_other(*args):
    return pl.pallas_call(
        other_kernel,
        out_shape=jax.ShapeDtypeStruct((HALF, HEAD), BF16),
        in_specs=[SMEM] + [VMEM] * 8,
        out_specs=VMEM,
        scratch_shapes=scratch(HEAD),
        cost_estimate=pl.CostEstimate(
            flops=4 * HALF * EVENTS * HEAD, bytes_accessed=4 << 20, transcendentals=HALF * EVENTS
        ),
        compiler_params=PARAMS,
    )(*args)


def attend_own(*args):
    shape = (HALF, HEAD)
    return pl.pallas_call(
        own_kernel,
        out_shape=[
            jax.ShapeDtypeStruct(shape, F32),
            jax.ShapeDtypeStruct(shape, BF16),
            jax.ShapeDtypeStruct(shape, F32),
        ],
        in_specs=[SMEM] + [VMEM] * 8,
        out_specs=[VMEM] * 3,
        scratch_shapes=scratch(512) + [pltpu.VMEM(shape, F32)],
        cost_estimate=pl.CostEstimate(
            flops=6 * HALF * EVENTS * HEAD, bytes_accessed=4 << 20, transcendentals=HALF * EVENTS
        ),
        compiler_params=PARAMS,
    )(*args)


def mix_kernel(place_ref, sum_ref, home_ref, den_ref, gate_ref, out_ref):
    x, core = place_ref[0], place_ref[1]
    for rel in range(2):
        for s in range(4):
            at = pl.ds(rel * 256 + s * ROWS, ROWS)
            attended = (sum_ref[at, :] + home_ref[at, :].astype(F32)) / den_ref[at, :]
            mixed = layer_norm(attended) * gate_ref[at, :].astype(F32)
            out_ref[((x - s + 4) & 3) * 2 + (core ^ rel)] = mixed.astype(BF16)


def mix(*args):
    return pl.pallas_call(
        mix_kernel,
        out_shape=jax.ShapeDtypeStruct((HEADS, ROWS, HEAD), BF16),
        in_specs=[SMEM] + [VMEM] * 4,
        out_specs=VMEM,
        compiler_params=PARAMS,
    )(*args)


def finish_kernel(x_ref, mixed_ref, w_ref, out_ref, mixed):
    for y in range(4):
        for h in range(HEADS):
            mixed[y, :, h * 32 : h * 32 + 32] = mixed_ref[h, :, y * 32 : y * 32 + 32]
    for part in range(8):
        at = pl.ds(part * HEAD, HEAD)
        total = x_ref[:, at].astype(F32)
        for y in range(4):
            total = total + jnp.dot(mixed[y], w_ref[part, y], preferred_element_type=F32)
        out_ref[:, at] = total.astype(BF16)


def finish(*args):
    return pl.pallas_call(
        finish_kernel,
        out_shape=jax.ShapeDtypeStruct((ROWS, D), BF16),
        in_specs=[VMEM] * 3,
        out_specs=VMEM,
        scratch_shapes=[pltpu.VMEM((4, ROWS, 256), BF16)],
        compiler_params=PARAMS,
    )(*args)


def body(cand_embed, hist_key, hist_value, block_owner, cand_user, cand_cutoff, w_in, w_out):
    x = cand_embed[0]
    place = [lax.axis_index("x"), lax.axis_index("c"), lax.axis_index("zh")]
    place = jnp.stack(place).astype(jnp.int32)

    mine = prepare(block_owner, x, cand_user, cand_cutoff)
    other = swap(mine, "zh")

    cols = lax.all_to_all(columns(place, w_in, w_out), "zl", 0, 0, tiled=True)

    kv = pairs(place, hist_key[0], hist_value[0])
    kv = [along_x(pair, s) if s else pair for s, pair in enumerate(kv)]
    kv_peer = swap(give(place, *kv), "c")

    cols = repeat(cols, other, *kv[1:])
    both = join(mine, other, cols)
    cols = lax.all_to_all(cols, "y", 0, 0, tiled=True)
    own_core = jnp.stack([along_x(both, s) if s else both for s in range(4)])
    peer_core = swap(own_core, "c")

    args = (place, own_core, peer_core, cols, *kv, kv_peer)
    away = attend_other(*args)
    home = swap(away, "zh")
    sums, gate, den = attend_own(*args)

    w_all = lax.all_gather(out_part(cols, own_core), LOCAL, axis=0)

    mixed = mix(place, sums, home, den, gate)
    mixed = lax.all_to_all(mixed, LOCAL, 0, 0, tiled=True)
    return finish(x, mixed, w_all)[None]


def solution(mesh):
    parts = Mesh(mesh.devices.reshape(2, 4, 2, 8, 4), ("zh", "x", "c", "zl", "y"))
    return jax.shard_map(
        body,
        mesh=parts,
        in_specs=(
            P(USER, HIST, None),
            P(USER, HIST, None),
            P(USER, HIST, None),
            P(USER, None),
            P(USER, HIST),
            P(USER, HIST),
            P(USER, None),
            P(USER, None),
        ),
        out_specs=P(USER, HIST, None),
        check_vma=False,
    )
```

time: 200 us -> 135 us (0.68)
  the two profiles are of different devices: /device:TPU:40 before, /device:TPU:168 now
where the time goes in v2:
time: 135 us; the launch traced here: 134 us
  starting transfers between devices  56.5 us (42%)
  waiting for transfers between devices  33.2 us (25%)
  Pallas kernels  16.9 us (13%)
  between operations  13.6 us (10%)
  blocking collectives  9.17 us (7%)
  local copies, waits for them, and re-layouts  4.17 us (3%)
    ppermute x4, waiting for transfers between devices, swap(): return lax.ppermute(value, axis, [(0, 1), (1, 0)])  23 us
    ppermute x4, starting transfers between devices, swap(): return lax.ppermute(value, axis, [(0, 1), (1, 0)])  21 us
    ppermute x6, starting transfers between devices, along_x(): return lax.ppermute(value, 'x', [(i, (i + steps) % 4) for i in range(4)])  19.8 us
    all_to_all x1, starting transfers between devices, body(): cols = lax.all_to_all(columns(place, w_in, w_out), 'zl', 0, 0, tiled=True)  10.8 us
    ppermute x6, waiting for transfers between devices, along_x(): return lax.ppermute(value, 'x', [(i, (i + steps) % 4) for i in range(4)])  10.2 us
    all_to_all x1, blocking collectives, body(): mixed = lax.all_to_all(mixed, LOCAL, 0, 0, tiled=True)  9.17 us
    pallas_call x1, Pallas kernels, attend_own(): pl.pallas_call(own_kernel, out_shape=[jax.ShapeDtypeStruct(shape, F32), j...  5.3 us
    all_to_all x1, starting transfers between devices, body(): cols = lax.all_to_all(cols, 'y', 0, 0, tiled=True)  4.91 us
  transfers between devices with their start and end apart: 13, of which 6 were waited for; matrix products, arithmetic and copies ran while one was open for 0% of the time, Pallas kernels for 10%

profile of v2, /device:TPU:168, one launch (start us, length us, event | category | flops | bytes accessed | tf_op | source)
XLA Modules:
  0.0 133.9 jit_solution(2782187731899021400)
XLA Ops:
  6.5 0.0 copy-start.4
  6.5 0.0 copy-start.5
  6.5 0.1 pad_add_fusion.place_ref
  6.6 0.0 copy-start.6
  6.6 1.0 copy-done.6
  7.6 0.0 copy-start.7
  7.6 0.8 copy-done.7
  8.5 0.0 copy-start.2
  8.5 0.0 copy-start.8
  8.5 0.0 copy-start.9
  8.5 0.0 copy-start.10
  8.5 1.3 shard_map.83
  9.8 10.8 %all-to-all-start = ((bf16[8,32,640]{2,1,0:T(8,128)(2,1)}), bf16[8,32,640]{2,1,0:T(8,128)(2,1)S(1)}, u32[]{:S(2)}, u32[]{:S(2)}) async-start(bf16[8,32,640]{2,1,0:T(8,128)(2,1)} %shard_map.83), calls=%async_computation | async-start | bytes 655360 | tf_op jit(solution)/shard_map/all_to_all | solution.py:381
  20.6 0.0 copy-done.4
  20.6 0.0 copy-done.5
  20.6 0.7 shard_map.84
  21.3 3.4 %collective-permute-start.1 = (bf16[2,256,256]{2,1,0:T(8,128)(2,1)S(1)}, bf16[2,256,256]{2,1,0:T(8,128)(2,1)S(1)}, u32[]{:S(2)}, u32[]{:S(2)}) collective-permute-start(bf16[2,256,256]{2,1,0:T(8,128)(2,1)S(1)} %get-tuple-element.12), channel_id=1, source_target_pairs={{0,64},{64,128},{128,192},{192,0},{1,65},{65,129},{129,193},{193,1... | collective-permute-start | bytes 786440 | tf_op jit(solution)/shard_map/ppermute | solution.py:45
  24.7 4.6 %collective-permute-start.2 = (bf16[2,256,256]{2,1,0:T(8,128)(2,1)S(1)}, bf16[2,256,256]{2,1,0:T(8,128)(2,1)S(1)}, u32[]{:S(2)}, u32[]{:S(2)}) collective-permute-start(bf16[2,256,256]{2,1,0:T(8,128)(2,1)S(1)} %get-tuple-element.13), channel_id=1, source_target_pairs={{0,128},{64,192},{128,0},{192,64},{1,129},{65,193},{129,1},{193,65... | collective-permute-start | bytes 786440 | tf_op jit(solution)/shard_map/ppermute | solution.py:45
  29.4 3.3 %collective-permute-start.3 = (bf16[2,256,256]{2,1,0:T(8,128)(2,1)S(1)}, bf16[2,256,256]{2,1,0:T(8,128)(2,1)S(1)}, u32[]{:S(2)}, u32[]{:S(2)}) collective-permute-start(bf16[2,256,256]{2,1,0:T(8,128)(2,1)S(1)} %get-tuple-element.14), channel_id=1, source_target_pairs={{0,192},{64,0},{128,64},{192,128},{1,193},{65,1},{129,65},{193,129... | collective-permute-start | bytes 786440 | tf_op jit(solution)/shard_map/ppermute | solution.py:45
  32.7 0.0 copy-done.2
  32.7 0.0 copy-done.8
  32.7 0.0 copy-done.9
  32.7 0.0 copy-done.10
  32.8 0.7 shard_map.82.mine_ref
  33.5 8.2 %collective-permute-start = (bf16[64,1152]{1,0:T(8,128)(2,1)S(1)}, bf16[64,1152]{1,0:T(8,128)(2,1)S(1)}, u32[]{:S(2)}, u32[]{:S(2)}) collective-permute-start(bf16[64,1152]{1,0:T(8,128)(2,1)S(1)} %shard_map.82.mine_ref), channel_id=1, source_target_pairs={{0,256},{256,0},{1,257},{257,1},{2,258},{258,2},{3,259},{259,3},{4... | collective-permute-start | bytes 442376 | tf_op jit(solution)/shard_map/ppermute | solution.py:41
  41.7 16.1 %collective-permute-done.refs_0_.other_ref = bf16[64,1152]{1,0:T(8,128)(2,1)S(1)} collective-permute-done((bf16[64,1152]{1,0:T(8,128)(2,1)S(1)}, bf16[64,1152]{1,0:T(8,128)(2,1)S(1)}, u32[]{:S(2)}, u32[]{:S(2)}) %collective-permute-start) | collective-permute-done | bytes 147488 | tf_op jit(solution)/shard_map/ppermute | solution.py:41
  57.8 0.0 collective-permute-done.1.refs_1_.kv1
  57.8 0.0 collective-permute-done.2.refs_2_.kv2
  57.8 0.0 collective-permute-done.3.refs_3_.kv3
  57.8 0.0 all-to-all-done.cols_ref
  57.9 1.2 shard_map.85.after_ref
  59.0 4.9 %all-to-all-start.1 = ((bf16[4,256,640]{2,1,0:T(8,128)(2,1)}), bf16[4,256,640]{2,1,0:T(8,128)(2,1)S(1)}, u32[]{:S(2)}, u32[]{:S(2)}) async-start(bf16[4,256,640]{2,1,0:T(8,128)(2,1)} %shard_map.85.after_ref), calls=%async_computation.1 | async-start | bytes 2621440 | tf_op jit(solution)/shard_map/all_to_all | solution.py:389
  63.9 0.0 all-gather.3.cloned.1.call-start
  64.0 2.2 %collective-permute-start.6 = (bf16[2,64,1152]{2,1,0:T(8,128)(2,1)S(1)}, bf16[2,64,1152]{2,1,0:T(8,128)(2,1)S(1)}, u32[]{:S(2)}, u32[]{:S(2)}) collective-permute-start(bf16[2,64,1152]{2,1,0:T(8,128)(2,1)S(1)} %shard_map.86), channel_id=1, source_target_pairs={{0,192},{64,0},{128,64},{192,128},{1,193},{65,1},{129,65},{193,129... | collective-permute-start | bytes 884744 | tf_op jit(solution)/shard_map/ppermute | solution.py:45
  66.2 4.3 %collective-permute-start.5 = (bf16[2,64,1152]{2,1,0:T(8,128)(2,1)S(1)}, bf16[2,64,1152]{2,1,0:T(8,128)(2,1)S(1)}, u32[]{:S(2)}, u32[]{:S(2)}) collective-permute-start(bf16[2,64,1152]{2,1,0:T(8,128)(2,1)S(1)} %shard_map.86), channel_id=1, source_target_pairs={{0,128},{64,192},{128,0},{192,64},{1,129},{65,193},{129,1},{193,65... | collective-permute-start | bytes 884744 | tf_op jit(solution)/shard_map/ppermute | solution.py:45
  70.5 1.9 %collective-permute-start.4 = (bf16[2,64,1152]{2,1,0:T(8,128)(2,1)S(1)}, bf16[2,64,1152]{2,1,0:T(8,128)(2,1)S(1)}, u32[]{:S(2)}, u32[]{:S(2)}) collective-permute-start(bf16[2,64,1152]{2,1,0:T(8,128)(2,1)S(1)} %shard_map.86), channel_id=1, source_target_pairs={{0,64},{64,128},{128,192},{192,0},{1,65},{65,129},{129,193},{193,1... | collective-permute-start | bytes 884744 | tf_op jit(solution)/shard_map/ppermute | solution.py:45
  72.4 3.2 %collective-permute-done.6 = bf16[2,64,1152]{2,1,0:T(8,128)(2,1)S(1)} collective-permute-done((bf16[2,64,1152]{2,1,0:T(8,128)(2,1)S(1)}, bf16[2,64,1152]{2,1,0:T(8,128)(2,1)S(1)}, u32[]{:S(2)}, u32[]{:S(2)}) %collective-permute-start.6) | collective-permute-done | bytes 294944 | tf_op jit(solution)/shard_map/ppermute | solution.py:45
  75.6 3.5 %collective-permute-done.5 = bf16[2,64,1152]{2,1,0:T(8,128)(2,1)S(1)} collective-permute-done((bf16[2,64,1152]{2,1,0:T(8,128)(2,1)S(1)}, bf16[2,64,1152]{2,1,0:T(8,128)(2,1)S(1)}, u32[]{:S(2)}, u32[]{:S(2)}) %collective-permute-start.5) | collective-permute-done | bytes 294944 | tf_op jit(solution)/shard_map/ppermute | solution.py:45
  79.1 3.5 %collective-permute-done.4 = bf16[2,64,1152]{2,1,0:T(8,128)(2,1)S(1)} collective-permute-done((bf16[2,64,1152]{2,1,0:T(8,128)(2,1)S(1)}, bf16[2,64,1152]{2,1,0:T(8,128)(2,1)S(1)}, u32[]{:S(2)}, u32[]{:S(2)}) %collective-permute-start.4) | collective-permute-done | bytes 294944 | tf_op jit(solution)/shard_map/ppermute | solution.py:45
  82.6 0.2 pad_maximum_fusion.own_ref.after_ref
  82.8 0.0 all-to-all-done.1.w_ref.cols_ref
  82.9 0.0 copy-start.1
  82.9 0.7 copy-done.1
  83.6 0.0 all-gather.3.cloned.1.call-update
  83.6 1.9 %collective-permute-start.7 = (bf16[4,2,64,1152]{3,2,1,0:T(8,128)(2,1)S(1)}, bf16[4,2,64,1152]{3,2,1,0:T(8,128)(2,1)S(1)}, u32[]{:S(2)}, u32[]{:S(2)}) collective-permute-start(bf16[4,2,64,1152]{3,2,1,0:T(8,128)(2,1)S(1)} %pad_maximum_fusion.own_ref.after_ref), channel_id=1, source_target_pairs={{0,32},{32,0},{1,33},{33,1},{2,34},{34,2},{3,35},{35,3},{4,36},{36... | collective-permute-start | bytes 3538952 | tf_op jit(solution)/shard_map/ppermute | solution.py:41
  85.5 0.6 shard_map.87
  86.2 2.4 %collective-permute-start.8 = (bf16[4,2,256,128]{3,2,1,0:T(8,128)(2,1)S(1)}, bf16[4,2,256,128]{3,2,1,0:T(8,128)(2,1)S(1)}, u32[]{:S(2)}, u32[]{:S(2)}) collective-permute-start(bf16[4,2,256,128]{3,2,1,0:T(8,128)(2,1)S(1)} %shard_map.87), channel_id=1, source_target_pairs={{0,32},{32,0},{1,33},{33,1},{2,34},{34,2},{3,35},{35,3},{4,36},{36... | collective-permute-start | bytes 1572872 | tf_op jit(solution)/shard_map/ppermute | solution.py:41
  88.6 1.5 %collective-permute-done.8.kv_peer = bf16[4,2,256,128]{3,2,1,0:T(8,128)(2,1)S(1)} collective-permute-done((bf16[4,2,256,128]{3,2,1,0:T(8,128)(2,1)S(1)}, bf16[4,2,256,128]{3,2,1,0:T(8,128)(2,1)S(1)}, u32[]{:S(2)}, u32[]{:S(2)}) %collective-permute-start.8) | collective-permute-done | bytes 524320 | tf_op jit(solution)/shard_map/ppermute | solution.py:41
  90.1 0.0 collective-permute-done.7.peer_ref
  90.1 4.9 %shard_map.89 = bf16[512,128]{1,0:T(8,128)(2,1)S(1)} custom-call(s32[3]{0:T(128)S(1)} %pad_add_fusion.place_ref, bf16[4,2,64,1152]{3,2,1,0:T(8,128)(2,1)S(1)} %pad_maximum_fusion.own_ref.after_ref, bf16[4,2,64,1152]{3,2,1,0:T(8,128)(2,1)S(1)} %collective-permute-done.7.peer_ref, bf16[4,256,640]{2,1,0:T(8,128)(2,1)S(1)} %all-to-all-done.1.w_ref.cols_ref, ...), custom_call_target="tpu_custom_call" | custom-call | flops 536870912 | bytes 4194304 | tf_op jit(solution)/shard_map/pallas_call | solution.py:298
  95.0 8.5 %collective-permute-start.9 = (bf16[512,128]{1,0:T(8,128)(2,1)S(1)}, bf16[512,128]{1,0:T(8,128)(2,1)S(1)}, u32[]{:S(2)}, u32[]{:S(2)}) collective-permute-start(bf16[512,128]{1,0:T(8,128)(2,1)S(1)} %shard_map.89), channel_id=1, source_target_pairs={{0,256},{256,0},{1,257},{257,1},{2,258},{258,2},{3,259},{259,3},{4... | collective-permute-start | bytes 393224 | tf_op jit(solution)/shard_map/ppermute | solution.py:41
  103.5 5.3 %shard_map.88 = (f32[512,128]{1,0:T(8,128)S(1)}, bf16[512,128]{1,0:T(8,128)(2,1)S(1)}, f32[512,128]{1,0:T(8,128)S(1)}) custom-call(s32[3]{0:T(128)S(1)} %pad_add_fusion.place_ref, bf16[4,2,64,1152]{3,2,1,0:T(8,128)(2,1)S(1)} %pad_maximum_fusion.own_ref.after_ref, bf16[4,2,64,1152]{3,2,1,0:T(8,128)(2,1)S(1)} %collective-permute-done.7.peer_ref, ...), custom_call_target="tpu_custom_call" | custom-call | flops 805306368 | bytes 4194304 | tf_op jit(solution)/shard_map/pallas_call | solution.py:313
  108.8 0.0 copy-start.3
  108.8 5.4 %collective-permute-done.9.home_ref = bf16[512,128]{1,0:T(8,128)(2,1)S(1)} collective-permute-done((bf16[512,128]{1,0:T(8,128)(2,1)S(1)}, bf16[512,128]{1,0:T(8,128)(2,1)S(1)}, u32[]{:S(2)}, u32[]{:S(2)}) %collective-permute-start.9) | collective-permute-done | bytes 131104 | tf_op jit(solution)/shard_map/ppermute | solution.py:41
  114.2 0.8 shard_map.90
  114.9 9.2 %all_to_all.15.mixed_ref = bf16[8,64,128]{2,1,0:T(8,128)(2,1)S(1)} all-to-all(bf16[8,64,128]{2,1,0:T(8,128)(2,1)S(1)} %shard_map.90), channel_id=1, replica_groups=mesh['zh'=2,'x'=4,'c'=2,'zl'=8,'y'=4] {'x','c'}, dimensions={0} | all-to-all | bytes 262144 | tf_op jit(solution)/shard_map/all_to_all | solution.py:401
  124.1 0.0 all-gather.3.cloned.1.call-done
  124.1 0.0 copy-done.3
  124.1 0.0 copy-start
  124.1 1.6 %copy-done = bf16[32,256,128]{2,1,0:T(8,128)(2,1)S(1)} copy-done((bf16[32,256,128]{2,1,0:T(8,128)(2,1)S(1)}, bf16[32,256,128]{2,1,0:T(8,128)(2,1)}, u32[]{:S(2)}) %copy-start) | copy-done | bytes 2097176
  125.7 1.3 shard_map.92
  (2 shorter events, 0.1 us)
Async XLA Ops:
  6.5 14.1 %copy-start.4 = (bf16[1,256,1024]{2,1,0:T(8,128)(2,1)S(1)}, bf16[1,256,1024]{2,1,0:T(8,128)(2,1)}, u32[]{:S(2)}) copy-start(bf16[1,256,1024]{2,1,0:T(8,128)(2,1)} %param.9) | copy-start | bytes 1572868
  6.5 14.1 %copy-start.5 = (bf16[1,256,1024]{2,1,0:T(8,128)(2,1)S(1)}, bf16[1,256,1024]{2,1,0:T(8,128)(2,1)}, u32[]{:S(2)}) copy-start(bf16[1,256,1024]{2,1,0:T(8,128)(2,1)} %param.10) | copy-start | bytes 1572868
  6.6 1.0 copy-start.6
  7.6 0.8 copy-start.7
  8.5 24.2 %copy-start.2 = (bf16[1,64,1024]{2,1,0:T(8,128)(2,1)S(1)}, bf16[1,64,1024]{2,1,0:T(8,128)(2,1)}, u32[]{:S(2)}) copy-start(bf16[1,64,1024]{2,1,0:T(8,128)(2,1)} %param.8) | copy-start | bytes 393220
  8.5 24.2 %copy-start.8 = (s32[1,32]{1,0:T(1,128)S(1)}, s32[1,32]{1,0:T(1,128)}, u32[]{:S(2)}) copy-start(s32[1,32]{1,0:T(1,128)} %owner_ref.1) | copy-start | bytes 388
  8.5 24.3 %copy-start.9 = (s32[1,64]{1,0:T(1,128)S(1)}, s32[1,64]{1,0:T(1,128)}, u32[]{:S(2)}) copy-start(s32[1,64]{1,0:T(1,128)} %user_ref.1) | copy-start | bytes 772
  8.5 24.3 %copy-start.10 = (s32[1,64]{1,0:T(1,128)S(1)}, s32[1,64]{1,0:T(1,128)}, u32[]{:S(2)}) copy-start(s32[1,64]{1,0:T(1,128)} %cutoff_ref.1) | copy-start | bytes 772
  9.8 48.0 %all-to-all-start = ((bf16[8,32,640]{2,1,0:T(8,128)(2,1)}), bf16[8,32,640]{2,1,0:T(8,128)(2,1)S(1)}, u32[]{:S(2)}, u32[]{:S(2)}) async-start(bf16[8,32,640]{2,1,0:T(8,128)(2,1)} %shard_map.83), calls=%async_computation | async-start | bytes 655360 | tf_op jit(solution)/shard_map/all_to_all | solution.py:381
  21.3 36.5 %collective-permute-start.1 = (bf16[2,256,256]{2,1,0:T(8,128)(2,1)S(1)}, bf16[2,256,256]{2,1,0:T(8,128)(2,1)S(1)}, u32[]{:S(2)}, u32[]{:S(2)}) collective-permute-start(bf16[2,256,256]{2,1,0:T(8,128)(2,1)S(1)} %get-tuple-element.12), channel_id=1, source_target_pairs={{0,64},{64,128},{128,192},{192,0},{1,65},{65,129},{129,193},{193,1... | collective-permute-start | bytes 786440 | tf_op jit(solution)/shard_map/ppermute | solution.py:45
  24.7 33.1 %collective-permute-start.2 = (bf16[2,256,256]{2,1,0:T(8,128)(2,1)S(1)}, bf16[2,256,256]{2,1,0:T(8,128)(2,1)S(1)}, u32[]{:S(2)}, u32[]{:S(2)}) collective-permute-start(bf16[2,256,256]{2,1,0:T(8,128)(2,1)S(1)} %get-tuple-element.13), channel_id=1, source_target_pairs={{0,128},{64,192},{128,0},{192,64},{1,129},{65,193},{129,1},{193,65... | collective-permute-start | bytes 786440 | tf_op jit(solution)/shard_map/ppermute | solution.py:45
  29.4 28.5 %collective-permute-start.3 = (bf16[2,256,256]{2,1,0:T(8,128)(2,1)S(1)}, bf16[2,256,256]{2,1,0:T(8,128)(2,1)S(1)}, u32[]{:S(2)}, u32[]{:S(2)}) collective-permute-start(bf16[2,256,256]{2,1,0:T(8,128)(2,1)S(1)} %get-tuple-element.14), channel_id=1, source_target_pairs={{0,192},{64,0},{128,64},{192,128},{1,193},{65,1},{129,65},{193,129... | collective-permute-start | bytes 786440 | tf_op jit(solution)/shard_map/ppermute | solution.py:45
  33.5 24.3 %collective-permute-start = (bf16[64,1152]{1,0:T(8,128)(2,1)S(1)}, bf16[64,1152]{1,0:T(8,128)(2,1)S(1)}, u32[]{:S(2)}, u32[]{:S(2)}) collective-permute-start(bf16[64,1152]{1,0:T(8,128)(2,1)S(1)} %shard_map.82.mine_ref), channel_id=1, source_target_pairs={{0,256},{256,0},{1,257},{257,1},{2,258},{258,2},{3,259},{259,3},{4... | collective-permute-start | bytes 442376 | tf_op jit(solution)/shard_map/ppermute | solution.py:41
  59.0 23.8 %all-to-all-start.1 = ((bf16[4,256,640]{2,1,0:T(8,128)(2,1)}), bf16[4,256,640]{2,1,0:T(8,128)(2,1)S(1)}, u32[]{:S(2)}, u32[]{:S(2)}) async-start(bf16[4,256,640]{2,1,0:T(8,128)(2,1)} %shard_map.85.after_ref), calls=%async_computation.1 | async-start | bytes 2621440 | tf_op jit(solution)/shard_map/all_to_all | solution.py:389
  63.9 60.2 %all-gather.3.cloned.1.call-start = ((), (), s32[]{:S(2)}) async-start(), calls=%async_computation.3 | async-start | bytes 2359296 | tf_op jit(solution)/shard_map/all_gather | solution.py:398
  64.0 11.7 %collective-permute-start.6 = (bf16[2,64,1152]{2,1,0:T(8,128)(2,1)S(1)}, bf16[2,64,1152]{2,1,0:T(8,128)(2,1)S(1)}, u32[]{:S(2)}, u32[]{:S(2)}) collective-permute-start(bf16[2,64,1152]{2,1,0:T(8,128)(2,1)S(1)} %shard_map.86), channel_id=1, source_target_pairs={{0,192},{64,0},{128,64},{192,128},{1,193},{65,1},{129,65},{193,129... | collective-permute-start | bytes 884744 | tf_op jit(solution)/shard_map/ppermute | solution.py:45
  66.2 13.0 %collective-permute-start.5 = (bf16[2,64,1152]{2,1,0:T(8,128)(2,1)S(1)}, bf16[2,64,1152]{2,1,0:T(8,128)(2,1)S(1)}, u32[]{:S(2)}, u32[]{:S(2)}) collective-permute-start(bf16[2,64,1152]{2,1,0:T(8,128)(2,1)S(1)} %shard_map.86), channel_id=1, source_target_pairs={{0,128},{64,192},{128,0},{192,64},{1,129},{65,193},{129,1},{193,65... | collective-permute-start | bytes 884744 | tf_op jit(solution)/shard_map/ppermute | solution.py:45
  70.5 12.2 %collective-permute-start.4 = (bf16[2,64,1152]{2,1,0:T(8,128)(2,1)S(1)}, bf16[2,64,1152]{2,1,0:T(8,128)(2,1)S(1)}, u32[]{:S(2)}, u32[]{:S(2)}) collective-permute-start(bf16[2,64,1152]{2,1,0:T(8,128)(2,1)S(1)} %shard_map.86), channel_id=1, source_target_pairs={{0,64},{64,128},{128,192},{192,0},{1,65},{65,129},{129,193},{193,1... | collective-permute-start | bytes 884744 | tf_op jit(solution)/shard_map/ppermute | solution.py:45
  82.9 0.7 copy-start.1
  83.6 6.5 %collective-permute-start.7 = (bf16[4,2,64,1152]{3,2,1,0:T(8,128)(2,1)S(1)}, bf16[4,2,64,1152]{3,2,1,0:T(8,128)(2,1)S(1)}, u32[]{:S(2)}, u32[]{:S(2)}) collective-permute-start(bf16[4,2,64,1152]{3,2,1,0:T(8,128)(2,1)S(1)} %pad_maximum_fusion.own_ref.after_ref), channel_id=1, source_target_pairs={{0,32},{32,0},{1,33},{33,1},{2,34},{34,2},{3,35},{35,3},{4,36},{36... | collective-permute-start | bytes 3538952 | tf_op jit(solution)/shard_map/ppermute | solution.py:41
  86.2 3.9 %collective-permute-start.8 = (bf16[4,2,256,128]{3,2,1,0:T(8,128)(2,1)S(1)}, bf16[4,2,256,128]{3,2,1,0:T(8,128)(2,1)S(1)}, u32[]{:S(2)}, u32[]{:S(2)}) collective-permute-start(bf16[4,2,256,128]{3,2,1,0:T(8,128)(2,1)S(1)} %shard_map.87), channel_id=1, source_target_pairs={{0,32},{32,0},{1,33},{33,1},{2,34},{34,2},{3,35},{35,3},{4,36},{36... | collective-permute-start | bytes 1572872 | tf_op jit(solution)/shard_map/ppermute | solution.py:41
  95.0 19.2 %collective-permute-start.9 = (bf16[512,128]{1,0:T(8,128)(2,1)S(1)}, bf16[512,128]{1,0:T(8,128)(2,1)S(1)}, u32[]{:S(2)}, u32[]{:S(2)}) collective-permute-start(bf16[512,128]{1,0:T(8,128)(2,1)S(1)} %shard_map.89), channel_id=1, source_target_pairs={{0,256},{256,0},{1,257},{257,1},{2,258},{258,2},{3,259},{259,3},{4... | collective-permute-start | bytes 393224 | tf_op jit(solution)/shard_map/ppermute | solution.py:41
  108.8 15.4 %copy-start.3 = (bf16[1,64,1024]{2,1,0:T(8,128)(2,1)S(1)}, bf16[1,64,1024]{2,1,0:T(8,128)(2,1)}, u32[]{:S(2)}) copy-start(bf16[1,64,1024]{2,1,0:T(8,128)(2,1)} %param.8) | copy-start | bytes 393220
  124.1 1.6 %copy-start = (bf16[32,256,128]{2,1,0:T(8,128)(2,1)S(1)}, bf16[32,256,128]{2,1,0:T(8,128)(2,1)}, u32[]{:S(2)}) copy-start(bf16[32,256,128]{2,1,0:T(8,128)(2,1)} %all-gather.3.cloned.1.call-done) | copy-start | bytes 6291460
Sparse Core Ops, SparseCore 0:
  83.7 31.2 all-gather.2

commit v3 on v2

v3 whole, which is shorter than its diff:
```python
import jax
import jax.numpy as jnp
from jax import lax
from jax.experimental import pallas as pl
from jax.experimental.pallas import tpu as pltpu
from jax.sharding import Mesh, PartitionSpec as P

D = 1024
HEADS = 8
HEAD = 128
BLOCK = 128
ROWS = 64
WIDE = D + 128
KV_ROWS = 1024
MY_ROWS = 576
HALF = 512
EVENTS = 2048
USER = ("zl", "y")
LOCAL = ("x", "c")
HIST = ("zh", "x", "c")
SCALE = HEAD ** (-0.5)
VMEM = pl.BlockSpec(memory_space=pltpu.VMEM)
ANY = pl.BlockSpec(memory_space=pl.ANY)
SMEM = pl.BlockSpec(memory_space=pltpu.SMEM)
PARAMS = pltpu.CompilerParams(vmem_limit_bytes=16 << 20)
WHOLE = pltpu.CompilerParams(vmem_limit_bytes=60 << 20)

def cost(megabytes):
    return pl.CostEstimate(flops=megabytes << 28, bytes_accessed=megabytes << 20, transcendentals=megabytes << 18)


C_PACKETS, C_COLS, C_OTHER, C_AWAY, C_OWN, C_MIX = 1, 2000, 1, 4, 4, 2000
F32 = jnp.float32
BF16 = jnp.bfloat16


def silu(v):
    h = v * 0.5
    return h + h * jnp.tanh(h)


def layer_norm(values):
    mean = jnp.mean(values, axis=-1, keepdims=True)
    centred = values - mean
    var = jnp.mean(centred * centred, axis=-1, keepdims=True)
    return centred * lax.rsqrt(var + 1e-05)


def swap(value, axis):
    return lax.ppermute(value, axis, [(0, 1), (1, 0)])


def along(value, axis, steps):
    return lax.ppermute(value, axis, [(i, (i + steps) % 4) for i in range(4)])


def prepare_kernel(owner_ref, x_ref, user_ref, cutoff_ref, after_ref, out_ref):
    out_ref[:, :D] = layer_norm(x_ref[...].astype(F32)).astype(BF16)
    square = (ROWS, ROWS)
    diagonal = lax.broadcasted_iota(jnp.int32, square, 0) == lax.broadcasted_iota(jnp.int32, square, 1)
    user = user_ref[...]
    before = jnp.zeros(user.shape, jnp.int32)
    for b in range(32):
        before = before + (owner_ref[0, b] < user).astype(jnp.int32)

    def column(row):
        spread_out = jnp.where(diagonal, jnp.broadcast_to(row.astype(F32), square), 0.0)
        return jnp.sum(spread_out, axis=1, keepdims=True)

    cutoff = cutoff_ref[...]
    lane = lax.broadcasted_iota(jnp.int32, (ROWS, 128), 1)
    tags = jnp.where(lane == 0, column(before), 0.0)
    tags = jnp.where(lane == 1, column(cutoff >> 6), tags)
    tags = jnp.where(lane == 2, column(cutoff & 63), tags)
    out_ref[:, D:] = tags.astype(BF16)


def prepare(*args):
    return pl.pallas_call(
        prepare_kernel,
        name="prepare",
        out_shape=jax.ShapeDtypeStruct((ROWS, WIDE), BF16),
        in_specs=[SMEM, VMEM, VMEM, VMEM, ANY],
        out_specs=VMEM,
        compiler_params=WHOLE,
    )(*args)


def columns_kernel(place_ref, in_ref, out_w_ref, out_ref, block, sems):
    first = (place_ref[0] * 2 + place_ref[1]) * HEAD
    copies = []
    for part in range(5):
        ref, start = (in_ref, first + part * D) if part < 4 else (out_w_ref, first)
        at = pl.ds(pl.multiple_of(start, HEAD), HEAD)
        to = block.at[:, pl.ds(part * HEAD, HEAD)]
        copies.append(pltpu.make_async_copy(ref.at[:, at], to, sems.at[part]))
        copies[part].start()
    for copy in copies:
        copy.wait()
    for z in range(8):
        out_ref[z] = block[...]


def columns(*args):
    return pl.pallas_call(
        columns_kernel,
        name="columns",
        out_shape=jax.ShapeDtypeStruct((8, 32, 640), BF16),
        in_specs=[SMEM, ANY, ANY],
        out_specs=VMEM,
        scratch_shapes=[pltpu.VMEM((32, 640), BF16), pltpu.SemaphoreType.DMA((5,))],
        compiler_params=WHOLE,
    )(*args)


def packets_kernel(place_ref, k_ref, v_ref, mine_ref, *out_refs):
    for s in range(4):
        for core in range(2):
            start = ((place_ref[0] + s) & 3) * 256 + core * HEAD
            at = pl.ds(pl.multiple_of(start, HEAD), HEAD)
            out_refs[s][core * 256 : core * 256 + 256, :] = k_ref[:, at]
            out_refs[s][512 + core * 256 : 768 + core * 256, :] = v_ref[:, at]
        for part in range(9):
            to = KV_ROWS + part * ROWS
            out_refs[s][to : to + ROWS, :] = mine_ref[:, part * HEAD : part * HEAD + HEAD]


def packets(*args):
    return pl.pallas_call(
        packets_kernel,
        name="packets",
        out_shape=[jax.ShapeDtypeStruct((KV_ROWS + MY_ROWS, HEAD), BF16)] * 4,
        in_specs=[SMEM, VMEM, VMEM, VMEM],
        out_specs=[VMEM] * 4,
        cost_estimate=cost(C_PACKETS),
        compiler_params=PARAMS,
    )(*args)


def give_kernel(place_ref, p0, p1, p2, p3, *refs):
    out_ref = refs[-1]
    other = 1 - place_ref[1]
    for s, ref in enumerate((p0, p1, p2, p3)):
        for i in range(2):
            at = pl.ds(pl.multiple_of(i * 512 + other * 256, 256), 256)
            out_ref[s, i * 256 : i * 256 + 256, :] = ref[at, :]
        out_ref[s, 512:, :] = ref[KV_ROWS:, :]


def give(*args):
    return pl.pallas_call(
        give_kernel,
        name="give",
        out_shape=jax.ShapeDtypeStruct((4, 512 + MY_ROWS, HEAD), BF16),
        in_specs=[SMEM] + [VMEM] * 4 + [ANY] * 6,
        out_specs=VMEM,
        compiler_params=PARAMS,
    )(*args)


def out_part_kernel(w0, w1, w2, w3, out_ref):
    for s, ref in enumerate((w0, w1, w2, w3)):
        out_ref[s] = ref[:, 512:]


def out_part(*args):
    return pl.pallas_call(
        out_part_kernel,
        name="out_part",
        out_shape=jax.ShapeDtypeStruct((4, 256, HEAD), BF16),
        in_specs=[VMEM] * 4,
        out_specs=VMEM,
        compiler_params=PARAMS,
    )(*args)


def hold_kernel(*refs):
    refs[-1][...] = refs[0][...]


def hold(value, estimate, *after):
    return pl.pallas_call(
        hold_kernel,
        name="hold",
        out_shape=jax.ShapeDtypeStruct(value.shape, value.dtype),
        in_specs=[VMEM] + [ANY] * len(after),
        out_specs=VMEM,
        cost_estimate=cost(estimate),
        compiler_params=PARAMS,
    )(value, *after)


def stack_kernel(*refs):
    for s in range(4):
        refs[-1][s] = refs[s][...]


def stack(first, *rest):
    return pl.pallas_call(
        stack_kernel,
        name="stack",
        out_shape=jax.ShapeDtypeStruct((4,) + first.shape, BF16),
        in_specs=[VMEM] * 4 + [ANY] * (len(rest) - 3),
        out_specs=VMEM,
        compiler_params=PARAMS,
    )(first, *rest)


def load_events(place_ref, packet_refs, peer_ref, k_all, v_all):
    core = place_ref[1]
    for s, ref in enumerate(packet_refs):
        for i, to in enumerate((k_all, v_all)):
            at = pl.ds(pl.multiple_of(i * 512 + core * 256, 256), 256)
            to[pl.ds(s * 512, 256), :] = ref[at, :]
            to[pl.ds(s * 512 + 256, 256), :] = peer_ref[s, i * 256 : i * 256 + 256, :]


def load_weight(place_ref, w_refs, w_all, first, count):
    for s, ref in enumerate(w_refs):
        y = (place_ref[3] - s + 4) & 3
        for z in range(8):
            at = pl.ds(pl.multiple_of(z * 128 + y * 32, 32), 32)
            w_all[at, :] = ref[pl.ds(z * 32, 32), pl.ds(first, count)]


def load_own_rows(packet_refs, peer_ref, rows):
    for s, ref in enumerate(packet_refs):
        for part in range(9):
            at = pl.ds(part * HEAD, HEAD)
            to, start = s * ROWS, KV_ROWS + part * ROWS
            rows[to : to + ROWS, at] = ref[start : start + ROWS, :]
            start = 512 + part * ROWS
            rows[256 + to : 256 + to + ROWS, at] = peer_ref[s, start : start + ROWS, :]


def load_other_rows(own_ref, peer_ref, rows):
    for core, ref in enumerate((own_ref, peer_ref)):
        for s in range(4):
            rows[pl.ds(core * 256 + s * ROWS, ROWS), :] = ref[s]


def visible(rows, half):
    tags = rows[:, D:].astype(F32)
    first = tags[:, 0:1] * BLOCK
    last = tags[:, 1:2] * 64.0 + tags[:, 2:3]
    return first, last


def attend_rows(place_ref, q_ref, lo_ref, hi_ref, k_all, v_all, store):
    tile, chunk = 128, 512
    x, core, half = place_ref[0], place_ref[1], place_ref[2]

    def rows(i, carry):
        at = pl.ds(pl.multiple_of(i * tile, tile), tile)
        q = q_ref[at, :]
        lo = jnp.broadcast_to(lo_ref[at, :], (tile, 256))
        hi = jnp.broadcast_to(hi_ref[at, :], (tile, 256))
        total = jnp.zeros((tile, HEAD), F32)
        for s in range(4):
            base = half * EVENTS + ((x - s + 4) & 3) * 512
            span = pl.ds(s * chunk, chunk)
            score = lax.dot_general(
                q, k_all[span, :], (((1,), (1,)), ((), ())), preferred_element_type=F32
            )
            parts = []
            for rel in range(2):
                h = score[:, rel * 256 : rel * 256 + 256] * (0.5 * SCALE)
                w = h + h * jnp.tanh(h)
                event = lax.broadcasted_iota(jnp.int32, (tile, 256), 1) + (base + (core ^ rel) * 256)
                seen = (event >= lo) & (event < hi)
                parts.append(jnp.where(seen, w, 0.0).astype(BF16))
            w = jnp.concatenate(parts, axis=1)
            total = total + jnp.dot(w, v_all[span, :], preferred_element_type=F32)
        store(at, total)
        return carry

    lax.fori_loop(0, HALF // tile, rows, 0)


def other_kernel(
    place_ref, own_ref, peer_ref, w0, w1, w2, w3, p0, p1, p2, p3, kv_peer, out_ref,
    rows, w_all, k_all, v_all, q_all, lo_all, hi_all,
):
    load_other_rows(own_ref, peer_ref, rows)
    load_weight(place_ref, (w0, w1, w2, w3), w_all, 256, HEAD)
    load_events(place_ref, (p0, p1, p2, p3), kv_peer, k_all, v_all)
    first, last = visible(rows, 0)
    lo_all[...] = first.astype(jnp.int32)
    hi_all[...] = last.astype(jnp.int32)
    query = jnp.dot(rows[:, :D], w_all[...], preferred_element_type=F32)
    q_all[...] = silu(query).astype(BF16)

    def store(at, total):
        out_ref[at, :] = total.astype(BF16)

    attend_rows(place_ref, q_all, lo_all, hi_all, k_all, v_all, store)


def own_kernel(
    place_ref, w0, w1, w2, w3, p0, p1, p2, p3, kv_peer, after_ref, sum_ref, gate_ref, den_ref,
    rows, w_all, k_all, v_all, q_all, lo_all, hi_all, self_all,
):
    load_own_rows((p0, p1, p2, p3), kv_peer, rows)
    load_weight(place_ref, (w0, w1, w2, w3), w_all, 0, 512)
    load_events(place_ref, (p0, p1, p2, p3), kv_peer, k_all, v_all)
    first, last = visible(rows, 0)
    lo_all[...] = first.astype(jnp.int32)
    hi_all[...] = last.astype(jnp.int32)
    den_ref[...] = jnp.broadcast_to(last - first + 1.0, (HALF, HEAD))
    for i in range(2):
        at = pl.ds(i * 256, 256)
        proj = jnp.dot(rows[at, :D], w_all[...], preferred_element_type=F32)
        proj = silu(proj).astype(BF16)
        gate_ref[at, :] = proj[:, 0:128]
        q_all[at, :] = proj[:, 256:384]
        query = proj[:, 256:384].astype(F32)
        score = jnp.sum(query * proj[:, 384:512].astype(F32), axis=-1, keepdims=True)
        self_all[at, :] = silu(score * SCALE) * proj[:, 128:256].astype(F32)

    def store(at, total):
        sum_ref[at, :] = total + self_all[at, :]

    attend_rows(place_ref, q_all, lo_all, hi_all, k_all, v_all, store)


def scratch(columns):
    return [
        pltpu.VMEM((HALF, WIDE), BF16),
        pltpu.VMEM((D, columns), BF16),
        pltpu.VMEM((EVENTS, HEAD), BF16),
        pltpu.VMEM((EVENTS, HEAD), BF16),
        pltpu.VMEM((HALF, HEAD), BF16),
        pltpu.VMEM((HALF, 1), jnp.int32),
        pltpu.VMEM((HALF, 1), jnp.int32),
    ]


def attend_other(*args):
    return pl.pallas_call(
        other_kernel,
        name="other",
        out_shape=jax.ShapeDtypeStruct((HALF, HEAD), BF16),
        in_specs=[SMEM] + [VMEM] * 11,
        out_specs=VMEM,
        scratch_shapes=scratch(HEAD),
        cost_estimate=cost(C_AWAY),
        compiler_params=PARAMS,
    )(*args)


def attend_own(*args):
    shape = (HALF, HEAD)
    return pl.pallas_call(
        own_kernel,
        name="own",
        out_shape=[
            jax.ShapeDtypeStruct(shape, F32),
            jax.ShapeDtypeStruct(shape, BF16),
            jax.ShapeDtypeStruct(shape, F32),
        ],
        in_specs=[SMEM] + [VMEM] * 9 + [ANY],
        out_specs=[VMEM] * 3,
        scratch_shapes=scratch(512) + [pltpu.VMEM(shape, F32)],
        cost_estimate=cost(C_OWN),
        compiler_params=PARAMS,
    )(*args)


def mix_kernel(place_ref, sum_ref, home_ref, den_ref, gate_ref, out_ref):
    x, core = place_ref[0], place_ref[1]
    for rel in range(2):
        for s in range(4):
            at = pl.ds(rel * 256 + s * ROWS, ROWS)
            attended = (sum_ref[at, :] + home_ref[at, :].astype(F32)) / den_ref[at, :]
            mixed = layer_norm(attended) * gate_ref[at, :].astype(F32)
            out_ref[((x - s + 4) & 3) * 2 + (core ^ rel)] = mixed.astype(BF16)


def mix(*args):
    return pl.pallas_call(
        mix_kernel,
        name="mix",
        out_shape=jax.ShapeDtypeStruct((HEADS, ROWS, HEAD), BF16),
        in_specs=[SMEM] + [VMEM] * 4,
        out_specs=VMEM,
        cost_estimate=cost(C_MIX),
        compiler_params=PARAMS,
    )(*args)


def finish_kernel(place_ref, x_ref, mixed_ref, own_ref, peer_ref, out_ref, mixed):
    along, core, line = place_ref[0], place_ref[1], place_ref[3]
    for y in range(4):
        for h in range(HEADS):
            mixed[y, :, h * 32 : h * 32 + 32] = mixed_ref[h, :, y * 32 : y * 32 + 32]
    for s in range(4):
        for rel, ref in enumerate((own_ref, peer_ref)):
            at = ((along - s + 4) & 3) * 2 + (core ^ rel)
            at = pl.ds(pl.multiple_of(at * HEAD, HEAD), HEAD)
            total = x_ref[:, at].astype(F32)
            for step in range(4):
                left = mixed[(line - step + 4) & 3]
                total = total + jnp.dot(left, ref[s, step], preferred_element_type=F32)
            out_ref[:, at] = total.astype(BF16)


def finish(*args):
    return pl.pallas_call(
        finish_kernel,
        name="finish",
        out_shape=jax.ShapeDtypeStruct((ROWS, D), BF16),
        in_specs=[SMEM] + [VMEM] * 4,
        out_specs=VMEM,
        scratch_shapes=[pltpu.VMEM((4, ROWS, 256), BF16)],
        compiler_params=PARAMS,
    )(*args)


def body(cand_embed, hist_key, hist_value, block_owner, cand_user, cand_cutoff, w_in, w_out):
    x = cand_embed[0]
    place = [lax.axis_index("x"), lax.axis_index("c"), lax.axis_index("zh"), lax.axis_index("y")]
    place = jnp.stack(place).astype(jnp.int32)

    cols = columns(place, w_in, w_out)
    mine = prepare(block_owner, x, cand_user, cand_cutoff, cols)
    other = swap(mine, "zh")
    cols = lax.all_to_all(cols, "zl", 0, 0, tiled=True)

    out = packets(place, hist_key[0], hist_value[0], mine)
    packs = [along(pack, "x", s) if s else pack for s, pack in enumerate(out)]
    cols = hold(cols.reshape(256, 640), C_COLS, other)
    other = hold(other, C_OTHER, cols)
    cols = [along(cols, "y", s) if s else cols for s in range(4)]
    others = [along(other, "x", s) if s else other for s in range(4)]
    kv_peer = swap(give(place, *packs, *cols[1:], *others[1:]), "c")
    own_core = stack(*others)
    peer_core = swap(own_core, "c")
    w_part = out_part(*cols)
    w_part = [along(w_part, "x", s) if s else w_part for s in range(4)]

    away = attend_other(place, own_core, peer_core, *cols, *packs, kv_peer)
    home = swap(away, "zh")
    sums, gate, den = attend_own(place, *cols, *packs, kv_peer, away)
    w_own = stack(*w_part, away)
    w_peer = swap(w_own, "c")

    mixed = mix(place, sums, home, den, gate)
    mixed = lax.all_to_all(mixed, LOCAL, 0, 0, tiled=True)
    return finish(place, x, mixed, w_own, w_peer)[None]


def solution(mesh):
    parts = Mesh(mesh.devices.reshape(2, 4, 2, 8, 4), ("zh", "x", "c", "zl", "y"))
    return jax.shard_map(
        body,
        mesh=parts,
        in_specs=(
            P(USER, HIST, None),
            P(USER, HIST, None),
            P(USER, HIST, None),
            P(USER, None),
            P(USER, HIST),
            P(USER, HIST),
            P(USER, None),
            P(USER, None),
        ),
        out_specs=P(USER, HIST, None),
        check_vma=False,
    )
```

time: 135 us -> 128 us (0.948)
  the two profiles are of different devices: /device:TPU:168 before, /device:TPU:32 now
where the time goes in v3:
time: 128 us; the launch traced here: 127 us
  starting transfers between devices  80 us (62%)
  Pallas kernels  23.9 us (19%)
  waiting for transfers between devices  12.4 us (10%)
  blocking collectives  9.15 us (7%)
    ppermute x12, starting transfers between devices, along(): return lax.ppermute(value, axis, [(i, (i + steps) % 4) for i in range(4)])  44.6 us
    ppermute x5, starting transfers between devices, swap(): return lax.ppermute(value, axis, [(0, 1), (1, 0)])  22.7 us
    all_to_all x1, starting transfers between devices, body(): cols = lax.all_to_all(cols, 'zl', 0, 0, tiled=True)  12.6 us
    all_to_all x1, blocking collectives, body(): mixed = lax.all_to_all(mixed, LOCAL, 0, 0, tiled=True)  9.15 us
    pallas_call x1, Pallas kernels, attend_own(): pl.pallas_call(own_kernel, name='own', out_shape=[jax.ShapeDtypeStruct(sh...  6.13 us
    all_to_all x1, waiting for transfers between devices, body(): cols = lax.all_to_all(cols, 'zl', 0, 0, tiled=True)  5.62 us
    pallas_call x1, Pallas kernels, attend_other(): pl.pallas_call(other_kernel, name='other', out_shape=jax.ShapeDtypeStruct...  5.58 us
    ppermute x12, waiting for transfers between devices, along(): return lax.ppermute(value, axis, [(i, (i + steps) % 4) for i in range(4)])  3.78 us
  transfers between devices with their start and end apart: 18, of which 5 were waited for; matrix products, arithmetic and copies ran while one was open for 0% of the time, Pallas kernels for 14%

profile of v3, /device:TPU:32, one launch (start us, length us, event | category | flops | bytes accessed | tf_op | source)
XLA Modules:
  0.0 127.4 jit_solution(6001551246991327289)
XLA Ops:
  0.0 0.0 copy-start.1
  0.0 0.0 copy-start.2
  0.0 0.7 pad_add_fusion.place_ref
  0.7 0.0 copy-start.4
  0.7 2.3 %columns.1.after_ref = bf16[8,32,640]{2,1,0:T(8,128)(2,1)} custom-call(s32[4]{0:T(128)} %pad_add_fusion.place_ref, bf16[32,4096]{1,0:T(8,128)(2,1)} %in_ref.1, bf16[32,1024]{1,0:T(8,128)(2,1)} %out_w_ref.1), custom_call_target="tpu_custom_call" | custom-call | tf_op jit(solution)/shard_map/columns/pallas_call | solution.py:105
  3.0 12.6 %all-to-all-start = ((bf16[8,32,640]{2,1,0:T(8,128)(2,1)}), bf16[8,32,640]{2,1,0:T(8,128)(2,1)S(1)}, u32[]{:S(2)}, u32[]{:S(2)}) async-start(bf16[8,32,640]{2,1,0:T(8,128)(2,1)} %columns.1.after_ref), calls=%async_computation | async-start | bytes 655360 | tf_op jit(solution)/shard_map/all_to_all | solution.py:427
  15.7 1.8 %prepare.1.mine_ref = bf16[64,1152]{1,0:T(8,128)(2,1)} custom-call(s32[1,32]{1,0:T(1,128)} %owner_ref.1, bf16[64,1024]{1,0:T(8,128)(2,1)} %bitcast.11, s32[1,64]{1,0:T(1,128)} %user_ref.1, s32[1,64]{1,0:T(1,128)} %cutoff_ref.1, bf16[8,32,640]{2,1,0:T(8,128)(2,1)} %columns.1.after_ref), custom_call_target="tpu_custom_call" | custom-call | tf_op jit(solution)/shard_map/prepare/pallas_call | solution.py:79
  17.5 8.2 %collective-permute-start = (bf16[64,1152]{1,0:T(8,128)(2,1)}, bf16[64,1152]{1,0:T(8,128)(2,1)S(1)}, u32[]{:S(2)}, u32[]{:S(2)}) collective-permute-start(bf16[64,1152]{1,0:T(8,128)(2,1)} %prepare.1.mine_ref), channel_id=1, source_target_pairs={{0,256},{256,0},{1,257},{257,1},{2,258},{258,2},{3,259},{259,3},{4... | collective-permute-start | bytes 442376 | tf_op jit(solution)/shard_map/ppermute | solution.py:50
  25.7 0.0 copy-done.1
  25.7 0.0 copy-done.2
  25.7 0.0 copy-done.4
  25.7 0.0 copy-start
  25.7 0.9 copy-done
  26.6 1.8 %packets.1 = (bf16[1600,128]{1,0:T(8,128)(2,1)S(1)}, bf16[1600,128]{1,0:T(8,128)(2,1)}, bf16[1600,128]{1,0:T(8,128)(2,1)}, bf16[1600,128]{1,0:T(8,128)(2,1)}) custom-call(s32[4]{0:T(128)S(1)} %copy-done.4, bf16[256,1024]{1,0:T(8,128)(2,1)S(1)} %bitcast.9, bf16[256,1024]{1,0:T(8,128)(2,1)S(1)} %bitcast.10, bf16[64,1152]{1,0:T(8,128)(2,1)S(1)} %copy-done), custom_call_target="tpu_custom_call" | custom-call | flops 268435456 | bytes 1048576 | tf_op jit(solution)/shard_map/packets/pallas_call | solution.py:129
  28.5 3.4 %collective-permute-start.4 = (bf16[1600,128]{1,0:T(8,128)(2,1)}, bf16[1600,128]{1,0:T(8,128)(2,1)}, u32[]{:S(2)}, u32[]{:S(2)}) collective-permute-start(bf16[1600,128]{1,0:T(8,128)(2,1)} %get-tuple-element.13), channel_id=1, source_target_pairs={{0,64},{64,128},{128,192},{192,0},{1,65},{65,129},{129,193},{193,1... | collective-permute-start | bytes 1228808 | tf_op jit(solution)/shard_map/ppermute | solution.py:54
  31.9 4.6 %collective-permute-start.5 = (bf16[1600,128]{1,0:T(8,128)(2,1)}, bf16[1600,128]{1,0:T(8,128)(2,1)}, u32[]{:S(2)}, u32[]{:S(2)}) collective-permute-start(bf16[1600,128]{1,0:T(8,128)(2,1)} %get-tuple-element.14), channel_id=1, source_target_pairs={{0,128},{64,192},{128,0},{192,64},{1,129},{65,193},{129,1},{193,65... | collective-permute-start | bytes 1228808 | tf_op jit(solution)/shard_map/ppermute | solution.py:54
  36.5 3.3 %collective-permute-start.6 = (bf16[1600,128]{1,0:T(8,128)(2,1)}, bf16[1600,128]{1,0:T(8,128)(2,1)}, u32[]{:S(2)}, u32[]{:S(2)}) collective-permute-start(bf16[1600,128]{1,0:T(8,128)(2,1)} %get-tuple-element.15), channel_id=1, source_target_pairs={{0,192},{64,0},{128,64},{192,128},{1,193},{65,1},{129,65},{193,129... | collective-permute-start | bytes 1228808 | tf_op jit(solution)/shard_map/ppermute | solution.py:54
  39.9 0.0 collective-permute-done.refs_1_.refs_0_
  39.9 5.6 %all-to-all-done = bf16[8,32,640]{2,1,0:T(8,128)(2,1)S(1)} async-done(((bf16[8,32,640]{2,1,0:T(8,128)(2,1)}), bf16[8,32,640]{2,1,0:T(8,128)(2,1)S(1)}, u32[]{:S(2)}, u32[]{:S(2)}) %all-to-all-start) | async-done | bytes 327712 | tf_op jit(solution)/shard_map/all_to_all | solution.py:427
  45.5 3.5 %collective-permute-start.1 = (bf16[256,640]{1,0:T(8,128)(2,1)S(1)}, bf16[256,640]{1,0:T(8,128)(2,1)S(1)}, u32[]{:S(2)}, u32[]{:S(2)}) collective-permute-start(bf16[256,640]{1,0:T(8,128)(2,1)S(1)} %hold.2.refs_1_.w0), channel_id=1, source_target_pairs={{0,1},{1,2},{2,3},{3,0},{4,5},{5,6},{6,7},{7,4},{8,9},{9,10},{10,1... | collective-permute-start | bytes 983048 | tf_op jit(solution)/shard_map/ppermute | solution.py:54
  49.0 4.8 %collective-permute-start.2 = (bf16[256,640]{1,0:T(8,128)(2,1)S(1)}, bf16[256,640]{1,0:T(8,128)(2,1)S(1)}, u32[]{:S(2)}, u32[]{:S(2)}) collective-permute-start(bf16[256,640]{1,0:T(8,128)(2,1)S(1)} %hold.2.refs_1_.w0), channel_id=1, source_target_pairs={{0,2},{1,3},{2,0},{3,1},{4,6},{5,7},{6,4},{7,5},{8,10},{9,11},{10,... | collective-permute-start | bytes 983048 | tf_op jit(solution)/shard_map/ppermute | solution.py:54
  53.8 0.0 collective-permute-done.4.p1
  53.9 3.3 %collective-permute-start.3 = (bf16[256,640]{1,0:T(8,128)(2,1)S(1)}, bf16[256,640]{1,0:T(8,128)(2,1)S(1)}, u32[]{:S(2)}, u32[]{:S(2)}) collective-permute-start(bf16[256,640]{1,0:T(8,128)(2,1)S(1)} %hold.2.refs_1_.w0), channel_id=1, source_target_pairs={{0,3},{1,0},{2,1},{3,2},{4,7},{5,4},{6,5},{7,6},{8,11},{9,8},{10,9... | collective-permute-start | bytes 983048 | tf_op jit(solution)/shard_map/ppermute | solution.py:54
  57.1 0.0 collective-permute-done.5.p2
  57.1 3.4 %collective-permute-start.7 = (bf16[64,1152]{1,0:T(8,128)(2,1)S(1)}, bf16[64,1152]{1,0:T(8,128)(2,1)S(1)}, u32[]{:S(2)}, u32[]{:S(2)}) collective-permute-start(bf16[64,1152]{1,0:T(8,128)(2,1)S(1)} %hold.3.refs_0_), channel_id=1, source_target_pairs={{0,64},{64,128},{128,192},{192,0},{1,65},{65,129},{129,193},{193,1... | collective-permute-start | bytes 442376 | tf_op jit(solution)/shard_map/ppermute | solution.py:54
  60.6 0.0 collective-permute-done.6.p3
  60.6 4.6 %collective-permute-start.8 = (bf16[64,1152]{1,0:T(8,128)(2,1)S(1)}, bf16[64,1152]{1,0:T(8,128)(2,1)S(1)}, u32[]{:S(2)}, u32[]{:S(2)}) collective-permute-start(bf16[64,1152]{1,0:T(8,128)(2,1)S(1)} %hold.3.refs_0_), channel_id=1, source_target_pairs={{0,128},{64,192},{128,0},{192,64},{1,129},{65,193},{129,1},{193,65... | collective-permute-start | bytes 442376 | tf_op jit(solution)/shard_map/ppermute | solution.py:54
  65.2 0.2 collective-permute-done.7.refs_3_.refs_1_
  65.4 3.4 %collective-permute-start.9 = (bf16[64,1152]{1,0:T(8,128)(2,1)S(1)}, bf16[64,1152]{1,0:T(8,128)(2,1)S(1)}, u32[]{:S(2)}, u32[]{:S(2)}) collective-permute-start(bf16[64,1152]{1,0:T(8,128)(2,1)S(1)} %hold.3.refs_0_), channel_id=1, source_target_pairs={{0,192},{64,0},{128,64},{192,128},{1,193},{65,1},{129,65},{193,129... | collective-permute-start | bytes 442376 | tf_op jit(solution)/shard_map/ppermute | solution.py:54
  68.8 0.3 collective-permute-done.8.refs_4_.refs_2_
  69.1 3.3 %collective-permute-done.9.refs_5_.refs_3_ = bf16[64,1152]{1,0:T(8,128)(2,1)S(1)} collective-permute-done((bf16[64,1152]{1,0:T(8,128)(2,1)S(1)}, bf16[64,1152]{1,0:T(8,128)(2,1)S(1)}, u32[]{:S(2)}, u32[]{:S(2)}) %collective-permute-start.9) | collective-permute-done | bytes 147488 | tf_op jit(solution)/shard_map/ppermute | solution.py:54
  72.4 0.0 collective-permute-done.1.refs_0_.w1
  72.4 0.0 collective-permute-done.2.refs_1_.w2
  72.4 0.0 collective-permute-done.3.refs_2_.w3
  72.4 1.3 %give.1 = bf16[4,1088,128]{2,1,0:T(8,128)(2,1)S(1)} custom-call(s32[4]{0:T(128)S(1)} %copy-done.4, bf16[1600,128]{1,0:T(8,128)(2,1)S(1)} %get-tuple-element.12.p0, bf16[1600,128]{1,0:T(8,128)(2,1)} %collective-permute-done.4.p1, bf16[1600,128]{1,0:T(8,128)(2,1)} %collective-permute-done.5.p2, bf16[1600,128]{1,0:T(8,128)(2,1)} %collective-permute-done.6.p3, ...), custom_call_target="tpu_custom_call" | custom-call | tf_op jit(solution)/shard_map/give/pallas_call | solution.py:151
  73.8 1.9 %collective-permute-start.10 = (bf16[4,1088,128]{2,1,0:T(8,128)(2,1)S(1)}, bf16[4,1088,128]{2,1,0:T(8,128)(2,1)S(1)}, u32[]{:S(2)}, u32[]{:S(2)}) collective-permute-start(bf16[4,1088,128]{2,1,0:T(8,128)(2,1)S(1)} %give.1), channel_id=1, source_target_pairs={{0,32},{32,0},{1,33},{33,1},{2,34},{34,2},{3,35},{35,3},{4,36},{36... | collective-permute-start | bytes 3342344 | tf_op jit(solution)/shard_map/ppermute | solution.py:50
  75.8 2.4 %collective-permute-start.11 = (bf16[4,64,1152]{2,1,0:T(8,128)(2,1)S(1)}, bf16[4,64,1152]{2,1,0:T(8,128)(2,1)S(1)}, u32[]{:S(2)}, u32[]{:S(2)}) collective-permute-start(bf16[4,64,1152]{2,1,0:T(8,128)(2,1)S(1)} %stack.22.own_ref), channel_id=1, source_target_pairs={{0,32},{32,0},{1,33},{33,1},{2,34},{34,2},{3,35},{35,3},{4,36},{36... | collective-permute-start | bytes 1769480 | tf_op jit(solution)/shard_map/ppermute | solution.py:50
  78.2 2.2 %collective-permute-start.13 = (bf16[4,256,128]{2,1,0:T(8,128)(2,1)S(1)}, bf16[4,256,128]{2,1,0:T(8,128)(2,1)S(1)}, u32[]{:S(2)}, u32[]{:S(2)}) collective-permute-start(bf16[4,256,128]{2,1,0:T(8,128)(2,1)S(1)} %out_part.1.refs_0_), channel_id=1, source_target_pairs={{0,64},{64,128},{128,192},{192,0},{1,65},{65,129},{129,193},{193,1... | collective-permute-start | bytes 786440 | tf_op jit(solution)/shard_map/ppermute | solution.py:54
  80.5 5.8 %collective-permute-start.14 = (bf16[4,256,128]{2,1,0:T(8,128)(2,1)S(1)}, bf16[4,256,128]{2,1,0:T(8,128)(2,1)S(1)}, u32[]{:S(2)}, u32[]{:S(2)}) collective-permute-start(bf16[4,256,128]{2,1,0:T(8,128)(2,1)S(1)} %out_part.1.refs_0_), channel_id=1, source_target_pairs={{0,128},{64,192},{128,0},{192,64},{1,129},{65,193},{129,1},{193,65... | collective-permute-start | bytes 786440 | tf_op jit(solution)/shard_map/ppermute | solution.py:54
  86.3 2.1 %collective-permute-start.15 = (bf16[4,256,128]{2,1,0:T(8,128)(2,1)S(1)}, bf16[4,256,128]{2,1,0:T(8,128)(2,1)S(1)}, u32[]{:S(2)}, u32[]{:S(2)}) collective-permute-start(bf16[4,256,128]{2,1,0:T(8,128)(2,1)S(1)} %out_part.1.refs_0_), channel_id=1, source_target_pairs={{0,192},{64,0},{128,64},{192,128},{1,193},{65,1},{129,65},{193,129... | collective-permute-start | bytes 786440 | tf_op jit(solution)/shard_map/ppermute | solution.py:54
  88.4 0.0 collective-permute-done.11.peer_ref
  88.4 0.0 collective-permute-done.10.kv_peer
  88.5 5.6 %other.1.after_ref.refs_4_ = bf16[512,128]{1,0:T(8,128)(2,1)S(1)} custom-call(s32[4]{0:T(128)S(1)} %copy-done.4, bf16[4,64,1152]{2,1,0:T(8,128)(2,1)S(1)} %stack.22.own_ref, bf16[4,64,1152]{2,1,0:T(8,128)(2,1)S(1)} %collective-permute-done.11.peer_ref, bf16[256,640]{1,0:T(8,128)(2,1)S(1)} %hold.2.refs_1_.w0, ...), custom_call_target="tpu_custom_call" | custom-call | flops 1073741824 | bytes 4194304 | tf_op jit(solution)/shard_map/other/pallas_call | solution.py:339
  94.0 8.3 %collective-permute-start.12 = (bf16[512,128]{1,0:T(8,128)(2,1)S(1)}, bf16[512,128]{1,0:T(8,128)(2,1)S(1)}, u32[]{:S(2)}, u32[]{:S(2)}) collective-permute-start(bf16[512,128]{1,0:T(8,128)(2,1)S(1)} %other.1.after_ref.refs_4_), channel_id=1, source_target_pairs={{0,256},{256,0},{1,257},{257,1},{2,258},{258,2},{3,259},{259,3},{4... | collective-permute-start | bytes 393224 | tf_op jit(solution)/shard_map/ppermute | solution.py:50
  102.3 0.0 collective-permute-done.13.refs_1_
  102.3 0.0 collective-permute-done.14.refs_2_
  102.4 0.0 collective-permute-done.15.refs_3_
  102.4 1.1 stack.23.own_ref
  103.4 1.9 %collective-permute-start.16 = (bf16[4,4,256,128]{3,2,1,0:T(8,128)(2,1)}, bf16[4,4,256,128]{3,2,1,0:T(8,128)(2,1)}, u32[]{:S(2)}, u32[]{:S(2)}) collective-permute-start(bf16[4,4,256,128]{3,2,1,0:T(8,128)(2,1)} %stack.23.own_ref), channel_id=1, source_target_pairs={{0,32},{32,0},{1,33},{33,1},{2,34},{34,2},{3,35},{35,3},{4,36},{36... | collective-permute-start | bytes 3145736 | tf_op jit(solution)/shard_map/ppermute | solution.py:50
  105.4 6.1 %own.1 = (f32[512,128]{1,0:T(8,128)S(1)}, bf16[512,128]{1,0:T(8,128)(2,1)S(1)}, f32[512,128]{1,0:T(8,128)S(1)}) custom-call(s32[4]{0:T(128)S(1)} %copy-done.4, bf16[256,640]{1,0:T(8,128)(2,1)S(1)} %hold.2.refs_1_.w0, bf16[256,640]{1,0:T(8,128)(2,1)S(1)} %collective-permute-done.1.refs_0_.w1, bf16[256,640]{1,0:T(8,128)(2,1)S(1)} %collective-permute-done.2.refs_1_.w2, ...), custom_call_target="tpu_custom_call" | custom-call | flops 1073741824 | bytes 4194304 | tf_op jit(solution)/shard_map/own/pallas_call | solution.py:353
  111.5 3.0 %collective-permute-done.12.home_ref = bf16[512,128]{1,0:T(8,128)(2,1)S(1)} collective-permute-done((bf16[512,128]{1,0:T(8,128)(2,1)S(1)}, bf16[512,128]{1,0:T(8,128)(2,1)S(1)}, u32[]{:S(2)}, u32[]{:S(2)}) %collective-permute-start.12) | collective-permute-done | bytes 131104 | tf_op jit(solution)/shard_map/ppermute | solution.py:50
  114.5 0.0 copy-start.3
  114.5 0.8 mix.1
  115.3 9.1 %all_to_all.10.mixed_ref = bf16[8,64,128]{2,1,0:T(8,128)(2,1)S(1)} all-to-all(bf16[8,64,128]{2,1,0:T(8,128)(2,1)S(1)} %mix.1), channel_id=1, replica_groups=mesh['zh'=2,'x'=4,'c'=2,'zl'=8,'y'=4] {'x','c'}, dimensions={0} | all-to-all | bytes 262144 | tf_op jit(solution)/shard_map/all_to_all | solution.py:448
  124.5 0.0 collective-permute-done.16.peer_ref
  124.5 0.0 copy-done.3
  124.5 2.9 %finish.1 = bf16[64,1024]{1,0:T(8,128)(2,1)} custom-call(s32[4]{0:T(128)S(1)} %copy-done.4, bf16[64,1024]{1,0:T(8,128)(2,1)S(1)} %bitcast.12, bf16[8,64,128]{2,1,0:T(8,128)(2,1)S(1)} %all_to_all.10.mixed_ref, bf16[4,4,256,128]{3,2,1,0:T(8,128)(2,1)} %stack.23.own_ref, bf16[4,4,256,128]{3,2,1,0:T(8,128)(2,1)} %collective-permute-done.16.peer_ref), custom_call_target="tpu_custom_call" | custom-call | tf_op jit(solution)/shard_map/finish/pallas_call | solution.py:408
  (4 shorter events, 0.1 us)
Async XLA Ops:
  0.0 25.7 %copy-start.1 = (bf16[1,256,1024]{2,1,0:T(8,128)(2,1)S(1)}, bf16[1,256,1024]{2,1,0:T(8,128)(2,1)}, u32[]{:S(2)}) copy-start(bf16[1,256,1024]{2,1,0:T(8,128)(2,1)} %param.9) | copy-start | bytes 1572868
  0.0 25.7 %copy-start.2 = (bf16[1,256,1024]{2,1,0:T(8,128)(2,1)S(1)}, bf16[1,256,1024]{2,1,0:T(8,128)(2,1)}, u32[]{:S(2)}) copy-start(bf16[1,256,1024]{2,1,0:T(8,128)(2,1)} %param.10) | copy-start | bytes 1572868
  0.7 25.0 %copy-start.4 = (s32[4]{0:T(128)S(1)}, s32[4]{0:T(128)}, u32[]{:S(2)}) copy-start(s32[4]{0:T(128)} %pad_add_fusion.place_ref) | copy-start | bytes 52
  3.0 42.5 %all-to-all-start = ((bf16[8,32,640]{2,1,0:T(8,128)(2,1)}), bf16[8,32,640]{2,1,0:T(8,128)(2,1)S(1)}, u32[]{:S(2)}, u32[]{:S(2)}) async-start(bf16[8,32,640]{2,1,0:T(8,128)(2,1)} %columns.1.after_ref), calls=%async_computation | async-start | bytes 655360 | tf_op jit(solution)/shard_map/all_to_all | solution.py:427
  17.5 22.4 %collective-permute-start = (bf16[64,1152]{1,0:T(8,128)(2,1)}, bf16[64,1152]{1,0:T(8,128)(2,1)S(1)}, u32[]{:S(2)}, u32[]{:S(2)}) collective-permute-start(bf16[64,1152]{1,0:T(8,128)(2,1)} %prepare.1.mine_ref), channel_id=1, source_target_pairs={{0,256},{256,0},{1,257},{257,1},{2,258},{258,2},{3,259},{259,3},{4... | collective-permute-start | bytes 442376 | tf_op jit(solution)/shard_map/ppermute | solution.py:50
  25.7 0.9 copy-start
  28.5 25.4 %collective-permute-start.4 = (bf16[1600,128]{1,0:T(8,128)(2,1)}, bf16[1600,128]{1,0:T(8,128)(2,1)}, u32[]{:S(2)}, u32[]{:S(2)}) collective-permute-start(bf16[1600,128]{1,0:T(8,128)(2,1)} %get-tuple-element.13), channel_id=1, source_target_pairs={{0,64},{64,128},{128,192},{192,0},{1,65},{65,129},{129,193},{193,1... | collective-permute-start | bytes 1228808 | tf_op jit(solution)/shard_map/ppermute | solution.py:54
  31.9 25.3 %collective-permute-start.5 = (bf16[1600,128]{1,0:T(8,128)(2,1)}, bf16[1600,128]{1,0:T(8,128)(2,1)}, u32[]{:S(2)}, u32[]{:S(2)}) collective-permute-start(bf16[1600,128]{1,0:T(8,128)(2,1)} %get-tuple-element.14), channel_id=1, source_target_pairs={{0,128},{64,192},{128,0},{192,64},{1,129},{65,193},{129,1},{193,65... | collective-permute-start | bytes 1228808 | tf_op jit(solution)/shard_map/ppermute | solution.py:54
  36.5 24.0 %collective-permute-start.6 = (bf16[1600,128]{1,0:T(8,128)(2,1)}, bf16[1600,128]{1,0:T(8,128)(2,1)}, u32[]{:S(2)}, u32[]{:S(2)}) collective-permute-start(bf16[1600,128]{1,0:T(8,128)(2,1)} %get-tuple-element.15), channel_id=1, source_target_pairs={{0,192},{64,0},{128,64},{192,128},{1,193},{65,1},{129,65},{193,129... | collective-permute-start | bytes 1228808 | tf_op jit(solution)/shard_map/ppermute | solution.py:54
  45.5 26.9 %collective-permute-start.1 = (bf16[256,640]{1,0:T(8,128)(2,1)S(1)}, bf16[256,640]{1,0:T(8,128)(2,1)S(1)}, u32[]{:S(2)}, u32[]{:S(2)}) collective-permute-start(bf16[256,640]{1,0:T(8,128)(2,1)S(1)} %hold.2.refs_1_.w0), channel_id=1, source_target_pairs={{0,1},{1,2},{2,3},{3,0},{4,5},{5,6},{6,7},{7,4},{8,9},{9,10},{10,1... | collective-permute-start | bytes 983048 | tf_op jit(solution)/shard_map/ppermute | solution.py:54
  49.0 23.4 %collective-permute-start.2 = (bf16[256,640]{1,0:T(8,128)(2,1)S(1)}, bf16[256,640]{1,0:T(8,128)(2,1)S(1)}, u32[]{:S(2)}, u32[]{:S(2)}) collective-permute-start(bf16[256,640]{1,0:T(8,128)(2,1)S(1)} %hold.2.refs_1_.w0), channel_id=1, source_target_pairs={{0,2},{1,3},{2,0},{3,1},{4,6},{5,7},{6,4},{7,5},{8,10},{9,11},{10,... | collective-permute-start | bytes 983048 | tf_op jit(solution)/shard_map/ppermute | solution.py:54
  53.9 18.6 %collective-permute-start.3 = (bf16[256,640]{1,0:T(8,128)(2,1)S(1)}, bf16[256,640]{1,0:T(8,128)(2,1)S(1)}, u32[]{:S(2)}, u32[]{:S(2)}) collective-permute-start(bf16[256,640]{1,0:T(8,128)(2,1)S(1)} %hold.2.refs_1_.w0), channel_id=1, source_target_pairs={{0,3},{1,0},{2,1},{3,2},{4,7},{5,4},{6,5},{7,6},{8,11},{9,8},{10,9... | collective-permute-start | bytes 983048 | tf_op jit(solution)/shard_map/ppermute | solution.py:54
  57.1 8.2 %collective-permute-start.7 = (bf16[64,1152]{1,0:T(8,128)(2,1)S(1)}, bf16[64,1152]{1,0:T(8,128)(2,1)S(1)}, u32[]{:S(2)}, u32[]{:S(2)}) collective-permute-start(bf16[64,1152]{1,0:T(8,128)(2,1)S(1)} %hold.3.refs_0_), channel_id=1, source_target_pairs={{0,64},{64,128},{128,192},{192,0},{1,65},{65,129},{129,193},{193,1... | collective-permute-start | bytes 442376 | tf_op jit(solution)/shard_map/ppermute | solution.py:54
  60.6 8.5 %collective-permute-start.8 = (bf16[64,1152]{1,0:T(8,128)(2,1)S(1)}, bf16[64,1152]{1,0:T(8,128)(2,1)S(1)}, u32[]{:S(2)}, u32[]{:S(2)}) collective-permute-start(bf16[64,1152]{1,0:T(8,128)(2,1)S(1)} %hold.3.refs_0_), channel_id=1, source_target_pairs={{0,128},{64,192},{128,0},{192,64},{1,129},{65,193},{129,1},{193,65... | collective-permute-start | bytes 442376 | tf_op jit(solution)/shard_map/ppermute | solution.py:54
  65.4 7.0 %collective-permute-start.9 = (bf16[64,1152]{1,0:T(8,128)(2,1)S(1)}, bf16[64,1152]{1,0:T(8,128)(2,1)S(1)}, u32[]{:S(2)}, u32[]{:S(2)}) collective-permute-start(bf16[64,1152]{1,0:T(8,128)(2,1)S(1)} %hold.3.refs_0_), channel_id=1, source_target_pairs={{0,192},{64,0},{128,64},{192,128},{1,193},{65,1},{129,65},{193,129... | collective-permute-start | bytes 442376 | tf_op jit(solution)/shard_map/ppermute | solution.py:54
  73.8 14.7 %collective-permute-start.10 = (bf16[4,1088,128]{2,1,0:T(8,128)(2,1)S(1)}, bf16[4,1088,128]{2,1,0:T(8,128)(2,1)S(1)}, u32[]{:S(2)}, u32[]{:S(2)}) collective-permute-start(bf16[4,1088,128]{2,1,0:T(8,128)(2,1)S(1)} %give.1), channel_id=1, source_target_pairs={{0,32},{32,0},{1,33},{33,1},{2,34},{34,2},{3,35},{35,3},{4,36},{36... | collective-permute-start | bytes 3342344 | tf_op jit(solution)/shard_map/ppermute | solution.py:50
  75.8 12.7 %collective-permute-start.11 = (bf16[4,64,1152]{2,1,0:T(8,128)(2,1)S(1)}, bf16[4,64,1152]{2,1,0:T(8,128)(2,1)S(1)}, u32[]{:S(2)}, u32[]{:S(2)}) collective-permute-start(bf16[4,64,1152]{2,1,0:T(8,128)(2,1)S(1)} %stack.22.own_ref), channel_id=1, source_target_pairs={{0,32},{32,0},{1,33},{33,1},{2,34},{34,2},{3,35},{35,3},{4,36},{36... | collective-permute-start | bytes 1769480 | tf_op jit(solution)/shard_map/ppermute | solution.py:50
  78.2 24.1 %collective-permute-start.13 = (bf16[4,256,128]{2,1,0:T(8,128)(2,1)S(1)}, bf16[4,256,128]{2,1,0:T(8,128)(2,1)S(1)}, u32[]{:S(2)}, u32[]{:S(2)}) collective-permute-start(bf16[4,256,128]{2,1,0:T(8,128)(2,1)S(1)} %out_part.1.refs_0_), channel_id=1, source_target_pairs={{0,64},{64,128},{128,192},{192,0},{1,65},{65,129},{129,193},{193,1... | collective-permute-start | bytes 786440 | tf_op jit(solution)/shard_map/ppermute | solution.py:54
  80.5 21.9 %collective-permute-start.14 = (bf16[4,256,128]{2,1,0:T(8,128)(2,1)S(1)}, bf16[4,256,128]{2,1,0:T(8,128)(2,1)S(1)}, u32[]{:S(2)}, u32[]{:S(2)}) collective-permute-start(bf16[4,256,128]{2,1,0:T(8,128)(2,1)S(1)} %out_part.1.refs_0_), channel_id=1, source_target_pairs={{0,128},{64,192},{128,0},{192,64},{1,129},{65,193},{129,1},{193,65... | collective-permute-start | bytes 786440 | tf_op jit(solution)/shard_map/ppermute | solution.py:54
  86.3 16.1 %collective-permute-start.15 = (bf16[4,256,128]{2,1,0:T(8,128)(2,1)S(1)}, bf16[4,256,128]{2,1,0:T(8,128)(2,1)S(1)}, u32[]{:S(2)}, u32[]{:S(2)}) collective-permute-start(bf16[4,256,128]{2,1,0:T(8,128)(2,1)S(1)} %out_part.1.refs_0_), channel_id=1, source_target_pairs={{0,192},{64,0},{128,64},{192,128},{1,193},{65,1},{129,65},{193,129... | collective-permute-start | bytes 786440 | tf_op jit(solution)/shard_map/ppermute | solution.py:54
  94.0 20.5 %collective-permute-start.12 = (bf16[512,128]{1,0:T(8,128)(2,1)S(1)}, bf16[512,128]{1,0:T(8,128)(2,1)S(1)}, u32[]{:S(2)}, u32[]{:S(2)}) collective-permute-start(bf16[512,128]{1,0:T(8,128)(2,1)S(1)} %other.1.after_ref.refs_4_), channel_id=1, source_target_pairs={{0,256},{256,0},{1,257},{257,1},{2,258},{258,2},{3,259},{259,3},{4... | collective-permute-start | bytes 393224 | tf_op jit(solution)/shard_map/ppermute | solution.py:50
  103.4 21.0 %collective-permute-start.16 = (bf16[4,4,256,128]{3,2,1,0:T(8,128)(2,1)}, bf16[4,4,256,128]{3,2,1,0:T(8,128)(2,1)}, u32[]{:S(2)}, u32[]{:S(2)}) collective-permute-start(bf16[4,4,256,128]{3,2,1,0:T(8,128)(2,1)} %stack.23.own_ref), channel_id=1, source_target_pairs={{0,32},{32,0},{1,33},{33,1},{2,34},{34,2},{3,35},{35,3},{4,36},{36... | collective-permute-start | bytes 3145736 | tf_op jit(solution)/shard_map/ppermute | solution.py:50
  114.5 9.9 %copy-start.3 = (bf16[1,64,1024]{2,1,0:T(8,128)(2,1)S(1)}, bf16[1,64,1024]{2,1,0:T(8,128)(2,1)}, u32[]{:S(2)}) copy-start(bf16[1,64,1024]{2,1,0:T(8,128)(2,1)} %param.8) | copy-start | bytes 393220

commit v4 on v3

v4 whole, which is shorter than its diff:
```python
import jax
import jax.numpy as jnp
from jax import lax
from jax.experimental import pallas as pl
from jax.experimental.pallas import tpu as pltpu
from jax.sharding import Mesh, PartitionSpec as P

D = 1024
HEADS = 8
HEAD = 128
BLOCK = 128
ROWS = 64
WIDE = D + 128
KV_ROWS = 1024
MY_ROWS = 576
HALF = 512
EVENTS = 2048
USER = ("zl", "y")
LOCAL = ("x", "c")
HIST = ("zh", "x", "c")
SCALE = HEAD ** (-0.5)
VMEM = pl.BlockSpec(memory_space=pltpu.VMEM)
ANY = pl.BlockSpec(memory_space=pl.ANY)
SMEM = pl.BlockSpec(memory_space=pltpu.SMEM)
PARAMS = pltpu.CompilerParams(vmem_limit_bytes=16 << 20)
WHOLE = pltpu.CompilerParams(vmem_limit_bytes=60 << 20)

def cost(megabytes):
    return pl.CostEstimate(flops=megabytes << 28, bytes_accessed=megabytes << 20, transcendentals=megabytes << 18)


C_PARTS, C_PACKETS, C_PROJECT, C_AWAY, C_OWN, C_MIX = 1, 1, 4, 4, 4, 2000
F32 = jnp.float32
BF16 = jnp.bfloat16


def silu(v):
    h = v * 0.5
    return h + h * jnp.tanh(h)


def layer_norm(values):
    mean = jnp.mean(values, axis=-1, keepdims=True)
    centred = values - mean
    var = jnp.mean(centred * centred, axis=-1, keepdims=True)
    return centred * lax.rsqrt(var + 1e-05)


def swap(value, axis):
    return lax.ppermute(value, axis, [(0, 1), (1, 0)])


def along(value, axis, steps):
    return lax.ppermute(value, axis, [(i, (i + steps) % 4) for i in range(4)])


def columns_kernel(in_ref, out_w_ref, out_ref, block, sems):
    first = (lax.axis_index("x") * 2 + lax.axis_index("c")) * HEAD
    copies = []
    for part in range(5):
        ref, start = (in_ref, first + part * D) if part < 4 else (out_w_ref, first)
        at = pl.ds(pl.multiple_of(start, HEAD), HEAD)
        to = block.at[:, pl.ds(part * HEAD, HEAD)]
        copies.append(pltpu.make_async_copy(ref.at[:, at], to, sems.at[part]))
        copies[part].start()
    for copy in copies:
        copy.wait()
    for z in range(8):
        out_ref[z] = block[...]


def columns(*args):
    return pl.pallas_call(
        columns_kernel,
        name="columns",
        out_shape=jax.ShapeDtypeStruct((8, 32, 640), BF16),
        in_specs=[ANY, ANY],
        out_specs=VMEM,
        scratch_shapes=[pltpu.VMEM((32, 640), BF16), pltpu.SemaphoreType.DMA((5,))],
        compiler_params=WHOLE,
    )(*args)


def tags_of(owner_ref, user, cutoff):
    square = (ROWS, ROWS)
    diagonal = lax.broadcasted_iota(jnp.int32, square, 0) == lax.broadcasted_iota(jnp.int32, square, 1)
    before = jnp.zeros(user.shape, jnp.int32)
    for b in range(32):
        before = before + (owner_ref[0, b] < user).astype(jnp.int32)

    def column(row):
        spread_out = jnp.where(diagonal, jnp.broadcast_to(row.astype(F32), square), 0.0)
        return jnp.sum(spread_out, axis=1, keepdims=True)

    lane = lax.broadcasted_iota(jnp.int32, (ROWS, 128), 1)
    tags = jnp.where(lane == 0, column(before), 0.0)
    tags = jnp.where(lane == 1, column(cutoff >> 6), tags)
    return jnp.where(lane == 2, column(cutoff & 63), tags)


def parts_kernel(
    place_ref, owner_ref, x_ref, user_ref, cutoff_ref, k_ref, v_ref, keep_ref, give_ref, rest_ref
):
    along, core = place_ref[0], place_ref[1]
    normed = layer_norm(x_ref[...].astype(F32)).astype(BF16)
    for part in range(8):
        give_ref[part * ROWS : part * ROWS + ROWS, :] = normed[:, part * HEAD : part * HEAD + HEAD]
    tags = tags_of(owner_ref, user_ref[...], cutoff_ref[...]).astype(BF16)
    give_ref[8 * ROWS : MY_ROWS, :] = tags
    keep_ref[2048:, :] = give_ref[0:MY_ROWS, :]
    places = ((give_ref, MY_ROWS), (rest_ref, 0), (rest_ref, 512), (rest_ref, 1024))
    for s in range(4):
        for (to, base), which in (((keep_ref, s * 512), core), (places[s], 1 - core)):
            start = ((along + s) & 3) * 256 + which * HEAD
            at = pl.ds(pl.multiple_of(start, HEAD), HEAD)
            to[base : base + 256, :] = k_ref[:, at]
            to[base + 256 : base + 512, :] = v_ref[:, at]


def parts(*args):
    rows = (2048 + MY_ROWS, MY_ROWS + 512, 1536)
    return pl.pallas_call(
        parts_kernel,
        name="parts",
        out_shape=[jax.ShapeDtypeStruct((n, HEAD), BF16) for n in rows],
        in_specs=[SMEM, SMEM] + [VMEM] * 5,
        out_specs=[VMEM] * 3,
        cost_estimate=cost(C_PARTS),
        compiler_params=PARAMS,
    )(*args)


def packets_kernel(keep_ref, got_ref, rest_ref, *out_refs):
    for s, ref in enumerate(out_refs):
        ref[0:512, :] = keep_ref[s * 512 : s * 512 + 512, :]
        if s == 0:
            ref[512:1024, :] = got_ref[MY_ROWS:, :]
        else:
            ref[512:1024, :] = rest_ref[s * 512 - 512 : s * 512, :]
        ref[KV_ROWS : KV_ROWS + MY_ROWS, :] = keep_ref[2048:, :]
        ref[KV_ROWS + MY_ROWS :, :] = got_ref[0:MY_ROWS, :]


def packets(*args):
    return pl.pallas_call(
        packets_kernel,
        name="packets",
        out_shape=[jax.ShapeDtypeStruct((KV_ROWS + 2 * MY_ROWS, HEAD), BF16)] * 4,
        in_specs=[VMEM] * 3,
        out_specs=[VMEM] * 4,
        cost_estimate=cost(C_PACKETS),
        compiler_params=PARAMS,
    )(*args)


def out_part_kernel(w0, w1, w2, w3, after_ref, out_ref):
    for s, ref in enumerate((w0, w1, w2, w3)):
        out_ref[s] = ref[:, 512:]


def out_part(*args):
    return pl.pallas_call(
        out_part_kernel,
        name="out_part",
        out_shape=jax.ShapeDtypeStruct((4, 256, HEAD), BF16),
        in_specs=[VMEM] * 4 + [ANY],
        out_specs=VMEM,
        compiler_params=PARAMS,
    )(*args)


def stack_kernel(*refs):
    for s in range(4):
        refs[-1][s] = refs[s][...]


def stack(first, *rest):
    return pl.pallas_call(
        stack_kernel,
        name="stack",
        out_shape=jax.ShapeDtypeStruct((4,) + first.shape, BF16),
        in_specs=[VMEM] * 4 + [ANY] * (len(rest) - 3),
        out_specs=VMEM,
        compiler_params=PARAMS,
    )(first, *rest)


def load_weight(place_ref, w_refs, w_all, first, count):
    for s, ref in enumerate(w_refs):
        y = (place_ref[3] - s + 4) & 3
        for z in range(8):
            at = pl.ds(pl.multiple_of(z * 128 + y * 32, 32), 32)
            w_all[at, :] = ref[pl.ds(z * 32, 32), pl.ds(first, count)]


def load_rows(packet_refs, rows):
    for s, ref in enumerate(packet_refs):
        for rel in range(2):
            for part in range(9):
                to, start = rel * 256 + s * ROWS, KV_ROWS + rel * MY_ROWS + part * ROWS
                rows[to : to + ROWS, pl.ds(part * HEAD, HEAD)] = ref[start : start + ROWS, :]


def visible(tags):
    return tags[:, 0:1] * BLOCK, tags[:, 1:2] * 64.0 + tags[:, 2:3]


def project_kernel(
    place_ref, w0, w1, w2, w3, p0, p1, p2, p3,
    query_ref, gate_ref, den_ref, self_ref, rows, w_all,
):
    load_rows((p0, p1, p2, p3), rows)
    load_weight(place_ref, (w0, w1, w2, w3), w_all, 0, 512)
    for i in range(2):
        at = pl.ds(i * 256, 256)
        proj = jnp.dot(rows[at, :D], w_all[...], preferred_element_type=F32)
        proj = silu(proj).astype(BF16)
        gate_ref[at, :] = proj[:, 0:128]
        query_ref[at, :] = proj[:, 256:384]
        query = proj[:, 256:384].astype(F32)
        score = jnp.sum(query * proj[:, 384:512].astype(F32), axis=-1, keepdims=True)
        self_ref[at, :] = silu(score * SCALE) * proj[:, 128:256].astype(F32)
    for i in range(4):
        at = pl.ds(i * 128, 128)
        tags = rows[at, D:].astype(F32)
        first, last = visible(tags)
        den_ref[at, :] = jnp.broadcast_to(last - first + 1.0, (128, HEAD))
        query_ref[HALF + i * 16 : HALF + i * 16 + 16, :] = tags.T[0:16, :].astype(BF16)


def project(*args):
    shape = (HALF, HEAD)
    return pl.pallas_call(
        project_kernel,
        name="project",
        out_shape=[
            jax.ShapeDtypeStruct((HALF + 64, HEAD), BF16),
            jax.ShapeDtypeStruct(shape, BF16),
            jax.ShapeDtypeStruct(shape, F32),
            jax.ShapeDtypeStruct(shape, F32),
        ],
        in_specs=[SMEM] + [VMEM] * 8,
        out_specs=[VMEM] * 4,
        scratch_shapes=[pltpu.VMEM((HALF, WIDE), BF16), pltpu.VMEM((D, 512), BF16)],
        cost_estimate=cost(C_PROJECT),
        compiler_params=PARAMS,
    )(*args)


def attend_kernel(place_ref, q_ref, p0, p1, p2, p3, plus_ref, out_ref):
    x, core, half = place_ref[0], place_ref[1], place_ref[2]
    event = lax.broadcasted_iota(jnp.int32, (256, 256), 1)
    for tile in range(2):
        at = pl.ds(tile * 256, 256)
        lows, counts = [], []
        for i in range(2):
            row = HALF + (tile * 2 + i) * 16
            tags = q_ref[row : row + 16, :].astype(F32)
            tags = jnp.concatenate([tags, jnp.zeros((112, 128), F32)], axis=0).T
            first, last = visible(tags)
            lows.append(first.astype(jnp.int32))
            counts.append((last - first).astype(jnp.uint32))
        low = jnp.broadcast_to(jnp.concatenate(lows, axis=0), (256, 256))
        count = jnp.broadcast_to(jnp.concatenate(counts, axis=0), (256, 256))
        query = q_ref[at, :]
        total = jnp.zeros((256, HEAD), F32)
        for s, ref in enumerate((p0, p1, p2, p3)):
            for rel in range(2):
                base = half * EVENTS + ((x - s + 4) & 3) * 512 + (core ^ rel) * 256
                row = rel * 512
                score = lax.dot_general(
                    query, ref[row : row + 256, :], (((1,), (1,)), ((), ())), preferred_element_type=F32
                )
                h = score * (0.5 * SCALE)
                w = h + h * jnp.tanh(h)
                seen = (event + base - low).astype(jnp.uint32) < count
                w = jnp.where(seen, w, 0.0).astype(BF16)
                total = total + jnp.dot(w, ref[row + 256 : row + 512, :], preferred_element_type=F32)
        if out_ref.dtype == F32:
            total = total + plus_ref[at, :]
        out_ref[at, :] = total.astype(out_ref.dtype)


def attend(name, dtype, *args):
    return pl.pallas_call(
        attend_kernel,
        name=name,
        out_shape=jax.ShapeDtypeStruct((HALF, HEAD), dtype),
        in_specs=[SMEM] + [VMEM] * 6,
        out_specs=VMEM,
        cost_estimate=cost(C_AWAY if name == "other" else C_OWN),
        compiler_params=PARAMS,
    )(*args)


def mix_kernel(place_ref, sum_ref, home_ref, den_ref, gate_ref, out_ref):
    x, core = place_ref[0], place_ref[1]
    for rel in range(2):
        for s in range(4):
            at = pl.ds(rel * 256 + s * ROWS, ROWS)
            attended = (sum_ref[at, :] + home_ref[at, :].astype(F32)) / den_ref[at, :]
            mixed = layer_norm(attended) * gate_ref[at, :].astype(F32)
            out_ref[((x - s + 4) & 3) * 2 + (core ^ rel)] = mixed.astype(BF16)


def mix(*args):
    return pl.pallas_call(
        mix_kernel,
        name="mix",
        out_shape=jax.ShapeDtypeStruct((HEADS, ROWS, HEAD), BF16),
        in_specs=[SMEM] + [VMEM] * 4,
        out_specs=VMEM,
        cost_estimate=cost(C_MIX),
        compiler_params=PARAMS,
    )(*args)


def finish_kernel(place_ref, x_ref, mixed_ref, w0, w1, w2, w3, peer_ref, out_ref, by_line):
    along, core, line = place_ref[0], place_ref[1], place_ref[3]
    for y in range(4):
        for h in range(HEADS):
            by_line[y, :, h * 32 : h * 32 + 32] = mixed_ref[h, :, y * 32 : y * 32 + 32]
    left = jnp.concatenate([by_line[(line - step + 4) & 3] for step in range(4)], axis=1)
    for s, ref in enumerate((w0, w1, w2, w3)):
        for rel in range(2):
            at = ((along - s + 4) & 3) * 2 + (core ^ rel)
            at = pl.ds(pl.multiple_of(at * HEAD, HEAD), HEAD)
            right = (ref[...] if rel == 0 else peer_ref[s]).reshape(D, HEAD)
            projected = jnp.dot(left, right, preferred_element_type=F32)
            out_ref[:, at] = (x_ref[:, at].astype(F32) + projected).astype(BF16)


def finish(*args):
    return pl.pallas_call(
        finish_kernel,
        name="finish",
        out_shape=jax.ShapeDtypeStruct((ROWS, D), BF16),
        in_specs=[SMEM] + [VMEM] * 7,
        out_specs=VMEM,
        scratch_shapes=[pltpu.VMEM((4, ROWS, 256), BF16)],
        compiler_params=PARAMS,
    )(*args)


def body(cand_embed, hist_key, hist_value, block_owner, cand_user, cand_cutoff, w_in, w_out):
    x = cand_embed[0]
    place = [lax.axis_index(a) for a in ("x", "c", "zh", "y")]
    place = jnp.stack(place).astype(jnp.int32)

    cols = columns(w_in, w_out)
    cols = lax.all_to_all(cols, "zl", 0, 0, tiled=True).reshape(256, 640)
    cols = [along(cols, "y", s) if s else cols for s in range(4)]

    keep, *got = parts(place, block_owner, x, cand_user, cand_cutoff, hist_key[0], hist_value[0])
    packs = packets(keep, *[swap(part, "c") for part in got])
    packs = [along(pack, "x", s) if s else pack for s, pack in enumerate(packs)]

    query, gate, den, self_term = project(place, *cols, *packs)
    query_other = swap(query, "zh")

    w_part = out_part(*cols, query)
    w_part = [along(w_part, "x", s) if s else w_part for s in range(4)]

    away = attend("other", BF16, place, query_other, *packs, self_term)
    home = swap(away, "zh")
    sums = attend("own", F32, place, query, *packs, self_term)
    w_own = stack(*w_part, away)
    w_peer = swap(w_own, "c")

    mixed = mix(place, sums, home, den, gate)
    mixed = lax.all_to_all(mixed, LOCAL, 0, 0, tiled=True)
    return finish(place, x, mixed, *w_part, w_peer)[None]


def solution(mesh):
    parts = Mesh(mesh.devices.reshape(2, 4, 2, 8, 4), ("zh", "x", "c", "zl", "y"))
    return jax.shard_map(
        body,
        mesh=parts,
        in_specs=(
            P(USER, HIST, None),
            P(USER, HIST, None),
            P(USER, HIST, None),
            P(USER, None),
            P(USER, HIST),
            P(USER, HIST),
            P(USER, None),
            P(USER, None),
        ),
        out_specs=P(USER, HIST, None),
        check_vma=False,
    )
```

time: 128 us -> 118 us (0.922)
  the two profiles are of different devices: /device:TPU:32 before, /device:TPU:160 now
where the time goes in v4:
time: 118 us; the launch traced here: 117 us
  starting transfers between devices  62.8 us (53%)
  waiting for transfers between devices  28.4 us (24%)
  Pallas kernels  16.7 us (14%)
  blocking collectives  8.52 us (7%)
    ppermute x9, starting transfers between devices, along(): return lax.ppermute(value, axis, [(i, (i + steps) % 4) for i in range(4)])  30.1 us
    ppermute x5, starting transfers between devices, swap(): return lax.ppermute(value, axis, [(0, 1), (1, 0)])  21.7 us
    ppermute x5, waiting for transfers between devices, swap(): return lax.ppermute(value, axis, [(0, 1), (1, 0)])  14.5 us
    ppermute x9, waiting for transfers between devices, along(): return lax.ppermute(value, axis, [(i, (i + steps) % 4) for i in range(4)])  13.8 us
    all_to_all x1, starting transfers between devices, body(): cols = lax.all_to_all(cols, 'zl', 0, 0, tiled=True).reshape(256, 640)  11 us
    all_to_all x1, blocking collectives, body(): mixed = lax.all_to_all(mixed, LOCAL, 0, 0, tiled=True)  8.52 us
    pallas_call x2, Pallas kernels, attend(): pl.pallas_call(attend_kernel, name=name, out_shape=jax.ShapeDtypeStruct((...  6.3 us
    pallas_call x1, Pallas kernels, finish(): pl.pallas_call(finish_kernel, name='finish', out_shape=jax.ShapeDtypeStru...  2.58 us
  transfers between devices with their start and end apart: 15, of which 6 were waited for; matrix products, arithmetic and copies ran while one was open for 0% of the time, Pallas kernels for 9%

profile of v4, /device:TPU:160, one launch (start us, length us, event | category | flops | bytes accessed | tf_op | source)
XLA Modules:
  0.0 117.4 jit_solution(18035348767552088753)
XLA Ops:
  0.0 0.0 copy-start.1
  0.0 0.0 copy-start
  0.0 1.7 %columns.1 = bf16[8,32,640]{2,1,0:T(8,128)(2,1)} custom-call(bf16[32,4096]{1,0:T(8,128)(2,1)} %in_ref.1, bf16[32,1024]{1,0:T(8,128)(2,1)} %out_w_ref.1), custom_call_target="tpu_custom_call" | custom-call | tf_op jit(solution)/shard_map/columns/pallas_call | solution.py:73
  1.7 0.0 copy-start.2
  1.7 11.0 %all-to-all-start = ((bf16[8,32,640]{2,1,0:T(8,128)(2,1)}), bf16[8,32,640]{2,1,0:T(8,128)(2,1)S(1)}, u32[]{:S(2)}, u32[]{:S(2)}) async-start(bf16[8,32,640]{2,1,0:T(8,128)(2,1)} %columns.1), calls=%async_computation | async-start | bytes 655360 | tf_op jit(solution)/shard_map/all_to_all | solution.py:351
  12.7 0.1 pad_add_fusion.place_ref
  12.7 0.0 copy-start.3
  12.7 0.0 copy-start.4
  12.7 0.0 copy-start.5
  12.7 0.0 copy-done.1
  12.7 0.0 copy-done
  12.8 0.0 copy-done.2
  12.8 0.6 copy-done.3
  13.4 0.0 copy-done.4
  13.4 0.0 copy-done.5
  13.4 1.0 parts.1
  14.4 1.9 %collective-permute-start.4 = (bf16[1536,128]{1,0:T(8,128)(2,1)S(1)}, bf16[1536,128]{1,0:T(8,128)(2,1)S(1)}, u32[]{:S(2)}, u32[]{:S(2)}) collective-permute-start(bf16[1536,128]{1,0:T(8,128)(2,1)S(1)} %get-tuple-element.18), channel_id=1, source_target_pairs={{0,32},{32,0},{1,33},{33,1},{2,34},{34,2},{3,35},{35,3},{4,36},{36... | collective-permute-start | bytes 1179656 | tf_op jit(solution)/shard_map/ppermute | solution.py:50
  16.3 2.4 %collective-permute-start.3 = (bf16[1088,128]{1,0:T(8,128)(2,1)S(1)}, bf16[1088,128]{1,0:T(8,128)(2,1)S(1)}, u32[]{:S(2)}, u32[]{:S(2)}) collective-permute-start(bf16[1088,128]{1,0:T(8,128)(2,1)S(1)} %get-tuple-element.17), channel_id=1, source_target_pairs={{0,32},{32,0},{1,33},{33,1},{2,34},{34,2},{3,35},{35,3},{4,36},{36... | collective-permute-start | bytes 835592 | tf_op jit(solution)/shard_map/ppermute | solution.py:50
  18.7 1.2 collective-permute-done.3.got_ref
  19.9 0.0 collective-permute-done.4.rest_ref
  19.9 1.2 %packets.1 = (bf16[2176,128]{1,0:T(8,128)(2,1)S(1)}, bf16[2176,128]{1,0:T(8,128)(2,1)S(1)}, bf16[2176,128]{1,0:T(8,128)(2,1)}, bf16[2176,128]{1,0:T(8,128)(2,1)}) custom-call(bf16[2624,128]{1,0:T(8,128)(2,1)S(1)} %get-tuple-element.16.keep_ref, bf16[1088,128]{1,0:T(8,128)(2,1)S(1)} %collective-permute-done.3.got_ref, ...), custom_call_target="tpu_custom_call" | custom-call | flops 268435456 | bytes 1048576 | tf_op jit(solution)/shard_map/packets/pallas_call | solution.py:145
  21.1 3.4 %collective-permute-start.5 = (bf16[2176,128]{1,0:T(8,128)(2,1)S(1)}, bf16[2176,128]{1,0:T(8,128)(2,1)S(1)}, u32[]{:S(2)}, u32[]{:S(2)}) collective-permute-start(bf16[2176,128]{1,0:T(8,128)(2,1)S(1)} %get-tuple-element.20), channel_id=1, source_target_pairs={{0,64},{64,128},{128,192},{192,0},{1,65},{65,129},{129,193},{193,1... | collective-permute-start | bytes 1671176 | tf_op jit(solution)/shard_map/ppermute | solution.py:54
  24.5 4.6 %collective-permute-start.6 = (bf16[2176,128]{1,0:T(8,128)(2,1)}, bf16[2176,128]{1,0:T(8,128)(2,1)S(1)}, u32[]{:S(2)}, u32[]{:S(2)}) collective-permute-start(bf16[2176,128]{1,0:T(8,128)(2,1)} %get-tuple-element.21), channel_id=1, source_target_pairs={{0,128},{64,192},{128,0},{192,64},{1,129},{65,193},{129,1},{193,65... | collective-permute-start | bytes 1671176 | tf_op jit(solution)/shard_map/ppermute | solution.py:54
  29.1 3.3 %collective-permute-start.7 = (bf16[2176,128]{1,0:T(8,128)(2,1)}, bf16[2176,128]{1,0:T(8,128)(2,1)}, u32[]{:S(2)}, u32[]{:S(2)}) collective-permute-start(bf16[2176,128]{1,0:T(8,128)(2,1)} %get-tuple-element.22), channel_id=1, source_target_pairs={{0,192},{64,0},{128,64},{192,128},{1,193},{65,1},{129,65},{193,129... | collective-permute-start | bytes 1671176 | tf_op jit(solution)/shard_map/ppermute | solution.py:54
  32.5 0.0 all-to-all-done
  32.5 4.9 %collective-permute-start.2 = (bf16[256,640]{1,0:T(8,128)(2,1)S(1)}, bf16[256,640]{1,0:T(8,128)(2,1)S(1)}, u32[]{:S(2)}, u32[]{:S(2)}) collective-permute-start(bf16[256,640]{1,0:T(8,128)(2,1)S(1)} %bitcast.9), channel_id=1, source_target_pairs={{0,3},{1,0},{2,1},{3,2},{4,7},{5,4},{6,5},{7,6},{8,11},{9,8},{10,9... | collective-permute-start | bytes 983048 | tf_op jit(solution)/shard_map/ppermute | solution.py:54
  37.4 2.5 %collective-permute-start.1 = (bf16[256,640]{1,0:T(8,128)(2,1)S(1)}, bf16[256,640]{1,0:T(8,128)(2,1)S(1)}, u32[]{:S(2)}, u32[]{:S(2)}) collective-permute-start(bf16[256,640]{1,0:T(8,128)(2,1)S(1)} %bitcast.10), channel_id=1, source_target_pairs={{0,2},{1,3},{2,0},{3,1},{4,6},{5,7},{6,4},{7,5},{8,10},{9,11},{10,... | collective-permute-start | bytes 983048 | tf_op jit(solution)/shard_map/ppermute | solution.py:54
  40.0 0.0 collective-permute-done.5.p1
  40.0 2.9 %collective-permute-start = (bf16[256,640]{1,0:T(8,128)(2,1)S(1)}, bf16[256,640]{1,0:T(8,128)(2,1)S(1)}, u32[]{:S(2)}, u32[]{:S(2)}) collective-permute-start(bf16[256,640]{1,0:T(8,128)(2,1)S(1)} %bitcast.11), channel_id=1, source_target_pairs={{0,1},{1,2},{2,3},{3,0},{4,5},{5,6},{6,7},{7,4},{8,9},{9,10},{10,1... | collective-permute-start | bytes 983048 | tf_op jit(solution)/shard_map/ppermute | solution.py:54
  42.9 9.1 %collective-permute-done.6.p2 = bf16[2176,128]{1,0:T(8,128)(2,1)S(1)} collective-permute-done((bf16[2176,128]{1,0:T(8,128)(2,1)}, bf16[2176,128]{1,0:T(8,128)(2,1)S(1)}, u32[]{:S(2)}, u32[]{:S(2)}) %collective-permute-start.6) | collective-permute-done | bytes 557088 | tf_op jit(solution)/shard_map/ppermute | solution.py:54
  52.0 1.9 %collective-permute-done.7.p3 = bf16[2176,128]{1,0:T(8,128)(2,1)} collective-permute-done((bf16[2176,128]{1,0:T(8,128)(2,1)}, bf16[2176,128]{1,0:T(8,128)(2,1)}, u32[]{:S(2)}, u32[]{:S(2)}) %collective-permute-start.7) | collective-permute-done | bytes 557088 | tf_op jit(solution)/shard_map/ppermute | solution.py:54
  53.9 0.0 collective-permute-done.2.w3
  53.9 0.0 collective-permute-done.1.w2
  53.9 2.8 %collective-permute-done.w1 = bf16[256,640]{1,0:T(8,128)(2,1)S(1)} collective-permute-done((bf16[256,640]{1,0:T(8,128)(2,1)S(1)}, bf16[256,640]{1,0:T(8,128)(2,1)S(1)}, u32[]{:S(2)}, u32[]{:S(2)}) %collective-permute-start) | collective-permute-done | bytes 327712 | tf_op jit(solution)/shard_map/ppermute | solution.py:54
  56.7 2.1 %project.1 = (bf16[576,128]{1,0:T(8,128)(2,1)S(1)}, bf16[512,128]{1,0:T(8,128)(2,1)S(1)}, f32[512,128]{1,0:T(8,128)S(1)}, f32[512,128]{1,0:T(8,128)S(1)}) custom-call(s32[4]{0:T(128)S(1)} %pad_add_fusion.place_ref, bf16[256,640]{1,0:T(8,128)(2,1)S(1)} %bitcast.12, bf16[256,640]{1,0:T(8,128)(2,1)S(1)} %collective-permute-done.w1, ...), custom_call_target="tpu_custom_call" | custom-call | flops 1073741824 | bytes 4194304 | tf_op jit(solution)/shard_map/project/pallas_call | solution.py:233
  58.8 8.2 %collective-permute-start.8 = (bf16[576,128]{1,0:T(8,128)(2,1)S(1)}, bf16[576,128]{1,0:T(8,128)(2,1)S(1)}, u32[]{:S(2)}, u32[]{:S(2)}) collective-permute-start(bf16[576,128]{1,0:T(8,128)(2,1)S(1)} %get-tuple-element.23.q_ref.after_ref), channel_id=1, source_target_pairs={{0,256},{256,0},{1,257},{257,1},{2,258},{258,2},{3,259},{259,3},{4... | collective-permute-start | bytes 442376 | tf_op jit(solution)/shard_map/ppermute | solution.py:50
  67.1 2.2 %collective-permute-start.12 = (bf16[4,256,128]{2,1,0:T(8,128)(2,1)S(1)}, bf16[4,256,128]{2,1,0:T(8,128)(2,1)S(1)}, u32[]{:S(2)}, u32[]{:S(2)}) collective-permute-start(bf16[4,256,128]{2,1,0:T(8,128)(2,1)S(1)} %out_part.1.refs_0_.w0), channel_id=1, source_target_pairs={{0,192},{64,0},{128,64},{192,128},{1,193},{65,1},{129,65},{193,129... | collective-permute-start | bytes 786440 | tf_op jit(solution)/shard_map/ppermute | solution.py:54
  69.3 4.3 %collective-permute-start.11 = (bf16[4,256,128]{2,1,0:T(8,128)(2,1)S(1)}, bf16[4,256,128]{2,1,0:T(8,128)(2,1)S(1)}, u32[]{:S(2)}, u32[]{:S(2)}) collective-permute-start(bf16[4,256,128]{2,1,0:T(8,128)(2,1)S(1)} %out_part.1.refs_0_.w0), channel_id=1, source_target_pairs={{0,128},{64,192},{128,0},{192,64},{1,129},{65,193},{129,1},{193,65... | collective-permute-start | bytes 786440 | tf_op jit(solution)/shard_map/ppermute | solution.py:54
  73.6 1.9 %collective-permute-start.10 = (bf16[4,256,128]{2,1,0:T(8,128)(2,1)S(1)}, bf16[4,256,128]{2,1,0:T(8,128)(2,1)S(1)}, u32[]{:S(2)}, u32[]{:S(2)}) collective-permute-start(bf16[4,256,128]{2,1,0:T(8,128)(2,1)S(1)} %out_part.1.refs_0_.w0), channel_id=1, source_target_pairs={{0,64},{64,128},{128,192},{192,0},{1,65},{65,129},{129,193},{193,1... | collective-permute-start | bytes 786440 | tf_op jit(solution)/shard_map/ppermute | solution.py:54
  75.5 9.2 %collective-permute-done.8.q_ref = bf16[576,128]{1,0:T(8,128)(2,1)S(1)} collective-permute-done((bf16[576,128]{1,0:T(8,128)(2,1)S(1)}, bf16[576,128]{1,0:T(8,128)(2,1)S(1)}, u32[]{:S(2)}, u32[]{:S(2)}) %collective-permute-start.8) | collective-permute-done | bytes 147488 | tf_op jit(solution)/shard_map/ppermute | solution.py:50
  84.7 3.2 %other.1.refs_4_ = bf16[512,128]{1,0:T(8,128)(2,1)S(1)} custom-call(s32[4]{0:T(128)S(1)} %pad_add_fusion.place_ref, bf16[576,128]{1,0:T(8,128)(2,1)S(1)} %collective-permute-done.8.q_ref, bf16[2176,128]{1,0:T(8,128)(2,1)S(1)} %get-tuple-element.19.p0, bf16[2176,128]{1,0:T(8,128)(2,1)S(1)} %collective-permute-done.5.p1, ...), custom_call_target="tpu_custom_call" | custom-call | flops 1073741824 | bytes 4194304 | tf_op jit(solution)/shard_map/other/pallas_call | solution.py:285
  87.9 7.2 %collective-permute-start.9 = (bf16[512,128]{1,0:T(8,128)(2,1)S(1)}, bf16[512,128]{1,0:T(8,128)(2,1)S(1)}, u32[]{:S(2)}, u32[]{:S(2)}) collective-permute-start(bf16[512,128]{1,0:T(8,128)(2,1)S(1)} %other.1.refs_4_), channel_id=1, source_target_pairs={{0,256},{256,0},{1,257},{257,1},{2,258},{258,2},{3,259},{259,3},{4... | collective-permute-start | bytes 393224 | tf_op jit(solution)/shard_map/ppermute | solution.py:50
  95.1 3.2 %own.1.sum_ref = f32[512,128]{1,0:T(8,128)S(1)} custom-call(s32[4]{0:T(128)S(1)} %pad_add_fusion.place_ref, bf16[576,128]{1,0:T(8,128)(2,1)S(1)} %get-tuple-element.23.q_ref.after_ref, bf16[2176,128]{1,0:T(8,128)(2,1)S(1)} %get-tuple-element.19.p0, bf16[2176,128]{1,0:T(8,128)(2,1)S(1)} %collective-permute-done.5.p1, ...), custom_call_target="tpu_custom_call" | custom-call | flops 1073741824 | bytes 4194304 | tf_op jit(solution)/shard_map/own/pallas_call | solution.py:285
  98.3 0.0 collective-permute-done.12.refs_3_.w3
  98.3 0.0 collective-permute-done.11.refs_2_.w2
  98.3 0.0 collective-permute-done.10.refs_1_.w1
  98.3 1.1 stack.21
  99.4 1.9 %collective-permute-start.13 = (bf16[4,4,256,128]{3,2,1,0:T(8,128)(2,1)}, bf16[4,4,256,128]{3,2,1,0:T(8,128)(2,1)}, u32[]{:S(2)}, u32[]{:S(2)}) collective-permute-start(bf16[4,4,256,128]{3,2,1,0:T(8,128)(2,1)} %stack.21), channel_id=1, source_target_pairs={{0,32},{32,0},{1,33},{33,1},{2,34},{34,2},{3,35},{35,3},{4,36},{36... | collective-permute-start | bytes 3145736 | tf_op jit(solution)/shard_map/ppermute | solution.py:50
  101.3 4.2 %collective-permute-done.9.home_ref = bf16[512,128]{1,0:T(8,128)(2,1)S(1)} collective-permute-done((bf16[512,128]{1,0:T(8,128)(2,1)S(1)}, bf16[512,128]{1,0:T(8,128)(2,1)S(1)}, u32[]{:S(2)}, u32[]{:S(2)}) %collective-permute-start.9) | collective-permute-done | bytes 131104 | tf_op jit(solution)/shard_map/ppermute | solution.py:50
  105.5 0.8 mix.1
  106.3 8.5 %all_to_all.10.mixed_ref = bf16[8,64,128]{2,1,0:T(8,128)(2,1)S(1)} all-to-all(bf16[8,64,128]{2,1,0:T(8,128)(2,1)S(1)} %mix.1), channel_id=1, replica_groups=mesh['zh'=2,'x'=4,'c'=2,'zl'=8,'y'=4] {'x','c'}, dimensions={0} | all-to-all | bytes 262144 | tf_op jit(solution)/shard_map/all_to_all | solution.py:371
  114.8 0.0 collective-permute-done.13.peer_ref
  114.8 2.6 %finish.1 = bf16[64,1024]{1,0:T(8,128)(2,1)} custom-call(s32[4]{0:T(128)S(1)} %pad_add_fusion.place_ref, bf16[64,1024]{1,0:T(8,128)(2,1)S(1)} %bitcast.17, bf16[8,64,128]{2,1,0:T(8,128)(2,1)S(1)} %all_to_all.10.mixed_ref, bf16[4,256,128]{2,1,0:T(8,128)(2,1)S(1)} %out_part.1.refs_0_.w0, bf16[4,256,128]{2,1,0:T(8,128)(2,1)S(1)} %collective-permute-done.10.refs_1_.w1, ...), custom_call_target="tpu_custom_call" | custom-call | tf_op jit(solution)/shard_map/finish/pallas_call | solution.py:334
  (1 shorter events, 0.0 us)
Async XLA Ops:
  0.0 12.7 %copy-start.1 = (bf16[1,256,1024]{2,1,0:T(8,128)(2,1)S(1)}, bf16[1,256,1024]{2,1,0:T(8,128)(2,1)}, u32[]{:S(2)}) copy-start(bf16[1,256,1024]{2,1,0:T(8,128)(2,1)} %param.10) | copy-start | bytes 1572868
  0.0 12.7 %copy-start = (bf16[1,256,1024]{2,1,0:T(8,128)(2,1)S(1)}, bf16[1,256,1024]{2,1,0:T(8,128)(2,1)}, u32[]{:S(2)}) copy-start(bf16[1,256,1024]{2,1,0:T(8,128)(2,1)} %param.9) | copy-start | bytes 1572868
  1.7 11.1 %copy-start.2 = (bf16[1,64,1024]{2,1,0:T(8,128)(2,1)S(1)}, bf16[1,64,1024]{2,1,0:T(8,128)(2,1)}, u32[]{:S(2)}) copy-start(bf16[1,64,1024]{2,1,0:T(8,128)(2,1)} %param.8) | copy-start | bytes 393220
  1.7 30.8 %all-to-all-start = ((bf16[8,32,640]{2,1,0:T(8,128)(2,1)}), bf16[8,32,640]{2,1,0:T(8,128)(2,1)S(1)}, u32[]{:S(2)}, u32[]{:S(2)}) async-start(bf16[8,32,640]{2,1,0:T(8,128)(2,1)} %columns.1), calls=%async_computation | async-start | bytes 655360 | tf_op jit(solution)/shard_map/all_to_all | solution.py:351
  12.7 0.7 copy-start.3
  12.7 0.7 copy-start.4
  12.7 0.7 copy-start.5
  14.4 5.5 %collective-permute-start.4 = (bf16[1536,128]{1,0:T(8,128)(2,1)S(1)}, bf16[1536,128]{1,0:T(8,128)(2,1)S(1)}, u32[]{:S(2)}, u32[]{:S(2)}) collective-permute-start(bf16[1536,128]{1,0:T(8,128)(2,1)S(1)} %get-tuple-element.18), channel_id=1, source_target_pairs={{0,32},{32,0},{1,33},{33,1},{2,34},{34,2},{3,35},{35,3},{4,36},{36... | collective-permute-start | bytes 1179656 | tf_op jit(solution)/shard_map/ppermute | solution.py:50
  16.3 3.6 %collective-permute-start.3 = (bf16[1088,128]{1,0:T(8,128)(2,1)S(1)}, bf16[1088,128]{1,0:T(8,128)(2,1)S(1)}, u32[]{:S(2)}, u32[]{:S(2)}) collective-permute-start(bf16[1088,128]{1,0:T(8,128)(2,1)S(1)} %get-tuple-element.17), channel_id=1, source_target_pairs={{0,32},{32,0},{1,33},{33,1},{2,34},{34,2},{3,35},{35,3},{4,36},{36... | collective-permute-start | bytes 835592 | tf_op jit(solution)/shard_map/ppermute | solution.py:50
  21.1 18.9 %collective-permute-start.5 = (bf16[2176,128]{1,0:T(8,128)(2,1)S(1)}, bf16[2176,128]{1,0:T(8,128)(2,1)S(1)}, u32[]{:S(2)}, u32[]{:S(2)}) collective-permute-start(bf16[2176,128]{1,0:T(8,128)(2,1)S(1)} %get-tuple-element.20), channel_id=1, source_target_pairs={{0,64},{64,128},{128,192},{192,0},{1,65},{65,129},{129,193},{193,1... | collective-permute-start | bytes 1671176 | tf_op jit(solution)/shard_map/ppermute | solution.py:54
  24.5 27.5 %collective-permute-start.6 = (bf16[2176,128]{1,0:T(8,128)(2,1)}, bf16[2176,128]{1,0:T(8,128)(2,1)S(1)}, u32[]{:S(2)}, u32[]{:S(2)}) collective-permute-start(bf16[2176,128]{1,0:T(8,128)(2,1)} %get-tuple-element.21), channel_id=1, source_target_pairs={{0,128},{64,192},{128,0},{192,64},{1,129},{65,193},{129,1},{193,65... | collective-permute-start | bytes 1671176 | tf_op jit(solution)/shard_map/ppermute | solution.py:54
  29.1 24.7 %collective-permute-start.7 = (bf16[2176,128]{1,0:T(8,128)(2,1)}, bf16[2176,128]{1,0:T(8,128)(2,1)}, u32[]{:S(2)}, u32[]{:S(2)}) collective-permute-start(bf16[2176,128]{1,0:T(8,128)(2,1)} %get-tuple-element.22), channel_id=1, source_target_pairs={{0,192},{64,0},{128,64},{192,128},{1,193},{65,1},{129,65},{193,129... | collective-permute-start | bytes 1671176 | tf_op jit(solution)/shard_map/ppermute | solution.py:54
  32.5 21.4 %collective-permute-start.2 = (bf16[256,640]{1,0:T(8,128)(2,1)S(1)}, bf16[256,640]{1,0:T(8,128)(2,1)S(1)}, u32[]{:S(2)}, u32[]{:S(2)}) collective-permute-start(bf16[256,640]{1,0:T(8,128)(2,1)S(1)} %bitcast.9), channel_id=1, source_target_pairs={{0,3},{1,0},{2,1},{3,2},{4,7},{5,4},{6,5},{7,6},{8,11},{9,8},{10,9... | collective-permute-start | bytes 983048 | tf_op jit(solution)/shard_map/ppermute | solution.py:54
  37.4 16.4 %collective-permute-start.1 = (bf16[256,640]{1,0:T(8,128)(2,1)S(1)}, bf16[256,640]{1,0:T(8,128)(2,1)S(1)}, u32[]{:S(2)}, u32[]{:S(2)}) collective-permute-start(bf16[256,640]{1,0:T(8,128)(2,1)S(1)} %bitcast.10), channel_id=1, source_target_pairs={{0,2},{1,3},{2,0},{3,1},{4,6},{5,7},{6,4},{7,5},{8,10},{9,11},{10,... | collective-permute-start | bytes 983048 | tf_op jit(solution)/shard_map/ppermute | solution.py:54
  40.0 16.7 %collective-permute-start = (bf16[256,640]{1,0:T(8,128)(2,1)S(1)}, bf16[256,640]{1,0:T(8,128)(2,1)S(1)}, u32[]{:S(2)}, u32[]{:S(2)}) collective-permute-start(bf16[256,640]{1,0:T(8,128)(2,1)S(1)} %bitcast.11), channel_id=1, source_target_pairs={{0,1},{1,2},{2,3},{3,0},{4,5},{5,6},{6,7},{7,4},{8,9},{9,10},{10,1... | collective-permute-start | bytes 983048 | tf_op jit(solution)/shard_map/ppermute | solution.py:54
  58.8 25.9 %collective-permute-start.8 = (bf16[576,128]{1,0:T(8,128)(2,1)S(1)}, bf16[576,128]{1,0:T(8,128)(2,1)S(1)}, u32[]{:S(2)}, u32[]{:S(2)}) collective-permute-start(bf16[576,128]{1,0:T(8,128)(2,1)S(1)} %get-tuple-element.23.q_ref.after_ref), channel_id=1, source_target_pairs={{0,256},{256,0},{1,257},{257,1},{2,258},{258,2},{3,259},{259,3},{4... | collective-permute-start | bytes 442376 | tf_op jit(solution)/shard_map/ppermute | solution.py:50
  67.1 31.2 %collective-permute-start.12 = (bf16[4,256,128]{2,1,0:T(8,128)(2,1)S(1)}, bf16[4,256,128]{2,1,0:T(8,128)(2,1)S(1)}, u32[]{:S(2)}, u32[]{:S(2)}) collective-permute-start(bf16[4,256,128]{2,1,0:T(8,128)(2,1)S(1)} %out_part.1.refs_0_.w0), channel_id=1, source_target_pairs={{0,192},{64,0},{128,64},{192,128},{1,193},{65,1},{129,65},{193,129... | collective-permute-start | bytes 786440 | tf_op jit(solution)/shard_map/ppermute | solution.py:54
  69.3 29.0 %collective-permute-start.11 = (bf16[4,256,128]{2,1,0:T(8,128)(2,1)S(1)}, bf16[4,256,128]{2,1,0:T(8,128)(2,1)S(1)}, u32[]{:S(2)}, u32[]{:S(2)}) collective-permute-start(bf16[4,256,128]{2,1,0:T(8,128)(2,1)S(1)} %out_part.1.refs_0_.w0), channel_id=1, source_target_pairs={{0,128},{64,192},{128,0},{192,64},{1,129},{65,193},{129,1},{193,65... | collective-permute-start | bytes 786440 | tf_op jit(solution)/shard_map/ppermute | solution.py:54
  73.6 24.7 %collective-permute-start.10 = (bf16[4,256,128]{2,1,0:T(8,128)(2,1)S(1)}, bf16[4,256,128]{2,1,0:T(8,128)(2,1)S(1)}, u32[]{:S(2)}, u32[]{:S(2)}) collective-permute-start(bf16[4,256,128]{2,1,0:T(8,128)(2,1)S(1)} %out_part.1.refs_0_.w0), channel_id=1, source_target_pairs={{0,64},{64,128},{128,192},{192,0},{1,65},{65,129},{129,193},{193,1... | collective-permute-start | bytes 786440 | tf_op jit(solution)/shard_map/ppermute | solution.py:54
  87.9 17.6 %collective-permute-start.9 = (bf16[512,128]{1,0:T(8,128)(2,1)S(1)}, bf16[512,128]{1,0:T(8,128)(2,1)S(1)}, u32[]{:S(2)}, u32[]{:S(2)}) collective-permute-start(bf16[512,128]{1,0:T(8,128)(2,1)S(1)} %other.1.refs_4_), channel_id=1, source_target_pairs={{0,256},{256,0},{1,257},{257,1},{2,258},{258,2},{3,259},{259,3},{4... | collective-permute-start | bytes 393224 | tf_op jit(solution)/shard_map/ppermute | solution.py:50
  99.4 15.4 %collective-permute-start.13 = (bf16[4,4,256,128]{3,2,1,0:T(8,128)(2,1)}, bf16[4,4,256,128]{3,2,1,0:T(8,128)(2,1)}, u32[]{:S(2)}, u32[]{:S(2)}) collective-permute-start(bf16[4,4,256,128]{3,2,1,0:T(8,128)(2,1)} %stack.21), channel_id=1, source_target_pairs={{0,32},{32,0},{1,33},{33,1},{2,34},{34,2},{3,35},{35,3},{4,36},{36... | collective-permute-start | bytes 3145736 | tf_op jit(solution)/shard_map/ppermute | solution.py:50

commit v5 on v4

--- a/solution.py
+++ b/solution.py
@@ -29,7 +29,7 @@
     return pl.CostEstimate(flops=megabytes << 28, bytes_accessed=megabytes << 20, transcendentals=megabytes << 18)
 
 
-C_PARTS, C_PACKETS, C_PROJECT, C_AWAY, C_OWN, C_MIX = 1, 1, 4, 4, 4, 2000
+C_PACKETS, C_GIVE, C_PROJECT, C_AWAY, C_OWN, C_MIX = 1, 1, 2000, 4, 4, 2000
 F32 = jnp.float32
 BF16 = jnp.bfloat16
 
@@ -98,57 +98,51 @@
     return jnp.where(lane == 2, column(cutoff & 63), tags)
 
 
-def parts_kernel(
-    place_ref, owner_ref, x_ref, user_ref, cutoff_ref, k_ref, v_ref, keep_ref, give_ref, rest_ref
-):
-    along, core = place_ref[0], place_ref[1]
+def packets_kernel(place_ref, owner_ref, x_ref, user_ref, cutoff_ref, k_ref, v_ref, *out_refs):
     normed = layer_norm(x_ref[...].astype(F32)).astype(BF16)
-    for part in range(8):
-        give_ref[part * ROWS : part * ROWS + ROWS, :] = normed[:, part * HEAD : part * HEAD + HEAD]
     tags = tags_of(owner_ref, user_ref[...], cutoff_ref[...]).astype(BF16)
-    give_ref[8 * ROWS : MY_ROWS, :] = tags
-    keep_ref[2048:, :] = give_ref[0:MY_ROWS, :]
-    places = ((give_ref, MY_ROWS), (rest_ref, 0), (rest_ref, 512), (rest_ref, 1024))
-    for s in range(4):
-        for (to, base), which in (((keep_ref, s * 512), core), (places[s], 1 - core)):
-            start = ((along + s) & 3) * 256 + which * HEAD
+    for s, ref in enumerate(out_refs):
+        for core in range(2):
+            start = ((place_ref[0] + s) & 3) * 256 + core * HEAD
             at = pl.ds(pl.multiple_of(start, HEAD), HEAD)
-            to[base : base + 256, :] = k_ref[:, at]
-            to[base + 256 : base + 512, :] = v_ref[:, at]
-
-
-def parts(*args):
-    rows = (2048 + MY_ROWS, MY_ROWS + 512, 1536)
-    return pl.pallas_call(
-        parts_kernel,
-        name="parts",
-        out_shape=[jax.ShapeDtypeStruct((n, HEAD), BF16) for n in rows],
-        in_specs=[SMEM, SMEM] + [VMEM] * 5,
-        out_specs=[VMEM] * 3,
-        cost_estimate=cost(C_PARTS),
-        compiler_params=PARAMS,
-    )(*args)
-
-
-def packets_kernel(keep_ref, got_ref, rest_ref, *out_refs):
-    for s, ref in enumerate(out_refs):
-        ref[0:512, :] = keep_ref[s * 512 : s * 512 + 512, :]
-        if s == 0:
-            ref[512:1024, :] = got_ref[MY_ROWS:, :]
-        else:
-            ref[512:1024, :] = rest_ref[s * 512 - 512 : s * 512, :]
-        ref[KV_ROWS : KV_ROWS + MY_ROWS, :] = keep_ref[2048:, :]
-        ref[KV_ROWS + MY_ROWS :, :] = got_ref[0:MY_ROWS, :]
+            ref[core * 256 : core * 256 + 256, :] = k_ref[:, at]
+            ref[512 + core * 256 : 768 + core * 256, :] = v_ref[:, at]
+        for part in range(8):
+            to = KV_ROWS + part * ROWS
+            ref[to : to + ROWS, :] = normed[:, part * HEAD : part * HEAD + HEAD]
+        ref[KV_ROWS + 512 :, :] = tags
 
 
 def packets(*args):
     return pl.pallas_call(
         packets_kernel,
         name="packets",
-        out_shape=[jax.ShapeDtypeStruct((KV_ROWS + 2 * MY_ROWS, HEAD), BF16)] * 4,
-        in_specs=[VMEM] * 3,
+        out_shape=[jax.ShapeDtypeStruct((KV_ROWS + MY_ROWS, HEAD), BF16)] * 4,
+        in_specs=[SMEM, SMEM] + [VMEM] * 5,
         out_specs=[VMEM] * 4,
         cost_estimate=cost(C_PACKETS),
+        compiler_params=PARAMS,
+    )(*args)
+
+
+def give_kernel(place_ref, p0, p1, p2, p3, rows_ref, more_ref, kv_ref):
+    other = 1 - place_ref[1]
+    for s, ref in enumerate((p0, p1, p2, p3)):
+        for i in range(2):
+            at = pl.ds(pl.multiple_of(i * 512 + other * 256, 256), 256)
+            kv_ref[s * 512 + i * 256 : s * 512 + i * 256 + 256, :] = ref[at, :]
+        to = (rows_ref, more_ref)[s // 2]
+        to[(s % 2) * MY_ROWS : (s % 2 + 1) * MY_ROWS, :] = ref[KV_ROWS:, :]
+
+
+def give(*args):
+    return pl.pallas_call(
+        give_kernel,
+        name="give",
+        out_shape=[jax.ShapeDtypeStruct((n, HEAD), BF16) for n in (2 * MY_ROWS, 2 * MY_ROWS, 2048)],
+        in_specs=[SMEM] + [VMEM] * 4,
+        out_specs=[VMEM] * 3,
+        cost_estimate=cost(C_GIVE),
         compiler_params=PARAMS,
     )(*args)
 
@@ -193,11 +187,12 @@
             w_all[at, :] = ref[pl.ds(z * 32, 32), pl.ds(first, count)]
 
 
-def load_rows(packet_refs, rows):
-    for s, ref in enumerate(packet_refs):
-        for rel in range(2):
+def load_rows(packet_refs, got_refs, rows):
+    for s in range(4):
+        got = (got_refs[s // 2], (s % 2) * MY_ROWS)
+        for rel, (ref, first) in enumerate(((packet_refs[s], KV_ROWS), got)):
             for part in range(9):
-                to, start = rel * 256 + s * ROWS, KV_ROWS + rel * MY_ROWS + part * ROWS
+                to, start = rel * 256 + s * ROWS, first + part * ROWS
                 rows[to : to + ROWS, pl.ds(part * HEAD, HEAD)] = ref[start : start + ROWS, :]
 
 
@@ -206,10 +201,10 @@
 
 
 def project_kernel(
-    place_ref, w0, w1, w2, w3, p0, p1, p2, p3,
+    place_ref, w0, w1, w2, w3, p0, p1, p2, p3, got, more,
     query_ref, gate_ref, den_ref, self_ref, rows, w_all,
 ):
-    load_rows((p0, p1, p2, p3), rows)
+    load_rows((p0, p1, p2, p3), (got, more), rows)
     load_weight(place_ref, (w0, w1, w2, w3), w_all, 0, 512)
     for i in range(2):
         at = pl.ds(i * 256, 256)
@@ -239,7 +234,7 @@
             jax.ShapeDtypeStruct(shape, F32),
             jax.ShapeDtypeStruct(shape, F32),
         ],
-        in_specs=[SMEM] + [VMEM] * 8,
+        in_specs=[SMEM] + [VMEM] * 10,
         out_specs=[VMEM] * 4,
         scratch_shapes=[pltpu.VMEM((HALF, WIDE), BF16), pltpu.VMEM((D, 512), BF16)],
         cost_estimate=cost(C_PROJECT),
@@ -247,7 +242,7 @@
     )(*args)
 
 
-def attend_kernel(place_ref, q_ref, p0, p1, p2, p3, plus_ref, out_ref):
+def attend_kernel(place_ref, q_ref, p0, p1, p2, p3, kv_peer, plus_ref, out_ref):
     x, core, half = place_ref[0], place_ref[1], place_ref[2]
     event = lax.broadcasted_iota(jnp.int32, (256, 256), 1)
     for tile in range(2):
@@ -264,18 +259,19 @@
         count = jnp.broadcast_to(jnp.concatenate(counts, axis=0), (256, 256))
         query = q_ref[at, :]
         total = jnp.zeros((256, HEAD), F32)
-        for s, ref in enumerate((p0, p1, p2, p3)):
-            for rel in range(2):
+        for s, pack in enumerate((p0, p1, p2, p3)):
+            for rel, ref in enumerate((pack, kv_peer)):
                 base = half * EVENTS + ((x - s + 4) & 3) * 512 + (core ^ rel) * 256
-                row = rel * 512
+                row = s * 512 if rel else pl.multiple_of(core * 256, 256)
+                keys, values = pl.ds(row, 256), pl.ds(row + (256 if rel else 512), 256)
                 score = lax.dot_general(
-                    query, ref[row : row + 256, :], (((1,), (1,)), ((), ())), preferred_element_type=F32
+                    query, ref[keys, :], (((1,), (1,)), ((), ())), preferred_element_type=F32
                 )
                 h = score * (0.5 * SCALE)
                 w = h + h * jnp.tanh(h)
                 seen = (event + base - low).astype(jnp.uint32) < count
                 w = jnp.where(seen, w, 0.0).astype(BF16)
-                total = total + jnp.dot(w, ref[row + 256 : row + 512, :], preferred_element_type=F32)
+                total = total + jnp.dot(w, ref[values, :], preferred_element_type=F32)
         if out_ref.dtype == F32:
             total = total + plus_ref[at, :]
         out_ref[at, :] = total.astype(out_ref.dtype)
@@ -286,7 +282,7 @@
         attend_kernel,
         name=name,
         out_shape=jax.ShapeDtypeStruct((HALF, HEAD), dtype),
-        in_specs=[SMEM] + [VMEM] * 6,
+        in_specs=[SMEM] + [VMEM] * 7,
         out_specs=VMEM,
         cost_estimate=cost(C_AWAY if name == "other" else C_OWN),
         compiler_params=PARAMS,
@@ -351,19 +347,19 @@
     cols = lax.all_to_all(cols, "zl", 0, 0, tiled=True).reshape(256, 640)
     cols = [along(cols, "y", s) if s else cols for s in range(4)]
 
-    keep, *got = parts(place, block_owner, x, cand_user, cand_cutoff, hist_key[0], hist_value[0])
-    packs = packets(keep, *[swap(part, "c") for part in got])
+    packs = packets(place, block_owner, x, cand_user, cand_cutoff, hist_key[0], hist_value[0])
     packs = [along(pack, "x", s) if s else pack for s, pack in enumerate(packs)]
-
-    query, gate, den, self_term = project(place, *cols, *packs)
+    got, more, kv_peer = [swap(part, "c") for part in give(place, *packs)]
+
+    query, gate, den, self_term = project(place, *cols, *packs, got, more)
     query_other = swap(query, "zh")
 
     w_part = out_part(*cols, query)
     w_part = [along(w_part, "x", s) if s else w_part for s in range(4)]
 
-    away = attend("other", BF16, place, query_other, *packs, self_term)
+    away = attend("other", BF16, place, query_other, *packs, kv_peer, self_term)
     home = swap(away, "zh")
-    sums = attend("own", F32, place, query, *packs, self_term)
+    sums = attend("own", F32, place, query, *packs, kv_peer, self_term)
     w_own = stack(*w_part, away)
     w_peer = swap(w_own, "c")
 

time: 118 us -> 113 us (0.958)
  the two profiles are of different devices: /device:TPU:160 before, /device:TPU:32 now
where the time goes in v5:
time: 113 us; the launch traced here: 112 us
  starting transfers between devices  68 us (60%)
  Pallas kernels  17.1 us (15%)
  waiting for transfers between devices  16.6 us (15%)
  blocking collectives  8.97 us (8%)
    ppermute x9, starting transfers between devices, along(): return lax.ppermute(value, axis, [(i, (i + steps) % 4) for i in range(4)])  31.9 us
    ppermute x6, starting transfers between devices, swap(): return lax.ppermute(value, axis, [(0, 1), (1, 0)])  23.4 us
    all_to_all x1, starting transfers between devices, body(): cols = lax.all_to_all(cols, 'zl', 0, 0, tiled=True).reshape(256, 640)  12.8 us
    all_to_all x1, blocking collectives, body(): mixed = lax.all_to_all(mixed, LOCAL, 0, 0, tiled=True)  8.97 us
    ppermute x6, waiting for transfers between devices, swap(): return lax.ppermute(value, axis, [(0, 1), (1, 0)])  6.61 us
    pallas_call x2, Pallas kernels, attend(): pl.pallas_call(attend_kernel, name=name, out_shape=jax.ShapeDtypeStruct((...  6.29 us
    all_to_all x1, waiting for transfers between devices, body(): cols = lax.all_to_all(cols, 'zl', 0, 0, tiled=True).reshape(256, 640)  5.06 us
    ppermute x9, waiting for transfers between devices, along(): return lax.ppermute(value, axis, [(i, (i + steps) % 4) for i in range(4)])  4.97 us
  transfers between devices with their start and end apart: 16, of which 5 were waited for; matrix products, arithmetic and copies ran while one was open for 0% of the time, Pallas kernels for 12%

profile of v5, /device:TPU:32, one launch (start us, length us, event | category | flops | bytes accessed | tf_op | source)
XLA Modules:
  0.0 111.8 jit_solution(13722684801372103870)
XLA Ops:
  0.0 0.0 copy-start.1
  0.0 0.0 copy-start
  0.0 1.6 %columns.1 = bf16[8,32,640]{2,1,0:T(8,128)(2,1)} custom-call(bf16[32,4096]{1,0:T(8,128)(2,1)} %in_ref.1, bf16[32,1024]{1,0:T(8,128)(2,1)} %out_w_ref.1), custom_call_target="tpu_custom_call" | custom-call | tf_op jit(solution)/shard_map/columns/pallas_call | solution.py:73
  1.7 0.0 copy-start.2
  1.7 12.8 %all-to-all-start = ((bf16[8,32,640]{2,1,0:T(8,128)(2,1)}), bf16[8,32,640]{2,1,0:T(8,128)(2,1)S(1)}, u32[]{:S(2)}, u32[]{:S(2)}) async-start(bf16[8,32,640]{2,1,0:T(8,128)(2,1)} %columns.1), calls=%async_computation | async-start | bytes 655360 | tf_op jit(solution)/shard_map/all_to_all | solution.py:347
  14.4 0.1 pad_add_fusion.place_ref
  14.5 0.0 copy-start.3
  14.5 0.0 copy-start.4
  14.5 0.0 copy-start.5
  14.5 0.0 copy-done.1
  14.5 0.0 copy-done
  14.5 0.0 copy-done.2
  14.6 0.6 copy-done.3
  15.2 0.0 copy-done.4
  15.2 0.0 copy-done.5
  15.2 1.7 %packets.1 = (bf16[1600,128]{1,0:T(8,128)(2,1)S(1)}, bf16[1600,128]{1,0:T(8,128)(2,1)}, bf16[1600,128]{1,0:T(8,128)(2,1)S(1)}, bf16[1600,128]{1,0:T(8,128)(2,1)S(1)}) custom-call(s32[4]{0:T(128)S(1)} %pad_add_fusion.place_ref, s32[1,32]{1,0:T(1,128)S(1)} %copy-done.3, bf16[64,1024]{1,0:T(8,128)(2,1)S(1)} %bitcast.16, s32[1,64]{1,0:T(1,128)S(1)} %copy-done.4, ...), custom_call_target="tpu_custom_call" | custom-call | flops 268435456 | bytes 1048576 | tf_op jit(solution)/shard_map/packets/pallas_call | solution.py:117
  16.9 3.4 %collective-permute-start.3 = (bf16[1600,128]{1,0:T(8,128)(2,1)}, bf16[1600,128]{1,0:T(8,128)(2,1)S(1)}, u32[]{:S(2)}, u32[]{:S(2)}) collective-permute-start(bf16[1600,128]{1,0:T(8,128)(2,1)} %get-tuple-element.17), channel_id=1, source_target_pairs={{0,64},{64,128},{128,192},{192,0},{1,65},{65,129},{129,193},{193,1... | collective-permute-start | bytes 1228808 | tf_op jit(solution)/shard_map/ppermute | solution.py:54
  20.3 4.6 %collective-permute-start.4 = (bf16[1600,128]{1,0:T(8,128)(2,1)S(1)}, bf16[1600,128]{1,0:T(8,128)(2,1)S(1)}, u32[]{:S(2)}, u32[]{:S(2)}) collective-permute-start(bf16[1600,128]{1,0:T(8,128)(2,1)S(1)} %get-tuple-element.18), channel_id=1, source_target_pairs={{0,128},{64,192},{128,0},{192,64},{1,129},{65,193},{129,1},{193,65... | collective-permute-start | bytes 1228808 | tf_op jit(solution)/shard_map/ppermute | solution.py:54
  24.9 3.3 %collective-permute-start.5 = (bf16[1600,128]{1,0:T(8,128)(2,1)S(1)}, bf16[1600,128]{1,0:T(8,128)(2,1)S(1)}, u32[]{:S(2)}, u32[]{:S(2)}) collective-permute-start(bf16[1600,128]{1,0:T(8,128)(2,1)S(1)} %get-tuple-element.19), channel_id=1, source_target_pairs={{0,192},{64,0},{128,64},{192,128},{1,193},{65,1},{129,65},{193,129... | collective-permute-start | bytes 1228808 | tf_op jit(solution)/shard_map/ppermute | solution.py:54
  28.3 5.1 %all-to-all-done = bf16[8,32,640]{2,1,0:T(8,128)(2,1)S(1)} async-done(((bf16[8,32,640]{2,1,0:T(8,128)(2,1)}), bf16[8,32,640]{2,1,0:T(8,128)(2,1)S(1)}, u32[]{:S(2)}, u32[]{:S(2)}) %all-to-all-start) | async-done | bytes 327712 | tf_op jit(solution)/shard_map/all_to_all | solution.py:347
  33.4 4.9 %collective-permute-start.2 = (bf16[256,640]{1,0:T(8,128)(2,1)S(1)}, bf16[256,640]{1,0:T(8,128)(2,1)S(1)}, u32[]{:S(2)}, u32[]{:S(2)}) collective-permute-start(bf16[256,640]{1,0:T(8,128)(2,1)S(1)} %bitcast.9), channel_id=1, source_target_pairs={{0,3},{1,0},{2,1},{3,2},{4,7},{5,4},{6,5},{7,6},{8,11},{9,8},{10,9... | collective-permute-start | bytes 983048 | tf_op jit(solution)/shard_map/ppermute | solution.py:54
  38.3 2.5 %collective-permute-start.1 = (bf16[256,640]{1,0:T(8,128)(2,1)S(1)}, bf16[256,640]{1,0:T(8,128)(2,1)S(1)}, u32[]{:S(2)}, u32[]{:S(2)}) collective-permute-start(bf16[256,640]{1,0:T(8,128)(2,1)S(1)} %bitcast.10), channel_id=1, source_target_pairs={{0,2},{1,3},{2,0},{3,1},{4,6},{5,7},{6,4},{7,5},{8,10},{9,11},{10,... | collective-permute-start | bytes 983048 | tf_op jit(solution)/shard_map/ppermute | solution.py:54
  40.8 0.0 collective-permute-done.3.p1
  40.8 2.9 %collective-permute-start = (bf16[256,640]{1,0:T(8,128)(2,1)S(1)}, bf16[256,640]{1,0:T(8,128)(2,1)S(1)}, u32[]{:S(2)}, u32[]{:S(2)}) collective-permute-start(bf16[256,640]{1,0:T(8,128)(2,1)S(1)} %bitcast.11), channel_id=1, source_target_pairs={{0,1},{1,2},{2,3},{3,0},{4,5},{5,6},{6,7},{7,4},{8,9},{9,10},{10,1... | collective-permute-start | bytes 983048 | tf_op jit(solution)/shard_map/ppermute | solution.py:54
  43.7 0.0 collective-permute-done.4.p2
  43.7 0.0 collective-permute-done.5.p3
  43.7 1.4 %give.1 = (bf16[1152,128]{1,0:T(8,128)(2,1)S(1)}, bf16[1152,128]{1,0:T(8,128)(2,1)S(1)}, bf16[2048,128]{1,0:T(8,128)(2,1)}) custom-call(s32[4]{0:T(128)S(1)} %pad_add_fusion.place_ref, bf16[1600,128]{1,0:T(8,128)(2,1)S(1)} %get-tuple-element.16.p0, bf16[1600,128]{1,0:T(8,128)(2,1)S(1)} %collective-permute-done.3.p1, ...), custom_call_target="tpu_custom_call" | custom-call | flops 268435456 | bytes 1048576 | tf_op jit(solution)/shard_map/give/pallas_call | solution.py:139
  45.2 1.9 %collective-permute-start.6 = (bf16[1152,128]{1,0:T(8,128)(2,1)S(1)}, bf16[1152,128]{1,0:T(8,128)(2,1)S(1)}, u32[]{:S(2)}, u32[]{:S(2)}) collective-permute-start(bf16[1152,128]{1,0:T(8,128)(2,1)S(1)} %get-tuple-element.20), channel_id=1, source_target_pairs={{0,32},{32,0},{1,33},{33,1},{2,34},{34,2},{3,35},{35,3},{4,36},{36... | collective-permute-start | bytes 884744 | tf_op jit(solution)/shard_map/ppermute | solution.py:50
  47.1 2.4 %collective-permute-start.7 = (bf16[1152,128]{1,0:T(8,128)(2,1)S(1)}, bf16[1152,128]{1,0:T(8,128)(2,1)S(1)}, u32[]{:S(2)}, u32[]{:S(2)}) collective-permute-start(bf16[1152,128]{1,0:T(8,128)(2,1)S(1)} %get-tuple-element.21), channel_id=1, source_target_pairs={{0,32},{32,0},{1,33},{33,1},{2,34},{34,2},{3,35},{35,3},{4,36},{36... | collective-permute-start | bytes 884744 | tf_op jit(solution)/shard_map/ppermute | solution.py:50
  49.5 0.0 collective-permute-done.6.got
  49.5 1.9 %collective-permute-start.8 = (bf16[2048,128]{1,0:T(8,128)(2,1)}, bf16[2048,128]{1,0:T(8,128)(2,1)}, u32[]{:S(2)}, u32[]{:S(2)}) collective-permute-start(bf16[2048,128]{1,0:T(8,128)(2,1)} %get-tuple-element.23), channel_id=1, source_target_pairs={{0,32},{32,0},{1,33},{33,1},{2,34},{34,2},{3,35},{35,3},{4,36},{36... | collective-permute-start | bytes 1572872 | tf_op jit(solution)/shard_map/ppermute | solution.py:50
  51.4 0.0 collective-permute-done.7.more
  51.4 0.0 collective-permute-done.2.w3
  51.5 0.9 collective-permute-done.1.w2
  52.4 4.0 %collective-permute-done.w1 = bf16[256,640]{1,0:T(8,128)(2,1)S(1)} collective-permute-done((bf16[256,640]{1,0:T(8,128)(2,1)S(1)}, bf16[256,640]{1,0:T(8,128)(2,1)S(1)}, u32[]{:S(2)}, u32[]{:S(2)}) %collective-permute-start) | collective-permute-done | bytes 327712 | tf_op jit(solution)/shard_map/ppermute | solution.py:54
  56.4 1.6 %project.1 = (bf16[576,128]{1,0:T(8,128)(2,1)S(1)}, bf16[512,128]{1,0:T(8,128)(2,1)S(1)}, f32[512,128]{1,0:T(8,128)S(1)}, f32[512,128]{1,0:T(8,128)S(1)}) custom-call(s32[4]{0:T(128)S(1)} %pad_add_fusion.place_ref, bf16[256,640]{1,0:T(8,128)(2,1)S(1)} %bitcast.12, bf16[256,640]{1,0:T(8,128)(2,1)S(1)} %collective-permute-done.w1, ...), custom_call_target="tpu_custom_call" | custom-call | flops 536870912000 | bytes 2097152000 | tf_op jit(solution)/shard_map/project/pallas_call | solution.py:228
  58.0 8.2 %collective-permute-start.9 = (bf16[576,128]{1,0:T(8,128)(2,1)S(1)}, bf16[576,128]{1,0:T(8,128)(2,1)S(1)}, u32[]{:S(2)}, u32[]{:S(2)}) collective-permute-start(bf16[576,128]{1,0:T(8,128)(2,1)S(1)} %get-tuple-element.22.q_ref.after_ref), channel_id=1, source_target_pairs={{0,256},{256,0},{1,257},{257,1},{2,258},{258,2},{3,259},{259,3},{4... | collective-permute-start | bytes 442376 | tf_op jit(solution)/shard_map/ppermute | solution.py:50
  66.3 4.7 %collective-permute-start.13 = (bf16[4,256,128]{2,1,0:T(8,128)(2,1)S(1)}, bf16[4,256,128]{2,1,0:T(8,128)(2,1)S(1)}, u32[]{:S(2)}, u32[]{:S(2)}) collective-permute-start(bf16[4,256,128]{2,1,0:T(8,128)(2,1)S(1)} %out_part.1.refs_0_.w0), channel_id=1, source_target_pairs={{0,192},{64,0},{128,64},{192,128},{1,193},{65,1},{129,65},{193,129... | collective-permute-start | bytes 786440 | tf_op jit(solution)/shard_map/ppermute | solution.py:54
  71.0 2.7 %collective-permute-start.12 = (bf16[4,256,128]{2,1,0:T(8,128)(2,1)S(1)}, bf16[4,256,128]{2,1,0:T(8,128)(2,1)S(1)}, u32[]{:S(2)}, u32[]{:S(2)}) collective-permute-start(bf16[4,256,128]{2,1,0:T(8,128)(2,1)S(1)} %out_part.1.refs_0_.w0), channel_id=1, source_target_pairs={{0,128},{64,192},{128,0},{192,64},{1,129},{65,193},{129,1},{193,65... | collective-permute-start | bytes 786440 | tf_op jit(solution)/shard_map/ppermute | solution.py:54
  73.7 2.8 %collective-permute-start.11 = (bf16[4,256,128]{2,1,0:T(8,128)(2,1)S(1)}, bf16[4,256,128]{2,1,0:T(8,128)(2,1)S(1)}, u32[]{:S(2)}, u32[]{:S(2)}) collective-permute-start(bf16[4,256,128]{2,1,0:T(8,128)(2,1)S(1)} %out_part.1.refs_0_.w0), channel_id=1, source_target_pairs={{0,64},{64,128},{128,192},{192,0},{1,65},{65,129},{129,193},{193,1... | collective-permute-start | bytes 786440 | tf_op jit(solution)/shard_map/ppermute | solution.py:54
  76.5 0.0 collective-permute-done.8.kv_peer
  76.5 2.7 %collective-permute-done.9.q_ref = bf16[576,128]{1,0:T(8,128)(2,1)S(1)} collective-permute-done((bf16[576,128]{1,0:T(8,128)(2,1)S(1)}, bf16[576,128]{1,0:T(8,128)(2,1)S(1)}, u32[]{:S(2)}, u32[]{:S(2)}) %collective-permute-start.9) | collective-permute-done | bytes 147488 | tf_op jit(solution)/shard_map/ppermute | solution.py:50
  79.2 3.1 %other.1.refs_4_ = bf16[512,128]{1,0:T(8,128)(2,1)S(1)} custom-call(s32[4]{0:T(128)S(1)} %pad_add_fusion.place_ref, bf16[576,128]{1,0:T(8,128)(2,1)S(1)} %collective-permute-done.9.q_ref, bf16[1600,128]{1,0:T(8,128)(2,1)S(1)} %get-tuple-element.16.p0, bf16[1600,128]{1,0:T(8,128)(2,1)S(1)} %collective-permute-done.3.p1, ...), custom_call_target="tpu_custom_call" | custom-call | flops 1073741824 | bytes 4194304 | tf_op jit(solution)/shard_map/other/pallas_call | solution.py:281
  82.4 7.0 %collective-permute-start.10 = (bf16[512,128]{1,0:T(8,128)(2,1)S(1)}, bf16[512,128]{1,0:T(8,128)(2,1)S(1)}, u32[]{:S(2)}, u32[]{:S(2)}) collective-permute-start(bf16[512,128]{1,0:T(8,128)(2,1)S(1)} %other.1.refs_4_), channel_id=1, source_target_pairs={{0,256},{256,0},{1,257},{257,1},{2,258},{258,2},{3,259},{259,3},{4... | collective-permute-start | bytes 393224 | tf_op jit(solution)/shard_map/ppermute | solution.py:50
  89.4 3.1 %own.1.sum_ref = f32[512,128]{1,0:T(8,128)S(1)} custom-call(s32[4]{0:T(128)S(1)} %pad_add_fusion.place_ref, bf16[576,128]{1,0:T(8,128)(2,1)S(1)} %get-tuple-element.22.q_ref.after_ref, bf16[1600,128]{1,0:T(8,128)(2,1)S(1)} %get-tuple-element.16.p0, bf16[1600,128]{1,0:T(8,128)(2,1)S(1)} %collective-permute-done.3.p1, ...), custom_call_target="tpu_custom_call" | custom-call | flops 1073741824 | bytes 4194304 | tf_op jit(solution)/shard_map/own/pallas_call | solution.py:281
  92.5 0.0 collective-permute-done.13.refs_3_.w3
  92.5 0.0 collective-permute-done.12.refs_2_.w2
  92.5 0.0 collective-permute-done.11.refs_1_.w1
  92.6 1.1 stack.21
  93.6 1.9 %collective-permute-start.14 = (bf16[4,4,256,128]{3,2,1,0:T(8,128)(2,1)}, bf16[4,4,256,128]{3,2,1,0:T(8,128)(2,1)}, u32[]{:S(2)}, u32[]{:S(2)}) collective-permute-start(bf16[4,4,256,128]{3,2,1,0:T(8,128)(2,1)} %stack.21), channel_id=1, source_target_pairs={{0,32},{32,0},{1,33},{33,1},{2,34},{34,2},{3,35},{35,3},{4,36},{36... | collective-permute-start | bytes 3145736 | tf_op jit(solution)/shard_map/ppermute | solution.py:50
  95.5 3.9 %collective-permute-done.10.home_ref = bf16[512,128]{1,0:T(8,128)(2,1)S(1)} collective-permute-done((bf16[512,128]{1,0:T(8,128)(2,1)S(1)}, bf16[512,128]{1,0:T(8,128)(2,1)S(1)}, u32[]{:S(2)}, u32[]{:S(2)}) %collective-permute-start.10) | collective-permute-done | bytes 131104 | tf_op jit(solution)/shard_map/ppermute | solution.py:50
  99.4 0.8 mix.1
  100.2 9.0 %all_to_all.10.mixed_ref = bf16[8,64,128]{2,1,0:T(8,128)(2,1)S(1)} all-to-all(bf16[8,64,128]{2,1,0:T(8,128)(2,1)S(1)} %mix.1), channel_id=1, replica_groups=mesh['zh'=2,'x'=4,'c'=2,'zl'=8,'y'=4] {'x','c'}, dimensions={0} | all-to-all | bytes 262144 | tf_op jit(solution)/shard_map/all_to_all | solution.py:367
  109.2 0.0 collective-permute-done.14.peer_ref
  109.2 2.6 %finish.1 = bf16[64,1024]{1,0:T(8,128)(2,1)} custom-call(s32[4]{0:T(128)S(1)} %pad_add_fusion.place_ref, bf16[64,1024]{1,0:T(8,128)(2,1)S(1)} %bitcast.17, bf16[8,64,128]{2,1,0:T(8,128)(2,1)S(1)} %all_to_all.10.mixed_ref, bf16[4,256,128]{2,1,0:T(8,128)(2,1)S(1)} %out_part.1.refs_0_.w0, bf16[4,256,128]{2,1,0:T(8,128)(2,1)S(1)} %collective-permute-done.11.refs_1_.w1, ...), custom_call_target="tpu_custom_call" | custom-call | tf_op jit(solution)/shard_map/finish/pallas_call | solution.py:330
  (1 shorter events, 0.0 us)
Async XLA Ops:
  0.0 14.5 %copy-start.1 = (bf16[1,256,1024]{2,1,0:T(8,128)(2,1)S(1)}, bf16[1,256,1024]{2,1,0:T(8,128)(2,1)}, u32[]{:S(2)}) copy-start(bf16[1,256,1024]{2,1,0:T(8,128)(2,1)} %param.10) | copy-start | bytes 1572868
  0.0 14.5 %copy-start = (bf16[1,256,1024]{2,1,0:T(8,128)(2,1)S(1)}, bf16[1,256,1024]{2,1,0:T(8,128)(2,1)}, u32[]{:S(2)}) copy-start(bf16[1,256,1024]{2,1,0:T(8,128)(2,1)} %param.9) | copy-start | bytes 1572868
  1.7 12.9 %copy-start.2 = (bf16[1,64,1024]{2,1,0:T(8,128)(2,1)S(1)}, bf16[1,64,1024]{2,1,0:T(8,128)(2,1)}, u32[]{:S(2)}) copy-start(bf16[1,64,1024]{2,1,0:T(8,128)(2,1)} %param.8) | copy-start | bytes 393220
  1.7 31.7 %all-to-all-start = ((bf16[8,32,640]{2,1,0:T(8,128)(2,1)}), bf16[8,32,640]{2,1,0:T(8,128)(2,1)S(1)}, u32[]{:S(2)}, u32[]{:S(2)}) async-start(bf16[8,32,640]{2,1,0:T(8,128)(2,1)} %columns.1), calls=%async_computation | async-start | bytes 655360 | tf_op jit(solution)/shard_map/all_to_all | solution.py:347
  14.5 0.7 copy-start.3
  14.5 0.7 copy-start.4
  14.5 0.7 copy-start.5
  16.9 23.9 %collective-permute-start.3 = (bf16[1600,128]{1,0:T(8,128)(2,1)}, bf16[1600,128]{1,0:T(8,128)(2,1)S(1)}, u32[]{:S(2)}, u32[]{:S(2)}) collective-permute-start(bf16[1600,128]{1,0:T(8,128)(2,1)} %get-tuple-element.17), channel_id=1, source_target_pairs={{0,64},{64,128},{128,192},{192,0},{1,65},{65,129},{129,193},{193,1... | collective-permute-start | bytes 1228808 | tf_op jit(solution)/shard_map/ppermute | solution.py:54
  20.3 23.4 %collective-permute-start.4 = (bf16[1600,128]{1,0:T(8,128)(2,1)S(1)}, bf16[1600,128]{1,0:T(8,128)(2,1)S(1)}, u32[]{:S(2)}, u32[]{:S(2)}) collective-permute-start(bf16[1600,128]{1,0:T(8,128)(2,1)S(1)} %get-tuple-element.18), channel_id=1, source_target_pairs={{0,128},{64,192},{128,0},{192,64},{1,129},{65,193},{129,1},{193,65... | collective-permute-start | bytes 1228808 | tf_op jit(solution)/shard_map/ppermute | solution.py:54
  24.9 18.8 %collective-permute-start.5 = (bf16[1600,128]{1,0:T(8,128)(2,1)S(1)}, bf16[1600,128]{1,0:T(8,128)(2,1)S(1)}, u32[]{:S(2)}, u32[]{:S(2)}) collective-permute-start(bf16[1600,128]{1,0:T(8,128)(2,1)S(1)} %get-tuple-element.19), channel_id=1, source_target_pairs={{0,192},{64,0},{128,64},{192,128},{1,193},{65,1},{129,65},{193,129... | collective-permute-start | bytes 1228808 | tf_op jit(solution)/shard_map/ppermute | solution.py:54
  33.4 18.1 %collective-permute-start.2 = (bf16[256,640]{1,0:T(8,128)(2,1)S(1)}, bf16[256,640]{1,0:T(8,128)(2,1)S(1)}, u32[]{:S(2)}, u32[]{:S(2)}) collective-permute-start(bf16[256,640]{1,0:T(8,128)(2,1)S(1)} %bitcast.9), channel_id=1, source_target_pairs={{0,3},{1,0},{2,1},{3,2},{4,7},{5,4},{6,5},{7,6},{8,11},{9,8},{10,9... | collective-permute-start | bytes 983048 | tf_op jit(solution)/shard_map/ppermute | solution.py:54
  38.3 14.1 %collective-permute-start.1 = (bf16[256,640]{1,0:T(8,128)(2,1)S(1)}, bf16[256,640]{1,0:T(8,128)(2,1)S(1)}, u32[]{:S(2)}, u32[]{:S(2)}) collective-permute-start(bf16[256,640]{1,0:T(8,128)(2,1)S(1)} %bitcast.10), channel_id=1, source_target_pairs={{0,2},{1,3},{2,0},{3,1},{4,6},{5,7},{6,4},{7,5},{8,10},{9,11},{10,... | collective-permute-start | bytes 983048 | tf_op jit(solution)/shard_map/ppermute | solution.py:54
  40.8 15.6 %collective-permute-start = (bf16[256,640]{1,0:T(8,128)(2,1)S(1)}, bf16[256,640]{1,0:T(8,128)(2,1)S(1)}, u32[]{:S(2)}, u32[]{:S(2)}) collective-permute-start(bf16[256,640]{1,0:T(8,128)(2,1)S(1)} %bitcast.11), channel_id=1, source_target_pairs={{0,1},{1,2},{2,3},{3,0},{4,5},{5,6},{6,7},{7,4},{8,9},{9,10},{10,1... | collective-permute-start | bytes 983048 | tf_op jit(solution)/shard_map/ppermute | solution.py:54
  45.2 4.3 %collective-permute-start.6 = (bf16[1152,128]{1,0:T(8,128)(2,1)S(1)}, bf16[1152,128]{1,0:T(8,128)(2,1)S(1)}, u32[]{:S(2)}, u32[]{:S(2)}) collective-permute-start(bf16[1152,128]{1,0:T(8,128)(2,1)S(1)} %get-tuple-element.20), channel_id=1, source_target_pairs={{0,32},{32,0},{1,33},{33,1},{2,34},{34,2},{3,35},{35,3},{4,36},{36... | collective-permute-start | bytes 884744 | tf_op jit(solution)/shard_map/ppermute | solution.py:50
  47.1 4.4 %collective-permute-start.7 = (bf16[1152,128]{1,0:T(8,128)(2,1)S(1)}, bf16[1152,128]{1,0:T(8,128)(2,1)S(1)}, u32[]{:S(2)}, u32[]{:S(2)}) collective-permute-start(bf16[1152,128]{1,0:T(8,128)(2,1)S(1)} %get-tuple-element.21), channel_id=1, source_target_pairs={{0,32},{32,0},{1,33},{33,1},{2,34},{34,2},{3,35},{35,3},{4,36},{36... | collective-permute-start | bytes 884744 | tf_op jit(solution)/shard_map/ppermute | solution.py:50
  49.5 27.0 %collective-permute-start.8 = (bf16[2048,128]{1,0:T(8,128)(2,1)}, bf16[2048,128]{1,0:T(8,128)(2,1)}, u32[]{:S(2)}, u32[]{:S(2)}) collective-permute-start(bf16[2048,128]{1,0:T(8,128)(2,1)} %get-tuple-element.23), channel_id=1, source_target_pairs={{0,32},{32,0},{1,33},{33,1},{2,34},{34,2},{3,35},{35,3},{4,36},{36... | collective-permute-start | bytes 1572872 | tf_op jit(solution)/shard_map/ppermute | solution.py:50
  58.0 21.2 %collective-permute-start.9 = (bf16[576,128]{1,0:T(8,128)(2,1)S(1)}, bf16[576,128]{1,0:T(8,128)(2,1)S(1)}, u32[]{:S(2)}, u32[]{:S(2)}) collective-permute-start(bf16[576,128]{1,0:T(8,128)(2,1)S(1)} %get-tuple-element.22.q_ref.after_ref), channel_id=1, source_target_pairs={{0,256},{256,0},{1,257},{257,1},{2,258},{258,2},{3,259},{259,3},{4... | collective-permute-start | bytes 442376 | tf_op jit(solution)/shard_map/ppermute | solution.py:50
  66.3 26.2 %collective-permute-start.13 = (bf16[4,256,128]{2,1,0:T(8,128)(2,1)S(1)}, bf16[4,256,128]{2,1,0:T(8,128)(2,1)S(1)}, u32[]{:S(2)}, u32[]{:S(2)}) collective-permute-start(bf16[4,256,128]{2,1,0:T(8,128)(2,1)S(1)} %out_part.1.refs_0_.w0), channel_id=1, source_target_pairs={{0,192},{64,0},{128,64},{192,128},{1,193},{65,1},{129,65},{193,129... | collective-permute-start | bytes 786440 | tf_op jit(solution)/shard_map/ppermute | solution.py:54
  71.0 21.5 %collective-permute-start.12 = (bf16[4,256,128]{2,1,0:T(8,128)(2,1)S(1)}, bf16[4,256,128]{2,1,0:T(8,128)(2,1)S(1)}, u32[]{:S(2)}, u32[]{:S(2)}) collective-permute-start(bf16[4,256,128]{2,1,0:T(8,128)(2,1)S(1)} %out_part.1.refs_0_.w0), channel_id=1, source_target_pairs={{0,128},{64,192},{128,0},{192,64},{1,129},{65,193},{129,1},{193,65... | collective-permute-start | bytes 786440 | tf_op jit(solution)/shard_map/ppermute | solution.py:54
  73.7 18.8 %collective-permute-start.11 = (bf16[4,256,128]{2,1,0:T(8,128)(2,1)S(1)}, bf16[4,256,128]{2,1,0:T(8,128)(2,1)S(1)}, u32[]{:S(2)}, u32[]{:S(2)}) collective-permute-start(bf16[4,256,128]{2,1,0:T(8,128)(2,1)S(1)} %out_part.1.refs_0_.w0), channel_id=1, source_target_pairs={{0,64},{64,128},{128,192},{192,0},{1,65},{65,129},{129,193},{193,1... | collective-permute-start | bytes 786440 | tf_op jit(solution)/shard_map/ppermute | solution.py:54
  82.4 17.1 %collective-permute-start.10 = (bf16[512,128]{1,0:T(8,128)(2,1)S(1)}, bf16[512,128]{1,0:T(8,128)(2,1)S(1)}, u32[]{:S(2)}, u32[]{:S(2)}) collective-permute-start(bf16[512,128]{1,0:T(8,128)(2,1)S(1)} %other.1.refs_4_), channel_id=1, source_target_pairs={{0,256},{256,0},{1,257},{257,1},{2,258},{258,2},{3,259},{259,3},{4... | collective-permute-start | bytes 393224 | tf_op jit(solution)/shard_map/ppermute | solution.py:50
  93.6 15.6 %collective-permute-start.14 = (bf16[4,4,256,128]{3,2,1,0:T(8,128)(2,1)}, bf16[4,4,256,128]{3,2,1,0:T(8,128)(2,1)}, u32[]{:S(2)}, u32[]{:S(2)}) collective-permute-start(bf16[4,4,256,128]{3,2,1,0:T(8,128)(2,1)} %stack.21), channel_id=1, source_target_pairs={{0,32},{32,0},{1,33},{33,1},{2,34},{34,2},{3,35},{35,3},{4,36},{36... | collective-permute-start | bytes 3145736 | tf_op jit(solution)/shard_map/ppermute | solution.py:50

commit v6 on v5

--- a/solution.py
+++ b/solution.py
@@ -54,7 +54,7 @@
     return lax.ppermute(value, axis, [(i, (i + steps) % 4) for i in range(4)])
 
 
-def columns_kernel(in_ref, out_w_ref, out_ref, block, sems):
+def columns_kernel(in_ref, out_w_ref, out_ref, block, sems, out_sems):
     first = (lax.axis_index("x") * 2 + lax.axis_index("c")) * HEAD
     copies = []
     for part in range(5):
@@ -65,8 +65,11 @@
         copies[part].start()
     for copy in copies:
         copy.wait()
-    for z in range(8):
-        out_ref[z] = block[...]
+    copies = [pltpu.make_async_copy(block, out_ref.at[z], out_sems.at[z]) for z in range(8)]
+    for copy in copies:
+        copy.start()
+    for copy in copies:
+        copy.wait()
 
 
 def columns(*args):
@@ -75,8 +78,12 @@
         name="columns",
         out_shape=jax.ShapeDtypeStruct((8, 32, 640), BF16),
         in_specs=[ANY, ANY],
-        out_specs=VMEM,
-        scratch_shapes=[pltpu.VMEM((32, 640), BF16), pltpu.SemaphoreType.DMA((5,))],
+        out_specs=ANY,
+        scratch_shapes=[
+            pltpu.VMEM((32, 640), BF16),
+            pltpu.SemaphoreType.DMA((5,)),
+            pltpu.SemaphoreType.DMA((8,)),
+        ],
         compiler_params=WHOLE,
     )(*args)
 
@@ -147,17 +154,16 @@
     )(*args)
 
 
-def out_part_kernel(w0, w1, w2, w3, after_ref, out_ref):
-    for s, ref in enumerate((w0, w1, w2, w3)):
-        out_ref[s] = ref[:, 512:]
-
-
-def out_part(*args):
-    return pl.pallas_call(
-        out_part_kernel,
-        name="out_part",
-        out_shape=jax.ShapeDtypeStruct((4, 256, HEAD), BF16),
-        in_specs=[VMEM] * 4 + [ANY],
+def rows_kernel(p0, p1, p2, p3, got, more, rows):
+    load_rows((p0, p1, p2, p3), (got, more), rows)
+
+
+def assemble(*args):
+    return pl.pallas_call(
+        rows_kernel,
+        name="assemble",
+        out_shape=jax.ShapeDtypeStruct((HALF, WIDE), BF16),
+        in_specs=[VMEM] * 6,
         out_specs=VMEM,
         compiler_params=PARAMS,
     )(*args)
@@ -201,10 +207,10 @@
 
 
 def project_kernel(
-    place_ref, w0, w1, w2, w3, p0, p1, p2, p3, got, more,
-    query_ref, gate_ref, den_ref, self_ref, rows, w_all,
+    place_ref, w0, w1, w2, w3, rows, query_ref, gate_ref, den_ref, self_ref, part_ref, w_all
 ):
-    load_rows((p0, p1, p2, p3), (got, more), rows)
+    for s, ref in enumerate((w0, w1, w2, w3)):
+        part_ref[(place_ref[3] - s + 4) & 3] = ref[:, 512:]
     load_weight(place_ref, (w0, w1, w2, w3), w_all, 0, 512)
     for i in range(2):
         at = pl.ds(i * 256, 256)
@@ -233,17 +239,20 @@
             jax.ShapeDtypeStruct(shape, BF16),
             jax.ShapeDtypeStruct(shape, F32),
             jax.ShapeDtypeStruct(shape, F32),
+            jax.ShapeDtypeStruct((4, 256, HEAD), BF16),
         ],
-        in_specs=[SMEM] + [VMEM] * 10,
-        out_specs=[VMEM] * 4,
-        scratch_shapes=[pltpu.VMEM((HALF, WIDE), BF16), pltpu.VMEM((D, 512), BF16)],
+        in_specs=[SMEM] + [VMEM] * 5,
+        out_specs=[VMEM] * 5,
+        scratch_shapes=[pltpu.VMEM((D, 512), BF16)],
         cost_estimate=cost(C_PROJECT),
         compiler_params=PARAMS,
     )(*args)
 
 
-def attend_kernel(place_ref, q_ref, p0, p1, p2, p3, kv_peer, plus_ref, out_ref):
+def attend_kernel(place_ref, q_ref, p0, p1, p2, p3, kv_peer, plus_ref, out_ref, kv_all, sem):
     x, core, half = place_ref[0], place_ref[1], place_ref[2]
+    copy = pltpu.make_async_copy(kv_peer, kv_all, sem)
+    copy.start()
     event = lax.broadcasted_iota(jnp.int32, (256, 256), 1)
     for tile in range(2):
         at = pl.ds(tile * 256, 256)
@@ -259,11 +268,14 @@
         count = jnp.broadcast_to(jnp.concatenate(counts, axis=0), (256, 256))
         query = q_ref[at, :]
         total = jnp.zeros((256, HEAD), F32)
-        for s, pack in enumerate((p0, p1, p2, p3)):
-            for rel, ref in enumerate((pack, kv_peer)):
+        for rel in range(2):
+            if tile == 0 and rel:
+                copy.wait()
+            for s, pack in enumerate((p0, p1, p2, p3)):
                 base = half * EVENTS + ((x - s + 4) & 3) * 512 + (core ^ rel) * 256
                 row = s * 512 if rel else pl.multiple_of(core * 256, 256)
                 keys, values = pl.ds(row, 256), pl.ds(row + (256 if rel else 512), 256)
+                ref = kv_all if rel else pack
                 score = lax.dot_general(
                     query, ref[keys, :], (((1,), (1,)), ((), ())), preferred_element_type=F32
                 )
@@ -282,8 +294,9 @@
         attend_kernel,
         name=name,
         out_shape=jax.ShapeDtypeStruct((HALF, HEAD), dtype),
-        in_specs=[SMEM] + [VMEM] * 7,
-        out_specs=VMEM,
+        in_specs=[SMEM] + [VMEM] * 5 + [ANY, VMEM],
+        out_specs=VMEM,
+        scratch_shapes=[pltpu.VMEM((2048, HEAD), BF16), pltpu.SemaphoreType.DMA],
         cost_estimate=cost(C_AWAY if name == "other" else C_OWN),
         compiler_params=PARAMS,
     )(*args)
@@ -311,12 +324,10 @@
     )(*args)
 
 
-def finish_kernel(place_ref, x_ref, mixed_ref, w0, w1, w2, w3, peer_ref, out_ref, by_line):
-    along, core, line = place_ref[0], place_ref[1], place_ref[3]
-    for y in range(4):
-        for h in range(HEADS):
-            by_line[y, :, h * 32 : h * 32 + 32] = mixed_ref[h, :, y * 32 : y * 32 + 32]
-    left = jnp.concatenate([by_line[(line - step + 4) & 3] for step in range(4)], axis=1)
+def finish_kernel(place_ref, x_ref, mixed_ref, w0, w1, w2, w3, peer_ref, out_ref):
+    along, core = place_ref[0], place_ref[1]
+    pieces = [mixed_ref[h, :, y * 32 : y * 32 + 32] for y in range(4) for h in range(HEADS)]
+    left = jnp.concatenate(pieces, axis=1)
     for s, ref in enumerate((w0, w1, w2, w3)):
         for rel in range(2):
             at = ((along - s + 4) & 3) * 2 + (core ^ rel)
@@ -333,7 +344,6 @@
         out_shape=jax.ShapeDtypeStruct((ROWS, D), BF16),
         in_specs=[SMEM] + [VMEM] * 7,
         out_specs=VMEM,
-        scratch_shapes=[pltpu.VMEM((4, ROWS, 256), BF16)],
         compiler_params=PARAMS,
     )(*args)
 
@@ -351,10 +361,9 @@
     packs = [along(pack, "x", s) if s else pack for s, pack in enumerate(packs)]
     got, more, kv_peer = [swap(part, "c") for part in give(place, *packs)]
 
-    query, gate, den, self_term = project(place, *cols, *packs, got, more)
+    rows = assemble(*packs, got, more)
+    query, gate, den, self_term, w_part = project(place, *cols, rows)
     query_other = swap(query, "zh")
-
-    w_part = out_part(*cols, query)
     w_part = [along(w_part, "x", s) if s else w_part for s in range(4)]
 
     away = attend("other", BF16, place, query_other, *packs, kv_peer, self_term)

time: 113 us -> 112 us (level)
  the two profiles are of different devices: /device:TPU:32 before, /device:TPU:40 now
where the time goes in v6:
time: 112 us; the launch traced here: 111 us
  starting transfers between devices  69.6 us (62%)
  Pallas kernels  16.3 us (15%)
  waiting for transfers between devices  14.1 us (13%)
  blocking collectives  10.2 us (9%)
    ppermute x9, starting transfers between devices, along(): return lax.ppermute(value, axis, [(i, (i + steps) % 4) for i in range(4)])  32.2 us
    ppermute x6, starting transfers between devices, swap(): return lax.ppermute(value, axis, [(0, 1), (1, 0)])  24.7 us
    all_to_all x1, starting transfers between devices, body(): cols = lax.all_to_all(cols, 'zl', 0, 0, tiled=True).reshape(256, 640)  12.6 us
    all_to_all x1, blocking collectives, body(): mixed = lax.all_to_all(mixed, LOCAL, 0, 0, tiled=True)  10.2 us
    all_to_all x1, waiting for transfers between devices, body(): cols = lax.all_to_all(cols, 'zl', 0, 0, tiled=True).reshape(256, 640)  6.42 us
    pallas_call x2, Pallas kernels, attend(): pl.pallas_call(attend_kernel, name=name, out_shape=jax.ShapeDtypeStruct((...  6.17 us
    ppermute x6, waiting for transfers between devices, swap(): return lax.ppermute(value, axis, [(0, 1), (1, 0)])  5.71 us
    pallas_call x1, Pallas kernels, finish(): pl.pallas_call(finish_kernel, name='finish', out_shape=jax.ShapeDtypeStru...  2.43 us
  transfers between devices with their start and end apart: 16, of which 4 were waited for; matrix products, arithmetic and copies ran while one was open for 0% of the time, Pallas kernels for 11%

profile of v6, /device:TPU:40, one launch (start us, length us, event | category | flops | bytes accessed | tf_op | source)
XLA Modules:
  0.0 111.4 jit_solution(14443539379591330724)
XLA Ops:
  0.0 0.0 copy-start.10
  0.0 0.0 copy-start.9
  0.0 0.0 copy-start.8
  0.0 0.0 copy-start.5
  0.0 0.0 copy-start.4
  0.0 0.0 copy-start.6
  0.0 1.7 %columns.1 = bf16[8,32,640]{2,1,0:T(8,128)(2,1)} custom-call(bf16[32,4096]{1,0:T(8,128)(2,1)} %in_ref.1, bf16[32,1024]{1,0:T(8,128)(2,1)} %out_w_ref.1), custom_call_target="tpu_custom_call" | custom-call | tf_op jit(solution)/shard_map/columns/pallas_call | solution.py:76
  1.8 12.6 %all-to-all-start = ((bf16[8,32,640]{2,1,0:T(8,128)(2,1)}), bf16[8,32,640]{2,1,0:T(8,128)(2,1)S(1)}, u32[]{:S(2)}, u32[]{:S(2)}) async-start(bf16[8,32,640]{2,1,0:T(8,128)(2,1)} %columns.1), calls=%async_computation | async-start | bytes 655360 | tf_op jit(solution)/shard_map/all_to_all | solution.py:357
  14.4 0.1 pad_add_fusion.place_ref
  14.5 0.0 copy-done.10
  14.5 0.0 copy-done.9
  14.5 0.0 copy-done.8
  14.5 0.0 copy-done.5
  14.5 0.0 copy-done.4
  14.5 0.0 copy-done.6
  14.5 1.0 packets.1
  15.5 3.4 %collective-permute-start.3 = (bf16[1600,128]{1,0:T(8,128)(2,1)S(1)}, bf16[1600,128]{1,0:T(8,128)(2,1)S(1)}, u32[]{:S(2)}, u32[]{:S(2)}) collective-permute-start(bf16[1600,128]{1,0:T(8,128)(2,1)S(1)} %get-tuple-element.18), channel_id=1, source_target_pairs={{0,64},{64,128},{128,192},{192,0},{1,65},{65,129},{129,193},{193,1... | collective-permute-start | bytes 1228808 | tf_op jit(solution)/shard_map/ppermute | solution.py:54
  18.9 4.6 %collective-permute-start.4 = (bf16[1600,128]{1,0:T(8,128)(2,1)S(1)}, bf16[1600,128]{1,0:T(8,128)(2,1)S(1)}, u32[]{:S(2)}, u32[]{:S(2)}) collective-permute-start(bf16[1600,128]{1,0:T(8,128)(2,1)S(1)} %get-tuple-element.19), channel_id=1, source_target_pairs={{0,128},{64,192},{128,0},{192,64},{1,129},{65,193},{129,1},{193,65... | collective-permute-start | bytes 1228808 | tf_op jit(solution)/shard_map/ppermute | solution.py:54
  23.5 3.3 %collective-permute-start.5 = (bf16[1600,128]{1,0:T(8,128)(2,1)S(1)}, bf16[1600,128]{1,0:T(8,128)(2,1)S(1)}, u32[]{:S(2)}, u32[]{:S(2)}) collective-permute-start(bf16[1600,128]{1,0:T(8,128)(2,1)S(1)} %get-tuple-element.20), channel_id=1, source_target_pairs={{0,192},{64,0},{128,64},{192,128},{1,193},{65,1},{129,65},{193,129... | collective-permute-start | bytes 1228808 | tf_op jit(solution)/shard_map/ppermute | solution.py:54
  26.9 6.4 %all-to-all-done = bf16[8,32,640]{2,1,0:T(8,128)(2,1)S(1)} async-done(((bf16[8,32,640]{2,1,0:T(8,128)(2,1)}), bf16[8,32,640]{2,1,0:T(8,128)(2,1)S(1)}, u32[]{:S(2)}, u32[]{:S(2)}) %all-to-all-start) | async-done | bytes 327712 | tf_op jit(solution)/shard_map/all_to_all | solution.py:357
  33.3 2.3 %collective-permute-start.2 = (bf16[256,640]{1,0:T(8,128)(2,1)S(1)}, bf16[256,640]{1,0:T(8,128)(2,1)S(1)}, u32[]{:S(2)}, u32[]{:S(2)}) collective-permute-start(bf16[256,640]{1,0:T(8,128)(2,1)S(1)} %bitcast.13), channel_id=1, source_target_pairs={{0,3},{1,0},{2,1},{3,2},{4,7},{5,4},{6,5},{7,6},{8,11},{9,8},{10,9... | collective-permute-start | bytes 983048 | tf_op jit(solution)/shard_map/ppermute | solution.py:54
  35.7 4.5 %collective-permute-start.1 = (bf16[256,640]{1,0:T(8,128)(2,1)S(1)}, bf16[256,640]{1,0:T(8,128)(2,1)S(1)}, u32[]{:S(2)}, u32[]{:S(2)}) collective-permute-start(bf16[256,640]{1,0:T(8,128)(2,1)S(1)} %bitcast.14), channel_id=1, source_target_pairs={{0,2},{1,3},{2,0},{3,1},{4,6},{5,7},{6,4},{7,5},{8,10},{9,11},{10,... | collective-permute-start | bytes 983048 | tf_op jit(solution)/shard_map/ppermute | solution.py:54
  40.2 0.0 collective-permute-done.3.p1
  40.2 3.8 %collective-permute-start = (bf16[256,640]{1,0:T(8,128)(2,1)S(1)}, bf16[256,640]{1,0:T(8,128)(2,1)S(1)}, u32[]{:S(2)}, u32[]{:S(2)}) collective-permute-start(bf16[256,640]{1,0:T(8,128)(2,1)S(1)} %bitcast.15), channel_id=1, source_target_pairs={{0,1},{1,2},{2,3},{3,0},{4,5},{5,6},{6,7},{7,4},{8,9},{9,10},{10,1... | collective-permute-start | bytes 983048 | tf_op jit(solution)/shard_map/ppermute | solution.py:54
  44.0 0.0 collective-permute-done.4.p2
  44.0 0.0 collective-permute-done.5.p3
  44.0 1.4 %give.1 = (bf16[1152,128]{1,0:T(8,128)(2,1)S(1)}, bf16[1152,128]{1,0:T(8,128)(2,1)S(1)}, bf16[2048,128]{1,0:T(8,128)(2,1)}) custom-call(s32[4]{0:T(128)S(1)} %pad_add_fusion.place_ref, bf16[1600,128]{1,0:T(8,128)(2,1)S(1)} %get-tuple-element.17.p0, bf16[1600,128]{1,0:T(8,128)(2,1)S(1)} %collective-permute-done.3.p1, ...), custom_call_target="tpu_custom_call" | custom-call | flops 268435456 | bytes 1048576 | tf_op jit(solution)/shard_map/give/pallas_call | solution.py:146
  45.4 1.9 %collective-permute-start.6 = (bf16[1152,128]{1,0:T(8,128)(2,1)S(1)}, bf16[1152,128]{1,0:T(8,128)(2,1)S(1)}, u32[]{:S(2)}, u32[]{:S(2)}) collective-permute-start(bf16[1152,128]{1,0:T(8,128)(2,1)S(1)} %get-tuple-element.21), channel_id=1, source_target_pairs={{0,32},{32,0},{1,33},{33,1},{2,34},{34,2},{3,35},{35,3},{4,36},{36... | collective-permute-start | bytes 884744 | tf_op jit(solution)/shard_map/ppermute | solution.py:50
  47.4 2.4 %collective-permute-start.7 = (bf16[1152,128]{1,0:T(8,128)(2,1)S(1)}, bf16[1152,128]{1,0:T(8,128)(2,1)S(1)}, u32[]{:S(2)}, u32[]{:S(2)}) collective-permute-start(bf16[1152,128]{1,0:T(8,128)(2,1)S(1)} %get-tuple-element.22), channel_id=1, source_target_pairs={{0,32},{32,0},{1,33},{33,1},{2,34},{34,2},{3,35},{35,3},{4,36},{36... | collective-permute-start | bytes 884744 | tf_op jit(solution)/shard_map/ppermute | solution.py:50
  49.8 0.0 collective-permute-done.6.got
  49.8 1.9 %collective-permute-start.8 = (bf16[2048,128]{1,0:T(8,128)(2,1)}, bf16[2048,128]{1,0:T(8,128)(2,1)}, u32[]{:S(2)}, u32[]{:S(2)}) collective-permute-start(bf16[2048,128]{1,0:T(8,128)(2,1)} %get-tuple-element.24), channel_id=1, source_target_pairs={{0,32},{32,0},{1,33},{33,1},{2,34},{34,2},{3,35},{35,3},{4,36},{36... | collective-permute-start | bytes 1572872 | tf_op jit(solution)/shard_map/ppermute | solution.py:50
  51.7 0.0 collective-permute-done.7.more
  51.7 0.2 assemble.1.rows
  51.9 0.0 collective-permute-done.2.w3
  52.0 0.0 collective-permute-done.1.w2
  52.0 1.9 %collective-permute-done.w1 = bf16[256,640]{1,0:T(8,128)(2,1)S(1)} collective-permute-done((bf16[256,640]{1,0:T(8,128)(2,1)S(1)}, bf16[256,640]{1,0:T(8,128)(2,1)S(1)}, u32[]{:S(2)}, u32[]{:S(2)}) %collective-permute-start) | collective-permute-done | bytes 327712 | tf_op jit(solution)/shard_map/ppermute | solution.py:54
  53.9 1.6 %project.1 = (bf16[576,128]{1,0:T(8,128)(2,1)S(1)}, bf16[512,128]{1,0:T(8,128)(2,1)S(1)}, f32[512,128]{1,0:T(8,128)S(1)}, f32[512,128]{1,0:T(8,128)S(1)}, bf16[4,256,128]{2,1,0:T(8,128)(2,1)S(1)}) custom-call(s32[4]{0:T(128)S(1)} %pad_add_fusion.place_ref, bf16[256,640]{1,0:T(8,128)(2,1)S(1)} %bitcast.16, bf16[256,640]{1,0:T(8,128)(2,1)S(1)} %collective-permute-done.w1, ...), custom_call_target="tpu_custom_call" | custom-call | flops 536870912000 | bytes 2097152000 | tf_op jit(solution)/shard_map/project/pallas_call | solution.py:234
  55.5 8.2 %collective-permute-start.9 = (bf16[576,128]{1,0:T(8,128)(2,1)S(1)}, bf16[576,128]{1,0:T(8,128)(2,1)S(1)}, u32[]{:S(2)}, u32[]{:S(2)}) collective-permute-start(bf16[576,128]{1,0:T(8,128)(2,1)S(1)} %get-tuple-element.23.q_ref), channel_id=1, source_target_pairs={{0,256},{256,0},{1,257},{257,1},{2,258},{258,2},{3,259},{259,3},{4... | collective-permute-start | bytes 442376 | tf_op jit(solution)/shard_map/ppermute | solution.py:50
  63.7 4.7 %collective-permute-start.13 = (bf16[4,256,128]{2,1,0:T(8,128)(2,1)S(1)}, bf16[4,256,128]{2,1,0:T(8,128)(2,1)S(1)}, u32[]{:S(2)}, u32[]{:S(2)}) collective-permute-start(bf16[4,256,128]{2,1,0:T(8,128)(2,1)S(1)} %get-tuple-element.28.refs_0_.w0), channel_id=1, source_target_pairs={{0,192},{64,0},{128,64},{192,128},{1,193},{65,1},{129,65},{193,129... | collective-permute-start | bytes 786440 | tf_op jit(solution)/shard_map/ppermute | solution.py:54
  68.4 2.7 %collective-permute-start.12 = (bf16[4,256,128]{2,1,0:T(8,128)(2,1)S(1)}, bf16[4,256,128]{2,1,0:T(8,128)(2,1)S(1)}, u32[]{:S(2)}, u32[]{:S(2)}) collective-permute-start(bf16[4,256,128]{2,1,0:T(8,128)(2,1)S(1)} %get-tuple-element.28.refs_0_.w0), channel_id=1, source_target_pairs={{0,128},{64,192},{128,0},{192,64},{1,129},{65,193},{129,1},{193,65... | collective-permute-start | bytes 786440 | tf_op jit(solution)/shard_map/ppermute | solution.py:54
  71.1 2.8 %collective-permute-start.11 = (bf16[4,256,128]{2,1,0:T(8,128)(2,1)S(1)}, bf16[4,256,128]{2,1,0:T(8,128)(2,1)S(1)}, u32[]{:S(2)}, u32[]{:S(2)}) collective-permute-start(bf16[4,256,128]{2,1,0:T(8,128)(2,1)S(1)} %get-tuple-element.28.refs_0_.w0), channel_id=1, source_target_pairs={{0,64},{64,128},{128,192},{192,0},{1,65},{65,129},{129,193},{193,1... | collective-permute-start | bytes 786440 | tf_op jit(solution)/shard_map/ppermute | solution.py:54
  73.9 0.0 collective-permute-done.8.kv_peer
  73.9 3.4 %collective-permute-done.9.q_ref = bf16[576,128]{1,0:T(8,128)(2,1)S(1)} collective-permute-done((bf16[576,128]{1,0:T(8,128)(2,1)S(1)}, bf16[576,128]{1,0:T(8,128)(2,1)S(1)}, u32[]{:S(2)}, u32[]{:S(2)}) %collective-permute-start.9) | collective-permute-done | bytes 147488 | tf_op jit(solution)/shard_map/ppermute | solution.py:50
  77.3 3.1 %other.1.refs_4_ = bf16[512,128]{1,0:T(8,128)(2,1)S(1)} custom-call(s32[4]{0:T(128)S(1)} %pad_add_fusion.place_ref, bf16[576,128]{1,0:T(8,128)(2,1)S(1)} %collective-permute-done.9.q_ref, bf16[1600,128]{1,0:T(8,128)(2,1)S(1)} %get-tuple-element.17.p0, bf16[1600,128]{1,0:T(8,128)(2,1)S(1)} %collective-permute-done.3.p1, ...), custom_call_target="tpu_custom_call" | custom-call | flops 1073741824 | bytes 4194304 | tf_op jit(solution)/shard_map/other/pallas_call | solution.py:293
  80.4 8.4 %collective-permute-start.10 = (bf16[512,128]{1,0:T(8,128)(2,1)S(1)}, bf16[512,128]{1,0:T(8,128)(2,1)S(1)}, u32[]{:S(2)}, u32[]{:S(2)}) collective-permute-start(bf16[512,128]{1,0:T(8,128)(2,1)S(1)} %other.1.refs_4_), channel_id=1, source_target_pairs={{0,256},{256,0},{1,257},{257,1},{2,258},{258,2},{3,259},{259,3},{4... | collective-permute-start | bytes 393224 | tf_op jit(solution)/shard_map/ppermute | solution.py:50
  88.8 3.1 %own.1.sum_ref = f32[512,128]{1,0:T(8,128)S(1)} custom-call(s32[4]{0:T(128)S(1)} %pad_add_fusion.place_ref, bf16[576,128]{1,0:T(8,128)(2,1)S(1)} %get-tuple-element.23.q_ref, bf16[1600,128]{1,0:T(8,128)(2,1)S(1)} %get-tuple-element.17.p0, bf16[1600,128]{1,0:T(8,128)(2,1)S(1)} %collective-permute-done.3.p1, bf16[1600,128]{1,0:T(8,128)(2,1)S(1)} %collective-permute-done.4.p2, ...), custom_call_target="tpu_custom_call" | custom-call | flops 1073741824 | bytes 4194304 | tf_op jit(solution)/shard_map/own/pallas_call | solution.py:293
  91.8 0.0 collective-permute-done.13.refs_3_.w3
  91.9 0.0 collective-permute-done.12.refs_2_.w2
  91.9 0.0 collective-permute-done.11.refs_1_.w1
  91.9 0.0 copy-start.2
  91.9 1.1 stack.21
  92.9 0.0 copy-start
  92.9 0.7 copy-done
  93.6 1.9 %collective-permute-start.14 = (bf16[4,4,256,128]{3,2,1,0:T(8,128)(2,1)}, bf16[4,4,256,128]{3,2,1,0:T(8,128)(2,1)}, u32[]{:S(2)}, u32[]{:S(2)}) collective-permute-start(bf16[4,4,256,128]{3,2,1,0:T(8,128)(2,1)} %stack.21), channel_id=1, source_target_pairs={{0,32},{32,0},{1,33},{33,1},{2,34},{34,2},{3,35},{35,3},{4,36},{36... | collective-permute-start | bytes 3145736 | tf_op jit(solution)/shard_map/ppermute | solution.py:50
  95.6 2.3 %collective-permute-done.10.home_ref = bf16[512,128]{1,0:T(8,128)(2,1)S(1)} collective-permute-done((bf16[512,128]{1,0:T(8,128)(2,1)S(1)}, bf16[512,128]{1,0:T(8,128)(2,1)S(1)}, u32[]{:S(2)}, u32[]{:S(2)}) %collective-permute-start.10) | collective-permute-done | bytes 131104 | tf_op jit(solution)/shard_map/ppermute | solution.py:50
  97.9 0.0 copy-done.2
  97.9 0.0 copy-start.1
  97.9 0.8 mix.1
  98.7 10.2 %all_to_all.10.mixed_ref = bf16[8,64,128]{2,1,0:T(8,128)(2,1)S(1)} all-to-all(bf16[8,64,128]{2,1,0:T(8,128)(2,1)S(1)} %mix.1), channel_id=1, replica_groups=mesh['zh'=2,'x'=4,'c'=2,'zl'=8,'y'=4] {'x','c'}, dimensions={0} | all-to-all | bytes 262144 | tf_op jit(solution)/shard_map/all_to_all | solution.py:376
  108.9 0.0 collective-permute-done.14.peer_ref
  108.9 0.0 copy-done.1
  108.9 0.0 copy-done.3
  108.9 0.0 copy-done.7
  108.9 2.4 %finish.1 = bf16[64,1024]{1,0:T(8,128)(2,1)} custom-call(s32[4]{0:T(128)S(1)} %pad_add_fusion.place_ref, bf16[64,1024]{1,0:T(8,128)(2,1)S(1)} %bitcast.12, bf16[8,64,128]{2,1,0:T(8,128)(2,1)S(1)} %all_to_all.10.mixed_ref, bf16[4,256,128]{2,1,0:T(8,128)(2,1)S(1)} %get-tuple-element.28.refs_0_.w0, bf16[4,256,128]{2,1,0:T(8,128)(2,1)S(1)} %copy-done.3, ...), custom_call_target="tpu_custom_call" | custom-call | tf_op jit(solution)/shard_map/finish/pallas_call | solution.py:341
  (2 shorter events, 0.0 us)
Async XLA Ops:
  0.0 14.5 %copy-start.10 = (s32[1,64]{1,0:T(1,128)S(1)}, s32[1,64]{1,0:T(1,128)}, u32[]{:S(2)}) copy-start(s32[1,64]{1,0:T(1,128)} %cutoff_ref.1) | copy-start | bytes 772
  0.0 14.5 %copy-start.9 = (s32[1,64]{1,0:T(1,128)S(1)}, s32[1,64]{1,0:T(1,128)}, u32[]{:S(2)}) copy-start(s32[1,64]{1,0:T(1,128)} %user_ref.1) | copy-start | bytes 772
  0.0 14.5 %copy-start.8 = (s32[1,32]{1,0:T(1,128)S(1)}, s32[1,32]{1,0:T(1,128)}, u32[]{:S(2)}) copy-start(s32[1,32]{1,0:T(1,128)} %owner_ref.1) | copy-start | bytes 388
  0.0 14.5 %copy-start.5 = (bf16[1,256,1024]{2,1,0:T(8,128)(2,1)S(1)}, bf16[1,256,1024]{2,1,0:T(8,128)(2,1)}, u32[]{:S(2)}) copy-start(bf16[1,256,1024]{2,1,0:T(8,128)(2,1)} %param.10) | copy-start | bytes 1572868
  0.0 14.5 %copy-start.4 = (bf16[1,256,1024]{2,1,0:T(8,128)(2,1)S(1)}, bf16[1,256,1024]{2,1,0:T(8,128)(2,1)}, u32[]{:S(2)}) copy-start(bf16[1,256,1024]{2,1,0:T(8,128)(2,1)} %param.9) | copy-start | bytes 1572868
  0.0 14.5 %copy-start.6 = (bf16[1,64,1024]{2,1,0:T(8,128)(2,1)S(1)}, bf16[1,64,1024]{2,1,0:T(8,128)(2,1)}, u32[]{:S(2)}) copy-start(bf16[1,64,1024]{2,1,0:T(8,128)(2,1)} %param.8) | copy-start | bytes 393220
  1.8 31.6 %all-to-all-start = ((bf16[8,32,640]{2,1,0:T(8,128)(2,1)}), bf16[8,32,640]{2,1,0:T(8,128)(2,1)S(1)}, u32[]{:S(2)}, u32[]{:S(2)}) async-start(bf16[8,32,640]{2,1,0:T(8,128)(2,1)} %columns.1), calls=%async_computation | async-start | bytes 655360 | tf_op jit(solution)/shard_map/all_to_all | solution.py:357
  15.5 24.7 %collective-permute-start.3 = (bf16[1600,128]{1,0:T(8,128)(2,1)S(1)}, bf16[1600,128]{1,0:T(8,128)(2,1)S(1)}, u32[]{:S(2)}, u32[]{:S(2)}) collective-permute-start(bf16[1600,128]{1,0:T(8,128)(2,1)S(1)} %get-tuple-element.18), channel_id=1, source_target_pairs={{0,64},{64,128},{128,192},{192,0},{1,65},{65,129},{129,193},{193,1... | collective-permute-start | bytes 1228808 | tf_op jit(solution)/shard_map/ppermute | solution.py:54
  18.9 25.1 %collective-permute-start.4 = (bf16[1600,128]{1,0:T(8,128)(2,1)S(1)}, bf16[1600,128]{1,0:T(8,128)(2,1)S(1)}, u32[]{:S(2)}, u32[]{:S(2)}) collective-permute-start(bf16[1600,128]{1,0:T(8,128)(2,1)S(1)} %get-tuple-element.19), channel_id=1, source_target_pairs={{0,128},{64,192},{128,0},{192,64},{1,129},{65,193},{129,1},{193,65... | collective-permute-start | bytes 1228808 | tf_op jit(solution)/shard_map/ppermute | solution.py:54
  23.5 20.5 %collective-permute-start.5 = (bf16[1600,128]{1,0:T(8,128)(2,1)S(1)}, bf16[1600,128]{1,0:T(8,128)(2,1)S(1)}, u32[]{:S(2)}, u32[]{:S(2)}) collective-permute-start(bf16[1600,128]{1,0:T(8,128)(2,1)S(1)} %get-tuple-element.20), channel_id=1, source_target_pairs={{0,192},{64,0},{128,64},{192,128},{1,193},{65,1},{129,65},{193,129... | collective-permute-start | bytes 1228808 | tf_op jit(solution)/shard_map/ppermute | solution.py:54
  33.3 18.6 %collective-permute-start.2 = (bf16[256,640]{1,0:T(8,128)(2,1)S(1)}, bf16[256,640]{1,0:T(8,128)(2,1)S(1)}, u32[]{:S(2)}, u32[]{:S(2)}) collective-permute-start(bf16[256,640]{1,0:T(8,128)(2,1)S(1)} %bitcast.13), channel_id=1, source_target_pairs={{0,3},{1,0},{2,1},{3,2},{4,7},{5,4},{6,5},{7,6},{8,11},{9,8},{10,9... | collective-permute-start | bytes 983048 | tf_op jit(solution)/shard_map/ppermute | solution.py:54
  35.7 16.3 %collective-permute-start.1 = (bf16[256,640]{1,0:T(8,128)(2,1)S(1)}, bf16[256,640]{1,0:T(8,128)(2,1)S(1)}, u32[]{:S(2)}, u32[]{:S(2)}) collective-permute-start(bf16[256,640]{1,0:T(8,128)(2,1)S(1)} %bitcast.14), channel_id=1, source_target_pairs={{0,2},{1,3},{2,0},{3,1},{4,6},{5,7},{6,4},{7,5},{8,10},{9,11},{10,... | collective-permute-start | bytes 983048 | tf_op jit(solution)/shard_map/ppermute | solution.py:54
  40.2 13.7 %collective-permute-start = (bf16[256,640]{1,0:T(8,128)(2,1)S(1)}, bf16[256,640]{1,0:T(8,128)(2,1)S(1)}, u32[]{:S(2)}, u32[]{:S(2)}) collective-permute-start(bf16[256,640]{1,0:T(8,128)(2,1)S(1)} %bitcast.15), channel_id=1, source_target_pairs={{0,1},{1,2},{2,3},{3,0},{4,5},{5,6},{6,7},{7,4},{8,9},{9,10},{10,1... | collective-permute-start | bytes 983048 | tf_op jit(solution)/shard_map/ppermute | solution.py:54
  45.4 4.3 %collective-permute-start.6 = (bf16[1152,128]{1,0:T(8,128)(2,1)S(1)}, bf16[1152,128]{1,0:T(8,128)(2,1)S(1)}, u32[]{:S(2)}, u32[]{:S(2)}) collective-permute-start(bf16[1152,128]{1,0:T(8,128)(2,1)S(1)} %get-tuple-element.21), channel_id=1, source_target_pairs={{0,32},{32,0},{1,33},{33,1},{2,34},{34,2},{3,35},{35,3},{4,36},{36... | collective-permute-start | bytes 884744 | tf_op jit(solution)/shard_map/ppermute | solution.py:50
  47.4 4.4 %collective-permute-start.7 = (bf16[1152,128]{1,0:T(8,128)(2,1)S(1)}, bf16[1152,128]{1,0:T(8,128)(2,1)S(1)}, u32[]{:S(2)}, u32[]{:S(2)}) collective-permute-start(bf16[1152,128]{1,0:T(8,128)(2,1)S(1)} %get-tuple-element.22), channel_id=1, source_target_pairs={{0,32},{32,0},{1,33},{33,1},{2,34},{34,2},{3,35},{35,3},{4,36},{36... | collective-permute-start | bytes 884744 | tf_op jit(solution)/shard_map/ppermute | solution.py:50
  49.8 24.1 %collective-permute-start.8 = (bf16[2048,128]{1,0:T(8,128)(2,1)}, bf16[2048,128]{1,0:T(8,128)(2,1)}, u32[]{:S(2)}, u32[]{:S(2)}) collective-permute-start(bf16[2048,128]{1,0:T(8,128)(2,1)} %get-tuple-element.24), channel_id=1, source_target_pairs={{0,32},{32,0},{1,33},{33,1},{2,34},{34,2},{3,35},{35,3},{4,36},{36... | collective-permute-start | bytes 1572872 | tf_op jit(solution)/shard_map/ppermute | solution.py:50
  55.5 21.8 %collective-permute-start.9 = (bf16[576,128]{1,0:T(8,128)(2,1)S(1)}, bf16[576,128]{1,0:T(8,128)(2,1)S(1)}, u32[]{:S(2)}, u32[]{:S(2)}) collective-permute-start(bf16[576,128]{1,0:T(8,128)(2,1)S(1)} %get-tuple-element.23.q_ref), channel_id=1, source_target_pairs={{0,256},{256,0},{1,257},{257,1},{2,258},{258,2},{3,259},{259,3},{4... | collective-permute-start | bytes 442376 | tf_op jit(solution)/shard_map/ppermute | solution.py:50
  63.7 28.1 %collective-permute-start.13 = (bf16[4,256,128]{2,1,0:T(8,128)(2,1)S(1)}, bf16[4,256,128]{2,1,0:T(8,128)(2,1)S(1)}, u32[]{:S(2)}, u32[]{:S(2)}) collective-permute-start(bf16[4,256,128]{2,1,0:T(8,128)(2,1)S(1)} %get-tuple-element.28.refs_0_.w0), channel_id=1, source_target_pairs={{0,192},{64,0},{128,64},{192,128},{1,193},{65,1},{129,65},{193,129... | collective-permute-start | bytes 786440 | tf_op jit(solution)/shard_map/ppermute | solution.py:54
  68.4 23.5 %collective-permute-start.12 = (bf16[4,256,128]{2,1,0:T(8,128)(2,1)S(1)}, bf16[4,256,128]{2,1,0:T(8,128)(2,1)S(1)}, u32[]{:S(2)}, u32[]{:S(2)}) collective-permute-start(bf16[4,256,128]{2,1,0:T(8,128)(2,1)S(1)} %get-tuple-element.28.refs_0_.w0), channel_id=1, source_target_pairs={{0,128},{64,192},{128,0},{192,64},{1,129},{65,193},{129,1},{193,65... | collective-permute-start | bytes 786440 | tf_op jit(solution)/shard_map/ppermute | solution.py:54
  71.1 20.8 %collective-permute-start.11 = (bf16[4,256,128]{2,1,0:T(8,128)(2,1)S(1)}, bf16[4,256,128]{2,1,0:T(8,128)(2,1)S(1)}, u32[]{:S(2)}, u32[]{:S(2)}) collective-permute-start(bf16[4,256,128]{2,1,0:T(8,128)(2,1)S(1)} %get-tuple-element.28.refs_0_.w0), channel_id=1, source_target_pairs={{0,64},{64,128},{128,192},{192,0},{1,65},{65,129},{129,193},{193,1... | collective-permute-start | bytes 786440 | tf_op jit(solution)/shard_map/ppermute | solution.py:54
  80.4 17.5 %collective-permute-start.10 = (bf16[512,128]{1,0:T(8,128)(2,1)S(1)}, bf16[512,128]{1,0:T(8,128)(2,1)S(1)}, u32[]{:S(2)}, u32[]{:S(2)}) collective-permute-start(bf16[512,128]{1,0:T(8,128)(2,1)S(1)} %other.1.refs_4_), channel_id=1, source_target_pairs={{0,256},{256,0},{1,257},{257,1},{2,258},{258,2},{3,259},{259,3},{4... | collective-permute-start | bytes 393224 | tf_op jit(solution)/shard_map/ppermute | solution.py:50
  91.9 6.0 %copy-start.2 = (bf16[4,256,128]{2,1,0:T(8,128)(2,1)}, bf16[4,256,128]{2,1,0:T(8,128)(2,1)S(1)}, u32[]{:S(2)}) copy-start(bf16[4,256,128]{2,1,0:T(8,128)(2,1)S(1)} %collective-permute-done.11.refs_1_.w1) | copy-start | bytes 786436
  92.9 0.7 copy-start
  93.6 15.3 %collective-permute-start.14 = (bf16[4,4,256,128]{3,2,1,0:T(8,128)(2,1)}, bf16[4,4,256,128]{3,2,1,0:T(8,128)(2,1)}, u32[]{:S(2)}, u32[]{:S(2)}) collective-permute-start(bf16[4,4,256,128]{3,2,1,0:T(8,128)(2,1)} %stack.21), channel_id=1, source_target_pairs={{0,32},{32,0},{1,33},{33,1},{2,34},{34,2},{3,35},{35,3},{4,36},{36... | collective-permute-start | bytes 3145736 | tf_op jit(solution)/shard_map/ppermute | solution.py:50
  97.9 11.0 %copy-start.1 = (bf16[4,256,128]{2,1,0:T(8,128)(2,1)S(1)}, bf16[4,256,128]{2,1,0:T(8,128)(2,1)}, u32[]{:S(2)}) copy-start(bf16[4,256,128]{2,1,0:T(8,128)(2,1)} %copy-done) | copy-start | bytes 786436
  97.9 11.0 %copy-start.3 = (bf16[4,256,128]{2,1,0:T(8,128)(2,1)S(1)}, bf16[4,256,128]{2,1,0:T(8,128)(2,1)}, u32[]{:S(2)}) copy-start(bf16[4,256,128]{2,1,0:T(8,128)(2,1)} %copy-done.2) | copy-start | bytes 786436
  97.9 11.0 %copy-start.7 = (bf16[1,64,1024]{2,1,0:T(8,128)(2,1)S(1)}, bf16[1,64,1024]{2,1,0:T(8,128)(2,1)}, u32[]{:S(2)}) copy-start(bf16[1,64,1024]{2,1,0:T(8,128)(2,1)} %param.8) | copy-start | bytes 393220

commit v7 on v6

--- a/solution.py
+++ b/solution.py
@@ -221,12 +221,14 @@
         query = proj[:, 256:384].astype(F32)
         score = jnp.sum(query * proj[:, 384:512].astype(F32), axis=-1, keepdims=True)
         self_ref[at, :] = silu(score * SCALE) * proj[:, 128:256].astype(F32)
+    labels = []
     for i in range(4):
         at = pl.ds(i * 128, 128)
         tags = rows[at, D:].astype(F32)
         first, last = visible(tags)
         den_ref[at, :] = jnp.broadcast_to(last - first + 1.0, (128, HEAD))
-        query_ref[HALF + i * 16 : HALF + i * 16 + 16, :] = tags.T[0:16, :].astype(BF16)
+        labels.append(tags.T[0:4, :])
+    query_ref[HALF:, :] = jnp.concatenate(labels, axis=0).astype(BF16)
 
 
 def project(*args):
@@ -235,7 +237,7 @@
         project_kernel,
         name="project",
         out_shape=[
-            jax.ShapeDtypeStruct((HALF + 64, HEAD), BF16),
+            jax.ShapeDtypeStruct((HALF + 16, HEAD), BF16),
             jax.ShapeDtypeStruct(shape, BF16),
             jax.ShapeDtypeStruct(shape, F32),
             jax.ShapeDtypeStruct(shape, F32),
@@ -254,13 +256,14 @@
     copy = pltpu.make_async_copy(kv_peer, kv_all, sem)
     copy.start()
     event = lax.broadcasted_iota(jnp.int32, (256, 256), 1)
+    labels = q_ref[HALF : HALF + 16, :].astype(F32)
     for tile in range(2):
         at = pl.ds(tile * 256, 256)
         lows, counts = [], []
         for i in range(2):
-            row = HALF + (tile * 2 + i) * 16
-            tags = q_ref[row : row + 16, :].astype(F32)
-            tags = jnp.concatenate([tags, jnp.zeros((112, 128), F32)], axis=0).T
+            row = (tile * 2 + i) * 4
+            tags = labels[row : row + 4, :]
+            tags = jnp.concatenate([tags, jnp.zeros((124, 128), F32)], axis=0).T
             first, last = visible(tags)
             lows.append(first.astype(jnp.int32))
             counts.append((last - first).astype(jnp.uint32))

time: 112 us -> 112 us (level)
  starting transfers between devices: 69.6 us -> 68.2 us
    ppermute x6, starting transfers between devices: 24.7 us -> 23.3 us  [swap(): return lax.ppermute(value, axis, [(0, 1), (1, 0)])]
where the time goes in v7:
time: 112 us; the launch traced here: 111 us
  starting transfers between devices  68.2 us (61%)
  Pallas kernels  16.5 us (15%)
  waiting for transfers between devices  15.2 us (14%)
  blocking collectives  10.1 us (9%)
    ppermute x9, starting transfers between devices, along(): return lax.ppermute(value, axis, [(i, (i + steps) % 4) for i in range(4)])  32.2 us
    ppermute x6, starting transfers between devices, swap(): return lax.ppermute(value, axis, [(0, 1), (1, 0)])  23.3 us
    all_to_all x1, starting transfers between devices, body(): cols = lax.all_to_all(cols, 'zl', 0, 0, tiled=True).reshape(256, 640)  12.6 us
    all_to_all x1, blocking collectives, body(): mixed = lax.all_to_all(mixed, LOCAL, 0, 0, tiled=True)  10.1 us
    ppermute x6, waiting for transfers between devices, swap(): return lax.ppermute(value, axis, [(0, 1), (1, 0)])  6.77 us
    all_to_all x1, waiting for transfers between devices, body(): cols = lax.all_to_all(cols, 'zl', 0, 0, tiled=True).reshape(256, 640)  6.42 us
    pallas_call x2, Pallas kernels, attend(): pl.pallas_call(attend_kernel, name=name, out_shape=jax.ShapeDtypeStruct((...  6.37 us
    pallas_call x1, Pallas kernels, finish(): pl.pallas_call(finish_kernel, name='finish', out_shape=jax.ShapeDtypeStru...  2.43 us
  transfers between devices with their start and end apart: 16, of which 4 were waited for; matrix products, arithmetic and copies ran while one was open for 0% of the time, Pallas kernels for 11%

profile of v7, /device:TPU:40, one launch (start us, length us, event | category | flops | bytes accessed | tf_op | source)
XLA Modules:
  0.0 111.1 jit_solution(12862611424053217358)
XLA Ops:
  0.0 0.0 copy-start.10
  0.0 0.0 copy-start.9
  0.0 0.0 copy-start.8
  0.0 0.0 copy-start.5
  0.0 0.0 copy-start.4
  0.0 0.0 copy-start.6
  0.0 1.7 %columns.1 = bf16[8,32,640]{2,1,0:T(8,128)(2,1)} custom-call(bf16[32,4096]{1,0:T(8,128)(2,1)} %in_ref.1, bf16[32,1024]{1,0:T(8,128)(2,1)} %out_w_ref.1), custom_call_target="tpu_custom_call" | custom-call | tf_op jit(solution)/shard_map/columns/pallas_call | solution.py:76
  1.8 12.6 %all-to-all-start = ((bf16[8,32,640]{2,1,0:T(8,128)(2,1)}), bf16[8,32,640]{2,1,0:T(8,128)(2,1)S(1)}, u32[]{:S(2)}, u32[]{:S(2)}) async-start(bf16[8,32,640]{2,1,0:T(8,128)(2,1)} %columns.1), calls=%async_computation | async-start | bytes 655360 | tf_op jit(solution)/shard_map/all_to_all | solution.py:360
  14.4 0.1 pad_add_fusion.place_ref
  14.5 0.0 copy-done.10
  14.5 0.0 copy-done.9
  14.5 0.0 copy-done.8
  14.5 0.0 copy-done.5
  14.5 0.0 copy-done.4
  14.5 0.0 copy-done.6
  14.5 1.0 packets.1
  15.5 3.4 %collective-permute-start.3 = (bf16[1600,128]{1,0:T(8,128)(2,1)S(1)}, bf16[1600,128]{1,0:T(8,128)(2,1)S(1)}, u32[]{:S(2)}, u32[]{:S(2)}) collective-permute-start(bf16[1600,128]{1,0:T(8,128)(2,1)S(1)} %get-tuple-element.18), channel_id=1, source_target_pairs={{0,64},{64,128},{128,192},{192,0},{1,65},{65,129},{129,193},{193,1... | collective-permute-start | bytes 1228808 | tf_op jit(solution)/shard_map/ppermute | solution.py:54
  18.9 4.6 %collective-permute-start.4 = (bf16[1600,128]{1,0:T(8,128)(2,1)S(1)}, bf16[1600,128]{1,0:T(8,128)(2,1)S(1)}, u32[]{:S(2)}, u32[]{:S(2)}) collective-permute-start(bf16[1600,128]{1,0:T(8,128)(2,1)S(1)} %get-tuple-element.19), channel_id=1, source_target_pairs={{0,128},{64,192},{128,0},{192,64},{1,129},{65,193},{129,1},{193,65... | collective-permute-start | bytes 1228808 | tf_op jit(solution)/shard_map/ppermute | solution.py:54
  23.5 3.3 %collective-permute-start.5 = (bf16[1600,128]{1,0:T(8,128)(2,1)S(1)}, bf16[1600,128]{1,0:T(8,128)(2,1)S(1)}, u32[]{:S(2)}, u32[]{:S(2)}) collective-permute-start(bf16[1600,128]{1,0:T(8,128)(2,1)S(1)} %get-tuple-element.20), channel_id=1, source_target_pairs={{0,192},{64,0},{128,64},{192,128},{1,193},{65,1},{129,65},{193,129... | collective-permute-start | bytes 1228808 | tf_op jit(solution)/shard_map/ppermute | solution.py:54
  26.9 6.4 %all-to-all-done = bf16[8,32,640]{2,1,0:T(8,128)(2,1)S(1)} async-done(((bf16[8,32,640]{2,1,0:T(8,128)(2,1)}), bf16[8,32,640]{2,1,0:T(8,128)(2,1)S(1)}, u32[]{:S(2)}, u32[]{:S(2)}) %all-to-all-start) | async-done | bytes 327712 | tf_op jit(solution)/shard_map/all_to_all | solution.py:360
  33.3 2.3 %collective-permute-start.2 = (bf16[256,640]{1,0:T(8,128)(2,1)S(1)}, bf16[256,640]{1,0:T(8,128)(2,1)S(1)}, u32[]{:S(2)}, u32[]{:S(2)}) collective-permute-start(bf16[256,640]{1,0:T(8,128)(2,1)S(1)} %bitcast.13), channel_id=1, source_target_pairs={{0,3},{1,0},{2,1},{3,2},{4,7},{5,4},{6,5},{7,6},{8,11},{9,8},{10,9... | collective-permute-start | bytes 983048 | tf_op jit(solution)/shard_map/ppermute | solution.py:54
  35.7 4.5 %collective-permute-start.1 = (bf16[256,640]{1,0:T(8,128)(2,1)S(1)}, bf16[256,640]{1,0:T(8,128)(2,1)S(1)}, u32[]{:S(2)}, u32[]{:S(2)}) collective-permute-start(bf16[256,640]{1,0:T(8,128)(2,1)S(1)} %bitcast.14), channel_id=1, source_target_pairs={{0,2},{1,3},{2,0},{3,1},{4,6},{5,7},{6,4},{7,5},{8,10},{9,11},{10,... | collective-permute-start | bytes 983048 | tf_op jit(solution)/shard_map/ppermute | solution.py:54
  40.2 0.0 collective-permute-done.3.p1
  40.2 3.8 %collective-permute-start = (bf16[256,640]{1,0:T(8,128)(2,1)S(1)}, bf16[256,640]{1,0:T(8,128)(2,1)S(1)}, u32[]{:S(2)}, u32[]{:S(2)}) collective-permute-start(bf16[256,640]{1,0:T(8,128)(2,1)S(1)} %bitcast.15), channel_id=1, source_target_pairs={{0,1},{1,2},{2,3},{3,0},{4,5},{5,6},{6,7},{7,4},{8,9},{9,10},{10,1... | collective-permute-start | bytes 983048 | tf_op jit(solution)/shard_map/ppermute | solution.py:54
  44.0 0.0 collective-permute-done.4.p2
  44.0 0.0 collective-permute-done.5.p3
  44.0 1.4 %give.1 = (bf16[1152,128]{1,0:T(8,128)(2,1)S(1)}, bf16[1152,128]{1,0:T(8,128)(2,1)S(1)}, bf16[2048,128]{1,0:T(8,128)(2,1)}) custom-call(s32[4]{0:T(128)S(1)} %pad_add_fusion.place_ref, bf16[1600,128]{1,0:T(8,128)(2,1)S(1)} %get-tuple-element.17.p0, bf16[1600,128]{1,0:T(8,128)(2,1)S(1)} %collective-permute-done.3.p1, ...), custom_call_target="tpu_custom_call" | custom-call | flops 268435456 | bytes 1048576 | tf_op jit(solution)/shard_map/give/pallas_call | solution.py:146
  45.4 1.9 %collective-permute-start.6 = (bf16[1152,128]{1,0:T(8,128)(2,1)S(1)}, bf16[1152,128]{1,0:T(8,128)(2,1)S(1)}, u32[]{:S(2)}, u32[]{:S(2)}) collective-permute-start(bf16[1152,128]{1,0:T(8,128)(2,1)S(1)} %get-tuple-element.21), channel_id=1, source_target_pairs={{0,32},{32,0},{1,33},{33,1},{2,34},{34,2},{3,35},{35,3},{4,36},{36... | collective-permute-start | bytes 884744 | tf_op jit(solution)/shard_map/ppermute | solution.py:50
  47.4 2.4 %collective-permute-start.7 = (bf16[1152,128]{1,0:T(8,128)(2,1)S(1)}, bf16[1152,128]{1,0:T(8,128)(2,1)S(1)}, u32[]{:S(2)}, u32[]{:S(2)}) collective-permute-start(bf16[1152,128]{1,0:T(8,128)(2,1)S(1)} %get-tuple-element.22), channel_id=1, source_target_pairs={{0,32},{32,0},{1,33},{33,1},{2,34},{34,2},{3,35},{35,3},{4,36},{36... | collective-permute-start | bytes 884744 | tf_op jit(solution)/shard_map/ppermute | solution.py:50
  49.8 0.0 collective-permute-done.6.got
  49.8 1.9 %collective-permute-start.8 = (bf16[2048,128]{1,0:T(8,128)(2,1)}, bf16[2048,128]{1,0:T(8,128)(2,1)}, u32[]{:S(2)}, u32[]{:S(2)}) collective-permute-start(bf16[2048,128]{1,0:T(8,128)(2,1)} %get-tuple-element.24), channel_id=1, source_target_pairs={{0,32},{32,0},{1,33},{33,1},{2,34},{34,2},{3,35},{35,3},{4,36},{36... | collective-permute-start | bytes 1572872 | tf_op jit(solution)/shard_map/ppermute | solution.py:50
  51.7 0.0 collective-permute-done.7.more
  51.7 0.2 assemble.1.rows
  51.9 0.0 collective-permute-done.2.w3
  52.0 0.0 collective-permute-done.1.w2
  52.0 1.9 %collective-permute-done.w1 = bf16[256,640]{1,0:T(8,128)(2,1)S(1)} collective-permute-done((bf16[256,640]{1,0:T(8,128)(2,1)S(1)}, bf16[256,640]{1,0:T(8,128)(2,1)S(1)}, u32[]{:S(2)}, u32[]{:S(2)}) %collective-permute-start) | collective-permute-done | bytes 327712 | tf_op jit(solution)/shard_map/ppermute | solution.py:54
  53.9 1.6 %project.1 = (bf16[528,128]{1,0:T(8,128)(2,1)S(1)}, bf16[512,128]{1,0:T(8,128)(2,1)S(1)}, f32[512,128]{1,0:T(8,128)S(1)}, f32[512,128]{1,0:T(8,128)S(1)}, bf16[4,256,128]{2,1,0:T(8,128)(2,1)S(1)}) custom-call(s32[4]{0:T(128)S(1)} %pad_add_fusion.place_ref, bf16[256,640]{1,0:T(8,128)(2,1)S(1)} %bitcast.16, bf16[256,640]{1,0:T(8,128)(2,1)S(1)} %collective-permute-done.w1, ...), custom_call_target="tpu_custom_call" | custom-call | flops 536870912000 | bytes 2097152000 | tf_op jit(solution)/shard_map/project/pallas_call | solution.py:236
  55.5 8.2 %collective-permute-start.9 = (bf16[528,128]{1,0:T(8,128)(2,1)S(1)}, bf16[528,128]{1,0:T(8,128)(2,1)S(1)}, u32[]{:S(2)}, u32[]{:S(2)}) collective-permute-start(bf16[528,128]{1,0:T(8,128)(2,1)S(1)} %get-tuple-element.23.q_ref), channel_id=1, source_target_pairs={{0,256},{256,0},{1,257},{257,1},{2,258},{258,2},{3,259},{259,3},{4... | collective-permute-start | bytes 405512 | tf_op jit(solution)/shard_map/ppermute | solution.py:50
  63.7 4.7 %collective-permute-start.13 = (bf16[4,256,128]{2,1,0:T(8,128)(2,1)S(1)}, bf16[4,256,128]{2,1,0:T(8,128)(2,1)S(1)}, u32[]{:S(2)}, u32[]{:S(2)}) collective-permute-start(bf16[4,256,128]{2,1,0:T(8,128)(2,1)S(1)} %get-tuple-element.28.refs_0_.w0), channel_id=1, source_target_pairs={{0,192},{64,0},{128,64},{192,128},{1,193},{65,1},{129,65},{193,129... | collective-permute-start | bytes 786440 | tf_op jit(solution)/shard_map/ppermute | solution.py:54
  68.4 2.7 %collective-permute-start.12 = (bf16[4,256,128]{2,1,0:T(8,128)(2,1)S(1)}, bf16[4,256,128]{2,1,0:T(8,128)(2,1)S(1)}, u32[]{:S(2)}, u32[]{:S(2)}) collective-permute-start(bf16[4,256,128]{2,1,0:T(8,128)(2,1)S(1)} %get-tuple-element.28.refs_0_.w0), channel_id=1, source_target_pairs={{0,128},{64,192},{128,0},{192,64},{1,129},{65,193},{129,1},{193,65... | collective-permute-start | bytes 786440 | tf_op jit(solution)/shard_map/ppermute | solution.py:54
  71.1 2.8 %collective-permute-start.11 = (bf16[4,256,128]{2,1,0:T(8,128)(2,1)S(1)}, bf16[4,256,128]{2,1,0:T(8,128)(2,1)S(1)}, u32[]{:S(2)}, u32[]{:S(2)}) collective-permute-start(bf16[4,256,128]{2,1,0:T(8,128)(2,1)S(1)} %get-tuple-element.28.refs_0_.w0), channel_id=1, source_target_pairs={{0,64},{64,128},{128,192},{192,0},{1,65},{65,129},{129,193},{193,1... | collective-permute-start | bytes 786440 | tf_op jit(solution)/shard_map/ppermute | solution.py:54
  73.9 0.0 collective-permute-done.8.kv_peer
  73.9 2.6 %collective-permute-done.9.q_ref = bf16[528,128]{1,0:T(8,128)(2,1)S(1)} collective-permute-done((bf16[528,128]{1,0:T(8,128)(2,1)S(1)}, bf16[528,128]{1,0:T(8,128)(2,1)S(1)}, u32[]{:S(2)}, u32[]{:S(2)}) %collective-permute-start.9) | collective-permute-done | bytes 135200 | tf_op jit(solution)/shard_map/ppermute | solution.py:50
  76.5 3.1 %other.1.refs_4_ = bf16[512,128]{1,0:T(8,128)(2,1)S(1)} custom-call(s32[4]{0:T(128)S(1)} %pad_add_fusion.place_ref, bf16[528,128]{1,0:T(8,128)(2,1)S(1)} %collective-permute-done.9.q_ref, bf16[1600,128]{1,0:T(8,128)(2,1)S(1)} %get-tuple-element.17.p0, bf16[1600,128]{1,0:T(8,128)(2,1)S(1)} %collective-permute-done.3.p1, ...), custom_call_target="tpu_custom_call" | custom-call | flops 1073741824 | bytes 4194304 | tf_op jit(solution)/shard_map/other/pallas_call | solution.py:296
  79.6 7.0 %collective-permute-start.10 = (bf16[512,128]{1,0:T(8,128)(2,1)S(1)}, bf16[512,128]{1,0:T(8,128)(2,1)S(1)}, u32[]{:S(2)}, u32[]{:S(2)}) collective-permute-start(bf16[512,128]{1,0:T(8,128)(2,1)S(1)} %other.1.refs_4_), channel_id=1, source_target_pairs={{0,256},{256,0},{1,257},{257,1},{2,258},{258,2},{3,259},{259,3},{4... | collective-permute-start | bytes 393224 | tf_op jit(solution)/shard_map/ppermute | solution.py:50
  86.6 3.3 %own.1.sum_ref = f32[512,128]{1,0:T(8,128)S(1)} custom-call(s32[4]{0:T(128)S(1)} %pad_add_fusion.place_ref, bf16[528,128]{1,0:T(8,128)(2,1)S(1)} %get-tuple-element.23.q_ref, bf16[1600,128]{1,0:T(8,128)(2,1)S(1)} %get-tuple-element.17.p0, bf16[1600,128]{1,0:T(8,128)(2,1)S(1)} %collective-permute-done.3.p1, bf16[1600,128]{1,0:T(8,128)(2,1)S(1)} %collective-permute-done.4.p2, ...), custom_call_target="tpu_custom_call" | custom-call | flops 1073741824 | bytes 4194304 | tf_op jit(solution)/shard_map/own/pallas_call | solution.py:296
  89.9 0.0 collective-permute-done.13.refs_3_.w3
  89.9 0.0 collective-permute-done.12.refs_2_.w2
  89.9 0.0 collective-permute-done.11.refs_1_.w1
  89.9 0.0 copy-start.2
  89.9 1.1 stack.21
  91.0 0.0 copy-start
  91.0 0.7 copy-done
  91.7 1.9 %collective-permute-start.14 = (bf16[4,4,256,128]{3,2,1,0:T(8,128)(2,1)}, bf16[4,4,256,128]{3,2,1,0:T(8,128)(2,1)}, u32[]{:S(2)}, u32[]{:S(2)}) collective-permute-start(bf16[4,4,256,128]{3,2,1,0:T(8,128)(2,1)} %stack.21), channel_id=1, source_target_pairs={{0,32},{32,0},{1,33},{33,1},{2,34},{34,2},{3,35},{35,3},{4,36},{36... | collective-permute-start | bytes 3145736 | tf_op jit(solution)/shard_map/ppermute | solution.py:50
  93.6 4.2 %collective-permute-done.10.home_ref = bf16[512,128]{1,0:T(8,128)(2,1)S(1)} collective-permute-done((bf16[512,128]{1,0:T(8,128)(2,1)S(1)}, bf16[512,128]{1,0:T(8,128)(2,1)S(1)}, u32[]{:S(2)}, u32[]{:S(2)}) %collective-permute-start.10) | collective-permute-done | bytes 131104 | tf_op jit(solution)/shard_map/ppermute | solution.py:50
  97.8 0.0 copy-done.2
  97.8 0.0 copy-start.1
  97.8 0.8 mix.1
  98.6 10.1 %all_to_all.10.mixed_ref = bf16[8,64,128]{2,1,0:T(8,128)(2,1)S(1)} all-to-all(bf16[8,64,128]{2,1,0:T(8,128)(2,1)S(1)} %mix.1), channel_id=1, replica_groups=mesh['zh'=2,'x'=4,'c'=2,'zl'=8,'y'=4] {'x','c'}, dimensions={0} | all-to-all | bytes 262144 | tf_op jit(solution)/shard_map/all_to_all | solution.py:379
  108.7 0.0 collective-permute-done.14.peer_ref
  108.7 0.0 copy-done.1
  108.7 0.0 copy-done.3
  108.7 0.0 copy-done.7
  108.7 2.4 %finish.1 = bf16[64,1024]{1,0:T(8,128)(2,1)} custom-call(s32[4]{0:T(128)S(1)} %pad_add_fusion.place_ref, bf16[64,1024]{1,0:T(8,128)(2,1)S(1)} %bitcast.12, bf16[8,64,128]{2,1,0:T(8,128)(2,1)S(1)} %all_to_all.10.mixed_ref, bf16[4,256,128]{2,1,0:T(8,128)(2,1)S(1)} %get-tuple-element.28.refs_0_.w0, bf16[4,256,128]{2,1,0:T(8,128)(2,1)S(1)} %copy-done.3, ...), custom_call_target="tpu_custom_call" | custom-call | tf_op jit(solution)/shard_map/finish/pallas_call | solution.py:344
  (2 shorter events, 0.0 us)
Async XLA Ops:
  0.0 14.5 %copy-start.10 = (s32[1,64]{1,0:T(1,128)S(1)}, s32[1,64]{1,0:T(1,128)}, u32[]{:S(2)}) copy-start(s32[1,64]{1,0:T(1,128)} %cutoff_ref.1) | copy-start | bytes 772
  0.0 14.5 %copy-start.9 = (s32[1,64]{1,0:T(1,128)S(1)}, s32[1,64]{1,0:T(1,128)}, u32[]{:S(2)}) copy-start(s32[1,64]{1,0:T(1,128)} %user_ref.1) | copy-start | bytes 772
  0.0 14.5 %copy-start.8 = (s32[1,32]{1,0:T(1,128)S(1)}, s32[1,32]{1,0:T(1,128)}, u32[]{:S(2)}) copy-start(s32[1,32]{1,0:T(1,128)} %owner_ref.1) | copy-start | bytes 388
  0.0 14.5 %copy-start.5 = (bf16[1,256,1024]{2,1,0:T(8,128)(2,1)S(1)}, bf16[1,256,1024]{2,1,0:T(8,128)(2,1)}, u32[]{:S(2)}) copy-start(bf16[1,256,1024]{2,1,0:T(8,128)(2,1)} %param.10) | copy-start | bytes 1572868
  0.0 14.5 %copy-start.4 = (bf16[1,256,1024]{2,1,0:T(8,128)(2,1)S(1)}, bf16[1,256,1024]{2,1,0:T(8,128)(2,1)}, u32[]{:S(2)}) copy-start(bf16[1,256,1024]{2,1,0:T(8,128)(2,1)} %param.9) | copy-start | bytes 1572868
  0.0 14.5 %copy-start.6 = (bf16[1,64,1024]{2,1,0:T(8,128)(2,1)S(1)}, bf16[1,64,1024]{2,1,0:T(8,128)(2,1)}, u32[]{:S(2)}) copy-start(bf16[1,64,1024]{2,1,0:T(8,128)(2,1)} %param.8) | copy-start | bytes 393220
  1.8 31.6 %all-to-all-start = ((bf16[8,32,640]{2,1,0:T(8,128)(2,1)}), bf16[8,32,640]{2,1,0:T(8,128)(2,1)S(1)}, u32[]{:S(2)}, u32[]{:S(2)}) async-start(bf16[8,32,640]{2,1,0:T(8,128)(2,1)} %columns.1), calls=%async_computation | async-start | bytes 655360 | tf_op jit(solution)/shard_map/all_to_all | solution.py:360
  15.5 24.7 %collective-permute-start.3 = (bf16[1600,128]{1,0:T(8,128)(2,1)S(1)}, bf16[1600,128]{1,0:T(8,128)(2,1)S(1)}, u32[]{:S(2)}, u32[]{:S(2)}) collective-permute-start(bf16[1600,128]{1,0:T(8,128)(2,1)S(1)} %get-tuple-element.18), channel_id=1, source_target_pairs={{0,64},{64,128},{128,192},{192,0},{1,65},{65,129},{129,193},{193,1... | collective-permute-start | bytes 1228808 | tf_op jit(solution)/shard_map/ppermute | solution.py:54
  18.9 25.1 %collective-permute-start.4 = (bf16[1600,128]{1,0:T(8,128)(2,1)S(1)}, bf16[1600,128]{1,0:T(8,128)(2,1)S(1)}, u32[]{:S(2)}, u32[]{:S(2)}) collective-permute-start(bf16[1600,128]{1,0:T(8,128)(2,1)S(1)} %get-tuple-element.19), channel_id=1, source_target_pairs={{0,128},{64,192},{128,0},{192,64},{1,129},{65,193},{129,1},{193,65... | collective-permute-start | bytes 1228808 | tf_op jit(solution)/shard_map/ppermute | solution.py:54
  23.5 20.5 %collective-permute-start.5 = (bf16[1600,128]{1,0:T(8,128)(2,1)S(1)}, bf16[1600,128]{1,0:T(8,128)(2,1)S(1)}, u32[]{:S(2)}, u32[]{:S(2)}) collective-permute-start(bf16[1600,128]{1,0:T(8,128)(2,1)S(1)} %get-tuple-element.20), channel_id=1, source_target_pairs={{0,192},{64,0},{128,64},{192,128},{1,193},{65,1},{129,65},{193,129... | collective-permute-start | bytes 1228808 | tf_op jit(solution)/shard_map/ppermute | solution.py:54
  33.3 18.6 %collective-permute-start.2 = (bf16[256,640]{1,0:T(8,128)(2,1)S(1)}, bf16[256,640]{1,0:T(8,128)(2,1)S(1)}, u32[]{:S(2)}, u32[]{:S(2)}) collective-permute-start(bf16[256,640]{1,0:T(8,128)(2,1)S(1)} %bitcast.13), channel_id=1, source_target_pairs={{0,3},{1,0},{2,1},{3,2},{4,7},{5,4},{6,5},{7,6},{8,11},{9,8},{10,9... | collective-permute-start | bytes 983048 | tf_op jit(solution)/shard_map/ppermute | solution.py:54
  35.7 16.3 %collective-permute-start.1 = (bf16[256,640]{1,0:T(8,128)(2,1)S(1)}, bf16[256,640]{1,0:T(8,128)(2,1)S(1)}, u32[]{:S(2)}, u32[]{:S(2)}) collective-permute-start(bf16[256,640]{1,0:T(8,128)(2,1)S(1)} %bitcast.14), channel_id=1, source_target_pairs={{0,2},{1,3},{2,0},{3,1},{4,6},{5,7},{6,4},{7,5},{8,10},{9,11},{10,... | collective-permute-start | bytes 983048 | tf_op jit(solution)/shard_map/ppermute | solution.py:54
  40.2 13.7 %collective-permute-start = (bf16[256,640]{1,0:T(8,128)(2,1)S(1)}, bf16[256,640]{1,0:T(8,128)(2,1)S(1)}, u32[]{:S(2)}, u32[]{:S(2)}) collective-permute-start(bf16[256,640]{1,0:T(8,128)(2,1)S(1)} %bitcast.15), channel_id=1, source_target_pairs={{0,1},{1,2},{2,3},{3,0},{4,5},{5,6},{6,7},{7,4},{8,9},{9,10},{10,1... | collective-permute-start | bytes 983048 | tf_op jit(solution)/shard_map/ppermute | solution.py:54
  45.4 4.3 %collective-permute-start.6 = (bf16[1152,128]{1,0:T(8,128)(2,1)S(1)}, bf16[1152,128]{1,0:T(8,128)(2,1)S(1)}, u32[]{:S(2)}, u32[]{:S(2)}) collective-permute-start(bf16[1152,128]{1,0:T(8,128)(2,1)S(1)} %get-tuple-element.21), channel_id=1, source_target_pairs={{0,32},{32,0},{1,33},{33,1},{2,34},{34,2},{3,35},{35,3},{4,36},{36... | collective-permute-start | bytes 884744 | tf_op jit(solution)/shard_map/ppermute | solution.py:50
  47.4 4.4 %collective-permute-start.7 = (bf16[1152,128]{1,0:T(8,128)(2,1)S(1)}, bf16[1152,128]{1,0:T(8,128)(2,1)S(1)}, u32[]{:S(2)}, u32[]{:S(2)}) collective-permute-start(bf16[1152,128]{1,0:T(8,128)(2,1)S(1)} %get-tuple-element.22), channel_id=1, source_target_pairs={{0,32},{32,0},{1,33},{33,1},{2,34},{34,2},{3,35},{35,3},{4,36},{36... | collective-permute-start | bytes 884744 | tf_op jit(solution)/shard_map/ppermute | solution.py:50
  49.8 24.1 %collective-permute-start.8 = (bf16[2048,128]{1,0:T(8,128)(2,1)}, bf16[2048,128]{1,0:T(8,128)(2,1)}, u32[]{:S(2)}, u32[]{:S(2)}) collective-permute-start(bf16[2048,128]{1,0:T(8,128)(2,1)} %get-tuple-element.24), channel_id=1, source_target_pairs={{0,32},{32,0},{1,33},{33,1},{2,34},{34,2},{3,35},{35,3},{4,36},{36... | collective-permute-start | bytes 1572872 | tf_op jit(solution)/shard_map/ppermute | solution.py:50
  55.5 21.0 %collective-permute-start.9 = (bf16[528,128]{1,0:T(8,128)(2,1)S(1)}, bf16[528,128]{1,0:T(8,128)(2,1)S(1)}, u32[]{:S(2)}, u32[]{:S(2)}) collective-permute-start(bf16[528,128]{1,0:T(8,128)(2,1)S(1)} %get-tuple-element.23.q_ref), channel_id=1, source_target_pairs={{0,256},{256,0},{1,257},{257,1},{2,258},{258,2},{3,259},{259,3},{4... | collective-permute-start | bytes 405512 | tf_op jit(solution)/shard_map/ppermute | solution.py:50
  63.7 26.2 %collective-permute-start.13 = (bf16[4,256,128]{2,1,0:T(8,128)(2,1)S(1)}, bf16[4,256,128]{2,1,0:T(8,128)(2,1)S(1)}, u32[]{:S(2)}, u32[]{:S(2)}) collective-permute-start(bf16[4,256,128]{2,1,0:T(8,128)(2,1)S(1)} %get-tuple-element.28.refs_0_.w0), channel_id=1, source_target_pairs={{0,192},{64,0},{128,64},{192,128},{1,193},{65,1},{129,65},{193,129... | collective-permute-start | bytes 786440 | tf_op jit(solution)/shard_map/ppermute | solution.py:54
  68.4 21.5 %collective-permute-start.12 = (bf16[4,256,128]{2,1,0:T(8,128)(2,1)S(1)}, bf16[4,256,128]{2,1,0:T(8,128)(2,1)S(1)}, u32[]{:S(2)}, u32[]{:S(2)}) collective-permute-start(bf16[4,256,128]{2,1,0:T(8,128)(2,1)S(1)} %get-tuple-element.28.refs_0_.w0), channel_id=1, source_target_pairs={{0,128},{64,192},{128,0},{192,64},{1,129},{65,193},{129,1},{193,65... | collective-permute-start | bytes 786440 | tf_op jit(solution)/shard_map/ppermute | solution.py:54
  71.1 18.8 %collective-permute-start.11 = (bf16[4,256,128]{2,1,0:T(8,128)(2,1)S(1)}, bf16[4,256,128]{2,1,0:T(8,128)(2,1)S(1)}, u32[]{:S(2)}, u32[]{:S(2)}) collective-permute-start(bf16[4,256,128]{2,1,0:T(8,128)(2,1)S(1)} %get-tuple-element.28.refs_0_.w0), channel_id=1, source_target_pairs={{0,64},{64,128},{128,192},{192,0},{1,65},{65,129},{129,193},{193,1... | collective-permute-start | bytes 786440 | tf_op jit(solution)/shard_map/ppermute | solution.py:54
  79.6 18.2 %collective-permute-start.10 = (bf16[512,128]{1,0:T(8,128)(2,1)S(1)}, bf16[512,128]{1,0:T(8,128)(2,1)S(1)}, u32[]{:S(2)}, u32[]{:S(2)}) collective-permute-start(bf16[512,128]{1,0:T(8,128)(2,1)S(1)} %other.1.refs_4_), channel_id=1, source_target_pairs={{0,256},{256,0},{1,257},{257,1},{2,258},{258,2},{3,259},{259,3},{4... | collective-permute-start | bytes 393224 | tf_op jit(solution)/shard_map/ppermute | solution.py:50
  89.9 7.9 %copy-start.2 = (bf16[4,256,128]{2,1,0:T(8,128)(2,1)}, bf16[4,256,128]{2,1,0:T(8,128)(2,1)S(1)}, u32[]{:S(2)}) copy-start(bf16[4,256,128]{2,1,0:T(8,128)(2,1)S(1)} %collective-permute-done.11.refs_1_.w1) | copy-start | bytes 786436
  91.0 0.7 copy-start
  91.7 17.0 %collective-permute-start.14 = (bf16[4,4,256,128]{3,2,1,0:T(8,128)(2,1)}, bf16[4,4,256,128]{3,2,1,0:T(8,128)(2,1)}, u32[]{:S(2)}, u32[]{:S(2)}) collective-permute-start(bf16[4,4,256,128]{3,2,1,0:T(8,128)(2,1)} %stack.21), channel_id=1, source_target_pairs={{0,32},{32,0},{1,33},{33,1},{2,34},{34,2},{3,35},{35,3},{4,36},{36... | collective-permute-start | bytes 3145736 | tf_op jit(solution)/shard_map/ppermute | solution.py:50
  97.8 10.9 %copy-start.1 = (bf16[4,256,128]{2,1,0:T(8,128)(2,1)S(1)}, bf16[4,256,128]{2,1,0:T(8,128)(2,1)}, u32[]{:S(2)}) copy-start(bf16[4,256,128]{2,1,0:T(8,128)(2,1)} %copy-done) | copy-start | bytes 786436
  97.8 10.9 %copy-start.3 = (bf16[4,256,128]{2,1,0:T(8,128)(2,1)S(1)}, bf16[4,256,128]{2,1,0:T(8,128)(2,1)}, u32[]{:S(2)}) copy-start(bf16[4,256,128]{2,1,0:T(8,128)(2,1)} %copy-done.2) | copy-start | bytes 786436
  97.8 10.9 %copy-start.7 = (bf16[1,64,1024]{2,1,0:T(8,128)(2,1)S(1)}, bf16[1,64,1024]{2,1,0:T(8,128)(2,1)}, u32[]{:S(2)}) copy-start(bf16[1,64,1024]{2,1,0:T(8,128)(2,1)} %param.8) | copy-start | bytes 393220

commit v8 on v7

--- a/solution.py
+++ b/solution.py
@@ -167,6 +167,21 @@
         out_specs=VMEM,
         compiler_params=PARAMS,
     )(*args)
+
+
+def near_kernel(value_ref, after_ref, out_ref):
+    out_ref[...] = value_ref[...]
+
+
+def near(value, after):
+    return pl.pallas_call(
+        near_kernel,
+        name="near",
+        out_shape=jax.ShapeDtypeStruct(value.shape, value.dtype),
+        in_specs=[VMEM, ANY],
+        out_specs=VMEM,
+        compiler_params=PARAMS,
+    )(value, after)
 
 
 def stack_kernel(*refs):
@@ -251,10 +266,8 @@
     )(*args)
 
 
-def attend_kernel(place_ref, q_ref, p0, p1, p2, p3, kv_peer, plus_ref, out_ref, kv_all, sem):
+def attend_kernel(place_ref, q_ref, p0, p1, p2, p3, kv_peer, plus_ref, out_ref):
     x, core, half = place_ref[0], place_ref[1], place_ref[2]
-    copy = pltpu.make_async_copy(kv_peer, kv_all, sem)
-    copy.start()
     event = lax.broadcasted_iota(jnp.int32, (256, 256), 1)
     labels = q_ref[HALF : HALF + 16, :].astype(F32)
     for tile in range(2):
@@ -272,13 +285,11 @@
         query = q_ref[at, :]
         total = jnp.zeros((256, HEAD), F32)
         for rel in range(2):
-            if tile == 0 and rel:
-                copy.wait()
             for s, pack in enumerate((p0, p1, p2, p3)):
                 base = half * EVENTS + ((x - s + 4) & 3) * 512 + (core ^ rel) * 256
                 row = s * 512 if rel else pl.multiple_of(core * 256, 256)
                 keys, values = pl.ds(row, 256), pl.ds(row + (256 if rel else 512), 256)
-                ref = kv_all if rel else pack
+                ref = kv_peer if rel else pack
                 score = lax.dot_general(
                     query, ref[keys, :], (((1,), (1,)), ((), ())), preferred_element_type=F32
                 )
@@ -297,9 +308,8 @@
         attend_kernel,
         name=name,
         out_shape=jax.ShapeDtypeStruct((HALF, HEAD), dtype),
-        in_specs=[SMEM] + [VMEM] * 5 + [ANY, VMEM],
-        out_specs=VMEM,
-        scratch_shapes=[pltpu.VMEM((2048, HEAD), BF16), pltpu.SemaphoreType.DMA],
+        in_specs=[SMEM] + [VMEM] * 7,
+        out_specs=VMEM,
         cost_estimate=cost(C_AWAY if name == "other" else C_OWN),
         compiler_params=PARAMS,
     )(*args)
@@ -368,6 +378,7 @@
     query, gate, den, self_term, w_part = project(place, *cols, rows)
     query_other = swap(query, "zh")
     w_part = [along(w_part, "x", s) if s else w_part for s in range(4)]
+    kv_peer = near(kv_peer, query)
 
     away = attend("other", BF16, place, query_other, *packs, kv_peer, self_term)
     home = swap(away, "zh")

time: 112 us -> 111 us (level)
  the two profiles are of different devices: /device:TPU:40 before, /device:TPU:32 now
where the time goes in v8:
time: 111 us; the launch traced here: 110 us
  starting transfers between devices  67.9 us (61%)
  Pallas kernels  16.5 us (15%)
  waiting for transfers between devices  16.1 us (15%)
  blocking collectives  9.55 us (9%)
    ppermute x9, starting transfers between devices, along(): return lax.ppermute(value, axis, [(i, (i + steps) % 4) for i in range(4)])  31.9 us
    ppermute x6, starting transfers between devices, swap(): return lax.ppermute(value, axis, [(0, 1), (1, 0)])  23.4 us
    all_to_all x1, starting transfers between devices, body(): cols = lax.all_to_all(cols, 'zl', 0, 0, tiled=True).reshape(256, 640)  12.6 us
    all_to_all x1, blocking collectives, body(): mixed = lax.all_to_all(mixed, LOCAL, 0, 0, tiled=True)  9.55 us
    all_to_all x1, waiting for transfers between devices, body(): cols = lax.all_to_all(cols, 'zl', 0, 0, tiled=True).reshape(256, 640)  6.42 us
    pallas_call x2, Pallas kernels, attend(): pl.pallas_call(attend_kernel, name=name, out_shape=jax.ShapeDtypeStruct((...  5.26 us
    ppermute x6, waiting for transfers between devices, swap(): return lax.ppermute(value, axis, [(0, 1), (1, 0)])  4.9 us
    ppermute x9, waiting for transfers between devices, along(): return lax.ppermute(value, axis, [(i, (i + steps) % 4) for i in range(4)])  4.76 us
  transfers between devices with their start and end apart: 16, of which 4 were waited for; matrix products, arithmetic and copies ran while one was open for 0% of the time, Pallas kernels for 11%

profile of v8, /device:TPU:32, one launch (start us, length us, event | category | flops | bytes accessed | tf_op | source)
XLA Modules:
  0.0 110.5 jit_solution(16420454601596192244)
XLA Ops:
  0.0 0.0 copy-start.6
  0.0 0.0 copy-start.5
  0.0 0.0 copy-start.4
  0.0 0.0 copy-start.1
  0.0 0.0 copy-start
  0.0 0.0 copy-start.2
  0.0 1.7 %columns.1 = bf16[8,32,640]{2,1,0:T(8,128)(2,1)} custom-call(bf16[32,4096]{1,0:T(8,128)(2,1)} %in_ref.1, bf16[32,1024]{1,0:T(8,128)(2,1)} %out_w_ref.1), custom_call_target="tpu_custom_call" | custom-call | tf_op jit(solution)/shard_map/columns/pallas_call | solution.py:76
  1.8 12.6 %all-to-all-start = ((bf16[8,32,640]{2,1,0:T(8,128)(2,1)}), bf16[8,32,640]{2,1,0:T(8,128)(2,1)S(1)}, u32[]{:S(2)}, u32[]{:S(2)}) async-start(bf16[8,32,640]{2,1,0:T(8,128)(2,1)} %columns.1), calls=%async_computation | async-start | bytes 655360 | tf_op jit(solution)/shard_map/all_to_all | solution.py:370
  14.4 0.1 pad_add_fusion.place_ref
  14.5 0.0 copy-done.6
  14.5 0.0 copy-done.5
  14.5 0.0 copy-done.4
  14.5 0.0 copy-done.1
  14.5 0.0 copy-done
  14.5 0.0 copy-done.2
  14.5 1.0 packets.1
  15.5 3.4 %collective-permute-start.3 = (bf16[1600,128]{1,0:T(8,128)(2,1)S(1)}, bf16[1600,128]{1,0:T(8,128)(2,1)S(1)}, u32[]{:S(2)}, u32[]{:S(2)}) collective-permute-start(bf16[1600,128]{1,0:T(8,128)(2,1)S(1)} %get-tuple-element.18), channel_id=1, source_target_pairs={{0,64},{64,128},{128,192},{192,0},{1,65},{65,129},{129,193},{193,1... | collective-permute-start | bytes 1228808 | tf_op jit(solution)/shard_map/ppermute | solution.py:54
  18.9 4.6 %collective-permute-start.4 = (bf16[1600,128]{1,0:T(8,128)(2,1)S(1)}, bf16[1600,128]{1,0:T(8,128)(2,1)S(1)}, u32[]{:S(2)}, u32[]{:S(2)}) collective-permute-start(bf16[1600,128]{1,0:T(8,128)(2,1)S(1)} %get-tuple-element.19), channel_id=1, source_target_pairs={{0,128},{64,192},{128,0},{192,64},{1,129},{65,193},{129,1},{193,65... | collective-permute-start | bytes 1228808 | tf_op jit(solution)/shard_map/ppermute | solution.py:54
  23.5 3.3 %collective-permute-start.5 = (bf16[1600,128]{1,0:T(8,128)(2,1)S(1)}, bf16[1600,128]{1,0:T(8,128)(2,1)S(1)}, u32[]{:S(2)}, u32[]{:S(2)}) collective-permute-start(bf16[1600,128]{1,0:T(8,128)(2,1)S(1)} %get-tuple-element.20), channel_id=1, source_target_pairs={{0,192},{64,0},{128,64},{192,128},{1,193},{65,1},{129,65},{193,129... | collective-permute-start | bytes 1228808 | tf_op jit(solution)/shard_map/ppermute | solution.py:54
  26.9 6.4 %all-to-all-done = bf16[8,32,640]{2,1,0:T(8,128)(2,1)S(1)} async-done(((bf16[8,32,640]{2,1,0:T(8,128)(2,1)}), bf16[8,32,640]{2,1,0:T(8,128)(2,1)S(1)}, u32[]{:S(2)}, u32[]{:S(2)}) %all-to-all-start) | async-done | bytes 327712 | tf_op jit(solution)/shard_map/all_to_all | solution.py:370
  33.3 4.9 %collective-permute-start.2 = (bf16[256,640]{1,0:T(8,128)(2,1)S(1)}, bf16[256,640]{1,0:T(8,128)(2,1)S(1)}, u32[]{:S(2)}, u32[]{:S(2)}) collective-permute-start(bf16[256,640]{1,0:T(8,128)(2,1)S(1)} %bitcast.13), channel_id=1, source_target_pairs={{0,3},{1,0},{2,1},{3,2},{4,7},{5,4},{6,5},{7,6},{8,11},{9,8},{10,9... | collective-permute-start | bytes 983048 | tf_op jit(solution)/shard_map/ppermute | solution.py:54
  38.2 2.5 %collective-permute-start.1 = (bf16[256,640]{1,0:T(8,128)(2,1)S(1)}, bf16[256,640]{1,0:T(8,128)(2,1)S(1)}, u32[]{:S(2)}, u32[]{:S(2)}) collective-permute-start(bf16[256,640]{1,0:T(8,128)(2,1)S(1)} %bitcast.14), channel_id=1, source_target_pairs={{0,2},{1,3},{2,0},{3,1},{4,6},{5,7},{6,4},{7,5},{8,10},{9,11},{10,... | collective-permute-start | bytes 983048 | tf_op jit(solution)/shard_map/ppermute | solution.py:54
  40.8 0.0 collective-permute-done.3.p1
  40.8 2.9 %collective-permute-start = (bf16[256,640]{1,0:T(8,128)(2,1)S(1)}, bf16[256,640]{1,0:T(8,128)(2,1)S(1)}, u32[]{:S(2)}, u32[]{:S(2)}) collective-permute-start(bf16[256,640]{1,0:T(8,128)(2,1)S(1)} %bitcast.15), channel_id=1, source_target_pairs={{0,1},{1,2},{2,3},{3,0},{4,5},{5,6},{6,7},{7,4},{8,9},{9,10},{10,1... | collective-permute-start | bytes 983048 | tf_op jit(solution)/shard_map/ppermute | solution.py:54
  43.7 0.0 collective-permute-done.4.p2
  43.7 0.0 collective-permute-done.5.p3
  43.7 1.4 %give.1 = (bf16[1152,128]{1,0:T(8,128)(2,1)S(1)}, bf16[1152,128]{1,0:T(8,128)(2,1)S(1)}, bf16[2048,128]{1,0:T(8,128)(2,1)}) custom-call(s32[4]{0:T(128)S(1)} %pad_add_fusion.place_ref, bf16[1600,128]{1,0:T(8,128)(2,1)S(1)} %get-tuple-element.17.p0, bf16[1600,128]{1,0:T(8,128)(2,1)S(1)} %collective-permute-done.3.p1, ...), custom_call_target="tpu_custom_call" | custom-call | flops 268435456 | bytes 1048576 | tf_op jit(solution)/shard_map/give/pallas_call | solution.py:146
  45.1 1.9 %collective-permute-start.6 = (bf16[1152,128]{1,0:T(8,128)(2,1)S(1)}, bf16[1152,128]{1,0:T(8,128)(2,1)S(1)}, u32[]{:S(2)}, u32[]{:S(2)}) collective-permute-start(bf16[1152,128]{1,0:T(8,128)(2,1)S(1)} %get-tuple-element.21), channel_id=1, source_target_pairs={{0,32},{32,0},{1,33},{33,1},{2,34},{34,2},{3,35},{35,3},{4,36},{36... | collective-permute-start | bytes 884744 | tf_op jit(solution)/shard_map/ppermute | solution.py:50
  47.0 2.4 %collective-permute-start.7 = (bf16[1152,128]{1,0:T(8,128)(2,1)S(1)}, bf16[1152,128]{1,0:T(8,128)(2,1)S(1)}, u32[]{:S(2)}, u32[]{:S(2)}) collective-permute-start(bf16[1152,128]{1,0:T(8,128)(2,1)S(1)} %get-tuple-element.22), channel_id=1, source_target_pairs={{0,32},{32,0},{1,33},{33,1},{2,34},{34,2},{3,35},{35,3},{4,36},{36... | collective-permute-start | bytes 884744 | tf_op jit(solution)/shard_map/ppermute | solution.py:50
  49.4 0.0 collective-permute-done.6.got
  49.5 1.9 %collective-permute-start.8 = (bf16[2048,128]{1,0:T(8,128)(2,1)}, bf16[2048,128]{1,0:T(8,128)(2,1)}, u32[]{:S(2)}, u32[]{:S(2)}) collective-permute-start(bf16[2048,128]{1,0:T(8,128)(2,1)} %get-tuple-element.24), channel_id=1, source_target_pairs={{0,32},{32,0},{1,33},{33,1},{2,34},{34,2},{3,35},{35,3},{4,36},{36... | collective-permute-start | bytes 1572872 | tf_op jit(solution)/shard_map/ppermute | solution.py:50
  51.4 0.0 collective-permute-done.7.more
  51.4 0.2 assemble.1.rows
  51.6 0.0 collective-permute-done.2.w3
  51.6 0.7 collective-permute-done.1.w2
  52.3 4.0 %collective-permute-done.w1 = bf16[256,640]{1,0:T(8,128)(2,1)S(1)} collective-permute-done((bf16[256,640]{1,0:T(8,128)(2,1)S(1)}, bf16[256,640]{1,0:T(8,128)(2,1)S(1)}, u32[]{:S(2)}, u32[]{:S(2)}) %collective-permute-start) | collective-permute-done | bytes 327712 | tf_op jit(solution)/shard_map/ppermute | solution.py:54
  56.4 1.6 %project.1 = (bf16[528,128]{1,0:T(8,128)(2,1)S(1)}, bf16[512,128]{1,0:T(8,128)(2,1)S(1)}, f32[512,128]{1,0:T(8,128)S(1)}, f32[512,128]{1,0:T(8,128)S(1)}, bf16[4,256,128]{2,1,0:T(8,128)(2,1)S(1)}) custom-call(s32[4]{0:T(128)S(1)} %pad_add_fusion.place_ref, bf16[256,640]{1,0:T(8,128)(2,1)S(1)} %bitcast.16, bf16[256,640]{1,0:T(8,128)(2,1)S(1)} %collective-permute-done.w1, ...), custom_call_target="tpu_custom_call" | custom-call | flops 536870912000 | bytes 2097152000 | tf_op jit(solution)/shard_map/project/pallas_call | solution.py:251
  57.9 8.2 %collective-permute-start.9 = (bf16[528,128]{1,0:T(8,128)(2,1)S(1)}, bf16[528,128]{1,0:T(8,128)(2,1)S(1)}, u32[]{:S(2)}, u32[]{:S(2)}) collective-permute-start(bf16[528,128]{1,0:T(8,128)(2,1)S(1)} %get-tuple-element.23.after_ref.q_ref), channel_id=1, source_target_pairs={{0,256},{256,0},{1,257},{257,1},{2,258},{258,2},{3,259},{259,3},{4... | collective-permute-start | bytes 405512 | tf_op jit(solution)/shard_map/ppermute | solution.py:50
  66.2 4.7 %collective-permute-start.13 = (bf16[4,256,128]{2,1,0:T(8,128)(2,1)S(1)}, bf16[4,256,128]{2,1,0:T(8,128)(2,1)S(1)}, u32[]{:S(2)}, u32[]{:S(2)}) collective-permute-start(bf16[4,256,128]{2,1,0:T(8,128)(2,1)S(1)} %get-tuple-element.28.refs_0_.w0), channel_id=1, source_target_pairs={{0,192},{64,0},{128,64},{192,128},{1,193},{65,1},{129,65},{193,129... | collective-permute-start | bytes 786440 | tf_op jit(solution)/shard_map/ppermute | solution.py:54
  70.8 2.7 %collective-permute-start.12 = (bf16[4,256,128]{2,1,0:T(8,128)(2,1)S(1)}, bf16[4,256,128]{2,1,0:T(8,128)(2,1)S(1)}, u32[]{:S(2)}, u32[]{:S(2)}) collective-permute-start(bf16[4,256,128]{2,1,0:T(8,128)(2,1)S(1)} %get-tuple-element.28.refs_0_.w0), channel_id=1, source_target_pairs={{0,128},{64,192},{128,0},{192,64},{1,129},{65,193},{129,1},{193,65... | collective-permute-start | bytes 786440 | tf_op jit(solution)/shard_map/ppermute | solution.py:54
  73.6 2.8 %collective-permute-start.11 = (bf16[4,256,128]{2,1,0:T(8,128)(2,1)S(1)}, bf16[4,256,128]{2,1,0:T(8,128)(2,1)S(1)}, u32[]{:S(2)}, u32[]{:S(2)}) collective-permute-start(bf16[4,256,128]{2,1,0:T(8,128)(2,1)S(1)} %get-tuple-element.28.refs_0_.w0), channel_id=1, source_target_pairs={{0,64},{64,128},{128,192},{192,0},{1,65},{65,129},{129,193},{193,1... | collective-permute-start | bytes 786440 | tf_op jit(solution)/shard_map/ppermute | solution.py:54
  76.4 0.0 collective-permute-done.8.value_ref
  76.4 1.1 near.1.kv_peer
  77.4 0.0 collective-permute-done.9.q_ref
  77.5 2.6 %other.1.refs_4_ = bf16[512,128]{1,0:T(8,128)(2,1)S(1)} custom-call(s32[4]{0:T(128)S(1)} %pad_add_fusion.place_ref, bf16[528,128]{1,0:T(8,128)(2,1)S(1)} %collective-permute-done.9.q_ref, bf16[1600,128]{1,0:T(8,128)(2,1)S(1)} %get-tuple-element.17.p0, bf16[1600,128]{1,0:T(8,128)(2,1)S(1)} %collective-permute-done.3.p1, ...), custom_call_target="tpu_custom_call" | custom-call | flops 1073741824 | bytes 4194304 | tf_op jit(solution)/shard_map/other/pallas_call | solution.py:307
  80.1 7.1 %collective-permute-start.10 = (bf16[512,128]{1,0:T(8,128)(2,1)S(1)}, bf16[512,128]{1,0:T(8,128)(2,1)S(1)}, u32[]{:S(2)}, u32[]{:S(2)}) collective-permute-start(bf16[512,128]{1,0:T(8,128)(2,1)S(1)} %other.1.refs_4_), channel_id=1, source_target_pairs={{0,256},{256,0},{1,257},{257,1},{2,258},{258,2},{3,259},{259,3},{4... | collective-permute-start | bytes 393224 | tf_op jit(solution)/shard_map/ppermute | solution.py:50
  87.2 2.6 %own.1.sum_ref = f32[512,128]{1,0:T(8,128)S(1)} custom-call(s32[4]{0:T(128)S(1)} %pad_add_fusion.place_ref, bf16[528,128]{1,0:T(8,128)(2,1)S(1)} %get-tuple-element.23.after_ref.q_ref, bf16[1600,128]{1,0:T(8,128)(2,1)S(1)} %get-tuple-element.17.p0, bf16[1600,128]{1,0:T(8,128)(2,1)S(1)} %collective-permute-done.3.p1, ...), custom_call_target="tpu_custom_call" | custom-call | flops 1073741824 | bytes 4194304 | tf_op jit(solution)/shard_map/own/pallas_call | solution.py:307
  89.8 0.0 collective-permute-done.13.refs_3_.w3
  89.8 0.0 collective-permute-done.12.refs_2_.w2
  89.8 0.0 collective-permute-done.11.refs_1_.w1
  89.8 1.1 stack.21
  90.9 1.9 %collective-permute-start.14 = (bf16[4,4,256,128]{3,2,1,0:T(8,128)(2,1)}, bf16[4,4,256,128]{3,2,1,0:T(8,128)(2,1)}, u32[]{:S(2)}, u32[]{:S(2)}) collective-permute-start(bf16[4,4,256,128]{3,2,1,0:T(8,128)(2,1)} %stack.21), channel_id=1, source_target_pairs={{0,32},{32,0},{1,33},{33,1},{2,34},{34,2},{3,35},{35,3},{4,36},{36... | collective-permute-start | bytes 3145736 | tf_op jit(solution)/shard_map/ppermute | solution.py:50
  92.8 4.9 %collective-permute-done.10.home_ref = bf16[512,128]{1,0:T(8,128)(2,1)S(1)} collective-permute-done((bf16[512,128]{1,0:T(8,128)(2,1)S(1)}, bf16[512,128]{1,0:T(8,128)(2,1)S(1)}, u32[]{:S(2)}, u32[]{:S(2)}) %collective-permute-start.10) | collective-permute-done | bytes 131104 | tf_op jit(solution)/shard_map/ppermute | solution.py:50
  97.7 0.0 copy-start.3
  97.7 0.8 mix.1
  98.5 9.6 %all_to_all.10.mixed_ref = bf16[8,64,128]{2,1,0:T(8,128)(2,1)S(1)} all-to-all(bf16[8,64,128]{2,1,0:T(8,128)(2,1)S(1)} %mix.1), channel_id=1, replica_groups=mesh['zh'=2,'x'=4,'c'=2,'zl'=8,'y'=4] {'x','c'}, dimensions={0} | all-to-all | bytes 262144 | tf_op jit(solution)/shard_map/all_to_all | solution.py:390
  108.1 0.0 collective-permute-done.14.peer_ref
  108.1 0.0 copy-done.3
  108.1 2.4 %finish.1 = bf16[64,1024]{1,0:T(8,128)(2,1)} custom-call(s32[4]{0:T(128)S(1)} %pad_add_fusion.place_ref, bf16[64,1024]{1,0:T(8,128)(2,1)S(1)} %bitcast.12, bf16[8,64,128]{2,1,0:T(8,128)(2,1)S(1)} %all_to_all.10.mixed_ref, bf16[4,256,128]{2,1,0:T(8,128)(2,1)S(1)} %get-tuple-element.28.refs_0_.w0, bf16[4,256,128]{2,1,0:T(8,128)(2,1)S(1)} %collective-permute-done.11.refs_1_.w1, ...), custom_call_target="tpu_custom_call" | custom-call | tf_op jit(solution)/shard_map/finish/pallas_call | solution.py:354
Async XLA Ops:
  0.0 14.5 %copy-start.6 = (s32[1,64]{1,0:T(1,128)S(1)}, s32[1,64]{1,0:T(1,128)}, u32[]{:S(2)}) copy-start(s32[1,64]{1,0:T(1,128)} %cutoff_ref.1) | copy-start | bytes 772
  0.0 14.5 %copy-start.5 = (s32[1,64]{1,0:T(1,128)S(1)}, s32[1,64]{1,0:T(1,128)}, u32[]{:S(2)}) copy-start(s32[1,64]{1,0:T(1,128)} %user_ref.1) | copy-start | bytes 772
  0.0 14.5 %copy-start.4 = (s32[1,32]{1,0:T(1,128)S(1)}, s32[1,32]{1,0:T(1,128)}, u32[]{:S(2)}) copy-start(s32[1,32]{1,0:T(1,128)} %owner_ref.1) | copy-start | bytes 388
  0.0 14.5 %copy-start.1 = (bf16[1,256,1024]{2,1,0:T(8,128)(2,1)S(1)}, bf16[1,256,1024]{2,1,0:T(8,128)(2,1)}, u32[]{:S(2)}) copy-start(bf16[1,256,1024]{2,1,0:T(8,128)(2,1)} %param.10) | copy-start | bytes 1572868
  0.0 14.5 %copy-start = (bf16[1,256,1024]{2,1,0:T(8,128)(2,1)S(1)}, bf16[1,256,1024]{2,1,0:T(8,128)(2,1)}, u32[]{:S(2)}) copy-start(bf16[1,256,1024]{2,1,0:T(8,128)(2,1)} %param.9) | copy-start | bytes 1572868
  0.0 14.5 %copy-start.2 = (bf16[1,64,1024]{2,1,0:T(8,128)(2,1)S(1)}, bf16[1,64,1024]{2,1,0:T(8,128)(2,1)}, u32[]{:S(2)}) copy-start(bf16[1,64,1024]{2,1,0:T(8,128)(2,1)} %param.8) | copy-start | bytes 393220
  1.8 31.6 %all-to-all-start = ((bf16[8,32,640]{2,1,0:T(8,128)(2,1)}), bf16[8,32,640]{2,1,0:T(8,128)(2,1)S(1)}, u32[]{:S(2)}, u32[]{:S(2)}) async-start(bf16[8,32,640]{2,1,0:T(8,128)(2,1)} %columns.1), calls=%async_computation | async-start | bytes 655360 | tf_op jit(solution)/shard_map/all_to_all | solution.py:370
  15.5 25.3 %collective-permute-start.3 = (bf16[1600,128]{1,0:T(8,128)(2,1)S(1)}, bf16[1600,128]{1,0:T(8,128)(2,1)S(1)}, u32[]{:S(2)}, u32[]{:S(2)}) collective-permute-start(bf16[1600,128]{1,0:T(8,128)(2,1)S(1)} %get-tuple-element.18), channel_id=1, source_target_pairs={{0,64},{64,128},{128,192},{192,0},{1,65},{65,129},{129,193},{193,1... | collective-permute-start | bytes 1228808 | tf_op jit(solution)/shard_map/ppermute | solution.py:54
  18.9 24.8 %collective-permute-start.4 = (bf16[1600,128]{1,0:T(8,128)(2,1)S(1)}, bf16[1600,128]{1,0:T(8,128)(2,1)S(1)}, u32[]{:S(2)}, u32[]{:S(2)}) collective-permute-start(bf16[1600,128]{1,0:T(8,128)(2,1)S(1)} %get-tuple-element.19), channel_id=1, source_target_pairs={{0,128},{64,192},{128,0},{192,64},{1,129},{65,193},{129,1},{193,65... | collective-permute-start | bytes 1228808 | tf_op jit(solution)/shard_map/ppermute | solution.py:54
  23.5 20.1 %collective-permute-start.5 = (bf16[1600,128]{1,0:T(8,128)(2,1)S(1)}, bf16[1600,128]{1,0:T(8,128)(2,1)S(1)}, u32[]{:S(2)}, u32[]{:S(2)}) collective-permute-start(bf16[1600,128]{1,0:T(8,128)(2,1)S(1)} %get-tuple-element.20), channel_id=1, source_target_pairs={{0,192},{64,0},{128,64},{192,128},{1,193},{65,1},{129,65},{193,129... | collective-permute-start | bytes 1228808 | tf_op jit(solution)/shard_map/ppermute | solution.py:54
  33.3 18.3 %collective-permute-start.2 = (bf16[256,640]{1,0:T(8,128)(2,1)S(1)}, bf16[256,640]{1,0:T(8,128)(2,1)S(1)}, u32[]{:S(2)}, u32[]{:S(2)}) collective-permute-start(bf16[256,640]{1,0:T(8,128)(2,1)S(1)} %bitcast.13), channel_id=1, source_target_pairs={{0,3},{1,0},{2,1},{3,2},{4,7},{5,4},{6,5},{7,6},{8,11},{9,8},{10,9... | collective-permute-start | bytes 983048 | tf_op jit(solution)/shard_map/ppermute | solution.py:54
  38.2 14.1 %collective-permute-start.1 = (bf16[256,640]{1,0:T(8,128)(2,1)S(1)}, bf16[256,640]{1,0:T(8,128)(2,1)S(1)}, u32[]{:S(2)}, u32[]{:S(2)}) collective-permute-start(bf16[256,640]{1,0:T(8,128)(2,1)S(1)} %bitcast.14), channel_id=1, source_target_pairs={{0,2},{1,3},{2,0},{3,1},{4,6},{5,7},{6,4},{7,5},{8,10},{9,11},{10,... | collective-permute-start | bytes 983048 | tf_op jit(solution)/shard_map/ppermute | solution.py:54
  40.8 15.6 %collective-permute-start = (bf16[256,640]{1,0:T(8,128)(2,1)S(1)}, bf16[256,640]{1,0:T(8,128)(2,1)S(1)}, u32[]{:S(2)}, u32[]{:S(2)}) collective-permute-start(bf16[256,640]{1,0:T(8,128)(2,1)S(1)} %bitcast.15), channel_id=1, source_target_pairs={{0,1},{1,2},{2,3},{3,0},{4,5},{5,6},{6,7},{7,4},{8,9},{9,10},{10,1... | collective-permute-start | bytes 983048 | tf_op jit(solution)/shard_map/ppermute | solution.py:54
  45.1 4.3 %collective-permute-start.6 = (bf16[1152,128]{1,0:T(8,128)(2,1)S(1)}, bf16[1152,128]{1,0:T(8,128)(2,1)S(1)}, u32[]{:S(2)}, u32[]{:S(2)}) collective-permute-start(bf16[1152,128]{1,0:T(8,128)(2,1)S(1)} %get-tuple-element.21), channel_id=1, source_target_pairs={{0,32},{32,0},{1,33},{33,1},{2,34},{34,2},{3,35},{35,3},{4,36},{36... | collective-permute-start | bytes 884744 | tf_op jit(solution)/shard_map/ppermute | solution.py:50
  47.0 4.4 %collective-permute-start.7 = (bf16[1152,128]{1,0:T(8,128)(2,1)S(1)}, bf16[1152,128]{1,0:T(8,128)(2,1)S(1)}, u32[]{:S(2)}, u32[]{:S(2)}) collective-permute-start(bf16[1152,128]{1,0:T(8,128)(2,1)S(1)} %get-tuple-element.22), channel_id=1, source_target_pairs={{0,32},{32,0},{1,33},{33,1},{2,34},{34,2},{3,35},{35,3},{4,36},{36... | collective-permute-start | bytes 884744 | tf_op jit(solution)/shard_map/ppermute | solution.py:50
  49.5 26.9 %collective-permute-start.8 = (bf16[2048,128]{1,0:T(8,128)(2,1)}, bf16[2048,128]{1,0:T(8,128)(2,1)}, u32[]{:S(2)}, u32[]{:S(2)}) collective-permute-start(bf16[2048,128]{1,0:T(8,128)(2,1)} %get-tuple-element.24), channel_id=1, source_target_pairs={{0,32},{32,0},{1,33},{33,1},{2,34},{34,2},{3,35},{35,3},{4,36},{36... | collective-permute-start | bytes 1572872 | tf_op jit(solution)/shard_map/ppermute | solution.py:50
  57.9 19.5 %collective-permute-start.9 = (bf16[528,128]{1,0:T(8,128)(2,1)S(1)}, bf16[528,128]{1,0:T(8,128)(2,1)S(1)}, u32[]{:S(2)}, u32[]{:S(2)}) collective-permute-start(bf16[528,128]{1,0:T(8,128)(2,1)S(1)} %get-tuple-element.23.after_ref.q_ref), channel_id=1, source_target_pairs={{0,256},{256,0},{1,257},{257,1},{2,258},{258,2},{3,259},{259,3},{4... | collective-permute-start | bytes 405512 | tf_op jit(solution)/shard_map/ppermute | solution.py:50
  66.2 23.6 %collective-permute-start.13 = (bf16[4,256,128]{2,1,0:T(8,128)(2,1)S(1)}, bf16[4,256,128]{2,1,0:T(8,128)(2,1)S(1)}, u32[]{:S(2)}, u32[]{:S(2)}) collective-permute-start(bf16[4,256,128]{2,1,0:T(8,128)(2,1)S(1)} %get-tuple-element.28.refs_0_.w0), channel_id=1, source_target_pairs={{0,192},{64,0},{128,64},{192,128},{1,193},{65,1},{129,65},{193,129... | collective-permute-start | bytes 786440 | tf_op jit(solution)/shard_map/ppermute | solution.py:54
  70.8 19.0 %collective-permute-start.12 = (bf16[4,256,128]{2,1,0:T(8,128)(2,1)S(1)}, bf16[4,256,128]{2,1,0:T(8,128)(2,1)S(1)}, u32[]{:S(2)}, u32[]{:S(2)}) collective-permute-start(bf16[4,256,128]{2,1,0:T(8,128)(2,1)S(1)} %get-tuple-element.28.refs_0_.w0), channel_id=1, source_target_pairs={{0,128},{64,192},{128,0},{192,64},{1,129},{65,193},{129,1},{193,65... | collective-permute-start | bytes 786440 | tf_op jit(solution)/shard_map/ppermute | solution.py:54
  73.6 16.3 %collective-permute-start.11 = (bf16[4,256,128]{2,1,0:T(8,128)(2,1)S(1)}, bf16[4,256,128]{2,1,0:T(8,128)(2,1)S(1)}, u32[]{:S(2)}, u32[]{:S(2)}) collective-permute-start(bf16[4,256,128]{2,1,0:T(8,128)(2,1)S(1)} %get-tuple-element.28.refs_0_.w0), channel_id=1, source_target_pairs={{0,64},{64,128},{128,192},{192,0},{1,65},{65,129},{129,193},{193,1... | collective-permute-start | bytes 786440 | tf_op jit(solution)/shard_map/ppermute | solution.py:54
  80.1 17.6 %collective-permute-start.10 = (bf16[512,128]{1,0:T(8,128)(2,1)S(1)}, bf16[512,128]{1,0:T(8,128)(2,1)S(1)}, u32[]{:S(2)}, u32[]{:S(2)}) collective-permute-start(bf16[512,128]{1,0:T(8,128)(2,1)S(1)} %other.1.refs_4_), channel_id=1, source_target_pairs={{0,256},{256,0},{1,257},{257,1},{2,258},{258,2},{3,259},{259,3},{4... | collective-permute-start | bytes 393224 | tf_op jit(solution)/shard_map/ppermute | solution.py:50
  90.9 17.1 %collective-permute-start.14 = (bf16[4,4,256,128]{3,2,1,0:T(8,128)(2,1)}, bf16[4,4,256,128]{3,2,1,0:T(8,128)(2,1)}, u32[]{:S(2)}, u32[]{:S(2)}) collective-permute-start(bf16[4,4,256,128]{3,2,1,0:T(8,128)(2,1)} %stack.21), channel_id=1, source_target_pairs={{0,32},{32,0},{1,33},{33,1},{2,34},{34,2},{3,35},{35,3},{4,36},{36... | collective-permute-start | bytes 3145736 | tf_op jit(solution)/shard_map/ppermute | solution.py:50
  97.7 10.3 %copy-start.3 = (bf16[1,64,1024]{2,1,0:T(8,128)(2,1)S(1)}, bf16[1,64,1024]{2,1,0:T(8,128)(2,1)}, u32[]{:S(2)}) copy-start(bf16[1,64,1024]{2,1,0:T(8,128)(2,1)} %param.8) | copy-start | bytes 393220

commit v9 on v8

--- a/solution.py
+++ b/solution.py
@@ -221,47 +221,62 @@
     return tags[:, 0:1] * BLOCK, tags[:, 1:2] * 64.0 + tags[:, 2:3]
 
 
-def project_kernel(
-    place_ref, w0, w1, w2, w3, rows, query_ref, gate_ref, den_ref, self_ref, part_ref, w_all
-):
+def project_kernel(place_ref, w0, w1, w2, w3, rows, query_ref, part_ref, w_all):
+    load_weight(place_ref, (w0, w1, w2, w3), w_all, 256, HEAD)
+    query = jnp.dot(rows[:, :D], w_all[...], preferred_element_type=F32)
+    query_ref[0:HALF, :] = silu(query).astype(BF16)
+    labels = [rows[i * 128 : i * 128 + 128, D:].astype(F32).T[0:4, :] for i in range(4)]
+    query_ref[HALF:, :] = jnp.concatenate(labels, axis=0).astype(BF16)
     for s, ref in enumerate((w0, w1, w2, w3)):
         part_ref[(place_ref[3] - s + 4) & 3] = ref[:, 512:]
-    load_weight(place_ref, (w0, w1, w2, w3), w_all, 0, 512)
+
+
+def project(*args):
+    return pl.pallas_call(
+        project_kernel,
+        name="project",
+        out_shape=[
+            jax.ShapeDtypeStruct((HALF + 16, HEAD), BF16),
+            jax.ShapeDtypeStruct((4, 256, HEAD), BF16),
+        ],
+        in_specs=[SMEM] + [VMEM] * 5,
+        out_specs=[VMEM] * 2,
+        scratch_shapes=[pltpu.VMEM((D, HEAD), BF16)],
+        cost_estimate=cost(C_PROJECT),
+        compiler_params=PARAMS,
+    )(*args)
+
+
+def gates_kernel(place_ref, w0, w1, w2, w3, rows, query_ref, gate_ref, den_ref, self_ref, w_all):
+    for first, to in ((0, 0), (384, 256)):
+        count = 256 if first == 0 else 128
+        for s, ref in enumerate((w0, w1, w2, w3)):
+            y = (place_ref[3] - s + 4) & 3
+            for z in range(8):
+                at = pl.ds(pl.multiple_of(z * 128 + y * 32, 32), 32)
+                w_all[at, to : to + count] = ref[pl.ds(z * 32, 32), first : first + count]
     for i in range(2):
         at = pl.ds(i * 256, 256)
         proj = jnp.dot(rows[at, :D], w_all[...], preferred_element_type=F32)
         proj = silu(proj).astype(BF16)
         gate_ref[at, :] = proj[:, 0:128]
-        query_ref[at, :] = proj[:, 256:384]
-        query = proj[:, 256:384].astype(F32)
-        score = jnp.sum(query * proj[:, 384:512].astype(F32), axis=-1, keepdims=True)
+        query = query_ref[at, :].astype(F32)
+        score = jnp.sum(query * proj[:, 256:384].astype(F32), axis=-1, keepdims=True)
         self_ref[at, :] = silu(score * SCALE) * proj[:, 128:256].astype(F32)
-    labels = []
-    for i in range(4):
-        at = pl.ds(i * 128, 128)
-        tags = rows[at, D:].astype(F32)
-        first, last = visible(tags)
-        den_ref[at, :] = jnp.broadcast_to(last - first + 1.0, (128, HEAD))
-        labels.append(tags.T[0:4, :])
-    query_ref[HALF:, :] = jnp.concatenate(labels, axis=0).astype(BF16)
-
-
-def project(*args):
+        first, last = visible(rows[at, D:].astype(F32))
+        den_ref[at, :] = jnp.broadcast_to(last - first + 1.0, (256, HEAD))
+
+
+def gates(*args):
     shape = (HALF, HEAD)
     return pl.pallas_call(
-        project_kernel,
-        name="project",
-        out_shape=[
-            jax.ShapeDtypeStruct((HALF + 16, HEAD), BF16),
-            jax.ShapeDtypeStruct(shape, BF16),
-            jax.ShapeDtypeStruct(shape, F32),
-            jax.ShapeDtypeStruct(shape, F32),
-            jax.ShapeDtypeStruct((4, 256, HEAD), BF16),
-        ],
-        in_specs=[SMEM] + [VMEM] * 5,
-        out_specs=[VMEM] * 5,
-        scratch_shapes=[pltpu.VMEM((D, 512), BF16)],
-        cost_estimate=cost(C_PROJECT),
+        gates_kernel,
+        name="gates",
+        out_shape=[jax.ShapeDtypeStruct(shape, t) for t in (BF16, F32, F32)],
+        in_specs=[SMEM] + [VMEM] * 6,
+        out_specs=[VMEM] * 3,
+        scratch_shapes=[pltpu.VMEM((D, 384), BF16)],
+        cost_estimate=cost(C_OWN),
         compiler_params=PARAMS,
     )(*args)
 
@@ -375,12 +390,13 @@
     got, more, kv_peer = [swap(part, "c") for part in give(place, *packs)]
 
     rows = assemble(*packs, got, more)
-    query, gate, den, self_term, w_part = project(place, *cols, rows)
+    query, w_part = project(place, *cols, rows)
+    gate, den, self_term = gates(place, *cols, rows, query)
     query_other = swap(query, "zh")
     w_part = [along(w_part, "x", s) if s else w_part for s in range(4)]
     kv_peer = near(kv_peer, query)
 
-    away = attend("other", BF16, place, query_other, *packs, kv_peer, self_term)
+    away = attend("other", BF16, place, query_other, *packs, kv_peer, query_other)
     home = swap(away, "zh")
     sums = attend("own", F32, place, query, *packs, kv_peer, self_term)
     w_own = stack(*w_part, away)

time: 111 us -> 111 us (level)
  the two profiles are of different devices: /device:TPU:32 before, /device:TPU:40 now
where the time goes in v9:
time: 111 us; the launch traced here: 110 us
  starting transfers between devices  68.2 us (61%)
  Pallas kernels  17.4 us (16%)
  waiting for transfers between devices  13.9 us (13%)
  blocking collectives  10.5 us (9%)
    ppermute x9, starting transfers between devices, along(): return lax.ppermute(value, axis, [(i, (i + steps) % 4) for i in range(4)])  32.2 us
    ppermute x6, starting transfers between devices, swap(): return lax.ppermute(value, axis, [(0, 1), (1, 0)])  23.4 us
    all_to_all x1, starting transfers between devices, body(): cols = lax.all_to_all(cols, 'zl', 0, 0, tiled=True).reshape(256, 640)  12.6 us
    all_to_all x1, blocking collectives, body(): mixed = lax.all_to_all(mixed, LOCAL, 0, 0, tiled=True)  10.5 us
    all_to_all x1, waiting for transfers between devices, body(): cols = lax.all_to_all(cols, 'zl', 0, 0, tiled=True).reshape(256, 640)  6.42 us
    ppermute x6, waiting for transfers between devices, swap(): return lax.ppermute(value, axis, [(0, 1), (1, 0)])  5.46 us
    pallas_call x2, Pallas kernels, attend(): pl.pallas_call(attend_kernel, name=name, out_shape=jax.ShapeDtypeStruct((...  5.25 us
    pallas_call x1, Pallas kernels, finish(): pl.pallas_call(finish_kernel, name='finish', out_shape=jax.ShapeDtypeStru...  2.43 us
  transfers between devices with their start and end apart: 16, of which 4 were waited for; matrix products, arithmetic and copies ran while one was open for 0% of the time, Pallas kernels for 12%

profile of v9, /device:TPU:40, one launch (start us, length us, event | category | flops | bytes accessed | tf_op | source)
XLA Modules:
  0.0 110.4 jit_solution(9227829384490998305)
XLA Ops:
  0.0 0.0 copy-start.6
  0.0 0.0 copy-start.5
  0.0 0.0 copy-start.4
  0.0 0.0 copy-start.1
  0.0 0.0 copy-start
  0.0 0.0 copy-start.2
  0.0 1.7 %columns.1 = bf16[8,32,640]{2,1,0:T(8,128)(2,1)} custom-call(bf16[32,4096]{1,0:T(8,128)(2,1)} %in_ref.1, bf16[32,1024]{1,0:T(8,128)(2,1)} %out_w_ref.1), custom_call_target="tpu_custom_call" | custom-call | tf_op jit(solution)/shard_map/columns/pallas_call | solution.py:76
  1.8 12.6 %all-to-all-start = ((bf16[8,32,640]{2,1,0:T(8,128)(2,1)}), bf16[8,32,640]{2,1,0:T(8,128)(2,1)S(1)}, u32[]{:S(2)}, u32[]{:S(2)}) async-start(bf16[8,32,640]{2,1,0:T(8,128)(2,1)} %columns.1), calls=%async_computation | async-start | bytes 655360 | tf_op jit(solution)/shard_map/all_to_all | solution.py:385
  14.4 0.1 pad_add_fusion.place_ref
  14.5 0.0 copy-done.6
  14.5 0.0 copy-done.5
  14.5 0.0 copy-done.4
  14.5 0.0 copy-done.1
  14.5 0.0 copy-done
  14.5 0.0 copy-done.2
  14.5 1.0 packets.1
  15.5 3.4 %collective-permute-start.3 = (bf16[1600,128]{1,0:T(8,128)(2,1)S(1)}, bf16[1600,128]{1,0:T(8,128)(2,1)S(1)}, u32[]{:S(2)}, u32[]{:S(2)}) collective-permute-start(bf16[1600,128]{1,0:T(8,128)(2,1)S(1)} %get-tuple-element.18), channel_id=1, source_target_pairs={{0,64},{64,128},{128,192},{192,0},{1,65},{65,129},{129,193},{193,1... | collective-permute-start | bytes 1228808 | tf_op jit(solution)/shard_map/ppermute | solution.py:54
  18.9 4.6 %collective-permute-start.4 = (bf16[1600,128]{1,0:T(8,128)(2,1)S(1)}, bf16[1600,128]{1,0:T(8,128)(2,1)S(1)}, u32[]{:S(2)}, u32[]{:S(2)}) collective-permute-start(bf16[1600,128]{1,0:T(8,128)(2,1)S(1)} %get-tuple-element.19), channel_id=1, source_target_pairs={{0,128},{64,192},{128,0},{192,64},{1,129},{65,193},{129,1},{193,65... | collective-permute-start | bytes 1228808 | tf_op jit(solution)/shard_map/ppermute | solution.py:54
  23.5 3.3 %collective-permute-start.5 = (bf16[1600,128]{1,0:T(8,128)(2,1)S(1)}, bf16[1600,128]{1,0:T(8,128)(2,1)S(1)}, u32[]{:S(2)}, u32[]{:S(2)}) collective-permute-start(bf16[1600,128]{1,0:T(8,128)(2,1)S(1)} %get-tuple-element.20), channel_id=1, source_target_pairs={{0,192},{64,0},{128,64},{192,128},{1,193},{65,1},{129,65},{193,129... | collective-permute-start | bytes 1228808 | tf_op jit(solution)/shard_map/ppermute | solution.py:54
  26.9 6.4 %all-to-all-done = bf16[8,32,640]{2,1,0:T(8,128)(2,1)S(1)} async-done(((bf16[8,32,640]{2,1,0:T(8,128)(2,1)}), bf16[8,32,640]{2,1,0:T(8,128)(2,1)S(1)}, u32[]{:S(2)}, u32[]{:S(2)}) %all-to-all-start) | async-done | bytes 327712 | tf_op jit(solution)/shard_map/all_to_all | solution.py:385
  33.3 2.3 %collective-permute-start.2 = (bf16[256,640]{1,0:T(8,128)(2,1)S(1)}, bf16[256,640]{1,0:T(8,128)(2,1)S(1)}, u32[]{:S(2)}, u32[]{:S(2)}) collective-permute-start(bf16[256,640]{1,0:T(8,128)(2,1)S(1)} %bitcast.13), channel_id=1, source_target_pairs={{0,3},{1,0},{2,1},{3,2},{4,7},{5,4},{6,5},{7,6},{8,11},{9,8},{10,9... | collective-permute-start | bytes 983048 | tf_op jit(solution)/shard_map/ppermute | solution.py:54
  35.7 4.5 %collective-permute-start.1 = (bf16[256,640]{1,0:T(8,128)(2,1)S(1)}, bf16[256,640]{1,0:T(8,128)(2,1)S(1)}, u32[]{:S(2)}, u32[]{:S(2)}) collective-permute-start(bf16[256,640]{1,0:T(8,128)(2,1)S(1)} %bitcast.14), channel_id=1, source_target_pairs={{0,2},{1,3},{2,0},{3,1},{4,6},{5,7},{6,4},{7,5},{8,10},{9,11},{10,... | collective-permute-start | bytes 983048 | tf_op jit(solution)/shard_map/ppermute | solution.py:54
  40.2 0.0 collective-permute-done.3.p1
  40.2 3.8 %collective-permute-start = (bf16[256,640]{1,0:T(8,128)(2,1)S(1)}, bf16[256,640]{1,0:T(8,128)(2,1)S(1)}, u32[]{:S(2)}, u32[]{:S(2)}) collective-permute-start(bf16[256,640]{1,0:T(8,128)(2,1)S(1)} %bitcast.15), channel_id=1, source_target_pairs={{0,1},{1,2},{2,3},{3,0},{4,5},{5,6},{6,7},{7,4},{8,9},{9,10},{10,1... | collective-permute-start | bytes 983048 | tf_op jit(solution)/shard_map/ppermute | solution.py:54
  44.0 0.0 collective-permute-done.4.p2
  44.0 0.0 collective-permute-done.5.p3
  44.0 1.4 %give.1 = (bf16[1152,128]{1,0:T(8,128)(2,1)S(1)}, bf16[1152,128]{1,0:T(8,128)(2,1)S(1)}, bf16[2048,128]{1,0:T(8,128)(2,1)}) custom-call(s32[4]{0:T(128)S(1)} %pad_add_fusion.place_ref, bf16[1600,128]{1,0:T(8,128)(2,1)S(1)} %get-tuple-element.17.p0, bf16[1600,128]{1,0:T(8,128)(2,1)S(1)} %collective-permute-done.3.p1, ...), custom_call_target="tpu_custom_call" | custom-call | flops 268435456 | bytes 1048576 | tf_op jit(solution)/shard_map/give/pallas_call | solution.py:146
  45.4 1.9 %collective-permute-start.6 = (bf16[1152,128]{1,0:T(8,128)(2,1)S(1)}, bf16[1152,128]{1,0:T(8,128)(2,1)S(1)}, u32[]{:S(2)}, u32[]{:S(2)}) collective-permute-start(bf16[1152,128]{1,0:T(8,128)(2,1)S(1)} %get-tuple-element.21), channel_id=1, source_target_pairs={{0,32},{32,0},{1,33},{33,1},{2,34},{34,2},{3,35},{35,3},{4,36},{36... | collective-permute-start | bytes 884744 | tf_op jit(solution)/shard_map/ppermute | solution.py:50
  47.4 2.4 %collective-permute-start.7 = (bf16[1152,128]{1,0:T(8,128)(2,1)S(1)}, bf16[1152,128]{1,0:T(8,128)(2,1)S(1)}, u32[]{:S(2)}, u32[]{:S(2)}) collective-permute-start(bf16[1152,128]{1,0:T(8,128)(2,1)S(1)} %get-tuple-element.22), channel_id=1, source_target_pairs={{0,32},{32,0},{1,33},{33,1},{2,34},{34,2},{3,35},{35,3},{4,36},{36... | collective-permute-start | bytes 884744 | tf_op jit(solution)/shard_map/ppermute | solution.py:50
  49.8 0.0 collective-permute-done.6.got
  49.8 1.9 %collective-permute-start.8 = (bf16[2048,128]{1,0:T(8,128)(2,1)}, bf16[2048,128]{1,0:T(8,128)(2,1)}, u32[]{:S(2)}, u32[]{:S(2)}) collective-permute-start(bf16[2048,128]{1,0:T(8,128)(2,1)} %get-tuple-element.24), channel_id=1, source_target_pairs={{0,32},{32,0},{1,33},{33,1},{2,34},{34,2},{3,35},{35,3},{4,36},{36... | collective-permute-start | bytes 1572872 | tf_op jit(solution)/shard_map/ppermute | solution.py:50
  51.7 0.0 collective-permute-done.7.more
  51.7 0.2 assemble.1.rows
  51.9 0.0 collective-permute-done.2.w3
  51.9 0.0 collective-permute-done.1.w2
  52.0 2.0 %collective-permute-done.w1 = bf16[256,640]{1,0:T(8,128)(2,1)S(1)} collective-permute-done((bf16[256,640]{1,0:T(8,128)(2,1)S(1)}, bf16[256,640]{1,0:T(8,128)(2,1)S(1)}, u32[]{:S(2)}, u32[]{:S(2)}) %collective-permute-start) | collective-permute-done | bytes 327712 | tf_op jit(solution)/shard_map/ppermute | solution.py:54
  53.9 1.0 project.1
  54.9 8.2 %collective-permute-start.9 = (bf16[528,128]{1,0:T(8,128)(2,1)S(1)}, bf16[528,128]{1,0:T(8,128)(2,1)S(1)}, u32[]{:S(2)}, u32[]{:S(2)}) collective-permute-start(bf16[528,128]{1,0:T(8,128)(2,1)S(1)} %get-tuple-element.23.after_ref.query_ref.q_ref), channel_id=1, source_target_pairs={{0,256},{256,0},{1,257},{257,1},{2,258},{258,2},{3,259},{259,3},{4... | collective-permute-start | bytes 405512 | tf_op jit(solution)/shard_map/ppermute | solution.py:50
  63.2 4.7 %collective-permute-start.13 = (bf16[4,256,128]{2,1,0:T(8,128)(2,1)S(1)}, bf16[4,256,128]{2,1,0:T(8,128)(2,1)S(1)}, u32[]{:S(2)}, u32[]{:S(2)}) collective-permute-start(bf16[4,256,128]{2,1,0:T(8,128)(2,1)S(1)} %get-tuple-element.28.refs_0_.w0), channel_id=1, source_target_pairs={{0,192},{64,0},{128,64},{192,128},{1,193},{65,1},{129,65},{193,129... | collective-permute-start | bytes 786440 | tf_op jit(solution)/shard_map/ppermute | solution.py:54
  67.8 2.7 %collective-permute-start.12 = (bf16[4,256,128]{2,1,0:T(8,128)(2,1)S(1)}, bf16[4,256,128]{2,1,0:T(8,128)(2,1)S(1)}, u32[]{:S(2)}, u32[]{:S(2)}) collective-permute-start(bf16[4,256,128]{2,1,0:T(8,128)(2,1)S(1)} %get-tuple-element.28.refs_0_.w0), channel_id=1, source_target_pairs={{0,128},{64,192},{128,0},{192,64},{1,129},{65,193},{129,1},{193,65... | collective-permute-start | bytes 786440 | tf_op jit(solution)/shard_map/ppermute | solution.py:54
  70.6 2.8 %collective-permute-start.11 = (bf16[4,256,128]{2,1,0:T(8,128)(2,1)S(1)}, bf16[4,256,128]{2,1,0:T(8,128)(2,1)S(1)}, u32[]{:S(2)}, u32[]{:S(2)}) collective-permute-start(bf16[4,256,128]{2,1,0:T(8,128)(2,1)S(1)} %get-tuple-element.28.refs_0_.w0), channel_id=1, source_target_pairs={{0,64},{64,128},{128,192},{192,0},{1,65},{65,129},{129,193},{193,1... | collective-permute-start | bytes 786440 | tf_op jit(solution)/shard_map/ppermute | solution.py:54
  73.4 0.0 collective-permute-done.8.value_ref
  73.4 1.1 near.1.kv_peer
  74.5 1.5 %collective-permute-done.9.q_ref.plus_ref = bf16[528,128]{1,0:T(8,128)(2,1)S(1)} collective-permute-done((bf16[528,128]{1,0:T(8,128)(2,1)S(1)}, bf16[528,128]{1,0:T(8,128)(2,1)S(1)}, u32[]{:S(2)}, u32[]{:S(2)}) %collective-permute-start.9) | collective-permute-done | bytes 135200 | tf_op jit(solution)/shard_map/ppermute | solution.py:50
  75.9 2.6 %other.1.refs_4_ = bf16[512,128]{1,0:T(8,128)(2,1)S(1)} custom-call(s32[4]{0:T(128)S(1)} %pad_add_fusion.place_ref, bf16[528,128]{1,0:T(8,128)(2,1)S(1)} %collective-permute-done.9.q_ref.plus_ref, bf16[1600,128]{1,0:T(8,128)(2,1)S(1)} %get-tuple-element.17.p0, bf16[1600,128]{1,0:T(8,128)(2,1)S(1)} %collective-permute-done.3.p1, ...), custom_call_target="tpu_custom_call" | custom-call | flops 1073741824 | bytes 4194304 | tf_op jit(solution)/shard_map/other/pallas_call | solution.py:322
  78.6 7.0 %collective-permute-start.10 = (bf16[512,128]{1,0:T(8,128)(2,1)S(1)}, bf16[512,128]{1,0:T(8,128)(2,1)S(1)}, u32[]{:S(2)}, u32[]{:S(2)}) collective-permute-start(bf16[512,128]{1,0:T(8,128)(2,1)S(1)} %other.1.refs_4_), channel_id=1, source_target_pairs={{0,256},{256,0},{1,257},{257,1},{2,258},{258,2},{3,259},{259,3},{4... | collective-permute-start | bytes 393224 | tf_op jit(solution)/shard_map/ppermute | solution.py:50
  85.5 1.5 %gates.1 = (bf16[512,128]{1,0:T(8,128)(2,1)S(1)}, f32[512,128]{1,0:T(8,128)S(1)}, f32[512,128]{1,0:T(8,128)S(1)}) custom-call(s32[4]{0:T(128)S(1)} %pad_add_fusion.place_ref, bf16[256,640]{1,0:T(8,128)(2,1)S(1)} %bitcast.17, bf16[256,640]{1,0:T(8,128)(2,1)S(1)} %collective-permute-done.w1, bf16[256,640]{1,0:T(8,128)(2,1)S(1)} %collective-permute-done.1.w2, ...), custom_call_target="tpu_custom_call" | custom-call | flops 1073741824 | bytes 4194304 | tf_op jit(solution)/shard_map/gates/pallas_call | solution.py:272
  87.0 2.6 %own.1.sum_ref = f32[512,128]{1,0:T(8,128)S(1)} custom-call(s32[4]{0:T(128)S(1)} %pad_add_fusion.place_ref, bf16[528,128]{1,0:T(8,128)(2,1)S(1)} %get-tuple-element.23.after_ref.query_ref.q_ref, bf16[1600,128]{1,0:T(8,128)(2,1)S(1)} %get-tuple-element.17.p0, bf16[1600,128]{1,0:T(8,128)(2,1)S(1)} %collective-permute-done.3.p1, ...), custom_call_target="tpu_custom_call" | custom-call | flops 1073741824 | bytes 4194304 | tf_op jit(solution)/shard_map/own/pallas_call | solution.py:322
  89.7 0.0 collective-permute-done.13.refs_3_.w3
  89.7 0.0 collective-permute-done.12.refs_2_.w2
  89.7 0.0 collective-permute-done.11.refs_1_.w1
  89.7 1.1 stack.21
  90.8 1.9 %collective-permute-start.14 = (bf16[4,4,256,128]{3,2,1,0:T(8,128)(2,1)}, bf16[4,4,256,128]{3,2,1,0:T(8,128)(2,1)}, u32[]{:S(2)}, u32[]{:S(2)}) collective-permute-start(bf16[4,4,256,128]{3,2,1,0:T(8,128)(2,1)} %stack.21), channel_id=1, source_target_pairs={{0,32},{32,0},{1,33},{33,1},{2,34},{34,2},{3,35},{35,3},{4,36},{36... | collective-permute-start | bytes 3145736 | tf_op jit(solution)/shard_map/ppermute | solution.py:50
  92.7 4.0 %collective-permute-done.10.home_ref = bf16[512,128]{1,0:T(8,128)(2,1)S(1)} collective-permute-done((bf16[512,128]{1,0:T(8,128)(2,1)S(1)}, bf16[512,128]{1,0:T(8,128)(2,1)S(1)}, u32[]{:S(2)}, u32[]{:S(2)}) %collective-permute-start.10) | collective-permute-done | bytes 131104 | tf_op jit(solution)/shard_map/ppermute | solution.py:50
  96.7 0.0 copy-start.3
  96.7 0.8 mix.1
  97.5 10.5 %all_to_all.10.mixed_ref = bf16[8,64,128]{2,1,0:T(8,128)(2,1)S(1)} all-to-all(bf16[8,64,128]{2,1,0:T(8,128)(2,1)S(1)} %mix.1), channel_id=1, replica_groups=mesh['zh'=2,'x'=4,'c'=2,'zl'=8,'y'=4] {'x','c'}, dimensions={0} | all-to-all | bytes 262144 | tf_op jit(solution)/shard_map/all_to_all | solution.py:406
  108.0 0.0 collective-permute-done.14.peer_ref
  108.0 0.0 copy-done.3
  108.0 2.4 %finish.1 = bf16[64,1024]{1,0:T(8,128)(2,1)} custom-call(s32[4]{0:T(128)S(1)} %pad_add_fusion.place_ref, bf16[64,1024]{1,0:T(8,128)(2,1)S(1)} %bitcast.12, bf16[8,64,128]{2,1,0:T(8,128)(2,1)S(1)} %all_to_all.10.mixed_ref, bf16[4,256,128]{2,1,0:T(8,128)(2,1)S(1)} %get-tuple-element.28.refs_0_.w0, bf16[4,256,128]{2,1,0:T(8,128)(2,1)S(1)} %collective-permute-done.11.refs_1_.w1, ...), custom_call_target="tpu_custom_call" | custom-call | tf_op jit(solution)/shard_map/finish/pallas_call | solution.py:369
Async XLA Ops:
  0.0 14.5 %copy-start.6 = (s32[1,64]{1,0:T(1,128)S(1)}, s32[1,64]{1,0:T(1,128)}, u32[]{:S(2)}) copy-start(s32[1,64]{1,0:T(1,128)} %cutoff_ref.1) | copy-start | bytes 772
  0.0 14.5 %copy-start.5 = (s32[1,64]{1,0:T(1,128)S(1)}, s32[1,64]{1,0:T(1,128)}, u32[]{:S(2)}) copy-start(s32[1,64]{1,0:T(1,128)} %user_ref.1) | copy-start | bytes 772
  0.0 14.5 %copy-start.4 = (s32[1,32]{1,0:T(1,128)S(1)}, s32[1,32]{1,0:T(1,128)}, u32[]{:S(2)}) copy-start(s32[1,32]{1,0:T(1,128)} %owner_ref.1) | copy-start | bytes 388
  0.0 14.5 %copy-start.1 = (bf16[1,256,1024]{2,1,0:T(8,128)(2,1)S(1)}, bf16[1,256,1024]{2,1,0:T(8,128)(2,1)}, u32[]{:S(2)}) copy-start(bf16[1,256,1024]{2,1,0:T(8,128)(2,1)} %param.10) | copy-start | bytes 1572868
  0.0 14.5 %copy-start = (bf16[1,256,1024]{2,1,0:T(8,128)(2,1)S(1)}, bf16[1,256,1024]{2,1,0:T(8,128)(2,1)}, u32[]{:S(2)}) copy-start(bf16[1,256,1024]{2,1,0:T(8,128)(2,1)} %param.9) | copy-start | bytes 1572868
  0.0 14.5 %copy-start.2 = (bf16[1,64,1024]{2,1,0:T(8,128)(2,1)S(1)}, bf16[1,64,1024]{2,1,0:T(8,128)(2,1)}, u32[]{:S(2)}) copy-start(bf16[1,64,1024]{2,1,0:T(8,128)(2,1)} %param.8) | copy-start | bytes 393220
  1.8 31.6 %all-to-all-start = ((bf16[8,32,640]{2,1,0:T(8,128)(2,1)}), bf16[8,32,640]{2,1,0:T(8,128)(2,1)S(1)}, u32[]{:S(2)}, u32[]{:S(2)}) async-start(bf16[8,32,640]{2,1,0:T(8,128)(2,1)} %columns.1), calls=%async_computation | async-start | bytes 655360 | tf_op jit(solution)/shard_map/all_to_all | solution.py:385
  15.5 24.7 %collective-permute-start.3 = (bf16[1600,128]{1,0:T(8,128)(2,1)S(1)}, bf16[1600,128]{1,0:T(8,128)(2,1)S(1)}, u32[]{:S(2)}, u32[]{:S(2)}) collective-permute-start(bf16[1600,128]{1,0:T(8,128)(2,1)S(1)} %get-tuple-element.18), channel_id=1, source_target_pairs={{0,64},{64,128},{128,192},{192,0},{1,65},{65,129},{129,193},{193,1... | collective-permute-start | bytes 1228808 | tf_op jit(solution)/shard_map/ppermute | solution.py:54
  18.9 25.1 %collective-permute-start.4 = (bf16[1600,128]{1,0:T(8,128)(2,1)S(1)}, bf16[1600,128]{1,0:T(8,128)(2,1)S(1)}, u32[]{:S(2)}, u32[]{:S(2)}) collective-permute-start(bf16[1600,128]{1,0:T(8,128)(2,1)S(1)} %get-tuple-element.19), channel_id=1, source_target_pairs={{0,128},{64,192},{128,0},{192,64},{1,129},{65,193},{129,1},{193,65... | collective-permute-start | bytes 1228808 | tf_op jit(solution)/shard_map/ppermute | solution.py:54
  23.5 20.5 %collective-permute-start.5 = (bf16[1600,128]{1,0:T(8,128)(2,1)S(1)}, bf16[1600,128]{1,0:T(8,128)(2,1)S(1)}, u32[]{:S(2)}, u32[]{:S(2)}) collective-permute-start(bf16[1600,128]{1,0:T(8,128)(2,1)S(1)} %get-tuple-element.20), channel_id=1, source_target_pairs={{0,192},{64,0},{128,64},{192,128},{1,193},{65,1},{129,65},{193,129... | collective-permute-start | bytes 1228808 | tf_op jit(solution)/shard_map/ppermute | solution.py:54
  33.3 18.6 %collective-permute-start.2 = (bf16[256,640]{1,0:T(8,128)(2,1)S(1)}, bf16[256,640]{1,0:T(8,128)(2,1)S(1)}, u32[]{:S(2)}, u32[]{:S(2)}) collective-permute-start(bf16[256,640]{1,0:T(8,128)(2,1)S(1)} %bitcast.13), channel_id=1, source_target_pairs={{0,3},{1,0},{2,1},{3,2},{4,7},{5,4},{6,5},{7,6},{8,11},{9,8},{10,9... | collective-permute-start | bytes 983048 | tf_op jit(solution)/shard_map/ppermute | solution.py:54
  35.7 16.3 %collective-permute-start.1 = (bf16[256,640]{1,0:T(8,128)(2,1)S(1)}, bf16[256,640]{1,0:T(8,128)(2,1)S(1)}, u32[]{:S(2)}, u32[]{:S(2)}) collective-permute-start(bf16[256,640]{1,0:T(8,128)(2,1)S(1)} %bitcast.14), channel_id=1, source_target_pairs={{0,2},{1,3},{2,0},{3,1},{4,6},{5,7},{6,4},{7,5},{8,10},{9,11},{10,... | collective-permute-start | bytes 983048 | tf_op jit(solution)/shard_map/ppermute | solution.py:54
  40.2 13.7 %collective-permute-start = (bf16[256,640]{1,0:T(8,128)(2,1)S(1)}, bf16[256,640]{1,0:T(8,128)(2,1)S(1)}, u32[]{:S(2)}, u32[]{:S(2)}) collective-permute-start(bf16[256,640]{1,0:T(8,128)(2,1)S(1)} %bitcast.15), channel_id=1, source_target_pairs={{0,1},{1,2},{2,3},{3,0},{4,5},{5,6},{6,7},{7,4},{8,9},{9,10},{10,1... | collective-permute-start | bytes 983048 | tf_op jit(solution)/shard_map/ppermute | solution.py:54
  45.4 4.3 %collective-permute-start.6 = (bf16[1152,128]{1,0:T(8,128)(2,1)S(1)}, bf16[1152,128]{1,0:T(8,128)(2,1)S(1)}, u32[]{:S(2)}, u32[]{:S(2)}) collective-permute-start(bf16[1152,128]{1,0:T(8,128)(2,1)S(1)} %get-tuple-element.21), channel_id=1, source_target_pairs={{0,32},{32,0},{1,33},{33,1},{2,34},{34,2},{3,35},{35,3},{4,36},{36... | collective-permute-start | bytes 884744 | tf_op jit(solution)/shard_map/ppermute | solution.py:50
  47.4 4.4 %collective-permute-start.7 = (bf16[1152,128]{1,0:T(8,128)(2,1)S(1)}, bf16[1152,128]{1,0:T(8,128)(2,1)S(1)}, u32[]{:S(2)}, u32[]{:S(2)}) collective-permute-start(bf16[1152,128]{1,0:T(8,128)(2,1)S(1)} %get-tuple-element.22), channel_id=1, source_target_pairs={{0,32},{32,0},{1,33},{33,1},{2,34},{34,2},{3,35},{35,3},{4,36},{36... | collective-permute-start | bytes 884744 | tf_op jit(solution)/shard_map/ppermute | solution.py:50
  49.8 23.6 %collective-permute-start.8 = (bf16[2048,128]{1,0:T(8,128)(2,1)}, bf16[2048,128]{1,0:T(8,128)(2,1)}, u32[]{:S(2)}, u32[]{:S(2)}) collective-permute-start(bf16[2048,128]{1,0:T(8,128)(2,1)} %get-tuple-element.24), channel_id=1, source_target_pairs={{0,32},{32,0},{1,33},{33,1},{2,34},{34,2},{3,35},{35,3},{4,36},{36... | collective-permute-start | bytes 1572872 | tf_op jit(solution)/shard_map/ppermute | solution.py:50
  54.9 21.0 %collective-permute-start.9 = (bf16[528,128]{1,0:T(8,128)(2,1)S(1)}, bf16[528,128]{1,0:T(8,128)(2,1)S(1)}, u32[]{:S(2)}, u32[]{:S(2)}) collective-permute-start(bf16[528,128]{1,0:T(8,128)(2,1)S(1)} %get-tuple-element.23.after_ref.query_ref.q_ref), channel_id=1, source_target_pairs={{0,256},{256,0},{1,257},{257,1},{2,258},{258,2},{3,259},{259,3},{4... | collective-permute-start | bytes 405512 | tf_op jit(solution)/shard_map/ppermute | solution.py:50
  63.2 26.5 %collective-permute-start.13 = (bf16[4,256,128]{2,1,0:T(8,128)(2,1)S(1)}, bf16[4,256,128]{2,1,0:T(8,128)(2,1)S(1)}, u32[]{:S(2)}, u32[]{:S(2)}) collective-permute-start(bf16[4,256,128]{2,1,0:T(8,128)(2,1)S(1)} %get-tuple-element.28.refs_0_.w0), channel_id=1, source_target_pairs={{0,192},{64,0},{128,64},{192,128},{1,193},{65,1},{129,65},{193,129... | collective-permute-start | bytes 786440 | tf_op jit(solution)/shard_map/ppermute | solution.py:54
  67.8 21.8 %collective-permute-start.12 = (bf16[4,256,128]{2,1,0:T(8,128)(2,1)S(1)}, bf16[4,256,128]{2,1,0:T(8,128)(2,1)S(1)}, u32[]{:S(2)}, u32[]{:S(2)}) collective-permute-start(bf16[4,256,128]{2,1,0:T(8,128)(2,1)S(1)} %get-tuple-element.28.refs_0_.w0), channel_id=1, source_target_pairs={{0,128},{64,192},{128,0},{192,64},{1,129},{65,193},{129,1},{193,65... | collective-permute-start | bytes 786440 | tf_op jit(solution)/shard_map/ppermute | solution.py:54
  70.6 19.1 %collective-permute-start.11 = (bf16[4,256,128]{2,1,0:T(8,128)(2,1)S(1)}, bf16[4,256,128]{2,1,0:T(8,128)(2,1)S(1)}, u32[]{:S(2)}, u32[]{:S(2)}) collective-permute-start(bf16[4,256,128]{2,1,0:T(8,128)(2,1)S(1)} %get-tuple-element.28.refs_0_.w0), channel_id=1, source_target_pairs={{0,64},{64,128},{128,192},{192,0},{1,65},{65,129},{129,193},{193,1... | collective-permute-start | bytes 786440 | tf_op jit(solution)/shard_map/ppermute | solution.py:54
  78.6 18.1 %collective-permute-start.10 = (bf16[512,128]{1,0:T(8,128)(2,1)S(1)}, bf16[512,128]{1,0:T(8,128)(2,1)S(1)}, u32[]{:S(2)}, u32[]{:S(2)}) collective-permute-start(bf16[512,128]{1,0:T(8,128)(2,1)S(1)} %other.1.refs_4_), channel_id=1, source_target_pairs={{0,256},{256,0},{1,257},{257,1},{2,258},{258,2},{3,259},{259,3},{4... | collective-permute-start | bytes 393224 | tf_op jit(solution)/shard_map/ppermute | solution.py:50
  90.8 17.2 %collective-permute-start.14 = (bf16[4,4,256,128]{3,2,1,0:T(8,128)(2,1)}, bf16[4,4,256,128]{3,2,1,0:T(8,128)(2,1)}, u32[]{:S(2)}, u32[]{:S(2)}) collective-permute-start(bf16[4,4,256,128]{3,2,1,0:T(8,128)(2,1)} %stack.21), channel_id=1, source_target_pairs={{0,32},{32,0},{1,33},{33,1},{2,34},{34,2},{3,35},{35,3},{4,36},{36... | collective-permute-start | bytes 3145736 | tf_op jit(solution)/shard_map/ppermute | solution.py:50
  96.7 11.3 %copy-start.3 = (bf16[1,64,1024]{2,1,0:T(8,128)(2,1)S(1)}, bf16[1,64,1024]{2,1,0:T(8,128)(2,1)}, u32[]{:S(2)}) copy-start(bf16[1,64,1024]{2,1,0:T(8,128)(2,1)} %param.8) | copy-start | bytes 393220
